TPU v7x, 32 devices: a whole 2x2x4 slice. The times are simulated.
32 devices in a mesh: stem: 2 (over y), tm: 16 (over z, x, core).
Axes of the slice: x: 2, y: 2, z: 4, core: 2. Of those that a mesh axis runs over, the one named last changes fastest.
Arguments:
- frames: bfloat16 [2, 6144, 1024], P('stem', 'tm'), may hold values from -6 to 6
- timestep: int32 [2], replicated, may hold values from 0 to 49, as said below
- modulation: float32 [50, 6, 1024], replicated, may hold values from -3 to 3
- qkv_self: bfloat16 [1024, 1536], replicated, may hold values from -0.1875 to 0.1875
- out_self: bfloat16 [512, 1024], replicated, may hold values from -0.25 to 0.25
- qk_gain_self: float32 [2, 64], replicated, may hold values from 1.5 to 6
- qkv_cross: bfloat16 [1024, 1536], replicated, may hold values from -0.1875 to 0.1875
- out_cross: bfloat16 [512, 1024], replicated, may hold values from -0.25 to 0.25
- qk_gain_cross: float32 [2, 64], replicated, may hold values from 1.5 to 6
Outputs:
- layer_out: bfloat16 [2, 6144, 1024], P('stem', 'tm')
Inputs may be any that keep to these rules, and one draw needn't show every extreme that they name: The stems' timestep indices are distinct, and index 0 and index 49 are always among them.
All inputs are finite; a program needn't handle non-finite values.
Results may differ from a plain program's by a relative error of at most 0.015.
The roundings to bfloat16 on the way count: a program that leaves them out, or rounds other values in their place, can miss the bound.
Values may be sent and summed in bfloat16 or wider, within the bound.
No kernel may reach another device: no remote copies, remote signals or barrier semaphores. Data moves between devices by JAX's collectives and lax.ppermute only.
A program may use at most 128 MiB of HBM per device.

v0:
```python
import jax
import jax.numpy as jnp
from jax import lax
from jax.sharding import PartitionSpec as P

D = 1024
H = 8
HD = 64
HALF = 256


EPS = 1e-06
NEG = -1e30


def padded_2(block, sides, width):
    for axis, dim in sides:
        count = lax.axis_size(axis)
        forward = [(i, i + 1) for i in range(count - 1)]
        backward = [(target, source) for source, target in forward]
        low = lax.ppermute(
            lax.slice_in_dim(block, block.shape[dim] - width, None, axis=dim), axis, forward
        )
        high = lax.ppermute(lax.slice_in_dim(block, 0, width, axis=dim), axis, backward)
        block = jnp.concatenate([low, block, high], axis=dim)
    return block


def rounded(values):
    return lax.optimization_barrier(values.astype(jnp.bfloat16))


def layer_norm(values):
    values = values.astype(jnp.float32)
    centred = values - jnp.mean(values, axis=-1, keepdims=True)
    return centred * lax.rsqrt(jnp.mean(centred * centred, axis=-1, keepdims=True) + EPS)


def modulate(values, shift, scale):
    return layer_norm(values) * (1.0 + scale) + shift


def head_norm(values, gain):
    shaped = values.reshape(values.shape[:-1] + (H, HD))
    return shaped * lax.rsqrt(jnp.mean(shaped * shaped, axis=-1, keepdims=True) + EPS) * gain


def split_heads(projected, gains):
    width = H * HD
    query = rounded(head_norm(projected[..., :width], gains[0]))
    keyset = rounded(head_norm(projected[..., width : 2 * width], gains[1]))
    valueset = rounded(projected[..., 2 * width :].reshape(projected.shape[:-1] + (H, HD)))
    return (query, keyset, valueset)


def softmax_rows(scores):
    top = jnp.max(scores, axis=-1, keepdims=True)
    raised = jnp.exp(scores - top)
    return rounded(raised / jnp.sum(raised, axis=-1, keepdims=True))


def window_attend(query, padded, offset, total):
    rows = query.shape[0]
    width = H * HD

    def one_block(index):
        start = index * rows
        k_block = padded[0].reshape(-1, H, HD)
        v_block = padded[1].reshape(-1, H, HD)
        scores = jnp.einsum(
            "qhd,khd->hqk", query, k_block, preferred_element_type=jnp.float32
        ) * HD ** (-0.5)
        q_pos = offset + start + jnp.arange(rows, dtype=jnp.int32)
        k_pos = offset + start - HALF + jnp.arange(rows + 2 * HALF, dtype=jnp.int32)
        keep = (
            (jnp.abs(q_pos[:, None] - k_pos[None, :]) <= HALF)
            & (k_pos[None, :] >= 0)
            & (k_pos[None, :] < total)
        )
        weights = softmax_rows(jnp.where(keep[None], scores, NEG))
        return jnp.einsum("hqk,khd->qhd", weights, v_block, preferred_element_type=jnp.float32)

    blocks = lax.map(one_block, jnp.arange(rows // rows, dtype=jnp.int32))
    return rounded(blocks.reshape(rows, width))


def on_device(
    frames,
    timestep,
    modulation,
    qkv_self,
    out_self,
    qk_gain_self,
    qkv_cross,
    out_cross,
    qk_gain_cross,
):
    stem_count = lax.axis_size("stem")
    time_count = lax.axis_size("tm")
    rows = frames.shape[1]
    width = H * HD
    steps_all = modulation.shape[0]
    picks = (timestep[:, None] == jnp.arange(steps_all, dtype=jnp.int32)[None, :]).astype(
        jnp.float32
    )
    table = jnp.dot(
        picks, modulation.reshape(steps_all, -1), precision=lax.Precision.HIGHEST
    ).reshape(stem_count, 6, D)
    own = lax.dynamic_index_in_dim(table, lax.axis_index("stem"), 0, keepdims=False)
    source = frames[0]
    normed_self = rounded(modulate(source, own[0], own[1]))
    projected = jnp.dot(normed_self, qkv_self, preferred_element_type=jnp.float32)
    query, keyset, valueset = split_heads(projected, qk_gain_self)
    stacked = jnp.stack([keyset.reshape(rows, width), valueset.reshape(rows, width)])
    padded = padded_2(stacked, (("tm", 1),), HALF)
    offset = lax.axis_index("tm") * rows
    attended = window_attend(query, padded, offset, rows * time_count)
    first = rounded(
        source.astype(jnp.float32)
        + own[2] * jnp.dot(attended, out_self, preferred_element_type=jnp.float32)
    )
    normed_cross = rounded(modulate(first, own[3], own[4]))
    projected_cross = jnp.dot(normed_cross, qkv_cross, preferred_element_type=jnp.float32)
    q_cross, k_cross, v_cross = split_heads(projected_cross, qk_gain_cross)
    pair = jnp.stack([k_cross.reshape(rows, width), v_cross.reshape(rows, width)])[None]
    every = lax.all_gather(pair, "stem", axis=0, tiled=True)
    k_all = every[:, 0].reshape(stem_count, rows, H, HD)
    v_all = every[:, 1].reshape(stem_count, rows, H, HD)
    scores = jnp.einsum(
        "fhd,tfhd->fht", q_cross, k_all, preferred_element_type=jnp.float32
    ) * HD ** (-0.5)
    weights = softmax_rows(scores)
    mixed = rounded(
        jnp.einsum("fht,tfhd->fhd", weights, v_all, preferred_element_type=jnp.float32)
    ).reshape(rows, width)
    cross_out = rounded(jnp.dot(mixed, out_cross, preferred_element_type=jnp.float32))
    result = (first.astype(jnp.float32) + own[5] * cross_out.astype(jnp.float32)).astype(
        jnp.bfloat16
    )
    return result[None]


def solution(mesh):
    return jax.shard_map(
        on_device,
        mesh=mesh,
        in_specs=(P("stem", "tm", None), P(), P(), P(), P(), P(), P(), P(), P()),
        out_specs=P("stem", "tm", None),
        check_vma=False,
    )
```

profile of v0, /device:TPU:0, one launch (start us, length us, event | category | flops | bytes accessed | tf_op | source)
XLA Modules:
  0.0 136.7 jit_solution(145508537842891630)
XLA Ops:
  6.5 2.2 %copy.46 = f32[50,6,1024]{2,1,0:T(8,128)S(1)} copy(f32[50,6,1024]{2,0,1:T(8,128)} %param.11) | data formatting | bytes 2457600 | tf_op args[2]
  9.0 1.9 %copy.73 = f32[7,8,6,1024]{3,1,2,0:T(8,128)} copy(f32[7,8,6,1024]{3,2,1,0:T(8,128)S(1)} %bitcast.93) | data formatting | bytes 2752512
  10.9 2.9 %dot_general.34 = f32[6,1024,50]{1,0,2:T(8,128)} reshape(f32[6144,50]{0,1:T(8,128)} %bitcast.94) | data formatting | bytes 2457600 | tf_op jit(solution)/shard_map/dot_general | solution.py:106
  15.1 1.5 %fusion.15 = f32[384]{0:T(512)S(1)} fusion(bf16[1,384,1024]{2,1,0:T(8,128)(2,1)} %param.9, f32[384]{0:T(512)S(1)} %broadcast_multiply_fusion.1), kind=kLoop, calls=%fused_computation.24 | loop fusion | flops 1572480 | bytes 789504 | tf_op jit(solution)/shard_map/reduce_sum | solution.py:36
  16.6 2.6 %fusion.21 = f32[2,6,1024]{2,0,1:T(2,128)S(1)} fusion(f32[6,1024,50]{1,0,2:T(8,128)} %dot_general.34, s32[2]{0:T(128)S(1)} %copy-done.12), kind=kOutput, calls=%fused_computation.33 | convolution fusion | flops 7372900 | bytes 1277960 | tf_op jit(solution)/shard_map/dot_general | solution.py:106
  19.9 1.5 %fusion.18 = bf16[384,1024]{1,0:T(8,128)(2,1)S(1)} fusion(bf16[1,384,1024]{2,1,0:T(8,128)(2,1)} %param.9, f32[1024]{0:T(1024)S(1)} %bitcast.111, f32[1024]{0:T(1024)S(1)} %bitcast.112, f32[384]{0:T(512)S(1)} %add_rsqrt_fusion.5, f32[384]{0:T(512)S(1)} %broadcast_multiply_fusion.1), kind=kLoop, calls=%fused_computation.27 | loop fusion | flops 2359296 | bytes 1584128 | tf_op jit(solution)/shard_map/convert_element_type | solution.py:30
  24.9 2.3 %copy.50 = f32[384,512]{0,1:T(8,128)} copy(f32[384,512]{1,0:T(8,128)} %get-tuple-element.20) | data formatting | bytes 1572864 | tf_op jit(solution)/shard_map/slice | solution.py:50
  28.4 2.3 %copy.48 = f32[384,512]{0,1:T(8,128)} copy(f32[384,512]{1,0:T(8,128)} %get-tuple-element.22) | data formatting | bytes 1572864 | tf_op jit(solution)/shard_map/slice | solution.py:51
  31.9 2.6 %multiply_convert_fusion.2 = (bf16[384,8,64]{0,2,1:T(8,128)(2,1)}, bf16[384,8,64]{0,2,1:T(8,128)(2,1)}) fusion(f32[64]{0:T(128)S(1)} %get-tuple-element.38, f32[384,8]{0,1:T(8,128)S(1)} %add_rsqrt_fusion.2, f32[384,512]{0,1:T(8,128)} %copy.50, f32[64]{0:T(128)S(1)} %get-tuple-element.39, f32[384,8]{0,1:T(8,128)S(1)} %add_rsqrt_fusion.3, f32[384,512]{0,1:T(8,128)} %copy.48), kind=kLoop, calls=%fused_computation.50 | loop fusion | flops 1179648 | bytes 2384384 | tf_op jit(solution)/shard_map/convert_element_type | solution.py:30
  35.7 2.1 %fusion.28 = (bf16[2,256,512]{1,2,0:T(8,128)(2,1)}, bf16[2,256,512]{1,2,0:T(8,128)(2,1)}) fusion(bf16[1,384,512]{1,2,0:T(8,128)(2,1)} %bitcast.98, bf16[1,384,512]{1,2,0:T(8,128)(2,1)S(1)} %bitcast.96), kind=kLoop, calls=%fused_computation.54 | loop fusion | flops 2097152 | bytes 1835008 | tf_op jit(solution)/shard_map/stack | solution.py:114
  39.0 3.9 %collective-permute-start = (bf16[2,256,512]{1,2,0:T(8,128)(2,1)}, bf16[2,256,512]{1,2,0:T(8,128)(2,1)}, u32[]{:S(2)}, u32[]{:S(2)}) collective-permute-start(bf16[2,256,512]{1,2,0:T(8,128)(2,1)} %get-tuple-element.28), channel_id=1, source_target_pairs={{0,1},{1,2},{2,3},{3,4},{4,5},{5,6},{6,7},{7,8},{8,9},{9,10},{10,1... | collective-permute-start | bytes 1572872 | tf_op jit(solution)/shard_map/ppermute | solution.py:21
  45.5 1.5 %pad_maximum_fusion = bf16[2,896,512]{1,2,0:T(8,128)(2,1)S(1)} fusion(bf16[2,256,512]{1,2,0:T(8,128)(2,1)} %collective-permute-done.1, bf16[1,384,512]{1,2,0:T(8,128)(2,1)S(1)} %bitcast.97, bf16[1,384,512]{1,2,0:T(8,128)(2,1)} %bitcast.99, bf16[2,256,512]{1,2,0:T(8,128)(2,1)} %collective-permute-done), kind=kLoop, calls=%fused_computation.19 | loop fusion | flops 7340032 | bytes 3670016 | tf_op jit(solution)/shard_map/concatenate | solution.py:25
  47.0 1.4 %fusion.40 = (bf16[1,896,512]{1,2,0:T(8,128)(2,1)}, bf16[1,896,512]{1,2,0:T(8,128)(2,1)}) fusion(bf16[2,896,512]{1,2,0:T(8,128)(2,1)S(1)} %pad_maximum_fusion), kind=kLoop, calls=%fused_computation.90 | loop fusion | bytes 3670016 | tf_op jit(solution)/shard_map/while/body/eval_jaxpr/slice | solution.py:68
  48.4 9.8 %fusion.42 = (f32[8,384]{1,0:T(8,128)}, f32[8,384,896]{2,1,0:T(8,128)}) fusion(pred[384,896]{1,0:T(8,128)(4,1)} %fusion.24, bf16[384,8,64]{0,2,1:T(8,128)(2,1)S(1)} %copy-done.7, bf16[896,8,64]{0,2,1:T(8,128)(2,1)} %bitcast.105), kind=kOutput, calls=%fused_computation.92 | convolution fusion | flops 363332480 | bytes 12677120 | tf_op jit(solution)/shard_map/while/body/eval_jaxpr/sub | solution.py:58
  58.2 5.1 %divide_convert_fusion = bf16[8,384,896]{2,1,0:T(8,128)(2,1)S(1)} fusion(f32[8,384,896]{2,1,0:T(8,128)} %get-tuple-element.41, f32[8,384]{1,0:T(8,128)} %get-tuple-element.40), kind=kLoop, calls=%fused_computation.1 | loop fusion | flops 5505024 | bytes 16527360 | tf_op jit(solution)/shard_map/while/body/eval_jaxpr/convert_element_type | solution.py:30
  63.4 1.9 %convolution_convert_fusion.1 = bf16[8,64,384]{2,1,0:T(8,128)(2,1)S(1)} fusion(bf16[896,8,64]{0,2,1:T(8,128)(2,1)S(1)} %bitcast.95, bf16[8,384,896]{2,1,0:T(8,128)(2,1)S(1)} %divide_convert_fusion), kind=kOutput, calls=%fused_computation.38 | convolution fusion | flops 352518144 | bytes 6815744 | tf_op jit(solution)/shard_map/while/body/eval_jaxpr/hqk,khd->qhd/dot_general | solution.py:81
  71.8 2.4 %copy.52 = f32[384,512]{0,1:T(8,128)} copy(f32[384,512]{1,0:T(8,128)} %get-tuple-element.14) | data formatting | bytes 1572864 | tf_op jit(solution)/shard_map/slice | solution.py:51
  77.6 2.3 %copy.54 = bf16[2,384,512]{2,1,0:T(8,128)(2,1)} copy(bf16[2,384,512]{1,2,0:T(8,128)(2,1)} %pad_maximum_fusion.1) | data formatting | bytes 1572864 | tf_op jit(solution)/shard_map/stack | solution.py:125
  79.9 2.3 %copy.51 = f32[384,512]{0,1:T(8,128)} copy(f32[384,512]{1,0:T(8,128)} %get-tuple-element.13) | data formatting | bytes 1572864 | tf_op jit(solution)/shard_map/slice | solution.py:50
  85.7 32.9 %all-gather.3.cloned.1.call-done = bf16[4,384,512]{2,1,0:T(8,128)(2,1)} async-done(((bf16[2,384,512]{2,1,0:T(8,128)(2,1)}), bf16[4,384,512]{2,1,0:T(8,128)(2,1)}) %all-gather.3.cloned.1.call-update) | async-done | bytes 1572880 | tf_op jit(solution)/shard_map/all_gather | solution.py:126
  118.6 2.6 %fusion.41 = (bf16[2,1,384,512]{3,2,1,0:T(8,128)(2,1)}, bf16[2,1,384,512]{3,2,1,0:T(8,128)(2,1)}) fusion(bf16[2,2,384,512]{3,2,1,0:T(8,128)(2,1)} %bitcast.102), kind=kLoop, calls=%fused_computation.91 | loop fusion | bytes 3145728 | tf_op jit(solution)/shard_map/slice | solution.py:127
  121.2 2.3 %copy.69 = bf16[2,1,384,512]{2,3,0,1:T(8,128)(2,1)} copy(bf16[2,1,384,512]{3,2,1,0:T(8,128)(2,1)} %get-tuple-element.27) | data formatting | bytes 1572864
  123.5 2.3 %copy.68 = bf16[2,1,384,512]{2,3,0,1:T(8,128)(2,1)} copy(bf16[2,1,384,512]{3,2,1,0:T(8,128)(2,1)} %get-tuple-element.26) | data formatting | bytes 1572864
  125.8 1.7 %multiply_reduce_fusion.1 = f32[384,8,2]{0,1,2:T(8,128)S(1)} fusion(bf16[384,8,64,2]{0,2,1,3:T(8,128)(2,1)} %bitcast.101, f32[384,8,64]{0,2,1:T(8,128)} %convert.8), kind=kLoop, calls=%fused_computation.31 | loop fusion | flops 1173504 | bytes 1597440 | tf_op jit(solution)/shard_map/fhd,tfhd->fht/dot_general | solution.py:129
  (81 shorter events, 28.9 us)
Async XLA Ops:
  6.5 14.8 %copy-start = (bf16[1024,1536]{1,0:T(8,128)(2,1)S(1)}, bf16[1024,1536]{1,0:T(8,128)(2,1)}, u32[]{:S(2)}) copy-start(bf16[1024,1536]{1,0:T(8,128)(2,1)} %param.12) | copy-start | bytes 9437188
  6.5 112.0 %all-gather.3.cloned.1.call-start = ((), (), s32[]{:S(2)}) async-start(), calls=%async_computation | async-start | bytes 2359296 | tf_op jit(solution)/shard_map/all_gather | solution.py:126
  10.9 5.7 %copy-start.12 = (s32[2]{0:T(128)S(1)}, s32[2]{0:T(128)}, u32[]{:S(2)}) copy-start(s32[2]{0:T(128)} %param.10) | copy-start | bytes 28
  22.8 2.1 %copy-start.11 = (f32[2,64]{1,0:T(2,128)S(1)}, f32[2,64]{1,0:T(2,128)}, u32[]{:S(2)}) copy-start(f32[2,64]{1,0:T(2,128)} %param.14) | copy-start | bytes 1540
  37.8 7.8 %collective-permute-start.1 = (bf16[2,256,512]{1,2,0:T(8,128)(2,1)}, bf16[2,256,512]{1,2,0:T(8,128)(2,1)}, u32[]{:S(2)}, u32[]{:S(2)}) collective-permute-start(bf16[2,256,512]{1,2,0:T(8,128)(2,1)} %get-tuple-element.29), channel_id=1, source_target_pairs={{1,0},{2,1},{3,2},{4,3},{5,4},{6,5},{7,6},{8,7},{9,8},{10,9},{11,1... | collective-permute-start | bytes 1572872 | tf_op jit(solution)/shard_map/ppermute | solution.py:24
  39.0 6.5 %collective-permute-start = (bf16[2,256,512]{1,2,0:T(8,128)(2,1)}, bf16[2,256,512]{1,2,0:T(8,128)(2,1)}, u32[]{:S(2)}, u32[]{:S(2)}) collective-permute-start(bf16[2,256,512]{1,2,0:T(8,128)(2,1)} %get-tuple-element.28), channel_id=1, source_target_pairs={{0,1},{1,2},{2,3},{3,4},{4,5},{5,6},{6,7},{7,8},{8,9},{9,10},{10,1... | collective-permute-start | bytes 1572872 | tf_op jit(solution)/shard_map/ppermute | solution.py:21
  47.0 1.4 %copy-start.7 = (bf16[384,8,64]{0,2,1:T(8,128)(2,1)S(1)}, bf16[384,8,64]{0,2,1:T(8,128)(2,1)}, u32[]{:S(2)}) copy-start(bf16[384,8,64]{0,2,1:T(8,128)(2,1)} %get-tuple-element.42) | copy-start | bytes 1179652
  58.2 5.1 %copy-start.4 = (bf16[1,896,512]{1,2,0:T(8,128)(2,1)S(1)}, bf16[1,896,512]{1,2,0:T(8,128)(2,1)}, u32[]{:S(2)}) copy-start(bf16[1,896,512]{1,2,0:T(8,128)(2,1)} %get-tuple-element.25) | copy-start | bytes 2752516
  63.4 1.9 %copy-start.3 = (bf16[1,384,1024]{2,1,0:T(8,128)(2,1)S(1)}, bf16[1,384,1024]{2,1,0:T(8,128)(2,1)}, u32[]{:S(2)}) copy-start(bf16[1,384,1024]{2,1,0:T(8,128)(2,1)} %param.9) | copy-start | bytes 2359300
  63.4 1.9 %copy-start.8 = (f32[1,1,1024]{2,0,1:T(1,128)S(1)}, f32[1,1,1024]{2,0,1:T(1,128)}, u32[]{:S(2)}) copy-start(f32[1,1,1024]{2,0,1:T(1,128)} %get-tuple-element.34) | copy-start | bytes 12292
  63.4 1.9 %copy-start.14 = (bf16[512,1024]{1,0:T(8,128)(2,1)S(1)}, bf16[512,1024]{1,0:T(8,128)(2,1)}, u32[]{:S(2)}) copy-start(bf16[512,1024]{1,0:T(8,128)(2,1)} %param.13) | copy-start | bytes 3145732
  66.0 0.9 copy-start.1
  66.0 2.2 %copy-start.13 = (bf16[1024,1536]{1,0:T(8,128)(2,1)S(1)}, bf16[1024,1536]{1,0:T(8,128)(2,1)}, u32[]{:S(2)}) copy-start(bf16[1024,1536]{1,0:T(8,128)(2,1)} %param.15) | copy-start | bytes 9437188
  70.9 4.5 %copy-start.10 = (f32[64]{0:T(128)S(1)}, f32[64]{0:T(128)}, u32[]{:S(2)}) copy-start(f32[64]{0:T(128)} %get-tuple-element.37) | copy-start | bytes 772
  71.8 4.9 %copy-start.6 = (bf16[384,512]{0,1:T(8,128)(2,1)S(1)}, bf16[384,512]{0,1:T(8,128)(2,1)}, u32[]{:S(2)}) copy-start(bf16[384,512]{0,1:T(8,128)(2,1)} %copy.53) | copy-start | bytes 1179652
  79.9 3.5 %copy-start.9 = (f32[64]{0:T(128)S(1)}, f32[64]{0:T(128)}, u32[]{:S(2)}) copy-start(f32[64]{0:T(128)} %get-tuple-element.36) | copy-start | bytes 772
  125.8 1.8 %copy-start.5 = (bf16[2,1,384,512]{2,3,0,1:T(8,128)(2,1)S(1)}, bf16[2,1,384,512]{2,3,0,1:T(8,128)(2,1)}, u32[]{:S(2)}) copy-start(bf16[2,1,384,512]{2,3,0,1:T(8,128)(2,1)} %copy.69) | copy-start | bytes 2359300
  125.8 2.0 %copy-start.15 = (bf16[512,1024]{1,0:T(8,128)(2,1)S(1)}, bf16[512,1024]{1,0:T(8,128)(2,1)}, u32[]{:S(2)}) copy-start(bf16[512,1024]{1,0:T(8,128)(2,1)} %param.16) | copy-start | bytes 3145732
  127.6 1.2 copy-start.2
Sparse Core Ops, SparseCore 0:
  80.1 38.4 all-gather.2
where the time goes:
time: 138 us; the launch traced here: 137 us
  local copies, waits for them, and re-layouts  35.9 us (26%)
  waiting for transfers between devices  32.9 us (24%)
  other arithmetic  30.7 us (22%)
  matrix products  18.3 us (13%)
  between operations  13.8 us (10%)
  starting transfers between devices  5.13 us (4%)
    all_gather x1, waiting for transfers between devices, on_device(): every = lax.all_gather(pair, 'stem', axis=0, tiled=True)  32.9 us
    convert_element_type x7, other arithmetic, rounded(): return lax.optimization_barrier(values.astype(jnp.bfloat16))  12.1 us
    unnamed x37, local copies, waits for them, and re-layouts  10.6 us
    sub x1, matrix products, softmax_rows(): raised = jnp.exp(scores - top)  9.82 us
    slice x4, local copies, waits for them, and re-layouts, split_heads(): query = rounded(head_norm(projected[..., :width], gains[0]))  7.1 us
    reduce_sum x4, other arithmetic, head_norm(): jnp.mean(shaped * shaped, axis=-1, keepdims=True) + EPS  4.83 us
    slice x2, local copies, waits for them, and re-layouts, split_heads(): keyset = rounded(head_norm(projected[..., width:2 * width], gains[1]))  4.64 us
    ppermute x1, starting transfers between devices, padded_2(): lax.ppermute(lax.slice_in_dim(block, block.shape[dim] - width, None, axis...  3.85 us
  transfers between devices with their start and end apart: 3, of which 1 were waited for; matrix products, arithmetic and copies ran while one was open for 6% of the time, Pallas kernels for 0%

commit v1 on v0

v1 whole, which is shorter than its diff:
```python
import jax
import jax.numpy as jnp
from jax import lax
from jax.experimental import pallas as pl
from jax.experimental.pallas import tpu as pltpu
from jax.sharding import PartitionSpec as P

D = 1024
H = 8
HD = 64
HW = H * HD
HALF = 256
BLOCK = 128
SLAB = 128
WINDOW = BLOCK + 2 * HALF
EPS = 1e-06
NEG = -1e30
F32 = jnp.float32
BF16 = jnp.bfloat16
VMEM = pl.BlockSpec(memory_space=pltpu.VMEM)
SMEM = pl.BlockSpec(memory_space=pltpu.SMEM)
ANY = pl.BlockSpec(memory_space=pl.ANY)
LIMIT = 48 * 1024 * 1024


def params():
    return pltpu.CompilerParams(vmem_limit_bytes=LIMIT)


def shape(*dims, dtype=BF16):
    return jax.ShapeDtypeStruct(dims, dtype)


def dot(a, b, dims=((1,), (0,))):
    return lax.dot_general(a, b, (dims, ((), ())), preferred_element_type=F32)


def modulated(rows, shift, scale):
    values = rows.astype(F32)
    centred = values - jnp.mean(values, axis=-1, keepdims=True)
    spread = jnp.mean(centred * centred, axis=-1, keepdims=True)
    normed = centred * lax.rsqrt(spread + EPS)
    return (normed * (1.0 + scale) + shift).astype(BF16)


def head_ones():
    row = lax.broadcasted_iota(jnp.int32, (2 * SLAB, 2 * SLAB), 0) // HD
    col = lax.broadcasted_iota(jnp.int32, (2 * SLAB, 2 * SLAB), 1) // HD
    return jnp.where(row == col, 1.0, 0.0).astype(BF16)


def head_sums(values, ones):
    high = values.astype(BF16)
    low = (values - high.astype(F32)).astype(BF16)
    parts = []
    for at in range(0, HW, 2 * SLAB):
        cols = slice(at, at + 2 * SLAB)
        parts.append(dot(high[:, cols], ones) + dot(low[:, cols], ones))
    return jnp.concatenate(parts, axis=1)


def head_norm(values, gain, ones):
    mean = head_sums(values * values, ones) * (1.0 / HD)
    return (values * lax.rsqrt(mean + EPS) * gain).astype(BF16)


def wide_gain(gain):
    return jnp.concatenate([gain] * H, axis=1)


def window_bias(first_key, total):
    i = lax.broadcasted_iota(jnp.int32, (BLOCK, WINDOW), 0)
    j = lax.broadcasted_iota(jnp.int32, (BLOCK, WINDOW), 1)
    frame = first_key + j
    keep = (j >= i) & (j <= i + 2 * HALF) & (frame >= 0) & (frame < total)
    return jnp.where(keep, 0.0, NEG)


def window_block(query, keys, values, bias):
    half = lax.broadcasted_iota(jnp.int32, (BLOCK, SLAB), 1) < HD
    ones = jnp.ones((WINDOW, SLAB), BF16)
    outs = []
    for at in range(0, HW, SLAB):
        cols = slice(at, at + SLAB)
        q = query(cols)
        zero = jnp.zeros_like(q)
        pair = jnp.concatenate([jnp.where(half, q, zero), jnp.where(half, zero, q)], axis=0)
        scores = dot(pair, keys(cols), ((1,), (1,)))
        scores = jnp.concatenate([scores[:BLOCK] + bias, scores[BLOCK:] + bias], axis=0)
        top = jnp.max(scores, axis=-1, keepdims=True)
        raised = jnp.exp(scores - top).astype(BF16)
        summed = dot(raised, jnp.concatenate([values(cols), ones], axis=1))
        out = summed[:, :SLAB] / summed[:, SLAB:]
        outs.append(jnp.where(half, out[:BLOCK], out[BLOCK:]).astype(BF16))
    return jnp.concatenate(outs, axis=1)


def cross_attend(query, keys, values, ones):
    query = query.astype(F32)
    scores = [head_sums(query * k.astype(F32), ones) * (HD ** -0.5) for k in keys]
    top = scores[0]
    for s in scores[1:]:
        top = jnp.maximum(top, s)
    raised = [jnp.exp(s - top) for s in scores]
    total = raised[0]
    for r in raised[1:]:
        total = total + r
    scale = 1.0 / total
    out = jnp.zeros_like(query)
    for r, v in zip(raised, values):
        out = out + (r * scale).astype(BF16).astype(F32) * v.astype(F32)
    return out.astype(BF16)


def blocks(rows):
    return [slice(at, min(at + BLOCK, rows)) for at in range(0, rows, BLOCK)]


def mod_copy(timestep, modulation, row, held, sem):
    return pltpu.make_async_copy(modulation.at[timestep[row]], held, sem)


def split_kernel(frames, near, far, sems):
    parity = lax.rem(lax.axis_index("tm"), 2)
    rows = frames.shape[1]
    near_at = pl.multiple_of((1 - parity) * (rows - HALF), BLOCK)
    far_at = pl.multiple_of(parity * (rows - HALF), BLOCK)
    a = pltpu.make_async_copy(frames.at[0, pl.ds(far_at, HALF)], far, sems.at[0])
    b = pltpu.make_async_copy(frames.at[0, pl.ds(near_at, HALF)], near, sems.at[1])
    a.start()
    b.start()
    a.wait()
    b.wait()


def near_kernel(timestep, modulation, frames, near, weight, gains, query, kv, attended, held, sem):
    parity = lax.rem(lax.axis_index("tm"), 2)
    stem = lax.axis_index("stem")
    copy = mod_copy(timestep, modulation, stem, held, sem)
    copy.start()
    copy.wait()
    shift, scale = held[0:1], held[1:2]
    ones = head_ones()
    rows = frames.shape[1]
    q_gain = wide_gain(gains[0:1]) * (HD ** -0.5)
    k_gain = wide_gain(gains[1:2])
    own_at = parity * HALF
    near_at = (1 - parity) * rows

    def keys_values(projected, at, count):
        kv[pl.ds(at, count), :HW] = head_norm(projected[:, :HW], k_gain, ones)
        kv[pl.ds(at, count), HW:] = projected[:, HW:].astype(BF16)

    for part in blocks(rows):
        normed = modulated(frames[0, part], shift, scale)
        projected = dot(normed, weight[...])
        query[part] = head_norm(projected[:, :HW], q_gain, ones)
        keys_values(projected[:, HW:], pl.multiple_of(own_at + part.start, BLOCK), BLOCK)
    for part in blocks(HALF):
        normed = modulated(near[part], shift, scale)
        projected = dot(normed, weight[:, HW:])
        keys_values(projected, pl.multiple_of(near_at + part.start, BLOCK), BLOCK)
    early = pl.multiple_of((1 - parity) * HALF, BLOCK)
    bias = window_bias(HALF, 1 << 30)
    attended[...] = window_block(
        lambda c: query[pl.ds(early, BLOCK), c],
        lambda c: kv[:, c],
        lambda c: kv[:, slice(HW + c.start, HW + c.stop)],
        bias,
    )


def far_kernel(timestep, modulation, far, weight, gains, query, kv, attended, held, full, sem, sem_kv):
    place = lax.axis_index("tm")
    parity = lax.rem(place, 2)
    stem = lax.axis_index("stem")
    copy = mod_copy(timestep, modulation, stem, held, sem)
    copy.start()
    rows = query.shape[0]
    local = rows + HALF
    local_at = pl.multiple_of((1 - parity) * HALF, BLOCK)
    far_at = parity * local
    moved = pltpu.make_async_copy(kv, full.at[pl.ds(local_at, local)], sem_kv)
    moved.start()
    copy.wait()
    shift, scale = held[0:1], held[1:2]
    ones = head_ones()
    k_gain = wide_gain(gains[1:2])
    for part in blocks(HALF):
        at = pl.multiple_of(far_at + part.start, BLOCK)
        normed = modulated(far[part], shift, scale)
        projected = dot(normed, weight[:, HW:])
        full[pl.ds(at, BLOCK), :HW] = head_norm(projected[:, :HW], k_gain, ones)
        full[pl.ds(at, BLOCK), HW:] = projected[:, HW:].astype(BF16)
    moved.wait()
    total = rows * lax.axis_size("tm")
    for part in blocks(HALF):
        at = pl.multiple_of(parity * (rows - HALF) + part.start, BLOCK)
        bias = window_bias(place * rows - HALF + at, total)
        attended[part] = window_block(
            lambda c, at=at: query[pl.ds(at, BLOCK), c],
            lambda c, at=at: full[pl.ds(at, WINDOW), c],
            lambda c, at=at: full[pl.ds(at, WINDOW), slice(HW + c.start, HW + c.stop)],
            bias,
        )


def first_of(frames, attended, weight, gate):
    mixed = dot(attended, weight[...])
    return (frames.astype(F32) + gate * mixed).astype(BF16)


def projected_cross(first, held, weight, gains, ones, with_query):
    normed = modulated(first, held[3:4], held[4:5])
    if with_query:
        projected = dot(normed, weight[...])
        query = head_norm(projected[:, :HW], wide_gain(gains[0:1]), ones)
        projected = projected[:, HW:]
    else:
        projected = dot(normed, weight[:, HW:])
        query = None
    keys = head_norm(projected[:, :HW], wide_gain(gains[1:2]), ones)
    return query, keys, projected[:, HW:].astype(BF16)


def finished(first, attended, weight, gate):
    out = dot(attended, weight[...]).astype(BF16)
    return (first.astype(F32) + gate * out.astype(F32)).astype(BF16)


def mods_of_all(timestep, modulation, held, sems):
    stem = lax.axis_index("stem")
    count = lax.axis_size("stem")
    copies = [
        mod_copy(timestep, modulation, lax.rem(stem + count - k, count), held.at[k], sems.at[k])
        for k in range(count)
    ]
    for copy in copies:
        copy.start()
    for copy in copies:
        copy.wait()


def own_kernel(count, timestep, modulation, frames, early, late, *refs):
    others = refs[: count - 1]
    their_frames = refs[count - 1 : 2 * count - 2]
    out_self, qkv_cross, gains, out_cross, first, qkv, out, held, sems = refs[2 * count - 2 :]
    parity = lax.rem(lax.axis_index("tm"), 2)
    rows = frames.shape[1]
    mods_of_all(timestep, modulation, held, sems)
    ones = head_ones()
    early_at = pl.multiple_of((1 - parity) * HALF, BLOCK)
    late_at = parity * (rows - HALF)
    own = held.at[0]
    for part in blocks(HALF):
        at = pl.multiple_of(late_at + part.start, BLOCK)
        f = first_of(frames[0, pl.ds(at, BLOCK)], late[part], out_self, own[2:3])
        first[part] = f
        q, k, v = projected_cross(f, own, qkv_cross, gains, ones, True)
        qkv[part, :HW] = q
        qkv[part, HW : 2 * HW] = k
        qkv[part, 2 * HW :] = v
    f = first_of(frames[0, pl.ds(early_at, BLOCK)], early[...], out_self, own[2:3])
    q, k, v = projected_cross(f, own, qkv_cross, gains, ones, True)
    keys, values = [k], [v]
    for n, (attended, source) in enumerate(zip(others, their_frames)):
        mods = held.at[n + 1]
        g = first_of(source[0, pl.ds(early_at, BLOCK)], attended[...], out_self, mods[2:3])
        _, k, v = projected_cross(g, mods, qkv_cross, gains, ones, False)
        keys.append(k)
        values.append(v)
    mixed = cross_attend(q, keys, values, ones)
    out[...] = finished(f, mixed, out_cross, own[5:6])


def last_kernel(count, timestep, modulation, first, qkv, early_out, *refs):
    others = refs[: count - 1]
    their_frames = refs[count - 1 : 2 * count - 2]
    out_self, qkv_cross, gains, out_cross, out, held, sems = refs[2 * count - 2 :]
    parity = lax.rem(lax.axis_index("tm"), 2)
    rows = out.shape[1]
    mods_of_all(timestep, modulation, held, sems)
    ones = head_ones()
    early_at = pl.multiple_of((1 - parity) * HALF, BLOCK)
    late_at = parity * (rows - HALF)
    out[0, pl.ds(early_at, rows - HALF)] = early_out[...]
    for part in blocks(HALF):
        at = pl.multiple_of(late_at + part.start, BLOCK)
        keys, values = [qkv[part, HW : 2 * HW]], [qkv[part, 2 * HW :]]
        for n, (attended, source) in enumerate(zip(others, their_frames)):
            mods = held.at[n + 1]
            g = first_of(source[0, pl.ds(at, BLOCK)], attended[part], out_self, mods[2:3])
            _, k, v = projected_cross(g, mods, qkv_cross, gains, ones, False)
            keys.append(k)
            values.append(v)
        mixed = cross_attend(qkv[part, :HW], keys, values, ones)
        out[0, pl.ds(at, BLOCK)] = finished(first[part], mixed, out_cross, held[0, 5:6])


def on_device(
    frames,
    timestep,
    modulation,
    qkv_self,
    out_self,
    qk_gain_self,
    qkv_cross,
    out_cross,
    qk_gain_cross,
):
    stems = lax.axis_size("stem")
    places = lax.axis_size("tm")
    rows = frames.shape[1]
    early = rows - HALF
    assert places % 2 == 0 and early == BLOCK
    inside = [(i, i ^ 1) for i in range(places)]
    across = [(i, i + 1) for i in range(1, places - 1, 2)]
    across += [(b, a) for a, b in across]

    def to_stems(array):
        return [
            lax.ppermute(array, "stem", [(i, (i + k) % stems) for i in range(stems)])
            for k in range(1, stems)
        ]

    near, far = pl.pallas_call(
        split_kernel,
        out_shape=(shape(HALF, D), shape(HALF, D)),
        in_specs=[ANY],
        out_specs=(ANY, ANY),
        scratch_shapes=[pltpu.SemaphoreType.DMA((2,))],
        compiler_params=params(),
        name="split",
    )(frames)
    far = lax.ppermute(far, "tm", across)
    near = lax.ppermute(near, "tm", inside)
    their_frames = to_stems(frames)

    query, kv, attended_early = pl.pallas_call(
        near_kernel,
        out_shape=(shape(rows, HW), shape(rows + HALF, 2 * HW), shape(early, HW)),
        in_specs=[SMEM, ANY, VMEM, VMEM, VMEM, VMEM],
        out_specs=(VMEM, VMEM, VMEM),
        scratch_shapes=[pltpu.VMEM((6, D), F32), pltpu.SemaphoreType.DMA],
        compiler_params=params(),
        name="near",
    )(timestep, modulation, frames, near, qkv_self, qk_gain_self)
    others_early = to_stems(attended_early)

    attended_late = pl.pallas_call(
        far_kernel,
        out_shape=shape(HALF, HW),
        in_specs=[SMEM, ANY, VMEM, VMEM, VMEM, VMEM, ANY],
        out_specs=VMEM,
        scratch_shapes=[
            pltpu.VMEM((6, D), F32),
            pltpu.VMEM((rows + 2 * HALF, 2 * HW), BF16),
            pltpu.SemaphoreType.DMA,
            pltpu.SemaphoreType.DMA,
        ],
        compiler_params=params(),
        name="far",
    )(timestep, modulation, far, qkv_self, qk_gain_self, query, kv)
    others_late = to_stems(attended_late)

    mods = [pltpu.VMEM((stems, 6, D), F32), pltpu.SemaphoreType.DMA((stems,))]
    pairs = 2 * (stems - 1)
    first, qkv, early_out = pl.pallas_call(
        lambda *refs: own_kernel(stems, *refs),
        out_shape=(shape(HALF, D), shape(HALF, 3 * HW), shape(early, D)),
        in_specs=[SMEM, ANY] + [VMEM] * (3 + pairs + 4),
        out_specs=(VMEM, VMEM, VMEM),
        scratch_shapes=mods,
        compiler_params=params(),
        name="own",
    )(
        timestep, modulation, frames, attended_early, attended_late, *others_early, *their_frames,
        out_self, qkv_cross, qk_gain_cross, out_cross,
    )
    return pl.pallas_call(
        lambda *refs: last_kernel(stems, *refs),
        out_shape=shape(1, rows, D),
        in_specs=[SMEM, ANY] + [VMEM] * (3 + pairs + 4),
        out_specs=VMEM,
        scratch_shapes=mods,
        compiler_params=params(),
        name="last",
    )(
        timestep, modulation, first, qkv, early_out, *others_late, *their_frames,
        out_self, qkv_cross, qk_gain_cross, out_cross,
    )


def solution(mesh):
    return jax.shard_map(
        on_device,
        mesh=mesh,
        in_specs=(P("stem", "tm", None), P(), P(), P(), P(), P(), P(), P(), P()),
        out_specs=P("stem", "tm", None),
        check_vma=False,
    )
```

time: 138 us -> 48.8 us (0.35)
  the two profiles are of different devices: /device:TPU:0 before, /device:TPU:25 now
where the time goes in v1:
time: 48.8 us; the launch traced here: 48.4 us
  Pallas kernels  29.2 us (60%)
  waiting for transfers between devices  9.93 us (20%)
  starting transfers between devices  6.86 us (14%)
  local copies, waits for them, and re-layouts  2.11 us (4%)
    pallas_call x1, Pallas kernels, on_device(): pl.pallas_call(lambda *refs: own_kernel(stems, *refs), out_shape=(shape(H...  7.83 us
    pallas_call x1, Pallas kernels, on_device(): pl.pallas_call(near_kernel, out_shape=(shape(rows, HW), shape(rows + HALF...  7.21 us
    pallas_call x1, Pallas kernels, on_device(): pl.pallas_call(lambda *refs: last_kernel(stems, *refs), out_shape=shape(1...  6.66 us
    pallas_call x1, Pallas kernels, on_device(): pl.pallas_call(far_kernel, out_shape=shape(HALF, HW), in_specs=[SMEM, ANY...  6.26 us
    ppermute x3, waiting for transfers between devices, to_stems(): lax.ppermute(array, 'stem', [(i, (i + k) % stems) for i in range(stems)])  6.21 us
    ppermute x1, waiting for transfers between devices, on_device(): far = lax.ppermute(far, 'tm', across)  3.72 us
    ppermute x1, starting transfers between devices, on_device(): far = lax.ppermute(far, 'tm', across)  3.34 us
    ppermute x3, starting transfers between devices, to_stems(): lax.ppermute(array, 'stem', [(i, (i + k) % stems) for i in range(stems)])  2.78 us
  transfers between devices with their start and end apart: 5, of which 2 were waited for; matrix products, arithmetic and copies ran while one was open for 4% of the time, Pallas kernels for 44%

profile of v1, /device:TPU:25, one launch (start us, length us, event | category | flops | bytes accessed | tf_op | source)
XLA Modules:
  0.0 48.4 jit_solution(1366893048725862420)
XLA Ops:
  0.0 1.3 %split.1 = (bf16[256,1024]{1,0:T(8,128)(2,1)S(1)}, bf16[256,1024]{1,0:T(8,128)(2,1)S(1)}) custom-call(bf16[1,384,1024]{2,1,0:T(8,128)(2,1)} %refs_2_.1), custom_call_target="tpu_custom_call" | custom-call | tf_op jit(solution)/shard_map/split/pallas_call | solution.py:326
  1.3 0.0 copy-start.3
  1.3 0.0 copy-start.5
  1.3 0.7 %collective-permute-start = (bf16[256,1024]{1,0:T(8,128)(2,1)S(1)}, bf16[256,1024]{1,0:T(8,128)(2,1)S(1)}, u32[]{:S(2)}, u32[]{:S(2)}) collective-permute-start(bf16[256,1024]{1,0:T(8,128)(2,1)S(1)} %get-tuple-element.13), channel_id=1, source_target_pairs={{0,1},{1,0},{2,3},{3,2},{4,5},{5,4},{6,7},{7,6},{8,9},{9,8},{10,11... | collective-permute-start | bytes 1572872 | tf_op jit(solution)/shard_map/ppermute | solution.py:336
  2.1 1.3 %collective-permute-start.3 = (bf16[1,384,1024]{2,1,0:T(8,128)(2,1)}, bf16[1,384,1024]{2,1,0:T(8,128)(2,1)S(1)}, u32[]{:S(2)}, u32[]{:S(2)}) collective-permute-start(bf16[1,384,1024]{2,1,0:T(8,128)(2,1)} %refs_2_.1), channel_id=1, source_target_pairs={{0,16},{16,0},{1,17},{17,1},{2,18},{18,2},{3,19},{19,3},{4,20},{20... | collective-permute-start | bytes 2359304 | tf_op jit(solution)/shard_map/ppermute | solution.py:322
  3.3 3.3 %collective-permute-start.1 = (bf16[256,1024]{1,0:T(8,128)(2,1)S(1)}, bf16[256,1024]{1,0:T(8,128)(2,1)S(1)}, u32[]{:S(2)}, u32[]{:S(2)}) collective-permute-start(bf16[256,1024]{1,0:T(8,128)(2,1)S(1)} %get-tuple-element.15), channel_id=1, source_target_pairs={{1,2},{3,4},{5,6},{7,8},{9,10},{11,12},{13,14},{2,1},{4,3},{6,5},{... | collective-permute-start | bytes 1572872 | tf_op jit(solution)/shard_map/ppermute | solution.py:335
  6.7 2.1 %copy.13.modulation.refs_1_ = f32[50,6,1024]{2,1,0:T(8,128)S(1)} copy(f32[50,6,1024]{2,0,1:T(8,128)} %param.11) | data formatting | bytes 2457600 | tf_op args[2]
  8.8 0.0 copy-start
  8.8 0.0 collective-permute-done.near
  8.8 0.0 copy-done.3
  8.8 0.0 copy-done.5
  8.8 7.2 %near.1 = (bf16[384,512]{1,0:T(8,128)(2,1)S(1)}, bf16[640,1024]{1,0:T(8,128)(2,1)S(1)}, bf16[128,512]{1,0:T(8,128)(2,1)S(1)}) custom-call(s32[2]{0:T(128)S(1)} %copy-done.3, f32[50,6,1024]{2,1,0:T(8,128)S(1)} %copy.13.modulation.refs_1_, bf16[1,384,1024]{2,1,0:T(8,128)(2,1)} %refs_2_.1, bf16[256,1024]{1,0:T(8,128)(2,1)S(1)} %collective-permute-done.near, ...), custom_call_target="tpu_custom_call" | custom-call | tf_op jit(solution)/shard_map/near/pallas_call | solution.py:339
  16.0 3.7 %collective-permute-done.1.far = bf16[256,1024]{1,0:T(8,128)(2,1)S(1)} collective-permute-done((bf16[256,1024]{1,0:T(8,128)(2,1)S(1)}, bf16[256,1024]{1,0:T(8,128)(2,1)S(1)}, u32[]{:S(2)}, u32[]{:S(2)}) %collective-permute-start.1) | collective-permute-done | bytes 524320 | tf_op jit(solution)/shard_map/ppermute | solution.py:335
  19.7 0.0 copy-done
  19.7 6.3 %far.1.refs_4_ = bf16[256,512]{1,0:T(8,128)(2,1)S(1)} custom-call(s32[2]{0:T(128)S(1)} %copy-done.3, f32[50,6,1024]{2,1,0:T(8,128)S(1)} %copy.13.modulation.refs_1_, bf16[256,1024]{1,0:T(8,128)(2,1)S(1)} %collective-permute-done.1.far, bf16[1024,1536]{1,0:T(8,128)(2,1)} %weight.3, f32[2,64]{1,0:T(2,128)S(1)} %copy-done.5, ...), custom_call_target="tpu_custom_call" | custom-call | tf_op jit(solution)/shard_map/far/pallas_call | solution.py:350
  26.0 0.3 collective-permute-start.4
  26.3 1.2 %collective-permute-start.2 = (bf16[128,512]{1,0:T(8,128)(2,1)S(1)}, bf16[128,512]{1,0:T(8,128)(2,1)S(1)}, u32[]{:S(2)}, u32[]{:S(2)}) collective-permute-start(bf16[128,512]{1,0:T(8,128)(2,1)S(1)} %get-tuple-element.14.refs_3_), channel_id=1, source_target_pairs={{0,16},{16,0},{1,17},{17,1},{2,18},{18,2},{3,19},{19,3},{4,20},{20... | collective-permute-start | bytes 393224 | tf_op jit(solution)/shard_map/ppermute | solution.py:322
  27.5 6.2 %collective-permute-done.2.refs_5_ = bf16[128,512]{1,0:T(8,128)(2,1)S(1)} collective-permute-done((bf16[128,512]{1,0:T(8,128)(2,1)S(1)}, bf16[128,512]{1,0:T(8,128)(2,1)S(1)}, u32[]{:S(2)}, u32[]{:S(2)}) %collective-permute-start.2) | collective-permute-done | bytes 131104 | tf_op jit(solution)/shard_map/ppermute | solution.py:322
  33.7 0.0 collective-permute-done.3.refs_6_
  33.8 0.0 copy-done.1
  33.8 0.0 copy-done.2
  33.8 7.8 %own.1 = (bf16[256,1024]{1,0:T(8,128)(2,1)S(1)}, bf16[256,1536]{1,0:T(8,128)(2,1)S(1)}, bf16[128,1024]{1,0:T(8,128)(2,1)S(1)}) custom-call(s32[2]{0:T(128)S(1)} %copy-done.3, f32[50,6,1024]{2,1,0:T(8,128)} %copy-done, bf16[1,384,1024]{2,1,0:T(8,128)(2,1)} %refs_2_.1, bf16[128,512]{1,0:T(8,128)(2,1)S(1)} %get-tuple-element.14.refs_3_, ...), custom_call_target="tpu_custom_call" | custom-call | tf_op jit(solution)/shard_map/own/pallas_call | solution.py:368
  41.6 0.0 collective-permute-done.4.refs_5_
  41.6 6.7 %last.1 = bf16[1,384,1024]{2,1,0:T(8,128)(2,1)} custom-call(s32[2]{0:T(128)S(1)} %copy-done.3, f32[50,6,1024]{2,1,0:T(8,128)} %copy-done, bf16[256,1024]{1,0:T(8,128)(2,1)S(1)} %get-tuple-element.18.refs_2_, bf16[256,1536]{1,0:T(8,128)(2,1)S(1)} %get-tuple-element.19.refs_3_, bf16[128,1024]{1,0:T(8,128)(2,1)S(1)} %get-tuple-element.20.refs_4_, ...), custom_call_target="tpu_custom_call" | custom-call | tf_op jit(solution)/shard_map/last/pallas_call | solution.py:380
  (4 shorter events, 0.0 us)
Async XLA Ops:
  1.3 7.5 %copy-start.3 = (s32[2]{0:T(128)S(1)}, s32[2]{0:T(128)}, u32[]{:S(2)}) copy-start(s32[2]{0:T(128)} %refs_0_.3) | copy-start | bytes 28
  1.3 7.5 %copy-start.5 = (f32[2,64]{1,0:T(2,128)S(1)}, f32[2,64]{1,0:T(2,128)}, u32[]{:S(2)}) copy-start(f32[2,64]{1,0:T(2,128)} %gains.3) | copy-start | bytes 1540
  1.3 7.4 %collective-permute-start = (bf16[256,1024]{1,0:T(8,128)(2,1)S(1)}, bf16[256,1024]{1,0:T(8,128)(2,1)S(1)}, u32[]{:S(2)}, u32[]{:S(2)}) collective-permute-start(bf16[256,1024]{1,0:T(8,128)(2,1)S(1)} %get-tuple-element.13), channel_id=1, source_target_pairs={{0,1},{1,0},{2,3},{3,2},{4,5},{5,4},{6,7},{7,6},{8,9},{9,8},{10,11... | collective-permute-start | bytes 1572872 | tf_op jit(solution)/shard_map/ppermute | solution.py:336
  2.1 31.7 %collective-permute-start.3 = (bf16[1,384,1024]{2,1,0:T(8,128)(2,1)}, bf16[1,384,1024]{2,1,0:T(8,128)(2,1)S(1)}, u32[]{:S(2)}, u32[]{:S(2)}) collective-permute-start(bf16[1,384,1024]{2,1,0:T(8,128)(2,1)} %refs_2_.1), channel_id=1, source_target_pairs={{0,16},{16,0},{1,17},{17,1},{2,18},{18,2},{3,19},{19,3},{4,20},{20... | collective-permute-start | bytes 2359304 | tf_op jit(solution)/shard_map/ppermute | solution.py:322
  3.3 16.4 %collective-permute-start.1 = (bf16[256,1024]{1,0:T(8,128)(2,1)S(1)}, bf16[256,1024]{1,0:T(8,128)(2,1)S(1)}, u32[]{:S(2)}, u32[]{:S(2)}) collective-permute-start(bf16[256,1024]{1,0:T(8,128)(2,1)S(1)} %get-tuple-element.15), channel_id=1, source_target_pairs={{1,2},{3,4},{5,6},{7,8},{9,10},{11,12},{13,14},{2,1},{4,3},{6,5},{... | collective-permute-start | bytes 1572872 | tf_op jit(solution)/shard_map/ppermute | solution.py:335
  8.8 11.0 %copy-start = (f32[50,6,1024]{2,1,0:T(8,128)}, f32[50,6,1024]{2,1,0:T(8,128)S(1)}, u32[]{:S(2)}) copy-start(f32[50,6,1024]{2,1,0:T(8,128)S(1)} %copy.13.modulation.refs_1_) | copy-start | bytes 3686404
  19.7 14.0 %copy-start.1 = (bf16[512,1024]{1,0:T(8,128)(2,1)S(1)}, bf16[512,1024]{1,0:T(8,128)(2,1)}, u32[]{:S(2)}) copy-start(bf16[512,1024]{1,0:T(8,128)(2,1)} %refs_7_.3) | copy-start | bytes 3145732
  19.7 14.0 %copy-start.2 = (bf16[512,1024]{1,0:T(8,128)(2,1)S(1)}, bf16[512,1024]{1,0:T(8,128)(2,1)}, u32[]{:S(2)}) copy-start(bf16[512,1024]{1,0:T(8,128)(2,1)} %refs_10_.3) | copy-start | bytes 3145732
  19.7 14.0 %copy-start.4 = (f32[2,64]{1,0:T(2,128)S(1)}, f32[2,64]{1,0:T(2,128)}, u32[]{:S(2)}) copy-start(f32[2,64]{1,0:T(2,128)} %refs_9_.3) | copy-start | bytes 1540
  26.0 15.6 %collective-permute-start.4 = (bf16[256,512]{1,0:T(8,128)(2,1)S(1)}, bf16[256,512]{1,0:T(8,128)(2,1)S(1)}, u32[]{:S(2)}, u32[]{:S(2)}) collective-permute-start(bf16[256,512]{1,0:T(8,128)(2,1)S(1)} %far.1.refs_4_), channel_id=1, source_target_pairs={{0,16},{16,0},{1,17},{17,1},{2,18},{18,2},{3,19},{19,3},{4,20},{20... | collective-permute-start | bytes 786440 | tf_op jit(solution)/shard_map/ppermute | solution.py:322
  26.3 7.4 %collective-permute-start.2 = (bf16[128,512]{1,0:T(8,128)(2,1)S(1)}, bf16[128,512]{1,0:T(8,128)(2,1)S(1)}, u32[]{:S(2)}, u32[]{:S(2)}) collective-permute-start(bf16[128,512]{1,0:T(8,128)(2,1)S(1)} %get-tuple-element.14.refs_3_), channel_id=1, source_target_pairs={{0,16},{16,0},{1,17},{17,1},{2,18},{18,2},{3,19},{19,3},{4,20},{20... | collective-permute-start | bytes 393224 | tf_op jit(solution)/shard_map/ppermute | solution.py:322

commit v2 on v1

--- a/solution.py
+++ b/solution.py
@@ -20,7 +20,11 @@
 VMEM = pl.BlockSpec(memory_space=pltpu.VMEM)
 SMEM = pl.BlockSpec(memory_space=pltpu.SMEM)
 ANY = pl.BlockSpec(memory_space=pl.ANY)
-LIMIT = 48 * 1024 * 1024
+LIMIT = 16 * 1024 * 1024
+
+
+def cost(us):
+    return pl.CostEstimate(flops=int(us * 1e9), bytes_accessed=int(us * 3e6), transcendentals=0)
 
 
 def params():
@@ -116,8 +120,10 @@
     return [slice(at, min(at + BLOCK, rows)) for at in range(0, rows, BLOCK)]
 
 
-def mod_copy(timestep, modulation, row, held, sem):
-    return pltpu.make_async_copy(modulation.at[timestep[row]], held, sem)
+def mods_of(timestep, modulation, back):
+    count = lax.axis_size("stem")
+    step = timestep[lax.rem(lax.axis_index("stem") + count - back, count)]
+    return lambda i: modulation[i, pl.ds(step, 1), :]
 
 
 def split_kernel(frames, near, far, sems):
@@ -133,13 +139,10 @@
     b.wait()
 
 
-def near_kernel(timestep, modulation, frames, near, weight, gains, query, kv, attended, held, sem):
+def near_kernel(timestep, modulation, frames, near, weight, gains, query, kv, attended):
     parity = lax.rem(lax.axis_index("tm"), 2)
-    stem = lax.axis_index("stem")
-    copy = mod_copy(timestep, modulation, stem, held, sem)
-    copy.start()
-    copy.wait()
-    shift, scale = held[0:1], held[1:2]
+    mods = mods_of(timestep, modulation, 0)
+    shift, scale = mods(0), mods(1)
     ones = head_ones()
     rows = frames.shape[1]
     q_gain = wide_gain(gains[0:1]) * (HD ** -0.5)
@@ -170,20 +173,17 @@
     )
 
 
-def far_kernel(timestep, modulation, far, weight, gains, query, kv, attended, held, full, sem, sem_kv):
+def far_kernel(timestep, modulation, far, weight, gains, query, kv, attended, full, sem_kv):
     place = lax.axis_index("tm")
     parity = lax.rem(place, 2)
-    stem = lax.axis_index("stem")
-    copy = mod_copy(timestep, modulation, stem, held, sem)
-    copy.start()
     rows = query.shape[0]
     local = rows + HALF
     local_at = pl.multiple_of((1 - parity) * HALF, BLOCK)
     far_at = parity * local
     moved = pltpu.make_async_copy(kv, full.at[pl.ds(local_at, local)], sem_kv)
     moved.start()
-    copy.wait()
-    shift, scale = held[0:1], held[1:2]
+    mods = mods_of(timestep, modulation, 0)
+    shift, scale = mods(0), mods(1)
     ones = head_ones()
     k_gain = wide_gain(gains[1:2])
     for part in blocks(HALF):
@@ -210,8 +210,8 @@
     return (frames.astype(F32) + gate * mixed).astype(BF16)
 
 
-def projected_cross(first, held, weight, gains, ones, with_query):
-    normed = modulated(first, held[3:4], held[4:5])
+def projected_cross(first, mods, weight, gains, ones, with_query):
+    normed = modulated(first, mods(3), mods(4))
     if with_query:
         projected = dot(normed, weight[...])
         query = head_norm(projected[:, :HW], wide_gain(gains[0:1]), ones)
@@ -228,58 +228,46 @@
     return (first.astype(F32) + gate * out.astype(F32)).astype(BF16)
 
 
-def mods_of_all(timestep, modulation, held, sems):
-    stem = lax.axis_index("stem")
-    count = lax.axis_size("stem")
-    copies = [
-        mod_copy(timestep, modulation, lax.rem(stem + count - k, count), held.at[k], sems.at[k])
-        for k in range(count)
-    ]
-    for copy in copies:
-        copy.start()
-    for copy in copies:
-        copy.wait()
-
-
 def own_kernel(count, timestep, modulation, frames, early, late, *refs):
     others = refs[: count - 1]
     their_frames = refs[count - 1 : 2 * count - 2]
-    out_self, qkv_cross, gains, out_cross, first, qkv, out, held, sems = refs[2 * count - 2 :]
+    out_self, qkv_cross, gains, out_cross, first, qkv, out = refs[2 * count - 2 :]
     parity = lax.rem(lax.axis_index("tm"), 2)
     rows = frames.shape[1]
-    mods_of_all(timestep, modulation, held, sems)
+    all_mods = [mods_of(timestep, modulation, k) for k in range(count)]
+    own = all_mods[0]
     ones = head_ones()
     early_at = pl.multiple_of((1 - parity) * HALF, BLOCK)
     late_at = parity * (rows - HALF)
-    own = held.at[0]
     for part in blocks(HALF):
         at = pl.multiple_of(late_at + part.start, BLOCK)
-        f = first_of(frames[0, pl.ds(at, BLOCK)], late[part], out_self, own[2:3])
+        f = first_of(frames[0, pl.ds(at, BLOCK)], late[part], out_self, own(2))
         first[part] = f
         q, k, v = projected_cross(f, own, qkv_cross, gains, ones, True)
         qkv[part, :HW] = q
         qkv[part, HW : 2 * HW] = k
         qkv[part, 2 * HW :] = v
-    f = first_of(frames[0, pl.ds(early_at, BLOCK)], early[...], out_self, own[2:3])
+    f = first_of(frames[0, pl.ds(early_at, BLOCK)], early[...], out_self, own(2))
     q, k, v = projected_cross(f, own, qkv_cross, gains, ones, True)
     keys, values = [k], [v]
     for n, (attended, source) in enumerate(zip(others, their_frames)):
-        mods = held.at[n + 1]
-        g = first_of(source[0, pl.ds(early_at, BLOCK)], attended[...], out_self, mods[2:3])
+        mods = all_mods[n + 1]
+        g = first_of(source[0, pl.ds(early_at, BLOCK)], attended[...], out_self, mods(2))
         _, k, v = projected_cross(g, mods, qkv_cross, gains, ones, False)
         keys.append(k)
         values.append(v)
     mixed = cross_attend(q, keys, values, ones)
-    out[...] = finished(f, mixed, out_cross, own[5:6])
+    out[...] = finished(f, mixed, out_cross, own(5))
 
 
 def last_kernel(count, timestep, modulation, first, qkv, early_out, *refs):
     others = refs[: count - 1]
     their_frames = refs[count - 1 : 2 * count - 2]
-    out_self, qkv_cross, gains, out_cross, out, held, sems = refs[2 * count - 2 :]
+    out_self, qkv_cross, gains, out_cross, out = refs[2 * count - 2 :]
     parity = lax.rem(lax.axis_index("tm"), 2)
     rows = out.shape[1]
-    mods_of_all(timestep, modulation, held, sems)
+    all_mods = [mods_of(timestep, modulation, k) for k in range(count)]
+    own = all_mods[0]
     ones = head_ones()
     early_at = pl.multiple_of((1 - parity) * HALF, BLOCK)
     late_at = parity * (rows - HALF)
@@ -288,13 +276,13 @@
         at = pl.multiple_of(late_at + part.start, BLOCK)
         keys, values = [qkv[part, HW : 2 * HW]], [qkv[part, 2 * HW :]]
         for n, (attended, source) in enumerate(zip(others, their_frames)):
-            mods = held.at[n + 1]
-            g = first_of(source[0, pl.ds(at, BLOCK)], attended[part], out_self, mods[2:3])
+            mods = all_mods[n + 1]
+            g = first_of(source[0, pl.ds(at, BLOCK)], attended[part], out_self, mods(2))
             _, k, v = projected_cross(g, mods, qkv_cross, gains, ones, False)
             keys.append(k)
             values.append(v)
         mixed = cross_attend(qkv[part, :HW], keys, values, ones)
-        out[0, pl.ds(at, BLOCK)] = finished(first[part], mixed, out_cross, held[0, 5:6])
+        out[0, pl.ds(at, BLOCK)] = finished(first[part], mixed, out_cross, own(5))
 
 
 def on_device(
@@ -311,6 +299,7 @@
     stems = lax.axis_size("stem")
     places = lax.axis_size("tm")
     rows = frames.shape[1]
+    modulation = jnp.transpose(modulation, (1, 0, 2))
     early = rows - HALF
     assert places % 2 == 0 and early == BLOCK
     inside = [(i, i ^ 1) for i in range(places)]
@@ -330,6 +319,7 @@
         out_specs=(ANY, ANY),
         scratch_shapes=[pltpu.SemaphoreType.DMA((2,))],
         compiler_params=params(),
+        cost_estimate=cost(4),
         name="split",
     )(frames)
     far = lax.ppermute(far, "tm", across)
@@ -339,10 +329,10 @@
     query, kv, attended_early = pl.pallas_call(
         near_kernel,
         out_shape=(shape(rows, HW), shape(rows + HALF, 2 * HW), shape(early, HW)),
-        in_specs=[SMEM, ANY, VMEM, VMEM, VMEM, VMEM],
+        in_specs=[SMEM, VMEM, VMEM, VMEM, VMEM, VMEM],
         out_specs=(VMEM, VMEM, VMEM),
-        scratch_shapes=[pltpu.VMEM((6, D), F32), pltpu.SemaphoreType.DMA],
-        compiler_params=params(),
+        compiler_params=params(),
+        cost_estimate=cost(4),
         name="near",
     )(timestep, modulation, frames, near, qkv_self, qk_gain_self)
     others_early = to_stems(attended_early)
@@ -350,28 +340,26 @@
     attended_late = pl.pallas_call(
         far_kernel,
         out_shape=shape(HALF, HW),
-        in_specs=[SMEM, ANY, VMEM, VMEM, VMEM, VMEM, ANY],
+        in_specs=[SMEM, VMEM, VMEM, VMEM, VMEM, VMEM, ANY],
         out_specs=VMEM,
         scratch_shapes=[
-            pltpu.VMEM((6, D), F32),
             pltpu.VMEM((rows + 2 * HALF, 2 * HW), BF16),
             pltpu.SemaphoreType.DMA,
-            pltpu.SemaphoreType.DMA,
         ],
         compiler_params=params(),
+        cost_estimate=cost(4),
         name="far",
     )(timestep, modulation, far, qkv_self, qk_gain_self, query, kv)
     others_late = to_stems(attended_late)
 
-    mods = [pltpu.VMEM((stems, 6, D), F32), pltpu.SemaphoreType.DMA((stems,))]
     pairs = 2 * (stems - 1)
     first, qkv, early_out = pl.pallas_call(
         lambda *refs: own_kernel(stems, *refs),
         out_shape=(shape(HALF, D), shape(HALF, 3 * HW), shape(early, D)),
-        in_specs=[SMEM, ANY] + [VMEM] * (3 + pairs + 4),
+        in_specs=[SMEM, VMEM] + [VMEM] * (3 + pairs + 4),
         out_specs=(VMEM, VMEM, VMEM),
-        scratch_shapes=mods,
-        compiler_params=params(),
+        compiler_params=params(),
+        cost_estimate=cost(8),
         name="own",
     )(
         timestep, modulation, frames, attended_early, attended_late, *others_early, *their_frames,
@@ -380,10 +368,10 @@
     return pl.pallas_call(
         lambda *refs: last_kernel(stems, *refs),
         out_shape=shape(1, rows, D),
-        in_specs=[SMEM, ANY] + [VMEM] * (3 + pairs + 4),
+        in_specs=[SMEM, VMEM] + [VMEM] * (3 + pairs + 4),
         out_specs=VMEM,
-        scratch_shapes=mods,
-        compiler_params=params(),
+        compiler_params=params(),
+        cost_estimate=cost(7),
         name="last",
     )(
         timestep, modulation, first, qkv, early_out, *others_late, *their_frames,

time: 48.8 us -> 39.6 us (0.81)
  the two profiles are of different devices: /device:TPU:25 before, /device:TPU:1 now
where the time goes in v2:
time: 39.6 us; the launch traced here: 39.4 us
  Pallas kernels  22.2 us (56%)
  waiting for transfers between devices  9.44 us (24%)
  starting transfers between devices  7.61 us (19%)
    pallas_call x1, Pallas kernels, on_device(): pl.pallas_call(lambda *refs: own_kernel(stems, *refs), out_shape=(shape(H...  5.97 us
    pallas_call x1, Pallas kernels, on_device(): pl.pallas_call(near_kernel, out_shape=(shape(rows, HW), shape(rows + HALF...  5.65 us
    ppermute x3, waiting for transfers between devices, to_stems(): lax.ppermute(array, 'stem', [(i, (i + k) % stems) for i in range(stems)])  5 us
    pallas_call x1, Pallas kernels, on_device(): pl.pallas_call(far_kernel, out_shape=shape(HALF, HW), in_specs=[SMEM, VME...  4.68 us
    ppermute x1, starting transfers between devices, on_device(): far = lax.ppermute(far, 'tm', across)  4.61 us
    pallas_call x1, Pallas kernels, on_device(): pl.pallas_call(lambda *refs: last_kernel(stems, *refs), out_shape=shape(1...  4.5 us
    ppermute x1, waiting for transfers between devices, on_device(): far = lax.ppermute(far, 'tm', across)  4.44 us
    ppermute x3, starting transfers between devices, to_stems(): lax.ppermute(array, 'stem', [(i, (i + k) % stems) for i in range(stems)])  2.89 us
  transfers between devices with their start and end apart: 5, of which 2 were waited for; matrix products, arithmetic and copies ran while one was open for 0% of the time, Pallas kernels for 41%

profile of v2, /device:TPU:1, one launch (start us, length us, event | category | flops | bytes accessed | tf_op | source)
XLA Modules:
  0.0 39.4 jit_solution(3171893539874295508)
XLA Ops:
  0.0 0.0 copy-start.5
  0.0 1.4 %split.1 = (bf16[256,1024]{1,0:T(8,128)(2,1)S(1)}, bf16[256,1024]{1,0:T(8,128)(2,1)S(1)}) custom-call(bf16[1,384,1024]{2,1,0:T(8,128)(2,1)} %refs_2_.1), custom_call_target="tpu_custom_call" | custom-call | flops 4000000000 | bytes 12000000 | tf_op jit(solution)/shard_map/split/pallas_call | solution.py:315
  1.4 0.1 collective-permute-start
  1.5 4.6 %collective-permute-start.1 = (bf16[256,1024]{1,0:T(8,128)(2,1)S(1)}, bf16[256,1024]{1,0:T(8,128)(2,1)S(1)}, u32[]{:S(2)}, u32[]{:S(2)}) collective-permute-start(bf16[256,1024]{1,0:T(8,128)(2,1)S(1)} %get-tuple-element.15), channel_id=1, source_target_pairs={{1,2},{3,4},{5,6},{7,8},{9,10},{11,12},{13,14},{2,1},{4,3},{6,5},{... | collective-permute-start | bytes 1572872 | tf_op jit(solution)/shard_map/ppermute | solution.py:325
  6.1 1.3 %collective-permute-start.3 = (bf16[1,384,1024]{2,1,0:T(8,128)(2,1)}, bf16[1,384,1024]{2,1,0:T(8,128)(2,1)S(1)}, u32[]{:S(2)}, u32[]{:S(2)}) collective-permute-start(bf16[1,384,1024]{2,1,0:T(8,128)(2,1)} %refs_2_.1), channel_id=1, source_target_pairs={{0,16},{16,0},{1,17},{17,1},{2,18},{18,2},{3,19},{19,3},{4,20},{20... | collective-permute-start | bytes 2359304 | tf_op jit(solution)/shard_map/ppermute | solution.py:311
  7.4 0.0 collective-permute-done.near
  7.4 0.0 copy-done.2
  7.4 0.0 copy-done.7
  7.5 0.0 copy-done
  7.5 0.0 copy-done.5
  7.5 5.7 %near.1 = (bf16[384,512]{1,0:T(8,128)(2,1)S(1)}, bf16[640,1024]{1,0:T(8,128)(2,1)S(1)}, bf16[128,512]{1,0:T(8,128)(2,1)S(1)}) custom-call(s32[2]{0:T(128)S(1)} %copy-done.7, f32[6,50,1024]{2,1,0:T(8,128)S(1)} %bitcast.1, bf16[1,384,1024]{2,1,0:T(8,128)(2,1)} %refs_2_.1, bf16[256,1024]{1,0:T(8,128)(2,1)S(1)} %collective-permute-done.near, ...), custom_call_target="tpu_custom_call" | custom-call | flops 4000000000 | bytes 12000000 | tf_op jit(solution)/shard_map/near/pallas_call | solution.py:329
  13.1 0.3 collective-permute-start.2
  13.4 4.4 %collective-permute-done.1.far = bf16[256,1024]{1,0:T(8,128)(2,1)S(1)} collective-permute-done((bf16[256,1024]{1,0:T(8,128)(2,1)S(1)}, bf16[256,1024]{1,0:T(8,128)(2,1)S(1)}, u32[]{:S(2)}, u32[]{:S(2)}) %collective-permute-start.1) | collective-permute-done | bytes 524320 | tf_op jit(solution)/shard_map/ppermute | solution.py:325
  17.9 4.7 %far.1.refs_4_ = bf16[256,512]{1,0:T(8,128)(2,1)S(1)} custom-call(s32[2]{0:T(128)S(1)} %copy-done.7, f32[6,50,1024]{2,1,0:T(8,128)S(1)} %bitcast.2, bf16[256,1024]{1,0:T(8,128)(2,1)S(1)} %collective-permute-done.1.far, bf16[1024,1536]{1,0:T(8,128)(2,1)S(1)} %copy-done, f32[2,64]{1,0:T(2,128)S(1)} %copy-done.5, bf16[384,512]{1,0:T(8,128)(2,1)S(1)} %get-tuple-element.16.query, ...), custom_call_target="tpu_custom_call" | custom-call | flops 4000000000 | bytes 12000000 | tf_op jit(solution)/shard_map/far/pallas_call | solution.py:340
  22.5 1.3 %collective-permute-start.4 = (bf16[256,512]{1,0:T(8,128)(2,1)S(1)}, bf16[256,512]{1,0:T(8,128)(2,1)S(1)}, u32[]{:S(2)}, u32[]{:S(2)}) collective-permute-start(bf16[256,512]{1,0:T(8,128)(2,1)S(1)} %far.1.refs_4_), channel_id=1, source_target_pairs={{0,16},{16,0},{1,17},{17,1},{2,18},{18,2},{3,19},{19,3},{4,20},{20... | collective-permute-start | bytes 786440 | tf_op jit(solution)/shard_map/ppermute | solution.py:311
  23.9 5.0 %collective-permute-done.2.refs_5_ = bf16[128,512]{1,0:T(8,128)(2,1)S(1)} collective-permute-done((bf16[128,512]{1,0:T(8,128)(2,1)S(1)}, bf16[128,512]{1,0:T(8,128)(2,1)S(1)}, u32[]{:S(2)}, u32[]{:S(2)}) %collective-permute-start.2) | collective-permute-done | bytes 131104 | tf_op jit(solution)/shard_map/ppermute | solution.py:311
  28.8 0.0 collective-permute-done.3.refs_6_
  28.8 0.0 copy-done.1
  28.9 0.0 copy-done.3
  28.9 0.0 copy-done.4
  28.9 0.0 copy-done.6
  28.9 6.0 %own.1 = (bf16[256,1024]{1,0:T(8,128)(2,1)S(1)}, bf16[256,1536]{1,0:T(8,128)(2,1)S(1)}, bf16[128,1024]{1,0:T(8,128)(2,1)S(1)}) custom-call(s32[2]{0:T(128)S(1)} %copy-done.7, f32[6,50,1024]{2,1,0:T(8,128)S(1)} %bitcast.3, bf16[1,384,1024]{2,1,0:T(8,128)(2,1)} %refs_2_.1, bf16[128,512]{1,0:T(8,128)(2,1)S(1)} %get-tuple-element.14.refs_3_, ...), custom_call_target="tpu_custom_call" | custom-call | flops 8000000000 | bytes 24000000 | tf_op jit(solution)/shard_map/own/pallas_call | solution.py:356
  34.8 0.0 collective-permute-done.4.refs_5_
  34.9 4.5 %last.1 = bf16[1,384,1024]{2,1,0:T(8,128)(2,1)} custom-call(s32[2]{0:T(128)S(1)} %copy-done.7, f32[6,50,1024]{2,1,0:T(8,128)S(1)} %bitcast.4, bf16[256,1024]{1,0:T(8,128)(2,1)S(1)} %get-tuple-element.18.refs_2_, bf16[256,1536]{1,0:T(8,128)(2,1)S(1)} %get-tuple-element.19.refs_3_, bf16[128,1024]{1,0:T(8,128)(2,1)S(1)} %get-tuple-element.20.refs_4_, ...), custom_call_target="tpu_custom_call" | custom-call | flops 7000000000 | bytes 21000000 | tf_op jit(solution)/shard_map/last/pallas_call | solution.py:368
  (7 shorter events, 0.0 us)
Async XLA Ops:
  0.0 7.4 %copy-start.2 = (f32[50,6,1024]{2,0,1:T(8,128)S(1)}, f32[50,6,1024]{2,0,1:T(8,128)}, u32[]{:S(2)}) copy-start(f32[50,6,1024]{2,0,1:T(8,128)} %param.11) | copy-start | bytes 3686404
  0.0 7.4 %copy-start.7 = (s32[2]{0:T(128)S(1)}, s32[2]{0:T(128)}, u32[]{:S(2)}) copy-start(s32[2]{0:T(128)} %refs_0_.3) | copy-start | bytes 28
  0.0 7.4 %copy-start = (bf16[1024,1536]{1,0:T(8,128)(2,1)S(1)}, bf16[1024,1536]{1,0:T(8,128)(2,1)}, u32[]{:S(2)}) copy-start(bf16[1024,1536]{1,0:T(8,128)(2,1)} %weight.3) | copy-start | bytes 9437188
  0.0 7.5 %copy-start.5 = (f32[2,64]{1,0:T(2,128)S(1)}, f32[2,64]{1,0:T(2,128)}, u32[]{:S(2)}) copy-start(f32[2,64]{1,0:T(2,128)} %gains.3) | copy-start | bytes 1540
  1.4 6.0 %collective-permute-start = (bf16[256,1024]{1,0:T(8,128)(2,1)S(1)}, bf16[256,1024]{1,0:T(8,128)(2,1)S(1)}, u32[]{:S(2)}, u32[]{:S(2)}) collective-permute-start(bf16[256,1024]{1,0:T(8,128)(2,1)S(1)} %get-tuple-element.13), channel_id=1, source_target_pairs={{0,1},{1,0},{2,3},{3,2},{4,5},{5,4},{6,7},{7,6},{8,9},{9,8},{10,11... | collective-permute-start | bytes 1572872 | tf_op jit(solution)/shard_map/ppermute | solution.py:326
  1.5 16.3 %collective-permute-start.1 = (bf16[256,1024]{1,0:T(8,128)(2,1)S(1)}, bf16[256,1024]{1,0:T(8,128)(2,1)S(1)}, u32[]{:S(2)}, u32[]{:S(2)}) collective-permute-start(bf16[256,1024]{1,0:T(8,128)(2,1)S(1)} %get-tuple-element.15), channel_id=1, source_target_pairs={{1,2},{3,4},{5,6},{7,8},{9,10},{11,12},{13,14},{2,1},{4,3},{6,5},{... | collective-permute-start | bytes 1572872 | tf_op jit(solution)/shard_map/ppermute | solution.py:325
  6.1 22.7 %collective-permute-start.3 = (bf16[1,384,1024]{2,1,0:T(8,128)(2,1)}, bf16[1,384,1024]{2,1,0:T(8,128)(2,1)S(1)}, u32[]{:S(2)}, u32[]{:S(2)}) collective-permute-start(bf16[1,384,1024]{2,1,0:T(8,128)(2,1)} %refs_2_.1), channel_id=1, source_target_pairs={{0,16},{16,0},{1,17},{17,1},{2,18},{18,2},{3,19},{19,3},{4,20},{20... | collective-permute-start | bytes 2359304 | tf_op jit(solution)/shard_map/ppermute | solution.py:311
  13.1 15.7 %collective-permute-start.2 = (bf16[128,512]{1,0:T(8,128)(2,1)S(1)}, bf16[128,512]{1,0:T(8,128)(2,1)S(1)}, u32[]{:S(2)}, u32[]{:S(2)}) collective-permute-start(bf16[128,512]{1,0:T(8,128)(2,1)S(1)} %get-tuple-element.14.refs_3_), channel_id=1, source_target_pairs={{0,16},{16,0},{1,17},{17,1},{2,18},{18,2},{3,19},{19,3},{4,20},{20... | collective-permute-start | bytes 393224 | tf_op jit(solution)/shard_map/ppermute | solution.py:311
  17.9 11.0 %copy-start.1 = (bf16[1024,1536]{1,0:T(8,128)(2,1)S(1)}, bf16[1024,1536]{1,0:T(8,128)(2,1)}, u32[]{:S(2)}) copy-start(bf16[1024,1536]{1,0:T(8,128)(2,1)} %refs_8_.3) | copy-start | bytes 9437188
  17.9 11.0 %copy-start.3 = (bf16[512,1024]{1,0:T(8,128)(2,1)S(1)}, bf16[512,1024]{1,0:T(8,128)(2,1)}, u32[]{:S(2)}) copy-start(bf16[512,1024]{1,0:T(8,128)(2,1)} %refs_7_.3) | copy-start | bytes 3145732
  17.9 11.0 %copy-start.4 = (bf16[512,1024]{1,0:T(8,128)(2,1)S(1)}, bf16[512,1024]{1,0:T(8,128)(2,1)}, u32[]{:S(2)}) copy-start(bf16[512,1024]{1,0:T(8,128)(2,1)} %refs_10_.3) | copy-start | bytes 3145732
  17.9 11.0 %copy-start.6 = (f32[2,64]{1,0:T(2,128)S(1)}, f32[2,64]{1,0:T(2,128)}, u32[]{:S(2)}) copy-start(f32[2,64]{1,0:T(2,128)} %refs_9_.3) | copy-start | bytes 1540
  22.5 12.3 %collective-permute-start.4 = (bf16[256,512]{1,0:T(8,128)(2,1)S(1)}, bf16[256,512]{1,0:T(8,128)(2,1)S(1)}, u32[]{:S(2)}, u32[]{:S(2)}) collective-permute-start(bf16[256,512]{1,0:T(8,128)(2,1)S(1)} %far.1.refs_4_), channel_id=1, source_target_pairs={{0,16},{16,0},{1,17},{17,1},{2,18},{18,2},{3,19},{19,3},{4,20},{20... | collective-permute-start | bytes 786440 | tf_op jit(solution)/shard_map/ppermute | solution.py:311

commit v3 on v2

v3 whole, which is shorter than its diff:
```python
import jax
import jax.numpy as jnp
from jax import lax
from jax.experimental import pallas as pl
from jax.experimental.pallas import tpu as pltpu
from jax.sharding import PartitionSpec as P

D = 1024
H = 8
HD = 64
HW = H * HD
HALF = 256
BLOCK = 128
SLAB = 128
EPS = 1e-06
NEG = -1e30
F32 = jnp.float32
BF16 = jnp.bfloat16
VMEM = pl.BlockSpec(memory_space=pltpu.VMEM)
SMEM = pl.BlockSpec(memory_space=pltpu.SMEM)
ANY = pl.BlockSpec(memory_space=pl.ANY)
LIMIT = 16 * 1024 * 1024


def cost(us):
    return pl.CostEstimate(flops=int(us * 1e9), bytes_accessed=int(us * 3e6), transcendentals=0)


def params():
    return pltpu.CompilerParams(vmem_limit_bytes=LIMIT)


def shape(*dims, dtype=BF16):
    return jax.ShapeDtypeStruct(dims, dtype)


def dot(a, b, dims=((1,), (0,))):
    return lax.dot_general(a, b, (dims, ((), ())), preferred_element_type=F32)


def modulated(rows, shift, scale):
    values = rows.astype(F32)
    centred = values - jnp.mean(values, axis=-1, keepdims=True)
    spread = jnp.mean(centred * centred, axis=-1, keepdims=True)
    normed = centred * lax.rsqrt(spread + EPS)
    return (normed * (1.0 + scale) + shift).astype(BF16)


def head_ones():
    row = lax.broadcasted_iota(jnp.int32, (2 * SLAB, 2 * SLAB), 0) // HD
    col = lax.broadcasted_iota(jnp.int32, (2 * SLAB, 2 * SLAB), 1) // HD
    return jnp.where(row == col, 1.0, 0.0).astype(BF16)


def head_sums(values, ones):
    parts = [dot(values[:, at : at + 2 * SLAB], ones) for at in range(0, HW, 2 * SLAB)]
    return jnp.concatenate(parts, axis=1)


def exact_head_sums(values, ones):
    high = values.astype(BF16)
    low = (values - high.astype(F32)).astype(BF16)
    return head_sums(high, ones) + head_sums(low, ones)


def head_norm(values, gain, ones):
    mean = head_sums((values * values).astype(BF16), ones) * (1.0 / HD)
    return (values * lax.rsqrt(mean + EPS) * gain).astype(BF16)


def wide_gain(gain):
    return jnp.concatenate([gain] * H, axis=1)


def window_bias(keys, ahead, first_frame=0, total=1 << 30):
    i = lax.broadcasted_iota(jnp.int32, (BLOCK, keys), 0)
    j = lax.broadcasted_iota(jnp.int32, (BLOCK, keys), 1)
    frame = first_frame + j
    keep = (j + ahead >= i) & (j + ahead <= i + 2 * HALF) & (frame >= 0) & (frame < total)
    return jnp.where(keep, 0.0, NEG)


def left_half():
    return lax.broadcasted_iota(jnp.int32, (BLOCK, SLAB), 1) < HD


def by_head(pair):
    return jnp.where(left_half(), pair[:BLOCK], pair[BLOCK:])


def raised_scores(query, keys, bias):
    half, zero = left_half(), jnp.zeros_like(query)
    pair = jnp.concatenate([jnp.where(half, query, zero), jnp.where(half, zero, query)], axis=0)
    scores = dot(pair, keys, ((1,), (1,)))
    scores = jnp.concatenate([scores[:BLOCK] + bias, scores[BLOCK:] + bias], axis=0)
    top = jnp.max(scores, axis=-1, keepdims=True)
    return jnp.exp(scores - top).astype(BF16), top


def weighted(raised, values):
    summed = dot(raised, jnp.concatenate([values, jnp.ones_like(values)], axis=1))
    return by_head(summed[:, :SLAB]), by_head(summed[:, SLAB:])


def cross_attend(query, keys, values, ones):
    query = query.astype(F32)
    base = keys[0].astype(F32)
    scores = [
        exact_head_sums(query * (k.astype(F32) - base), ones) * (HD ** -0.5) for k in keys[1:]
    ]
    top = jnp.zeros_like(query)
    for s in scores:
        top = jnp.maximum(top, s)
    raised = [jnp.exp(-top)] + [jnp.exp(s - top) for s in scores]
    total = raised[0]
    for r in raised[1:]:
        total = total + r
    scale = 1.0 / total
    out = jnp.zeros_like(query)
    for r, v in zip(raised, values):
        out = out + (r * scale).astype(BF16).astype(F32) * v.astype(F32)
    return out.astype(BF16)


def mods_of(timestep, modulation, back):
    count = lax.axis_size("stem")
    step = timestep[lax.rem(lax.axis_index("stem") + count - back, count)]
    return lambda i: modulation[i, pl.ds(step, 1), :]


def places(rows):
    parity = lax.rem(lax.axis_index("tm"), 2)
    outer = pl.multiple_of(parity * HALF, BLOCK)
    early = pl.multiple_of((1 - parity) * HALF, BLOCK)
    return parity, outer, rows - HALF, early


def pending(parity):
    return pl.multiple_of(parity * BLOCK, BLOCK), pl.multiple_of((1 - parity) * BLOCK, BLOCK)


def split_kernel(frames, far, sem):
    parity = lax.rem(lax.axis_index("tm"), 2)
    at = pl.multiple_of(parity * (frames.shape[1] - HALF), BLOCK)
    copy = pltpu.make_async_copy(frames.at[0, pl.ds(at, HALF)], far, sem)
    copy.start()
    copy.wait()


def near_kernel(
    timestep, modulation, frames, near, qkv_self, gains, out_self, qkv_cross, gains_cross,
    query, part_out, part_sum, part_top, first, first_q, first_kv, kv,
):
    rows = frames.shape[1]
    parity, outer, inner, early = places(rows)
    mods = mods_of(timestep, modulation, 0)
    shift, scale = mods(0), mods(1)
    ones = head_ones()
    q_gain = wide_gain(gains[0:1]) * (HD ** -0.5)
    k_gain = wide_gain(gains[1:2])
    own_at = parity * HALF
    near_at = (1 - parity) * rows
    near_from = parity * (rows - HALF)

    sources = [(frames, at, own_at + at) for at in (early, outer, inner)]
    sources += [(near, near_from + at, near_at + at) for at in range(0, HALF, BLOCK)]
    queries = []
    for n, (source, at, to) in enumerate(sources):
        normed = modulated(source[0, pl.ds(pl.multiple_of(at, BLOCK), BLOCK)], shift, scale)
        if n < 3:
            projected = dot(normed, qkv_self[...])
            queries.append(head_norm(projected[:, :HW], q_gain, ones))
            projected = projected[:, HW:]
        else:
            projected = dot(normed, qkv_self[:, HW:])
        to = pl.multiple_of(to, BLOCK)
        kv[pl.ds(to, BLOCK), :HW] = head_norm(projected[:, :HW], k_gain, ones)
        kv[pl.ds(to, BLOCK), HW:] = projected[:, HW:].astype(BF16)
    query[:BLOCK] = queries[1]
    query[BLOCK:] = queries[2]

    window = rows + HALF
    bias = window_bias(window, 0)
    attended = []
    for at in range(0, HW, SLAB):
        raised, _ = raised_scores(queries[0][:, at : at + SLAB], kv[:, at : at + SLAB], bias)
        out, total = weighted(raised, kv[:, HW + at : HW + at + SLAB])
        attended.append((out / total).astype(BF16))
    attended = jnp.concatenate(attended, axis=1)

    f = first_of(frames[0, pl.ds(early, BLOCK)], attended, out_self, mods(2))
    first[...] = f
    first_q[...], first_kv[:, :HW], first_kv[:, HW:] = projected_cross(
        f, mods, qkv_cross, gains_cross, ones, True
    )

    for n, width in ((0, HALF), (1, BLOCK)):
        start = pl.multiple_of(parity * width, BLOCK)
        count = window - width
        bias = window_bias(count, (1 - parity) * width)
        to = slice(n * BLOCK, (n + 1) * BLOCK)
        for at in range(0, HW, SLAB):
            cols = slice(at, at + SLAB)
            raised, top = raised_scores(
                queries[n + 1][:, cols], kv[pl.ds(start, count), cols], bias
            )
            out, total = weighted(raised, kv[pl.ds(start, count), HW + at : HW + at + SLAB])
            part_out[to, cols] = out
            part_sum[to, cols] = total
            part_top[to, cols] = by_head(jnp.broadcast_to(top, (2 * BLOCK, SLAB)))


def far_kernel(
    rows, timestep, modulation, far, qkv_self, gains, query, part_out, part_sum, part_top, attended
):
    parity, _, _, _ = places(rows)
    mods = mods_of(timestep, modulation, 0)
    shift, scale = mods(0), mods(1)
    ones = head_ones()
    k_gain = wide_gain(gains[1:2])
    keys, values = [], []
    for at in range(0, HALF, BLOCK):
        normed = modulated(far[at : at + BLOCK], shift, scale)
        projected = dot(normed, qkv_self[:, HW:])
        keys.append(head_norm(projected[:, :HW], k_gain, ones))
        values.append(projected[:, HW:].astype(BF16))
    keys = jnp.concatenate(keys, axis=0)
    values = jnp.concatenate(values, axis=0)
    place = lax.axis_index("tm")
    total = rows * lax.axis_size("tm")
    first_frame = place * rows + jnp.where(parity == 0, -HALF, rows)
    outer_bias = window_bias(HALF, jnp.where(parity == 0, 0, rows), first_frame, total)
    inner_bias = window_bias(HALF, jnp.where(parity == 0, -BLOCK, rows + BLOCK), first_frame, total)
    for at in range(0, HW, SLAB):
        cols = slice(at, at + SLAB)
        for n, bias in enumerate((outer_bias, inner_bias)):
            to = slice(n * BLOCK, (n + 1) * BLOCK)
            raised, top = raised_scores(query[to, cols], keys[:, cols], bias)
            out, summed = weighted(raised, values[:, cols])
            top = by_head(jnp.broadcast_to(top, (2 * BLOCK, SLAB)))
            both = jnp.maximum(top, part_top[to, cols])
            here = jnp.exp(top - both)
            before = jnp.exp(part_top[to, cols] - both)
            out = out * here + part_out[to, cols] * before
            summed = summed * here + part_sum[to, cols] * before
            attended[to, cols] = (out / summed).astype(BF16)


def first_of(frames, attended, weight, gate):
    mixed = dot(attended, weight[...])
    return (frames.astype(F32) + gate * mixed).astype(BF16)


def projected_cross(first, mods, weight, gains, ones, with_query):
    normed = modulated(first, mods(3), mods(4))
    if with_query:
        projected = dot(normed, weight[...])
        query = head_norm(projected[:, :HW], wide_gain(gains[0:1]), ones)
        projected = projected[:, HW:]
    else:
        projected = dot(normed, weight[:, HW:])
        query = None
    keys = head_norm(projected[:, :HW], wide_gain(gains[1:2]), ones)
    return query, keys, projected[:, HW:].astype(BF16)


def finished(first, attended, weight, gate):
    out = dot(attended, weight[...]).astype(BF16)
    return (first.astype(F32) + gate * out.astype(F32)).astype(BF16)


def own_kernel(
    rows, timestep, modulation, frames, attended, out_self, qkv_cross, gains, first, qkv
):
    mods = mods_of(timestep, modulation, 0)
    ones = head_ones()
    parity, _, _, _ = places(rows)
    for n, at in enumerate(pending(parity)):
        to = slice(n * BLOCK, (n + 1) * BLOCK)
        f = first_of(frames[pl.ds(at, BLOCK)], attended[to], out_self, mods(2))
        first[to] = f
        q, k, v = projected_cross(f, mods, qkv_cross, gains, ones, True)
        qkv[to, :HW] = q
        qkv[to, HW : 2 * HW] = k
        qkv[to, 2 * HW :] = v


def early_kernel(timestep, modulation, first, query, kv, out_cross, *refs):
    others, out = refs[:-1], refs[-1]
    mods = mods_of(timestep, modulation, 0)
    keys = [each[:, :HW] for each in (kv, *others)]
    values = [each[:, HW:] for each in (kv, *others)]
    mixed = cross_attend(query[...], keys, values, head_ones())
    out[...] = finished(first[...], mixed, out_cross, mods(5))


def last_kernel(count, timestep, modulation, first, qkv, early_out, *refs):
    others = refs[: count - 1]
    their_frames = refs[count - 1 : 2 * count - 2]
    out_self, qkv_cross, gains, out_cross, out = refs[2 * count - 2 :]
    rows = out.shape[1]
    own, *mods = [mods_of(timestep, modulation, k) for k in range(count)]
    ones = head_ones()
    parity, outer, inner, early = places(rows)
    out[0, pl.ds(early, BLOCK)] = early_out[...]
    for n, (at, to) in enumerate(zip(pending(parity), (outer, inner))):
        part = slice(n * BLOCK, (n + 1) * BLOCK)
        keys, values = [qkv[part, HW : 2 * HW]], [qkv[part, 2 * HW :]]
        for attended, source, their in zip(others, their_frames, mods):
            g = first_of(source[pl.ds(at, BLOCK)], attended[part], out_self, their(2))
            _, k, v = projected_cross(g, their, qkv_cross, gains, ones, False)
            keys.append(k)
            values.append(v)
        mixed = cross_attend(qkv[part, :HW], keys, values, ones)
        out[0, pl.ds(to, BLOCK)] = finished(first[part], mixed, out_cross, own(5))


def on_device(
    frames,
    timestep,
    modulation,
    qkv_self,
    out_self,
    qk_gain_self,
    qkv_cross,
    out_cross,
    qk_gain_cross,
):
    stems = lax.axis_size("stem")
    count = lax.axis_size("tm")
    rows = frames.shape[1]
    assert count % 2 == 0 and rows == HALF + BLOCK
    modulation = jnp.transpose(modulation, (1, 0, 2))
    inside = [(i, i ^ 1) for i in range(count)]
    across = [(i, i + 1) for i in range(1, count - 1, 2)]
    across += [(b, a) for a, b in across]

    def to_stems(array):
        return [
            lax.ppermute(array, "stem", [(i, (i + k) % stems) for i in range(stems)])
            for k in range(1, stems)
        ]

    near = lax.ppermute(frames, "tm", inside)
    far_own = pl.pallas_call(
        split_kernel,
        out_shape=shape(HALF, D),
        in_specs=[ANY],
        out_specs=ANY,
        scratch_shapes=[pltpu.SemaphoreType.DMA],
        compiler_params=params(),
        cost_estimate=cost(4),
        name="split",
    )(frames)
    far = lax.ppermute(far_own, "tm", across)
    their_frames = to_stems(far_own)

    query, part_out, part_sum, part_top, first_early, q_early, kv_early = pl.pallas_call(
        near_kernel,
        out_shape=(
            shape(HALF, HW),
            shape(HALF, HW, dtype=F32),
            shape(HALF, HW, dtype=F32),
            shape(HALF, HW, dtype=F32),
            shape(BLOCK, D),
            shape(BLOCK, HW),
            shape(BLOCK, 2 * HW),
        ),
        in_specs=[SMEM] + [VMEM] * 8,
        out_specs=(VMEM,) * 7,
        scratch_shapes=[pltpu.VMEM((rows + HALF, 2 * HW), BF16)],
        compiler_params=params(),
        cost_estimate=cost(4),
        name="near",
    )(
        timestep, modulation, frames, near, qkv_self, qk_gain_self, out_self, qkv_cross,
        qk_gain_cross,
    )
    others_early = to_stems(kv_early)

    attended = pl.pallas_call(
        lambda *refs: far_kernel(rows, *refs),
        out_shape=shape(HALF, HW),
        in_specs=[SMEM] + [VMEM] * 8,
        out_specs=VMEM,
        compiler_params=params(),
        cost_estimate=cost(4),
        name="far",
    )(timestep, modulation, far, qkv_self, qk_gain_self, query, part_out, part_sum, part_top)
    others_attended = to_stems(attended)

    first, qkv = pl.pallas_call(
        lambda *refs: own_kernel(rows, *refs),
        out_shape=(shape(HALF, D), shape(HALF, 3 * HW)),
        in_specs=[SMEM] + [VMEM] * 6,
        out_specs=(VMEM, VMEM),
        compiler_params=params(),
        cost_estimate=cost(4),
        name="own",
    )(timestep, modulation, far_own, attended, out_self, qkv_cross, qk_gain_cross)
    early_out = pl.pallas_call(
        early_kernel,
        out_shape=shape(BLOCK, D),
        in_specs=[SMEM] + [VMEM] * (4 + stems),
        out_specs=VMEM,
        compiler_params=params(),
        cost_estimate=cost(2),
        name="early",
    )(timestep, modulation, first_early, q_early, kv_early, out_cross, *others_early)
    return pl.pallas_call(
        lambda *refs: last_kernel(stems, *refs),
        out_shape=shape(1, rows, D),
        in_specs=[SMEM] + [VMEM] * (6 + 2 * stems),
        out_specs=VMEM,
        compiler_params=params(),
        cost_estimate=cost(4),
        name="last",
    )(
        timestep, modulation, first, qkv, early_out, *others_attended, *their_frames,
        out_self, qkv_cross, qk_gain_cross, out_cross,
    )


def solution(mesh):
    return jax.shard_map(
        on_device,
        mesh=mesh,
        in_specs=(P("stem", "tm", None), P(), P(), P(), P(), P(), P(), P(), P()),
        out_specs=P("stem", "tm", None),
        check_vma=False,
    )
```

time: 39.6 us -> 35.2 us (0.89)
  the two profiles are of different devices: /device:TPU:1 before, /device:TPU:15 now
where the time goes in v3:
time: 35.2 us; the launch traced here: 35.1 us
  Pallas kernels  19.1 us (54%)
  waiting for transfers between devices  8.59 us (24%)
  starting transfers between devices  5.75 us (16%)
  local copies, waits for them, and re-layouts  1.53 us (4%)
    ppermute x3, waiting for transfers between devices, to_stems(): lax.ppermute(array, 'stem', [(i, (i + k) % stems) for i in range(stems)])  8.58 us
    pallas_call x1, Pallas kernels, on_device(): pl.pallas_call(near_kernel, out_shape=(shape(HALF, HW), shape(HALF, HW, d...  8.01 us
    pallas_call x1, Pallas kernels, on_device(): pl.pallas_call(lambda *refs: last_kernel(stems, *refs), out_shape=shape(1...  4.42 us
    ppermute x1, starting transfers between devices, on_device(): far = lax.ppermute(far_own, 'tm', across)  3.12 us
    pallas_call x1, Pallas kernels, on_device(): pl.pallas_call(lambda *refs: own_kernel(rows, *refs), out_shape=(shape(HA...  2.78 us
    pallas_call x1, Pallas kernels, on_device(): pl.pallas_call(lambda *refs: far_kernel(rows, *refs), out_shape=shape(HAL...  2.67 us
    ppermute x3, starting transfers between devices, to_stems(): lax.ppermute(array, 'stem', [(i, (i + k) % stems) for i in range(stems)])  1.89 us
    unnamed x18, local copies, waits for them, and re-layouts  1.53 us
  transfers between devices with their start and end apart: 5, of which 2 were waited for; matrix products, arithmetic and copies ran while one was open for 0% of the time, Pallas kernels for 42%

profile of v3, /device:TPU:15, one launch (start us, length us, event | category | flops | bytes accessed | tf_op | source)
XLA Modules:
  0.0 35.1 jit_solution(6810300221501669516)
XLA Ops:
  0.0 0.0 copy-start.1
  0.0 0.7 %collective-permute-start.1 = (bf16[1,384,1024]{2,1,0:T(8,128)(2,1)}, bf16[1,384,1024]{2,1,0:T(8,128)(2,1)S(1)}, u32[]{:S(2)}, u32[]{:S(2)}) collective-permute-start(bf16[1,384,1024]{2,1,0:T(8,128)(2,1)} %frames.3), channel_id=1, source_target_pairs={{0,1},{1,0},{2,3},{3,2},{4,5},{5,4},{6,7},{7,6},{8,9},{9,8},{10,11... | collective-permute-start | bytes 2359304 | tf_op jit(solution)/shard_map/ppermute | solution.py:344
  0.8 1.5 %copy-done.5 = bf16[1,384,1024]{2,1,0:T(8,128)(2,1)S(1)} copy-done((bf16[1,384,1024]{2,1,0:T(8,128)(2,1)S(1)}, bf16[1,384,1024]{2,1,0:T(8,128)(2,1)}, u32[]{:S(2)}) %copy-start.5) | copy-done | bytes 786456
  2.3 3.1 %collective-permute-start = (bf16[256,1024]{1,0:T(8,128)(2,1)S(1)}, bf16[256,1024]{1,0:T(8,128)(2,1)S(1)}, u32[]{:S(2)}, u32[]{:S(2)}) collective-permute-start(bf16[256,1024]{1,0:T(8,128)(2,1)S(1)} %split.1.refs_2_), channel_id=1, source_target_pairs={{1,2},{3,4},{5,6},{7,8},{9,10},{11,12},{13,14},{2,1},{4,3},{6,5},{... | collective-permute-start | bytes 1572872 | tf_op jit(solution)/shard_map/ppermute | solution.py:355
  5.5 0.3 collective-permute-start.4
  5.7 0.0 collective-permute-done.1.near
  5.7 0.0 copy-done.2
  5.7 0.0 copy-done
  5.8 0.0 copy-done.3
  5.8 0.0 copy-done.1
  5.8 0.0 copy-done.6
  5.8 0.0 copy-done.7
  5.8 8.0 %near.1 = (bf16[256,512]{1,0:T(8,128)(2,1)S(1)}, f32[256,512]{1,0:T(8,128)S(1)}, f32[256,512]{1,0:T(8,128)S(1)}, f32[256,512]{1,0:T(8,128)S(1)}, bf16[128,1024]{...) custom-call(s32[2]{0:T(128)S(1)} %copy-done.8, f32[6,50,1024]{2,1,0:T(8,128)S(1)} %bitcast.1, ...), custom_call_target="tpu_custom_call" | custom-call | flops 4000000000 | bytes 12000000 | tf_op jit(solution)/shard_map/near/pallas_call | solution.py:358
  13.8 1.3 %collective-permute-start.2 = (bf16[128,1024]{1,0:T(8,128)(2,1)S(1)}, bf16[128,1024]{1,0:T(8,128)(2,1)S(1)}, u32[]{:S(2)}, u32[]{:S(2)}) collective-permute-start(bf16[128,1024]{1,0:T(8,128)(2,1)S(1)} %get-tuple-element.22.kv), channel_id=1, source_target_pairs={{0,16},{16,0},{1,17},{17,1},{2,18},{18,2},{3,19},{19,3},{4,20},{20... | collective-permute-start | bytes 786440 | tf_op jit(solution)/shard_map/ppermute | solution.py:340
  15.1 0.0 collective-permute-done.refs_2_
  15.1 2.7 %far.1.refs_3_ = bf16[256,512]{1,0:T(8,128)(2,1)S(1)} custom-call(s32[2]{0:T(128)S(1)} %copy-done.8, f32[6,50,1024]{2,1,0:T(8,128)S(1)} %bitcast.2, bf16[256,1024]{1,0:T(8,128)(2,1)S(1)} %collective-permute-done.refs_2_, bf16[1024,1536]{1,0:T(8,128)(2,1)S(1)} %copy-done, f32[2,64]{1,0:T(2,128)S(1)} %copy-done.6, ...), custom_call_target="tpu_custom_call" | custom-call | flops 4000000000 | bytes 12000000 | tf_op jit(solution)/shard_map/far/pallas_call | solution.py:381
  17.8 0.0 copy-start.4
  17.8 0.3 collective-permute-start.3
  18.1 2.8 %own.1 = (bf16[256,1024]{1,0:T(8,128)(2,1)S(1)}, bf16[256,1536]{1,0:T(8,128)(2,1)S(1)}) custom-call(s32[2]{0:T(128)S(1)} %copy-done.8, f32[6,50,1024]{2,1,0:T(8,128)S(1)} %bitcast.3, bf16[256,1024]{1,0:T(8,128)(2,1)S(1)} %split.1.refs_2_, bf16[256,512]{1,0:T(8,128)(2,1)S(1)} %far.1.refs_3_, bf16[512,1024]{1,0:T(8,128)(2,1)S(1)} %copy-done.3, ...), custom_call_target="tpu_custom_call" | custom-call | flops 4000000000 | bytes 12000000 | tf_op jit(solution)/shard_map/own/pallas_call | solution.py:392
  20.9 4.2 %collective-permute-done.2.refs_0_ = bf16[128,1024]{1,0:T(8,128)(2,1)S(1)} collective-permute-done((bf16[128,1024]{1,0:T(8,128)(2,1)S(1)}, bf16[128,1024]{1,0:T(8,128)(2,1)S(1)}, u32[]{:S(2)}, u32[]{:S(2)}) %collective-permute-start.2) | collective-permute-done | bytes 262176 | tf_op jit(solution)/shard_map/ppermute | solution.py:340
  25.0 1.2 %early.1.refs_4_ = bf16[128,1024]{1,0:T(8,128)(2,1)S(1)} custom-call(s32[2]{0:T(128)S(1)} %copy-done.8, f32[6,50,1024]{2,1,0:T(8,128)S(1)} %bitcast.4, bf16[128,1024]{1,0:T(8,128)(2,1)S(1)} %get-tuple-element.20.first, bf16[128,512]{1,0:T(8,128)(2,1)S(1)} %get-tuple-element.21.query, bf16[128,1024]{1,0:T(8,128)(2,1)S(1)} %get-tuple-element.22.kv, ...), custom_call_target="tpu_custom_call" | custom-call | flops 2000000000 | bytes 6000000 | tf_op jit(solution)/shard_map/early/pallas_call | solution.py:401
  26.2 0.0 collective-permute-done.4.refs_6_
  26.2 4.4 %collective-permute-done.3.refs_5_ = bf16[256,512]{1,0:T(8,128)(2,1)S(1)} collective-permute-done((bf16[256,512]{1,0:T(8,128)(2,1)S(1)}, bf16[256,512]{1,0:T(8,128)(2,1)S(1)}, u32[]{:S(2)}, u32[]{:S(2)}) %collective-permute-start.3) | collective-permute-done | bytes 262176 | tf_op jit(solution)/shard_map/ppermute | solution.py:340
  30.7 4.4 %last.1 = bf16[1,384,1024]{2,1,0:T(8,128)(2,1)} custom-call(s32[2]{0:T(128)S(1)} %copy-done.8, f32[6,50,1024]{2,1,0:T(8,128)S(1)} %bitcast.5, bf16[256,1024]{1,0:T(8,128)(2,1)S(1)} %get-tuple-element.18.refs_2_, bf16[256,1536]{1,0:T(8,128)(2,1)S(1)} %get-tuple-element.19.refs_3_, bf16[128,1024]{1,0:T(8,128)(2,1)S(1)} %early.1.refs_4_, ...), custom_call_target="tpu_custom_call" | custom-call | flops 4000000000 | bytes 12000000 | tf_op jit(solution)/shard_map/last/pallas_call | solution.py:410
  (10 shorter events, 0.1 us)
Async XLA Ops:
  0.0 5.7 %copy-start.2 = (f32[50,6,1024]{2,0,1:T(8,128)S(1)}, f32[50,6,1024]{2,0,1:T(8,128)}, u32[]{:S(2)}) copy-start(f32[50,6,1024]{2,0,1:T(8,128)} %param.11) | copy-start | bytes 3686404
  0.0 5.7 %copy-start = (bf16[1024,1536]{1,0:T(8,128)(2,1)S(1)}, bf16[1024,1536]{1,0:T(8,128)(2,1)}, u32[]{:S(2)}) copy-start(bf16[1024,1536]{1,0:T(8,128)(2,1)} %refs_3_.1) | copy-start | bytes 9437188
  0.0 5.8 %copy-start.3 = (bf16[512,1024]{1,0:T(8,128)(2,1)S(1)}, bf16[512,1024]{1,0:T(8,128)(2,1)}, u32[]{:S(2)}) copy-start(bf16[512,1024]{1,0:T(8,128)(2,1)} %refs_7_.1) | copy-start | bytes 3145732
  0.0 5.8 %copy-start.1 = (bf16[1024,1536]{1,0:T(8,128)(2,1)S(1)}, bf16[1024,1536]{1,0:T(8,128)(2,1)}, u32[]{:S(2)}) copy-start(bf16[1024,1536]{1,0:T(8,128)(2,1)} %refs_8_.1) | copy-start | bytes 9437188
  0.0 5.7 %collective-permute-start.1 = (bf16[1,384,1024]{2,1,0:T(8,128)(2,1)}, bf16[1,384,1024]{2,1,0:T(8,128)(2,1)S(1)}, u32[]{:S(2)}, u32[]{:S(2)}) collective-permute-start(bf16[1,384,1024]{2,1,0:T(8,128)(2,1)} %frames.3), channel_id=1, source_target_pairs={{0,1},{1,0},{2,3},{3,2},{4,5},{5,4},{6,7},{7,6},{8,9},{9,8},{10,11... | collective-permute-start | bytes 2359304 | tf_op jit(solution)/shard_map/ppermute | solution.py:344
  0.8 1.5 %copy-start.5 = (bf16[1,384,1024]{2,1,0:T(8,128)(2,1)S(1)}, bf16[1,384,1024]{2,1,0:T(8,128)(2,1)}, u32[]{:S(2)}) copy-start(bf16[1,384,1024]{2,1,0:T(8,128)(2,1)} %frames.3) | copy-start | bytes 2359300
  2.3 3.5 %copy-start.6 = (f32[2,64]{1,0:T(2,128)S(1)}, f32[2,64]{1,0:T(2,128)}, u32[]{:S(2)}) copy-start(f32[2,64]{1,0:T(2,128)} %refs_4_.2) | copy-start | bytes 1540
  2.3 3.5 %copy-start.7 = (f32[2,64]{1,0:T(2,128)S(1)}, f32[2,64]{1,0:T(2,128)}, u32[]{:S(2)}) copy-start(f32[2,64]{1,0:T(2,128)} %refs_9_.1) | copy-start | bytes 1540
  2.3 3.5 %copy-start.8 = (s32[2]{0:T(128)S(1)}, s32[2]{0:T(128)}, u32[]{:S(2)}) copy-start(s32[2]{0:T(128)} %refs_0_.5) | copy-start | bytes 28
  2.3 12.8 %collective-permute-start = (bf16[256,1024]{1,0:T(8,128)(2,1)S(1)}, bf16[256,1024]{1,0:T(8,128)(2,1)S(1)}, u32[]{:S(2)}, u32[]{:S(2)}) collective-permute-start(bf16[256,1024]{1,0:T(8,128)(2,1)S(1)} %split.1.refs_2_), channel_id=1, source_target_pairs={{1,2},{3,4},{5,6},{7,8},{9,10},{11,12},{13,14},{2,1},{4,3},{6,5},{... | collective-permute-start | bytes 1572872 | tf_op jit(solution)/shard_map/ppermute | solution.py:355
  5.5 20.8 %collective-permute-start.4 = (bf16[256,1024]{1,0:T(8,128)(2,1)S(1)}, bf16[256,1024]{1,0:T(8,128)(2,1)S(1)}, u32[]{:S(2)}, u32[]{:S(2)}) collective-permute-start(bf16[256,1024]{1,0:T(8,128)(2,1)S(1)} %split.1.refs_2_), channel_id=1, source_target_pairs={{0,16},{16,0},{1,17},{17,1},{2,18},{18,2},{3,19},{19,3},{4,20},{20... | collective-permute-start | bytes 1572872 | tf_op jit(solution)/shard_map/ppermute | solution.py:340
  13.8 11.2 %collective-permute-start.2 = (bf16[128,1024]{1,0:T(8,128)(2,1)S(1)}, bf16[128,1024]{1,0:T(8,128)(2,1)S(1)}, u32[]{:S(2)}, u32[]{:S(2)}) collective-permute-start(bf16[128,1024]{1,0:T(8,128)(2,1)S(1)} %get-tuple-element.22.kv), channel_id=1, source_target_pairs={{0,16},{16,0},{1,17},{17,1},{2,18},{18,2},{3,19},{19,3},{4,20},{20... | collective-permute-start | bytes 786440 | tf_op jit(solution)/shard_map/ppermute | solution.py:340
  17.8 7.2 %copy-start.4 = (bf16[512,1024]{1,0:T(8,128)(2,1)S(1)}, bf16[512,1024]{1,0:T(8,128)(2,1)}, u32[]{:S(2)}) copy-start(bf16[512,1024]{1,0:T(8,128)(2,1)} %refs_10_.1) | copy-start | bytes 3145732
  17.8 12.8 %collective-permute-start.3 = (bf16[256,512]{1,0:T(8,128)(2,1)S(1)}, bf16[256,512]{1,0:T(8,128)(2,1)S(1)}, u32[]{:S(2)}, u32[]{:S(2)}) collective-permute-start(bf16[256,512]{1,0:T(8,128)(2,1)S(1)} %far.1.refs_3_), channel_id=1, source_target_pairs={{0,16},{16,0},{1,17},{17,1},{2,18},{18,2},{3,19},{19,3},{4,20},{20... | collective-permute-start | bytes 786440 | tf_op jit(solution)/shard_map/ppermute | solution.py:340

commit v4 on v3

v4 whole, which is shorter than its diff:
```python
import jax
import jax.numpy as jnp
from jax import lax
from jax.experimental import pallas as pl
from jax.experimental.pallas import tpu as pltpu
from jax.sharding import PartitionSpec as P

D = 1024
H = 8
HD = 64
HW = H * HD
HALF = 256
BLOCK = 128
SLAB = 128
EPS = 1e-06
NEG = -1e30
F32 = jnp.float32
BF16 = jnp.bfloat16
VMEM = pl.BlockSpec(memory_space=pltpu.VMEM)
SMEM = pl.BlockSpec(memory_space=pltpu.SMEM)
ANY = pl.BlockSpec(memory_space=pl.ANY)
LIMIT = 16 * 1024 * 1024


def cost(us):
    return pl.CostEstimate(flops=int(us * 1e9), bytes_accessed=int(us * 3e6), transcendentals=0)


def params():
    return pltpu.CompilerParams(vmem_limit_bytes=LIMIT)


def shape(*dims, dtype=BF16):
    return jax.ShapeDtypeStruct(dims, dtype)


def dot(a, b, dims=((1,), (0,))):
    return lax.dot_general(a, b, (dims, ((), ())), preferred_element_type=F32)


def modulated(rows, shift, scale):
    values = rows.astype(F32)
    centred = values - jnp.mean(values, axis=-1, keepdims=True)
    spread = jnp.mean(centred * centred, axis=-1, keepdims=True)
    normed = centred * lax.rsqrt(spread + EPS)
    return (normed * (1.0 + scale) + shift).astype(BF16)


def head_ones():
    row = lax.broadcasted_iota(jnp.int32, (2 * SLAB, 2 * SLAB), 0) // HD
    col = lax.broadcasted_iota(jnp.int32, (2 * SLAB, 2 * SLAB), 1) // HD
    return jnp.where(row == col, 1.0, 0.0).astype(BF16)


def head_sums(values, ones):
    parts = [dot(values[:, at : at + 2 * SLAB], ones) for at in range(0, HW, 2 * SLAB)]
    return jnp.concatenate(parts, axis=1)


def exact_head_sums(values, ones):
    high = values.astype(BF16)
    low = (values - high.astype(F32)).astype(BF16)
    return head_sums(high, ones) + head_sums(low, ones)


def head_norm(values, gain, ones):
    mean = head_sums((values * values).astype(BF16), ones) * (1.0 / HD)
    return (values * lax.rsqrt(mean + EPS) * gain).astype(BF16)


def wide_gain(gain):
    return jnp.concatenate([gain] * H, axis=1)


def window_bias(keys, ahead, first_frame=0, total=1 << 30):
    i = lax.broadcasted_iota(jnp.int32, (BLOCK, keys), 0)
    j = lax.broadcasted_iota(jnp.int32, (BLOCK, keys), 1)
    frame = first_frame + j
    keep = (j + ahead >= i) & (j + ahead <= i + 2 * HALF) & (frame >= 0) & (frame < total)
    return jnp.where(keep, 0.0, NEG)


def left_half():
    return lax.broadcasted_iota(jnp.int32, (BLOCK, SLAB), 1) < HD


def by_head(pair):
    return jnp.where(left_half(), pair[:BLOCK], pair[BLOCK:])


def raised_scores(query, keys, bias):
    half, zero = left_half(), jnp.zeros_like(query)
    pair = jnp.concatenate([jnp.where(half, query, zero), jnp.where(half, zero, query)], axis=0)
    scores = dot(pair, keys, ((1,), (1,)))
    scores = jnp.concatenate([scores[:BLOCK] + bias, scores[BLOCK:] + bias], axis=0)
    top = jnp.max(scores, axis=-1, keepdims=True)
    return jnp.exp(scores - top).astype(BF16), top


def weighted(raised, values):
    summed = dot(raised, jnp.concatenate([values, jnp.ones_like(values)], axis=1))
    return by_head(summed[:, :SLAB]), by_head(summed[:, SLAB:])


def cross_attend(query, keys, values, ones):
    query = query.astype(F32)
    base = keys[0].astype(F32)
    scores = [
        exact_head_sums(query * (k.astype(F32) - base), ones) * (HD ** -0.5) for k in keys[1:]
    ]
    top = jnp.zeros_like(query)
    for s in scores:
        top = jnp.maximum(top, s)
    raised = [jnp.exp(-top)] + [jnp.exp(s - top) for s in scores]
    total = raised[0]
    for r in raised[1:]:
        total = total + r
    scale = 1.0 / total
    out = jnp.zeros_like(query)
    for r, v in zip(raised, values):
        out = out + (r * scale).astype(BF16).astype(F32) * v.astype(F32)
    return out.astype(BF16)


def mods_of(timestep, modulation, back):
    count = lax.axis_size("stem")
    step = timestep[lax.rem(lax.axis_index("stem") + count - back, count)]
    return lambda i: modulation[i, pl.ds(step, 1), :]


def mods_held(held, back):
    return lambda i: held[back, i : i + 1]


def places(rows):
    parity = lax.rem(lax.axis_index("tm"), 2)
    outer = pl.multiple_of(parity * HALF, BLOCK)
    early = pl.multiple_of((1 - parity) * HALF, BLOCK)
    return parity, outer, rows - HALF, early


def split_kernel(frames, outer_rows, inner_rows, early_rows, sems):
    copies = [
        pltpu.make_async_copy(frames.at[0, pl.ds(at, BLOCK)], to, sems.at[n])
        for n, (at, to) in enumerate(zip(places(frames.shape[1])[1:], (outer_rows, inner_rows, early_rows)))
    ]
    for copy in copies:
        copy.start()
    for copy in copies:
        copy.wait()


def join_kernel(outer_rows, inner_rows, both):
    both[:BLOCK] = outer_rows[...]
    both[BLOCK:] = inner_rows[...]


def near_kernel(
    timestep, modulation, early_rows, late_rows, near, qkv_self, gains, out_self, qkv_cross, gains_cross,
    query, part_out, part_sum, part_top, first, first_q, first_kv, held, kv,
):
    rows = near.shape[1]
    for k in range(held.shape[0]):
        row = mods_of(timestep, modulation, k)
        for i in range(6):
            held[k, i : i + 1] = row(i)
    parity, outer, inner, early = places(rows)
    mods = mods_of(timestep, modulation, 0)
    shift, scale = mods(0), mods(1)
    ones = head_ones()
    q_gain = wide_gain(gains[0:1]) * (HD ** -0.5)
    k_gain = wide_gain(gains[1:2])
    own_at = parity * HALF
    near_at = (1 - parity) * rows
    near_from = parity * (rows - HALF)

    sources = [(early_rows[...], own_at + early)]
    sources += [(late_rows[:BLOCK], own_at + outer), (late_rows[BLOCK:], own_at + inner)]
    sources += [
        (near[0, pl.ds(pl.multiple_of(near_from + at, BLOCK), BLOCK)], near_at + at)
        for at in range(0, HALF, BLOCK)
    ]
    queries = []
    for n, (source, to) in enumerate(sources):
        normed = modulated(source, shift, scale)
        if n < 3:
            projected = dot(normed, qkv_self[...])
            queries.append(head_norm(projected[:, :HW], q_gain, ones))
            projected = projected[:, HW:]
        else:
            projected = dot(normed, qkv_self[:, HW:])
        to = pl.multiple_of(to, BLOCK)
        kv[pl.ds(to, BLOCK), :HW] = head_norm(projected[:, :HW], k_gain, ones)
        kv[pl.ds(to, BLOCK), HW:] = projected[:, HW:].astype(BF16)
    query[:BLOCK] = queries[1]
    query[BLOCK:] = queries[2]

    window = rows + HALF
    bias = window_bias(window, 0)
    attended = []
    for at in range(0, HW, SLAB):
        raised, _ = raised_scores(queries[0][:, at : at + SLAB], kv[:, at : at + SLAB], bias)
        out, total = weighted(raised, kv[:, HW + at : HW + at + SLAB])
        attended.append((out / total).astype(BF16))
    attended = jnp.concatenate(attended, axis=1)

    f = first_of(early_rows[...], attended, out_self, mods(2))
    first[...] = f
    first_q[...], first_kv[:, :HW], first_kv[:, HW:] = projected_cross(
        f, mods, qkv_cross, gains_cross, ones, True
    )

    for n, width in ((0, HALF), (1, BLOCK)):
        start = pl.multiple_of(parity * width, BLOCK)
        count = window - width
        bias = window_bias(count, (1 - parity) * width)
        to = slice(n * BLOCK, (n + 1) * BLOCK)
        for at in range(0, HW, SLAB):
            cols = slice(at, at + SLAB)
            raised, top = raised_scores(
                queries[n + 1][:, cols], kv[pl.ds(start, count), cols], bias
            )
            out, total = weighted(raised, kv[pl.ds(start, count), HW + at : HW + at + SLAB])
            part_out[to, cols] = out
            part_sum[to, cols] = total
            part_top[to, cols] = by_head(jnp.broadcast_to(top, (2 * BLOCK, SLAB)))


def far_kernel(
    outermost, rows, held, far, qkv_self, gains, query, part_out, part_sum, part_top, *outs
):
    parity = lax.rem(lax.axis_index("tm"), 2)
    mods = mods_held(held, 0)
    ones = head_ones()
    normed = modulated(far[...], mods(0), mods(1))
    keys = dot(normed, qkv_self[:, HW : 2 * HW])
    values = dot(normed, qkv_self[:, 2 * HW :]).astype(BF16)
    keys = head_norm(keys, wide_gain(gains[1:2]), ones)
    start = jnp.where(parity == 0, -2 * BLOCK if outermost else -BLOCK, rows + (BLOCK if outermost else 0))
    place = lax.axis_index("tm")
    total = rows * lax.axis_size("tm")

    def attend(block, block_start):
        bias = window_bias(BLOCK, start - block_start + HALF, place * rows + start, total)
        to = slice(block * BLOCK, (block + 1) * BLOCK)
        for at in range(0, HW, SLAB):
            cols = slice(at, at + SLAB)
            raised, top = raised_scores(query[to, cols], keys[:, cols], bias)
            out, summed = weighted(raised, values[:, cols])
            top = by_head(jnp.broadcast_to(top, (2 * BLOCK, SLAB)))
            both = jnp.maximum(top, part_top[to, cols])
            here = jnp.exp(top - both)
            before = jnp.exp(part_top[to, cols] - both)
            out = out * here + part_out[to, cols] * before
            summed = summed * here + part_sum[to, cols] * before
            yield cols, out, summed, both

    if outermost:
        for cols, out, summed, _ in attend(0, parity * HALF):
            outs[0][:, cols] = (out / summed).astype(BF16)
    else:
        for cols, out, summed, _ in attend(1, rows - HALF):
            outs[0][:, cols] = (out / summed).astype(BF16)
        for cols, out, summed, top in attend(0, parity * HALF):
            outs[1][:, cols], outs[2][:, cols], outs[3][:, cols] = out, summed, top


def first_of(frames, attended, weight, gate):
    mixed = dot(attended, weight[...])
    return (frames.astype(F32) + gate * mixed).astype(BF16)


def projected_cross(first, mods, weight, gains, ones, with_query):
    normed = modulated(first, mods(3), mods(4))
    raw = [dot(normed, weight[:, at : at + HW]) for at in range(0 if with_query else HW, 3 * HW, HW)]
    query = head_norm(raw[0], wide_gain(gains[0:1]), ones) if with_query else None
    keys = head_norm(raw[-2], wide_gain(gains[1:2]), ones)
    return query, keys, raw[-1].astype(BF16)


def finished(first, attended, weight, gate):
    out = dot(attended, weight[...]).astype(BF16)
    return (first.astype(F32) + gate * out.astype(F32)).astype(BF16)


def own_kernel(held, frames, attended, out_self, qkv_cross, gains, first, query, kv):
    mods = mods_held(held, 0)
    f = first_of(frames[...], attended[...], out_self, mods(2))
    first[...] = f
    query[...], kv[:, :HW], kv[:, HW:] = projected_cross(
        f, mods, qkv_cross, gains, head_ones(), True
    )


def early_kernel(held, first, query, kv, out_cross, *refs):
    others, out = refs[:-1], refs[-1]
    keys = [each[:, :HW] for each in (kv, *others)]
    values = [each[:, HW:] for each in (kv, *others)]
    mixed = cross_attend(query[...], keys, values, head_ones())
    out[...] = finished(first[...], mixed, out_cross, mods_held(held, 0)(5))


def late_block(block, held, first, query, kv, others, their_frames, out_self, qkv_cross, gains, out_cross):
    ones = head_ones()
    part = slice(block * BLOCK, (block + 1) * BLOCK)
    keys, values = [kv[:, :HW]], [kv[:, HW:]]
    for n, (attended, source) in enumerate(zip(others, their_frames)):
        mods = mods_held(held, n + 1)
        g = first_of(source[part], attended[...], out_self, mods(2))
        _, k, v = projected_cross(g, mods, qkv_cross, gains, ones, False)
        keys.append(k)
        values.append(v)
    mixed = cross_attend(query[...], keys, values, ones)
    return finished(first[...], mixed, out_cross, mods_held(held, 0)(5))


def inner_kernel(count, _, held, first, query, kv, *refs):
    others, their_frames = refs[: count - 1], refs[count - 1 : 2 * count - 2]
    *weights, out = refs[2 * count - 2 :]
    out[...] = late_block(1, held, first, query, kv, others, their_frames, *weights)


def outer_kernel(count, held, first, query, kv, early_out, inner_out, *refs):
    others, their_frames = refs[: count - 1], refs[count - 1 : 2 * count - 2]
    *weights, out, outer_out, sems = refs[2 * count - 2 :]
    _, outer, inner, early = places(out.shape[1])
    copies = [
        pltpu.make_async_copy(source, out.at[0, pl.ds(at, BLOCK)], sems.at[n])
        for n, (source, at) in enumerate(((early_out, early), (inner_out, inner), (outer_out, outer)))
    ]
    copies[0].start()
    copies[1].start()
    outer_out[...] = late_block(0, held, first, query, kv, others, their_frames, *weights)
    copies[2].start()
    for copy in copies:
        copy.wait()


def on_device(
    frames,
    timestep,
    modulation,
    qkv_self,
    out_self,
    qk_gain_self,
    qkv_cross,
    out_cross,
    qk_gain_cross,
):
    stems = lax.axis_size("stem")
    count = lax.axis_size("tm")
    rows = frames.shape[1]
    assert count % 2 == 0 and rows == HALF + BLOCK
    modulation = jnp.transpose(modulation, (1, 0, 2))
    inside = [(i, i ^ 1) for i in range(count)]
    across = [(i, i + 1) for i in range(1, count - 1, 2)]
    across += [(b, a) for a, b in across]

    def to_stems(array):
        return [
            lax.ppermute(array, "stem", [(i, (i + k) % stems) for i in range(stems)])
            for k in range(1, stems)
        ]

    def call(kernel, name, us, outs, *args, scratch=(), in_specs=None, out_specs=None):
        out_specs = out_specs or jax.tree.map(lambda _: VMEM, outs)
        return pl.pallas_call(
            kernel,
            out_shape=outs,
            in_specs=in_specs or [VMEM] * len(args),
            out_specs=out_specs,
            scratch_shapes=list(scratch),
            compiler_params=params(),
            cost_estimate=cost(us),
            name=name,
        )(*args)

    half = shape(BLOCK, D)
    outer_rows, inner_rows, early_rows = call(
        split_kernel, "split", 4, (half, half, half), frames,
        scratch=[pltpu.SemaphoreType.DMA((3,))], in_specs=[ANY], out_specs=(ANY, ANY, ANY),
    )
    far_inner = lax.ppermute(outer_rows, "tm", across)
    far_outer = lax.ppermute(inner_rows, "tm", across)
    after, _ = lax.optimization_barrier((frames, outer_rows))
    near = lax.ppermute(after, "tm", inside)
    late_rows = call(join_kernel, "join", 0.1, shape(HALF, D), outer_rows, inner_rows)
    their_frames = to_stems(late_rows)

    part = shape(HALF, HW, dtype=F32)
    query, part_out, part_sum, part_top, first_early, q_early, kv_early, held = call(
        near_kernel, "near", 4,
        (shape(HALF, HW), part, part, part, half, shape(BLOCK, HW), half, shape(stems, 8, D, dtype=F32)),
        timestep, modulation, early_rows, late_rows, near, qkv_self, qk_gain_self, out_self, qkv_cross, qk_gain_cross,
        scratch=[pltpu.VMEM((rows + HALF, 2 * HW), BF16)], in_specs=[SMEM] + [VMEM] * 9,
    )
    others_early = to_stems(kv_early)

    block, part = shape(BLOCK, HW), shape(BLOCK, HW, dtype=F32)
    att_inner, *parts = call(
        lambda *refs: far_kernel(False, rows, *refs), "far_inner", 1, (block, part, part, part),
        held, far_inner, qkv_self, qk_gain_self, query, part_out, part_sum, part_top,
    )
    others_inner = to_stems(att_inner)
    att_outer = call(
        lambda *refs: far_kernel(True, rows, *refs), "far_outer", 1, block,
        held, far_outer, qkv_self, qk_gain_self, query, *parts,
    )
    others_outer = to_stems(att_outer)

    weights = (out_self, qkv_cross, qk_gain_cross)
    own_inner = call(
        own_kernel, "own_inner", 0.3, (half, block, half), held, inner_rows, att_inner, *weights
    )
    own_outer = call(
        own_kernel, "own_outer", 0.3, (half, block, half), held, outer_rows, att_outer, *weights
    )
    early_out = call(
        early_kernel, "early", 0.3, half, held, first_early, q_early, kv_early, out_cross, *others_early
    )
    inner_out = call(
        lambda *refs: inner_kernel(stems, *refs), "inner", 0.5, half,
        early_out, held, *own_inner, *others_inner, *their_frames, *weights, out_cross,
        in_specs=[ANY] + [VMEM] * (6 + 2 * stems),
    )
    return call(
        lambda *refs: outer_kernel(stems, *refs), "outer", 2, shape(1, rows, D),
        held, *own_outer, early_out, inner_out, *others_outer, *their_frames, *weights, out_cross,
        scratch=[pltpu.VMEM((BLOCK, D), BF16), pltpu.SemaphoreType.DMA((3,))], out_specs=ANY,
    )


def solution(mesh):
    return jax.shard_map(
        on_device,
        mesh=mesh,
        in_specs=(P("stem", "tm", None), P(), P(), P(), P(), P(), P(), P(), P()),
        out_specs=P("stem", "tm", None),
        check_vma=False,
    )
```

time: 35.2 us -> 36 us (1.023)
  the two profiles are of different devices: /device:TPU:15 before, /device:TPU:7 now
where the time goes in v4:
time: 36 us; the launch traced here: 35.9 us
  Pallas kernels  19.6 us (54%)
  starting transfers between devices  10.5 us (29%)
  waiting for transfers between devices  5.32 us (15%)
    pallas_call x10, Pallas kernels, call(): pl.pallas_call(kernel, out_shape=outs, in_specs=in_specs or [VMEM] * len(...  19.6 us
    ppermute x4, waiting for transfers between devices, to_stems(): lax.ppermute(array, 'stem', [(i, (i + k) % stems) for i in range(stems)])  5.31 us
    ppermute x1, starting transfers between devices, on_device(): far_inner = lax.ppermute(outer_rows, 'tm', across)  3.34 us
    ppermute x1, starting transfers between devices, on_device(): far_outer = lax.ppermute(inner_rows, 'tm', across)  3.24 us
    ppermute x4, starting transfers between devices, to_stems(): lax.ppermute(array, 'stem', [(i, (i + k) % stems) for i in range(stems)])  3.22 us
    ppermute x1, starting transfers between devices, on_device(): near = lax.ppermute(after, 'tm', inside)  0.74 us
  transfers between devices with their start and end apart: 7, of which 3 were waited for; matrix products, arithmetic and copies ran while one was open for 0% of the time, Pallas kernels for 45%

profile of v4, /device:TPU:7, one launch (start us, length us, event | category | flops | bytes accessed | tf_op | source)
XLA Modules:
  0.0 35.9 jit_solution(10120770748514360825)
XLA Ops:
  0.0 1.3 %split.1 = (bf16[128,1024]{1,0:T(8,128)(2,1)S(1)}, bf16[128,1024]{1,0:T(8,128)(2,1)S(1)}, bf16[128,1024]{1,0:T(8,128)(2,1)S(1)}) custom-call(bf16[1,384,1024]{2,1,0:T(8,128)(2,1)} %frames.1), custom_call_target="tpu_custom_call" | custom-call | flops 4000000000 | bytes 12000000 | tf_op jit(solution)/shard_map/split/pallas_call | solution.py:367
  1.4 0.7 %collective-permute-start = (bf16[1,384,1024]{2,1,0:T(8,128)(2,1)}, bf16[1,384,1024]{2,1,0:T(8,128)(2,1)S(1)}, u32[]{:S(2)}, u32[]{:S(2)}) collective-permute-start(bf16[1,384,1024]{2,1,0:T(8,128)(2,1)} %frames.1), channel_id=1, source_target_pairs={{0,1},{1,0},{2,3},{3,2},{4,5},{5,4},{6,7},{7,6},{8,9},{9,8},{10,11... | collective-permute-start | bytes 2359304 | tf_op jit(solution)/shard_map/ppermute | solution.py:386
  2.1 3.3 %collective-permute-start.2 = (bf16[128,1024]{1,0:T(8,128)(2,1)S(1)}, bf16[128,1024]{1,0:T(8,128)(2,1)S(1)}, u32[]{:S(2)}, u32[]{:S(2)}) collective-permute-start(bf16[128,1024]{1,0:T(8,128)(2,1)S(1)} %get-tuple-element.28.outer_rows.frames), channel_id=1, source_target_pairs={{1,2},{3,4},{5,6},{7,8},{9,10},{11,12},{13,14},{2,1},{4,3},{6,5},{... | collective-permute-start | bytes 786440 | tf_op jit(solution)/shard_map/ppermute | solution.py:383
  5.4 3.2 %collective-permute-start.1 = (bf16[128,1024]{1,0:T(8,128)(2,1)S(1)}, bf16[128,1024]{1,0:T(8,128)(2,1)S(1)}, u32[]{:S(2)}, u32[]{:S(2)}) collective-permute-start(bf16[128,1024]{1,0:T(8,128)(2,1)S(1)} %get-tuple-element.29.inner_rows.frames), channel_id=1, source_target_pairs={{1,2},{3,4},{5,6},{7,8},{9,10},{11,12},{13,14},{2,1},{4,3},{6,5},{... | collective-permute-start | bytes 786440 | tf_op jit(solution)/shard_map/ppermute | solution.py:384
  8.7 0.3 collective-permute-start.5
  9.0 0.0 collective-permute-done.near
  9.1 7.9 %near.1 = (bf16[256,512]{1,0:T(8,128)(2,1)S(1)}, f32[256,512]{1,0:T(8,128)S(1)}, f32[256,512]{1,0:T(8,128)S(1)}, f32[256,512]{1,0:T(8,128)S(1)}, bf16[128,1024]{...) custom-call(s32[2]{0:T(128)S(1)} %copy-done.7, ...), custom_call_target="tpu_custom_call" | custom-call | flops 4000000000 | bytes 12000000 | tf_op jit(solution)/shard_map/near/pallas_call | solution.py:367
  17.0 1.3 %collective-permute-start.3 = (bf16[128,1024]{1,0:T(8,128)(2,1)S(1)}, bf16[128,1024]{1,0:T(8,128)(2,1)S(1)}, u32[]{:S(2)}, u32[]{:S(2)}) collective-permute-start(bf16[128,1024]{1,0:T(8,128)(2,1)S(1)} %get-tuple-element.44.kv), channel_id=1, source_target_pairs={{0,16},{16,0},{1,17},{17,1},{2,18},{18,2},{3,19},{19,3},{4,20},{20... | collective-permute-start | bytes 786440 | tf_op jit(solution)/shard_map/ppermute | solution.py:361
  18.3 0.0 collective-permute-done.2.refs_1_
  18.3 2.1 %far_inner.1 = (bf16[128,512]{1,0:T(8,128)(2,1)S(1)}, f32[128,512]{1,0:T(8,128)S(1)}, f32[128,512]{1,0:T(8,128)S(1)}, f32[128,512]{1,0:T(8,128)S(1)}) custom-call(f32[2,8,1024]{2,1,0:T(8,128)S(1)} %get-tuple-element.31.refs_0_.held.refs_1_, bf16[128,1024]{1,0:T(8,128)(2,1)S(1)} %collective-permute-done.2.refs_1_, bf16[1024,1536]{1,0:T(8,128)(2,1)S(1)} %copy-done.2, ...), custom_call_target="tpu_custom_call" | custom-call | flops 1000000000 | bytes 3000000 | tf_op jit(solution)/shard_map/far_inner/pallas_call | solution.py:367
  20.4 0.3 collective-permute-start.4
  20.7 0.0 collective-permute-done.1.refs_1_
  20.7 1.4 %far_outer.1.attended = bf16[128,512]{1,0:T(8,128)(2,1)S(1)} custom-call(f32[2,8,1024]{2,1,0:T(8,128)S(1)} %get-tuple-element.31.refs_0_.held.refs_1_, bf16[128,1024]{1,0:T(8,128)(2,1)S(1)} %collective-permute-done.1.refs_1_, bf16[1024,1536]{1,0:T(8,128)(2,1)S(1)} %copy-done.2, f32[2,64]{1,0:T(2,128)S(1)} %copy-done.5, ...), custom_call_target="tpu_custom_call" | custom-call | flops 1000000000 | bytes 3000000 | tf_op jit(solution)/shard_map/far_outer/pallas_call | solution.py:367
  22.1 1.3 %collective-permute-start.6 = (bf16[128,512]{1,0:T(8,128)(2,1)S(1)}, bf16[128,512]{1,0:T(8,128)(2,1)S(1)}, u32[]{:S(2)}, u32[]{:S(2)}) collective-permute-start(bf16[128,512]{1,0:T(8,128)(2,1)S(1)} %far_outer.1.attended), channel_id=1, source_target_pairs={{0,16},{16,0},{1,17},{17,1},{2,18},{18,2},{3,19},{19,3},{4,20},{20... | collective-permute-start | bytes 393224 | tf_op jit(solution)/shard_map/ppermute | solution.py:361
  23.4 1.1 %own_inner.1 = (bf16[128,1024]{1,0:T(8,128)(2,1)S(1)}, bf16[128,512]{1,0:T(8,128)(2,1)S(1)}, bf16[128,1024]{1,0:T(8,128)(2,1)S(1)}) custom-call(f32[2,8,1024]{2,1,0:T(8,128)S(1)} %get-tuple-element.31.refs_0_.held.refs_1_, bf16[128,1024]{1,0:T(8,128)(2,1)S(1)} %get-tuple-element.29.inner_rows.frames, bf16[128,512]{1,0:T(8,128)(2,1)S(1)} %get-tuple-element.45.attended, ...), custom_call_target="tpu_custom_call" | custom-call | flops 300000000 | bytes 900000 | tf_op jit(solution)/shard_map/own_inner/pallas_call | solution.py:367
  24.6 0.0 copy-start.3
  24.6 1.2 %own_outer.1 = (bf16[128,1024]{1,0:T(8,128)(2,1)S(1)}, bf16[128,512]{1,0:T(8,128)(2,1)S(1)}, bf16[128,1024]{1,0:T(8,128)(2,1)S(1)}) custom-call(f32[2,8,1024]{2,1,0:T(8,128)S(1)} %get-tuple-element.31.refs_0_.held.refs_1_, bf16[128,1024]{1,0:T(8,128)(2,1)S(1)} %get-tuple-element.28.outer_rows.frames, bf16[128,512]{1,0:T(8,128)(2,1)S(1)} %far_outer.1.attended, ...), custom_call_target="tpu_custom_call" | custom-call | flops 300000000 | bytes 900000 | tf_op jit(solution)/shard_map/own_outer/pallas_call | solution.py:367
  25.8 2.6 %collective-permute-done.3.refs_0_ = bf16[128,1024]{1,0:T(8,128)(2,1)S(1)} collective-permute-done((bf16[128,1024]{1,0:T(8,128)(2,1)S(1)}, bf16[128,1024]{1,0:T(8,128)(2,1)S(1)}, u32[]{:S(2)}, u32[]{:S(2)}) %collective-permute-start.3) | collective-permute-done | bytes 262176 | tf_op jit(solution)/shard_map/ppermute | solution.py:361
  28.4 0.8 %early.1.refs_0_.refs_4_ = bf16[128,1024]{1,0:T(8,128)(2,1)S(1)} custom-call(f32[2,8,1024]{2,1,0:T(8,128)S(1)} %get-tuple-element.31.refs_0_.held.refs_1_, bf16[128,1024]{1,0:T(8,128)(2,1)S(1)} %get-tuple-element.42.first, bf16[128,512]{1,0:T(8,128)(2,1)S(1)} %get-tuple-element.43.query, bf16[128,1024]{1,0:T(8,128)(2,1)S(1)} %get-tuple-element.44.kv, ...), custom_call_target="tpu_custom_call" | custom-call | flops 300000000 | bytes 900000 | tf_op jit(solution)/shard_map/early/pallas_call | solution.py:367
  29.1 0.0 collective-permute-done.5.refs_6_.refs_7_
  29.2 2.0 %collective-permute-done.4.refs_5_ = bf16[128,512]{1,0:T(8,128)(2,1)S(1)} collective-permute-done((bf16[128,512]{1,0:T(8,128)(2,1)S(1)}, bf16[128,512]{1,0:T(8,128)(2,1)S(1)}, u32[]{:S(2)}, u32[]{:S(2)}) %collective-permute-start.4) | collective-permute-done | bytes 131104 | tf_op jit(solution)/shard_map/ppermute | solution.py:361
  31.2 1.5 %inner.1.refs_5_ = bf16[128,1024]{1,0:T(8,128)(2,1)S(1)} custom-call(bf16[128,1024]{1,0:T(8,128)(2,1)S(1)} %early.1.refs_0_.refs_4_, f32[2,8,1024]{2,1,0:T(8,128)S(1)} %get-tuple-element.31.refs_0_.held.refs_1_, bf16[128,1024]{1,0:T(8,128)(2,1)S(1)} %get-tuple-element.46.refs_2_, bf16[128,512]{1,0:T(8,128)(2,1)S(1)} %get-tuple-element.47.refs_3_, ...), custom_call_target="tpu_custom_call" | custom-call | flops 500000000 | bytes 1500000 | tf_op jit(solution)/shard_map/inner/pallas_call | solution.py:367
  32.7 0.7 %collective-permute-done.6.refs_6_ = bf16[128,512]{1,0:T(8,128)(2,1)S(1)} collective-permute-done((bf16[128,512]{1,0:T(8,128)(2,1)S(1)}, bf16[128,512]{1,0:T(8,128)(2,1)S(1)}, u32[]{:S(2)}, u32[]{:S(2)}) %collective-permute-start.6) | collective-permute-done | bytes 131104 | tf_op jit(solution)/shard_map/ppermute | solution.py:361
  33.4 2.3 %outer.1 = bf16[1,384,1024]{2,1,0:T(8,128)(2,1)} custom-call(f32[2,8,1024]{2,1,0:T(8,128)S(1)} %get-tuple-element.31.refs_0_.held.refs_1_, bf16[128,1024]{1,0:T(8,128)(2,1)S(1)} %get-tuple-element.39.refs_1_, bf16[128,512]{1,0:T(8,128)(2,1)S(1)} %get-tuple-element.40.refs_2_, bf16[128,1024]{1,0:T(8,128)(2,1)S(1)} %get-tuple-element.41.refs_3_, ...), custom_call_target="tpu_custom_call" | custom-call | flops 2000000000 | bytes 6000000 | tf_op jit(solution)/shard_map/outer/pallas_call | solution.py:367
  (16 shorter events, 0.1 us)
Async XLA Ops:
  0.0 9.0 %copy-start.6 = (f32[50,6,1024]{2,0,1:T(8,128)S(1)}, f32[50,6,1024]{2,0,1:T(8,128)}, u32[]{:S(2)}) copy-start(f32[50,6,1024]{2,0,1:T(8,128)} %param.11) | copy-start | bytes 3686404
  0.0 9.0 %copy-start.7 = (s32[2]{0:T(128)S(1)}, s32[2]{0:T(128)}, u32[]{:S(2)}) copy-start(s32[2]{0:T(128)} %timestep.1) | copy-start | bytes 28
  0.0 9.0 %copy-start.2 = (bf16[1024,1536]{1,0:T(8,128)(2,1)S(1)}, bf16[1024,1536]{1,0:T(8,128)(2,1)}, u32[]{:S(2)}) copy-start(bf16[1024,1536]{1,0:T(8,128)(2,1)} %refs_2_.3) | copy-start | bytes 9437188
  0.0 9.0 %copy-start.1 = (bf16[512,1024]{1,0:T(8,128)(2,1)S(1)}, bf16[512,1024]{1,0:T(8,128)(2,1)}, u32[]{:S(2)}) copy-start(bf16[512,1024]{1,0:T(8,128)(2,1)} %refs_8_.3) | copy-start | bytes 3145732
  0.0 9.0 %copy-start.5 = (f32[2,64]{1,0:T(2,128)S(1)}, f32[2,64]{1,0:T(2,128)}, u32[]{:S(2)}) copy-start(f32[2,64]{1,0:T(2,128)} %refs_3_.3) | copy-start | bytes 1540
  0.0 9.0 %copy-start = (bf16[1024,1536]{1,0:T(8,128)(2,1)S(1)}, bf16[1024,1536]{1,0:T(8,128)(2,1)}, u32[]{:S(2)}) copy-start(bf16[1024,1536]{1,0:T(8,128)(2,1)} %refs_9_.3) | copy-start | bytes 9437188
  0.0 9.0 %copy-start.4 = (f32[2,64]{1,0:T(2,128)S(1)}, f32[2,64]{1,0:T(2,128)}, u32[]{:S(2)}) copy-start(f32[2,64]{1,0:T(2,128)} %refs_10_.3) | copy-start | bytes 1540
  1.4 7.7 %collective-permute-start = (bf16[1,384,1024]{2,1,0:T(8,128)(2,1)}, bf16[1,384,1024]{2,1,0:T(8,128)(2,1)S(1)}, u32[]{:S(2)}, u32[]{:S(2)}) collective-permute-start(bf16[1,384,1024]{2,1,0:T(8,128)(2,1)} %frames.1), channel_id=1, source_target_pairs={{0,1},{1,0},{2,3},{3,2},{4,5},{5,4},{6,7},{7,6},{8,9},{9,8},{10,11... | collective-permute-start | bytes 2359304 | tf_op jit(solution)/shard_map/ppermute | solution.py:386
  2.1 16.2 %collective-permute-start.2 = (bf16[128,1024]{1,0:T(8,128)(2,1)S(1)}, bf16[128,1024]{1,0:T(8,128)(2,1)S(1)}, u32[]{:S(2)}, u32[]{:S(2)}) collective-permute-start(bf16[128,1024]{1,0:T(8,128)(2,1)S(1)} %get-tuple-element.28.outer_rows.frames), channel_id=1, source_target_pairs={{1,2},{3,4},{5,6},{7,8},{9,10},{11,12},{13,14},{2,1},{4,3},{6,5},{... | collective-permute-start | bytes 786440 | tf_op jit(solution)/shard_map/ppermute | solution.py:383
  5.4 15.2 %collective-permute-start.1 = (bf16[128,1024]{1,0:T(8,128)(2,1)S(1)}, bf16[128,1024]{1,0:T(8,128)(2,1)S(1)}, u32[]{:S(2)}, u32[]{:S(2)}) collective-permute-start(bf16[128,1024]{1,0:T(8,128)(2,1)S(1)} %get-tuple-element.29.inner_rows.frames), channel_id=1, source_target_pairs={{1,2},{3,4},{5,6},{7,8},{9,10},{11,12},{13,14},{2,1},{4,3},{6,5},{... | collective-permute-start | bytes 786440 | tf_op jit(solution)/shard_map/ppermute | solution.py:384
  8.7 20.4 %collective-permute-start.5 = (bf16[256,1024]{1,0:T(8,128)(2,1)S(1)}, bf16[256,1024]{1,0:T(8,128)(2,1)S(1)}, u32[]{:S(2)}, u32[]{:S(2)}) collective-permute-start(bf16[256,1024]{1,0:T(8,128)(2,1)S(1)} %join.1.late_rows), channel_id=1, source_target_pairs={{0,16},{16,0},{1,17},{17,1},{2,18},{18,2},{3,19},{19,3},{4,20},{20... | collective-permute-start | bytes 1572872 | tf_op jit(solution)/shard_map/ppermute | solution.py:361
  17.0 11.3 %collective-permute-start.3 = (bf16[128,1024]{1,0:T(8,128)(2,1)S(1)}, bf16[128,1024]{1,0:T(8,128)(2,1)S(1)}, u32[]{:S(2)}, u32[]{:S(2)}) collective-permute-start(bf16[128,1024]{1,0:T(8,128)(2,1)S(1)} %get-tuple-element.44.kv), channel_id=1, source_target_pairs={{0,16},{16,0},{1,17},{17,1},{2,18},{18,2},{3,19},{19,3},{4,20},{20... | collective-permute-start | bytes 786440 | tf_op jit(solution)/shard_map/ppermute | solution.py:361
  20.4 10.8 %collective-permute-start.4 = (bf16[128,512]{1,0:T(8,128)(2,1)S(1)}, bf16[128,512]{1,0:T(8,128)(2,1)S(1)}, u32[]{:S(2)}, u32[]{:S(2)}) collective-permute-start(bf16[128,512]{1,0:T(8,128)(2,1)S(1)} %get-tuple-element.45.attended), channel_id=1, source_target_pairs={{0,16},{16,0},{1,17},{17,1},{2,18},{18,2},{3,19},{19,3},{4,20},{20... | collective-permute-start | bytes 393224 | tf_op jit(solution)/shard_map/ppermute | solution.py:361
  22.1 11.3 %collective-permute-start.6 = (bf16[128,512]{1,0:T(8,128)(2,1)S(1)}, bf16[128,512]{1,0:T(8,128)(2,1)S(1)}, u32[]{:S(2)}, u32[]{:S(2)}) collective-permute-start(bf16[128,512]{1,0:T(8,128)(2,1)S(1)} %far_outer.1.attended), channel_id=1, source_target_pairs={{0,16},{16,0},{1,17},{17,1},{2,18},{18,2},{3,19},{19,3},{4,20},{20... | collective-permute-start | bytes 393224 | tf_op jit(solution)/shard_map/ppermute | solution.py:361
  24.6 3.8 %copy-start.3 = (bf16[512,1024]{1,0:T(8,128)(2,1)S(1)}, bf16[512,1024]{1,0:T(8,128)(2,1)}, u32[]{:S(2)}) copy-start(bf16[512,1024]{1,0:T(8,128)(2,1)} %refs_11_.1) | copy-start | bytes 3145732

commit v5 on v4

--- a/solution.py
+++ b/solution.py
@@ -139,10 +139,12 @@
     return parity, outer, rows - HALF, early
 
 
-def split_kernel(frames, outer_rows, inner_rows, early_rows, sems):
+def split_kernel(frames, late_rows, early_rows, sems):
+    _, outer, inner, early = places(frames.shape[1])
+    targets = (late_rows.at[pl.ds(0, BLOCK)], late_rows.at[pl.ds(BLOCK, BLOCK)], early_rows)
     copies = [
         pltpu.make_async_copy(frames.at[0, pl.ds(at, BLOCK)], to, sems.at[n])
-        for n, (at, to) in enumerate(zip(places(frames.shape[1])[1:], (outer_rows, inner_rows, early_rows)))
+        for n, (at, to) in enumerate(zip((outer, inner, early), targets))
     ]
     for copy in copies:
         copy.start()
@@ -150,14 +152,9 @@
         copy.wait()
 
 
-def join_kernel(outer_rows, inner_rows, both):
-    both[:BLOCK] = outer_rows[...]
-    both[BLOCK:] = inner_rows[...]
-
-
 def near_kernel(
     timestep, modulation, early_rows, late_rows, near, qkv_self, gains, out_self, qkv_cross, gains_cross,
-    query, part_out, part_sum, part_top, first, first_q, first_kv, held, kv,
+    query, kv, first, first_q, first_kv, held,
 ):
     rows = near.shape[1]
     for k in range(held.shape[0]):
@@ -210,15 +207,18 @@
         f, mods, qkv_cross, gains_cross, ones, True
     )
 
+
+def part_kernel(query, kv, part_out, part_sum, part_top):
+    parity = lax.rem(lax.axis_index("tm"), 2)
     for n, width in ((0, HALF), (1, BLOCK)):
         start = pl.multiple_of(parity * width, BLOCK)
-        count = window - width
+        count = kv.shape[0] - width
         bias = window_bias(count, (1 - parity) * width)
         to = slice(n * BLOCK, (n + 1) * BLOCK)
         for at in range(0, HW, SLAB):
             cols = slice(at, at + SLAB)
             raised, top = raised_scores(
-                queries[n + 1][:, cols], kv[pl.ds(start, count), cols], bias
+                query[to, cols], kv[pl.ds(start, count), cols], bias
             )
             out, total = weighted(raised, kv[pl.ds(start, count), HW + at : HW + at + SLAB])
             part_out[to, cols] = out
@@ -226,43 +226,52 @@
             part_top[to, cols] = by_head(jnp.broadcast_to(top, (2 * BLOCK, SLAB)))
 
 
-def far_kernel(
-    outermost, rows, held, far, qkv_self, gains, query, part_out, part_sum, part_top, *outs
-):
-    parity = lax.rem(lax.axis_index("tm"), 2)
+def far_keys(rows, held, qkv_self, gains):
     mods = mods_held(held, 0)
-    ones = head_ones()
-    normed = modulated(far[...], mods(0), mods(1))
+    normed = modulated(rows, mods(0), mods(1))
     keys = dot(normed, qkv_self[:, HW : 2 * HW])
     values = dot(normed, qkv_self[:, 2 * HW :]).astype(BF16)
-    keys = head_norm(keys, wide_gain(gains[1:2]), ones)
-    start = jnp.where(parity == 0, -2 * BLOCK if outermost else -BLOCK, rows + (BLOCK if outermost else 0))
+    return head_norm(keys, wide_gain(gains[1:2]), head_ones()), values
+
+
+def far_bias(rows, block_start, outermost):
     place = lax.axis_index("tm")
+    below = -2 * BLOCK if outermost else -BLOCK
+    start = jnp.where(lax.rem(place, 2) == 0, below, rows + (BLOCK if outermost else 0))
     total = rows * lax.axis_size("tm")
-
-    def attend(block, block_start):
-        bias = window_bias(BLOCK, start - block_start + HALF, place * rows + start, total)
-        to = slice(block * BLOCK, (block + 1) * BLOCK)
-        for at in range(0, HW, SLAB):
-            cols = slice(at, at + SLAB)
-            raised, top = raised_scores(query[to, cols], keys[:, cols], bias)
-            out, summed = weighted(raised, values[:, cols])
-            top = by_head(jnp.broadcast_to(top, (2 * BLOCK, SLAB)))
-            both = jnp.maximum(top, part_top[to, cols])
-            here = jnp.exp(top - both)
-            before = jnp.exp(part_top[to, cols] - both)
-            out = out * here + part_out[to, cols] * before
-            summed = summed * here + part_sum[to, cols] * before
-            yield cols, out, summed, both
-
-    if outermost:
-        for cols, out, summed, _ in attend(0, parity * HALF):
-            outs[0][:, cols] = (out / summed).astype(BF16)
-    else:
-        for cols, out, summed, _ in attend(1, rows - HALF):
-            outs[0][:, cols] = (out / summed).astype(BF16)
-        for cols, out, summed, top in attend(0, parity * HALF):
-            outs[1][:, cols], outs[2][:, cols], outs[3][:, cols] = out, summed, top
+    return window_bias(BLOCK, start - block_start + HALF, place * rows + start, total)
+
+
+def far_attend(block, bias, query, keys, values, part_out, part_sum, part_top, attended):
+    to = slice(block * BLOCK, (block + 1) * BLOCK)
+    for at in range(0, HW, SLAB):
+        cols = slice(at, at + SLAB)
+        raised, top = raised_scores(query[to, cols], keys[:, cols], bias)
+        out, summed = weighted(raised, values[:, cols])
+        top = by_head(jnp.broadcast_to(top, (2 * BLOCK, SLAB)))
+        both = jnp.maximum(top, part_top[to, cols])
+        here = jnp.exp(top - both)
+        before = jnp.exp(part_top[to, cols] - both)
+        out = out * here + part_out[to, cols] * before
+        summed = summed * here + part_sum[to, cols] * before
+        attended[:, cols] = (out / summed).astype(BF16)
+
+
+def far_inner_kernel(rows, held, far, qkv_self, gains, query, *refs):
+    *parts, attended, kv = refs
+    keys, values = far_keys(far[:BLOCK], held, qkv_self, gains)
+    far_attend(1, far_bias(rows, rows - HALF, False), query, keys, values, *parts, attended)
+    kv[:, :HW], kv[:, HW:] = keys, values
+
+
+def far_outer_kernel(rows, held, far, qkv_self, gains, query, *refs):
+    *parts, kv, attended = refs
+    keys, values = far_keys(far[BLOCK:], held, qkv_self, gains)
+    keys = jnp.concatenate([kv[:, :HW], keys], axis=0)
+    values = jnp.concatenate([kv[:, HW:], values], axis=0)
+    start = lax.rem(lax.axis_index("tm"), 2) * HALF
+    bias = [far_bias(rows, start, outermost) for outermost in (False, True)]
+    far_attend(0, jnp.concatenate(bias, axis=1), query, keys, values, *parts, attended)
 
 
 def first_of(frames, attended, weight, gate):
@@ -283,13 +292,26 @@
     return (first.astype(F32) + gate * out.astype(F32)).astype(BF16)
 
 
-def own_kernel(held, frames, attended, out_self, qkv_cross, gains, first, query, kv):
+def own_kernel(held, frames, inner, outer, out_self, qkv_cross, gains, first, query, kv):
     mods = mods_held(held, 0)
-    f = first_of(frames[...], attended[...], out_self, mods(2))
-    first[...] = f
-    query[...], kv[:, :HW], kv[:, HW:] = projected_cross(
-        f, mods, qkv_cross, gains, head_ones(), True
-    )
+    ones = head_ones()
+    parts = [slice(0, BLOCK), slice(BLOCK, HALF)]
+    mixed = [dot(attended[...], out_self[...]) for attended in (outer, inner)]
+    gains = [wide_gain(gains[i : i + 1]) for i in range(2)]
+
+    def normed(n):
+        f = (frames[parts[n]].astype(F32) + mods(2) * mixed[n]).astype(BF16)
+        first[parts[n]] = f
+        return modulated(f, mods(3), mods(4))
+
+    rows = normed(0)
+    for n, part in enumerate(parts):
+        raw = [dot(rows, qkv_cross[:, at : at + HW]) for at in (2 * HW, 0, HW)]
+        if n + 1 < len(parts):
+            rows = normed(n + 1)
+        kv[part, HW:] = raw[0].astype(BF16)
+        query[part] = head_norm(raw[1], gains[0], ones)
+        kv[part, :HW] = head_norm(raw[2], gains[1], ones)
 
 
 def early_kernel(held, first, query, kv, out_cross, *refs):
@@ -303,15 +325,15 @@
 def late_block(block, held, first, query, kv, others, their_frames, out_self, qkv_cross, gains, out_cross):
     ones = head_ones()
     part = slice(block * BLOCK, (block + 1) * BLOCK)
-    keys, values = [kv[:, :HW]], [kv[:, HW:]]
+    keys, values = [kv[part, :HW]], [kv[part, HW:]]
     for n, (attended, source) in enumerate(zip(others, their_frames)):
         mods = mods_held(held, n + 1)
         g = first_of(source[part], attended[...], out_self, mods(2))
         _, k, v = projected_cross(g, mods, qkv_cross, gains, ones, False)
         keys.append(k)
         values.append(v)
-    mixed = cross_attend(query[...], keys, values, ones)
-    return finished(first[...], mixed, out_cross, mods_held(held, 0)(5))
+    mixed = cross_attend(query[part], keys, values, ones)
+    return finished(first[part], mixed, out_cross, mods_held(held, 0)(5))
 
 
 def inner_kernel(count, _, held, first, query, kv, *refs):
@@ -376,56 +398,53 @@
         )(*args)
 
     half = shape(BLOCK, D)
-    outer_rows, inner_rows, early_rows = call(
-        split_kernel, "split", 4, (half, half, half), frames,
-        scratch=[pltpu.SemaphoreType.DMA((3,))], in_specs=[ANY], out_specs=(ANY, ANY, ANY),
-    )
-    far_inner = lax.ppermute(outer_rows, "tm", across)
-    far_outer = lax.ppermute(inner_rows, "tm", across)
-    after, _ = lax.optimization_barrier((frames, outer_rows))
+    late_rows, early_rows = call(
+        split_kernel, "split", 6, (shape(HALF, D), half), frames,
+        scratch=[pltpu.SemaphoreType.DMA((3,))], in_specs=[ANY], out_specs=(ANY, ANY),
+    )
+    their_frames = to_stems(late_rows)
+    far = lax.ppermute(late_rows, "tm", across)
+    after, _ = lax.optimization_barrier((frames, late_rows))
     near = lax.ppermute(after, "tm", inside)
-    late_rows = call(join_kernel, "join", 0.1, shape(HALF, D), outer_rows, inner_rows)
-    their_frames = to_stems(late_rows)
-
-    part = shape(HALF, HW, dtype=F32)
-    query, part_out, part_sum, part_top, first_early, q_early, kv_early, held = call(
-        near_kernel, "near", 4,
-        (shape(HALF, HW), part, part, part, half, shape(BLOCK, HW), half, shape(stems, 8, D, dtype=F32)),
+
+    late, block, part = shape(HALF, HW), shape(BLOCK, HW), shape(HALF, HW, dtype=F32)
+    query, kv, first_early, q_early, kv_early, held = call(
+        near_kernel, "near", 2,
+        (late, shape(rows + HALF, 2 * HW), half, block, half, shape(stems, 8, D, dtype=F32)),
         timestep, modulation, early_rows, late_rows, near, qkv_self, qk_gain_self, out_self, qkv_cross, qk_gain_cross,
-        scratch=[pltpu.VMEM((rows + HALF, 2 * HW), BF16)], in_specs=[SMEM] + [VMEM] * 9,
+        in_specs=[SMEM] + [VMEM] * 9,
     )
     others_early = to_stems(kv_early)
-
-    block, part = shape(BLOCK, HW), shape(BLOCK, HW, dtype=F32)
-    att_inner, *parts = call(
-        lambda *refs: far_kernel(False, rows, *refs), "far_inner", 1, (block, part, part, part),
-        held, far_inner, qkv_self, qk_gain_self, query, part_out, part_sum, part_top,
+    parts = call(part_kernel, "part", 0.3, (part, part, part), query, kv)
+
+    self_weights = (qkv_self, qk_gain_self)
+    att_inner, far_kv = call(
+        lambda *refs: far_inner_kernel(rows, *refs), "far_inner", 2, (block, half),
+        held, far, *self_weights, query, *parts,
     )
     others_inner = to_stems(att_inner)
     att_outer = call(
-        lambda *refs: far_kernel(True, rows, *refs), "far_outer", 1, block,
-        held, far_outer, qkv_self, qk_gain_self, query, *parts,
+        lambda *refs: far_outer_kernel(rows, *refs), "far_outer", 0.3, block,
+        held, far, *self_weights, query, *parts, far_kv,
     )
     others_outer = to_stems(att_outer)
 
     weights = (out_self, qkv_cross, qk_gain_cross)
-    own_inner = call(
-        own_kernel, "own_inner", 0.3, (half, block, half), held, inner_rows, att_inner, *weights
-    )
-    own_outer = call(
-        own_kernel, "own_outer", 0.3, (half, block, half), held, outer_rows, att_outer, *weights
+    own = call(
+        own_kernel, "own", 0.3, (shape(HALF, D), late, shape(HALF, D)),
+        held, late_rows, att_inner, att_outer, *weights,
     )
     early_out = call(
         early_kernel, "early", 0.3, half, held, first_early, q_early, kv_early, out_cross, *others_early
     )
     inner_out = call(
-        lambda *refs: inner_kernel(stems, *refs), "inner", 0.5, half,
-        early_out, held, *own_inner, *others_inner, *their_frames, *weights, out_cross,
+        lambda *refs: inner_kernel(stems, *refs), "inner", 0.6, half,
+        early_out, held, *own, *others_inner, *their_frames, *weights, out_cross,
         in_specs=[ANY] + [VMEM] * (6 + 2 * stems),
     )
     return call(
-        lambda *refs: outer_kernel(stems, *refs), "outer", 2, shape(1, rows, D),
-        held, *own_outer, early_out, inner_out, *others_outer, *their_frames, *weights, out_cross,
+        lambda *refs: outer_kernel(stems, *refs), "outer", 0.3, shape(1, rows, D),
+        held, *own, early_out, inner_out, *others_outer, *their_frames, *weights, out_cross,
         scratch=[pltpu.VMEM((BLOCK, D), BF16), pltpu.SemaphoreType.DMA((3,))], out_specs=ANY,
     )
 

time: 36 us -> 32.8 us (0.911)
  the two profiles are of different devices: /device:TPU:7 before, /device:TPU:16 now
where the time goes in v5:
time: 32.8 us; the launch traced here: 32.6 us
  Pallas kernels  18.9 us (58%)
  starting transfers between devices  7.88 us (24%)
  waiting for transfers between devices  5.66 us (17%)
    pallas_call x9, Pallas kernels, call(): pl.pallas_call(kernel, out_shape=outs, in_specs=in_specs or [VMEM] * len(...  18.9 us
    ppermute x4, waiting for transfers between devices, to_stems(): lax.ppermute(array, 'stem', [(i, (i + k) % stems) for i in range(stems)])  5.65 us
    ppermute x4, starting transfers between devices, to_stems(): lax.ppermute(array, 'stem', [(i, (i + k) % stems) for i in range(stems)])  4.3 us
    ppermute x1, starting transfers between devices, on_device(): far = lax.ppermute(late_rows, 'tm', across)  3.5 us
  transfers between devices with their start and end apart: 6, of which 3 were waited for; matrix products, arithmetic and copies ran while one was open for 0% of the time, Pallas kernels for 47%

profile of v5, /device:TPU:16, one launch (start us, length us, event | category | flops | bytes accessed | tf_op | source)
XLA Modules:
  0.0 32.6 jit_solution(1454773632864513297)
XLA Ops:
  0.0 0.0 copy-start.1
  0.0 0.0 copy-start.6
  0.0 1.3 %split.1 = (bf16[256,1024]{1,0:T(8,128)(2,1)S(1)}, bf16[128,1024]{1,0:T(8,128)(2,1)S(1)}) custom-call(bf16[1,384,1024]{2,1,0:T(8,128)(2,1)} %frames.1), custom_call_target="tpu_custom_call" | custom-call | flops 6000000000 | bytes 18000000 | tf_op jit(solution)/shard_map/split/pallas_call | solution.py:389
  1.4 0.1 collective-permute-start
  1.4 3.5 %collective-permute-start.1 = (bf16[256,1024]{1,0:T(8,128)(2,1)S(1)}, bf16[256,1024]{1,0:T(8,128)(2,1)S(1)}, u32[]{:S(2)}, u32[]{:S(2)}) collective-permute-start(bf16[256,1024]{1,0:T(8,128)(2,1)S(1)} %get-tuple-element.23.late_rows.frames), channel_id=1, source_target_pairs={{1,2},{3,4},{5,6},{7,8},{9,10},{11,12},{13,14},{2,1},{4,3},{6,5},{... | collective-permute-start | bytes 1572872 | tf_op jit(solution)/shard_map/ppermute | solution.py:406
  4.9 1.6 %collective-permute-start.4 = (bf16[256,1024]{1,0:T(8,128)(2,1)S(1)}, bf16[256,1024]{1,0:T(8,128)(2,1)S(1)}, u32[]{:S(2)}, u32[]{:S(2)}) collective-permute-start(bf16[256,1024]{1,0:T(8,128)(2,1)S(1)} %get-tuple-element.23.late_rows.frames), channel_id=1, source_target_pairs={{0,16},{16,0},{1,17},{17,1},{2,18},{18,2},{3,19},{19,3},{4,20},{20... | collective-permute-start | bytes 1572872 | tf_op jit(solution)/shard_map/ppermute | solution.py:383
  6.5 0.0 collective-permute-done.near
  6.6 6.5 %near.1 = (bf16[256,512]{1,0:T(8,128)(2,1)S(1)}, bf16[640,1024]{1,0:T(8,128)(2,1)S(1)}, bf16[128,1024]{1,0:T(8,128)(2,1)S(1)}, bf16[128,512]{1,0:T(8,128)(2,1)S(...) custom-call(s32[2]{0:T(128)S(1)} %copy-done.7, f32[6,50,1024]{2,1,0:T(8,128)S(1)} %bitcast.1, ...), custom_call_target="tpu_custom_call" | custom-call | flops 2000000000 | bytes 6000000 | tf_op jit(solution)/shard_map/near/pallas_call | solution.py:389
  13.1 0.6 %collective-permute-start.2 = (bf16[128,1024]{1,0:T(8,128)(2,1)S(1)}, bf16[128,1024]{1,0:T(8,128)(2,1)S(1)}, u32[]{:S(2)}, u32[]{:S(2)}) collective-permute-start(bf16[128,1024]{1,0:T(8,128)(2,1)S(1)} %get-tuple-element.38.kv), channel_id=1, source_target_pairs={{0,16},{16,0},{1,17},{17,1},{2,18},{18,2},{3,19},{19,3},{4,20},{20... | collective-permute-start | bytes 786440 | tf_op jit(solution)/shard_map/ppermute | solution.py:383
  13.6 1.9 %part.1 = (f32[256,512]{1,0:T(8,128)S(1)}, f32[256,512]{1,0:T(8,128)S(1)}, f32[256,512]{1,0:T(8,128)S(1)}) custom-call(bf16[256,512]{1,0:T(8,128)(2,1)S(1)} %get-tuple-element.26.query.refs_4_, bf16[640,1024]{1,0:T(8,128)(2,1)S(1)} %get-tuple-element.27.kv), custom_call_target="tpu_custom_call" | custom-call | flops 300000000 | bytes 900000 | tf_op jit(solution)/shard_map/part/pallas_call | solution.py:389
  15.6 0.0 collective-permute-done.1.refs_1_
  15.6 1.4 %far_inner.1 = (bf16[128,512]{1,0:T(8,128)(2,1)S(1)}, bf16[128,1024]{1,0:T(8,128)(2,1)S(1)}) custom-call(f32[2,8,1024]{2,1,0:T(8,128)S(1)} %get-tuple-element.25.refs_0_.held.refs_1_, bf16[256,1024]{1,0:T(8,128)(2,1)S(1)} %collective-permute-done.1.refs_1_, bf16[1024,1536]{1,0:T(8,128)(2,1)S(1)} %copy-done.2, f32[2,64]{1,0:T(2,128)S(1)} %copy-done.6, ...), custom_call_target="tpu_custom_call" | custom-call | flops 2000000000 | bytes 6000000 | tf_op jit(solution)/shard_map/far_inner/pallas_call | solution.py:389
  17.0 1.6 %collective-permute-start.3 = (bf16[128,512]{1,0:T(8,128)(2,1)S(1)}, bf16[128,512]{1,0:T(8,128)(2,1)S(1)}, u32[]{:S(2)}, u32[]{:S(2)}) collective-permute-start(bf16[128,512]{1,0:T(8,128)(2,1)S(1)} %get-tuple-element.31.inner), channel_id=1, source_target_pairs={{0,16},{16,0},{1,17},{17,1},{2,18},{18,2},{3,19},{19,3},{4,20},{20... | collective-permute-start | bytes 393224 | tf_op jit(solution)/shard_map/ppermute | solution.py:383
  18.6 1.3 %far_outer.1.outer = bf16[128,512]{1,0:T(8,128)(2,1)S(1)} custom-call(f32[2,8,1024]{2,1,0:T(8,128)S(1)} %get-tuple-element.25.refs_0_.held.refs_1_, bf16[256,1024]{1,0:T(8,128)(2,1)S(1)} %collective-permute-done.1.refs_1_, bf16[1024,1536]{1,0:T(8,128)(2,1)S(1)} %copy-done.2, f32[2,64]{1,0:T(2,128)S(1)} %copy-done.6, ...), custom_call_target="tpu_custom_call" | custom-call | flops 300000000 | bytes 900000 | tf_op jit(solution)/shard_map/far_outer/pallas_call | solution.py:389
  19.9 0.0 copy-start.3
  20.0 0.6 %collective-permute-start.5 = (bf16[128,512]{1,0:T(8,128)(2,1)S(1)}, bf16[128,512]{1,0:T(8,128)(2,1)S(1)}, u32[]{:S(2)}, u32[]{:S(2)}) collective-permute-start(bf16[128,512]{1,0:T(8,128)(2,1)S(1)} %far_outer.1.outer), channel_id=1, source_target_pairs={{0,16},{16,0},{1,17},{17,1},{2,18},{18,2},{3,19},{19,3},{4,20},{20... | collective-permute-start | bytes 393224 | tf_op jit(solution)/shard_map/ppermute | solution.py:383
  20.5 2.0 %own.1 = (bf16[256,1024]{1,0:T(8,128)(2,1)S(1)}, bf16[256,512]{1,0:T(8,128)(2,1)S(1)}, bf16[256,1024]{1,0:T(8,128)(2,1)S(1)}) custom-call(f32[2,8,1024]{2,1,0:T(8,128)S(1)} %get-tuple-element.25.refs_0_.held.refs_1_, bf16[256,1024]{1,0:T(8,128)(2,1)S(1)} %get-tuple-element.23.late_rows.frames, bf16[128,512]{1,0:T(8,128)(2,1)S(1)} %get-tuple-element.31.inner, ...), custom_call_target="tpu_custom_call" | custom-call | flops 300000000 | bytes 900000 | tf_op jit(solution)/shard_map/own/pallas_call | solution.py:389
  22.5 2.9 %collective-permute-done.2.refs_0_ = bf16[128,1024]{1,0:T(8,128)(2,1)S(1)} collective-permute-done((bf16[128,1024]{1,0:T(8,128)(2,1)S(1)}, bf16[128,1024]{1,0:T(8,128)(2,1)S(1)}, u32[]{:S(2)}, u32[]{:S(2)}) %collective-permute-start.2) | collective-permute-done | bytes 262176 | tf_op jit(solution)/shard_map/ppermute | solution.py:383
  25.4 0.6 %early.1.refs_0_.refs_4_ = bf16[128,1024]{1,0:T(8,128)(2,1)S(1)} custom-call(f32[2,8,1024]{2,1,0:T(8,128)S(1)} %get-tuple-element.25.refs_0_.held.refs_1_, bf16[128,1024]{1,0:T(8,128)(2,1)S(1)} %get-tuple-element.36.first, bf16[128,512]{1,0:T(8,128)(2,1)S(1)} %get-tuple-element.37.query, bf16[128,1024]{1,0:T(8,128)(2,1)S(1)} %get-tuple-element.38.kv, ...), custom_call_target="tpu_custom_call" | custom-call | flops 300000000 | bytes 900000 | tf_op jit(solution)/shard_map/early/pallas_call | solution.py:389
  26.0 0.0 collective-permute-done.4.refs_6_.refs_7_
  26.0 2.2 %collective-permute-done.3.refs_5_ = bf16[128,512]{1,0:T(8,128)(2,1)S(1)} collective-permute-done((bf16[128,512]{1,0:T(8,128)(2,1)S(1)}, bf16[128,512]{1,0:T(8,128)(2,1)S(1)}, u32[]{:S(2)}, u32[]{:S(2)}) %collective-permute-start.3) | collective-permute-done | bytes 131104 | tf_op jit(solution)/shard_map/ppermute | solution.py:383
  28.2 1.5 %inner.1.refs_5_ = bf16[128,1024]{1,0:T(8,128)(2,1)S(1)} custom-call(bf16[128,1024]{1,0:T(8,128)(2,1)S(1)} %early.1.refs_0_.refs_4_, f32[2,8,1024]{2,1,0:T(8,128)S(1)} %get-tuple-element.25.refs_0_.held.refs_1_, bf16[256,1024]{1,0:T(8,128)(2,1)S(1)} %get-tuple-element.33.refs_2_.refs_1_, bf16[256,512]{1,0:T(8,128)(2,1)S(1)} %get-tuple-element.34.refs_3_.refs_2_, ...), custom_call_target="tpu_custom_call" | custom-call | flops 600000000 | bytes 1800000 | tf_op jit(solution)/shard_map/inner/pallas_call | solution.py:389
  29.7 0.6 %collective-permute-done.5.refs_6_ = bf16[128,512]{1,0:T(8,128)(2,1)S(1)} collective-permute-done((bf16[128,512]{1,0:T(8,128)(2,1)S(1)}, bf16[128,512]{1,0:T(8,128)(2,1)S(1)}, u32[]{:S(2)}, u32[]{:S(2)}) %collective-permute-start.5) | collective-permute-done | bytes 131104 | tf_op jit(solution)/shard_map/ppermute | solution.py:383
  30.3 2.3 %outer.1 = bf16[1,384,1024]{2,1,0:T(8,128)(2,1)} custom-call(f32[2,8,1024]{2,1,0:T(8,128)S(1)} %get-tuple-element.25.refs_0_.held.refs_1_, bf16[256,1024]{1,0:T(8,128)(2,1)S(1)} %get-tuple-element.33.refs_2_.refs_1_, bf16[256,512]{1,0:T(8,128)(2,1)S(1)} %get-tuple-element.34.refs_3_.refs_2_, bf16[256,1024]{1,0:T(8,128)(2,1)S(1)} %get-tuple-element.35.refs_4_.refs_3_, ...), custom_call_target="tpu_custom_call" | custom-call | flops 300000000 | bytes 900000 | tf_op jit(solution)/shard_map/outer/pallas_call | solution.py:389
  (13 shorter events, 0.0 us)
Async XLA Ops:
  0.0 6.5 %copy-start.4 = (f32[50,6,1024]{2,0,1:T(8,128)S(1)}, f32[50,6,1024]{2,0,1:T(8,128)}, u32[]{:S(2)}) copy-start(f32[50,6,1024]{2,0,1:T(8,128)} %param.11) | copy-start | bytes 3686404
  0.0 6.5 %copy-start.7 = (s32[2]{0:T(128)S(1)}, s32[2]{0:T(128)}, u32[]{:S(2)}) copy-start(s32[2]{0:T(128)} %timestep.1) | copy-start | bytes 28
  0.0 6.5 %copy-start.2 = (bf16[1024,1536]{1,0:T(8,128)(2,1)S(1)}, bf16[1024,1536]{1,0:T(8,128)(2,1)}, u32[]{:S(2)}) copy-start(bf16[1024,1536]{1,0:T(8,128)(2,1)} %refs_2_.3) | copy-start | bytes 9437188
  0.0 6.5 %copy-start.1 = (bf16[512,1024]{1,0:T(8,128)(2,1)S(1)}, bf16[512,1024]{1,0:T(8,128)(2,1)}, u32[]{:S(2)}) copy-start(bf16[512,1024]{1,0:T(8,128)(2,1)} %refs_8_.3) | copy-start | bytes 3145732
  0.0 6.5 %copy-start.6 = (f32[2,64]{1,0:T(2,128)S(1)}, f32[2,64]{1,0:T(2,128)}, u32[]{:S(2)}) copy-start(f32[2,64]{1,0:T(2,128)} %refs_3_.3) | copy-start | bytes 1540
  0.0 6.5 %copy-start = (bf16[1024,1536]{1,0:T(8,128)(2,1)S(1)}, bf16[1024,1536]{1,0:T(8,128)(2,1)}, u32[]{:S(2)}) copy-start(bf16[1024,1536]{1,0:T(8,128)(2,1)} %refs_9_.3) | copy-start | bytes 9437188
  0.0 6.5 %copy-start.5 = (f32[2,64]{1,0:T(2,128)S(1)}, f32[2,64]{1,0:T(2,128)}, u32[]{:S(2)}) copy-start(f32[2,64]{1,0:T(2,128)} %refs_10_.3) | copy-start | bytes 1540
  1.4 5.2 %collective-permute-start = (bf16[1,384,1024]{2,1,0:T(8,128)(2,1)}, bf16[1,384,1024]{2,1,0:T(8,128)(2,1)S(1)}, u32[]{:S(2)}, u32[]{:S(2)}) collective-permute-start(bf16[1,384,1024]{2,1,0:T(8,128)(2,1)} %frames.1), channel_id=1, source_target_pairs={{0,1},{1,0},{2,3},{3,2},{4,5},{5,4},{6,7},{7,6},{8,9},{9,8},{10,11... | collective-permute-start | bytes 2359304 | tf_op jit(solution)/shard_map/ppermute | solution.py:408
  1.4 14.1 %collective-permute-start.1 = (bf16[256,1024]{1,0:T(8,128)(2,1)S(1)}, bf16[256,1024]{1,0:T(8,128)(2,1)S(1)}, u32[]{:S(2)}, u32[]{:S(2)}) collective-permute-start(bf16[256,1024]{1,0:T(8,128)(2,1)S(1)} %get-tuple-element.23.late_rows.frames), channel_id=1, source_target_pairs={{1,2},{3,4},{5,6},{7,8},{9,10},{11,12},{13,14},{2,1},{4,3},{6,5},{... | collective-permute-start | bytes 1572872 | tf_op jit(solution)/shard_map/ppermute | solution.py:406
  4.9 21.1 %collective-permute-start.4 = (bf16[256,1024]{1,0:T(8,128)(2,1)S(1)}, bf16[256,1024]{1,0:T(8,128)(2,1)S(1)}, u32[]{:S(2)}, u32[]{:S(2)}) collective-permute-start(bf16[256,1024]{1,0:T(8,128)(2,1)S(1)} %get-tuple-element.23.late_rows.frames), channel_id=1, source_target_pairs={{0,16},{16,0},{1,17},{17,1},{2,18},{18,2},{3,19},{19,3},{4,20},{20... | collective-permute-start | bytes 1572872 | tf_op jit(solution)/shard_map/ppermute | solution.py:383
  13.1 12.3 %collective-permute-start.2 = (bf16[128,1024]{1,0:T(8,128)(2,1)S(1)}, bf16[128,1024]{1,0:T(8,128)(2,1)S(1)}, u32[]{:S(2)}, u32[]{:S(2)}) collective-permute-start(bf16[128,1024]{1,0:T(8,128)(2,1)S(1)} %get-tuple-element.38.kv), channel_id=1, source_target_pairs={{0,16},{16,0},{1,17},{17,1},{2,18},{18,2},{3,19},{19,3},{4,20},{20... | collective-permute-start | bytes 786440 | tf_op jit(solution)/shard_map/ppermute | solution.py:383
  17.0 11.2 %collective-permute-start.3 = (bf16[128,512]{1,0:T(8,128)(2,1)S(1)}, bf16[128,512]{1,0:T(8,128)(2,1)S(1)}, u32[]{:S(2)}, u32[]{:S(2)}) collective-permute-start(bf16[128,512]{1,0:T(8,128)(2,1)S(1)} %get-tuple-element.31.inner), channel_id=1, source_target_pairs={{0,16},{16,0},{1,17},{17,1},{2,18},{18,2},{3,19},{19,3},{4,20},{20... | collective-permute-start | bytes 393224 | tf_op jit(solution)/shard_map/ppermute | solution.py:383
  19.9 5.4 %copy-start.3 = (bf16[512,1024]{1,0:T(8,128)(2,1)S(1)}, bf16[512,1024]{1,0:T(8,128)(2,1)}, u32[]{:S(2)}) copy-start(bf16[512,1024]{1,0:T(8,128)(2,1)} %refs_11_.1) | copy-start | bytes 3145732
  20.0 10.4 %collective-permute-start.5 = (bf16[128,512]{1,0:T(8,128)(2,1)S(1)}, bf16[128,512]{1,0:T(8,128)(2,1)S(1)}, u32[]{:S(2)}, u32[]{:S(2)}) collective-permute-start(bf16[128,512]{1,0:T(8,128)(2,1)S(1)} %far_outer.1.outer), channel_id=1, source_target_pairs={{0,16},{16,0},{1,17},{17,1},{2,18},{18,2},{3,19},{19,3},{4,20},{20... | collective-permute-start | bytes 393224 | tf_op jit(solution)/shard_map/ppermute | solution.py:383

commit v6 on v5

--- a/solution.py
+++ b/solution.py
@@ -150,6 +150,12 @@
         copy.start()
     for copy in copies:
         copy.wait()
+
+
+def mate_kernel(mate, rows):
+    _, _, inner, outer = places(mate.shape[1])
+    rows[:BLOCK] = mate[0, pl.ds(outer, BLOCK)]
+    rows[BLOCK:] = mate[0, inner : inner + BLOCK]
 
 
 def near_kernel(
@@ -258,7 +264,7 @@
 
 
 def far_inner_kernel(rows, held, far, qkv_self, gains, query, *refs):
-    *parts, attended, kv = refs
+    parts, (attended, kv) = refs[:3], refs[-2:]
     keys, values = far_keys(far[:BLOCK], held, qkv_self, gains)
     far_attend(1, far_bias(rows, rows - HALF, False), query, keys, values, *parts, attended)
     kv[:, :HW], kv[:, HW:] = keys, values
@@ -314,7 +320,7 @@
         kv[part, :HW] = head_norm(raw[2], gains[1], ones)
 
 
-def early_kernel(held, first, query, kv, out_cross, *refs):
+def early_kernel(_, held, first, query, kv, out_cross, *refs):
     others, out = refs[:-1], refs[-1]
     keys = [each[:, :HW] for each in (kv, *others)]
     values = [each[:, HW:] for each in (kv, *others)]
@@ -375,8 +381,8 @@
     assert count % 2 == 0 and rows == HALF + BLOCK
     modulation = jnp.transpose(modulation, (1, 0, 2))
     inside = [(i, i ^ 1) for i in range(count)]
-    across = [(i, i + 1) for i in range(1, count - 1, 2)]
-    across += [(b, a) for a, b in across]
+    across = [(i, i + 2) for i in range(0, count - 2, 2)]
+    across += [(i + 3, i + 1) for i in range(0, count - 2, 2)]
 
     def to_stems(array):
         return [
@@ -403,9 +409,9 @@
         scratch=[pltpu.SemaphoreType.DMA((3,))], in_specs=[ANY], out_specs=(ANY, ANY),
     )
     their_frames = to_stems(late_rows)
-    far = lax.ppermute(late_rows, "tm", across)
-    after, _ = lax.optimization_barrier((frames, late_rows))
-    near = lax.ppermute(after, "tm", inside)
+    near = lax.ppermute(frames, "tm", inside)
+    mate_rows = call(mate_kernel, "mate", 0.1, shape(HALF, D), near)
+    far = lax.ppermute(mate_rows, "tm", across)
 
     late, block, part = shape(HALF, HW), shape(BLOCK, HW), shape(HALF, HW, dtype=F32)
     query, kv, first_early, q_early, kv_early, held = call(
@@ -420,7 +426,8 @@
     self_weights = (qkv_self, qk_gain_self)
     att_inner, far_kv = call(
         lambda *refs: far_inner_kernel(rows, *refs), "far_inner", 2, (block, half),
-        held, far, *self_weights, query, *parts,
+        held, far, *self_weights, query, *parts, *their_frames,
+        in_specs=[VMEM] * 8 + [ANY] * (stems - 1),
     )
     others_inner = to_stems(att_inner)
     att_outer = call(
@@ -435,7 +442,8 @@
         held, late_rows, att_inner, att_outer, *weights,
     )
     early_out = call(
-        early_kernel, "early", 0.3, half, held, first_early, q_early, kv_early, out_cross, *others_early
+        early_kernel, "early", 0.3, half, own[0], held, first_early, q_early, kv_early, out_cross, *others_early,
+        in_specs=[ANY] + [VMEM] * (4 + stems),
     )
     inner_out = call(
         lambda *refs: inner_kernel(stems, *refs), "inner", 0.6, half,

time: 32.8 us -> 32 us (0.976)
  the two profiles are of different devices: /device:TPU:16 before, /device:TPU:0 now
where the time goes in v6:
time: 32 us; the launch traced here: 31.8 us
  Pallas kernels  17.7 us (55%)
  starting transfers between devices  9.9 us (31%)
  waiting for transfers between devices  2.67 us (8%)
  local copies, waits for them, and re-layouts  1.39 us (4%)
    pallas_call x10, Pallas kernels, call(): pl.pallas_call(kernel, out_shape=outs, in_specs=in_specs or [VMEM] * len(...  17.7 us
    ppermute x4, starting transfers between devices, to_stems(): lax.ppermute(array, 'stem', [(i, (i + k) % stems) for i in range(stems)])  5.81 us
    ppermute x1, starting transfers between devices, on_device(): far = lax.ppermute(mate_rows, 'tm', across)  3.56 us
    ppermute x1, waiting for transfers between devices, on_device(): far = lax.ppermute(mate_rows, 'tm', across)  2.66 us
    unnamed x18, local copies, waits for them, and re-layouts  1.39 us
  transfers between devices with their start and end apart: 6, of which 1 were waited for; matrix products, arithmetic and copies ran while one was open for 0% of the time, Pallas kernels for 48%

profile of v6, /device:TPU:0, one launch (start us, length us, event | category | flops | bytes accessed | tf_op | source)
XLA Modules:
  0.0 31.8 jit_solution(12559704624614750784)
XLA Ops:
  0.0 0.5 %collective-permute-start = (bf16[1,384,1024]{2,1,0:T(8,128)(2,1)}, bf16[1,384,1024]{2,1,0:T(8,128)(2,1)S(1)}, u32[]{:S(2)}, u32[]{:S(2)}) collective-permute-start(bf16[1,384,1024]{2,1,0:T(8,128)(2,1)} %frames.1), channel_id=1, source_target_pairs={{0,1},{1,0},{2,3},{3,2},{4,5},{5,4},{6,7},{7,6},{8,9},{9,8},{10,11... | collective-permute-start | bytes 2359304 | tf_op jit(solution)/shard_map/ppermute | solution.py:412
  0.6 1.4 %copy-done.8 = bf16[1,384,1024]{2,1,0:T(8,128)(2,1)S(1)} copy-done((bf16[1,384,1024]{2,1,0:T(8,128)(2,1)S(1)}, bf16[1,384,1024]{2,1,0:T(8,128)(2,1)}, u32[]{:S(2)}) %copy-start.8) | copy-done | bytes 786456
  1.9 0.1 split.1
  2.0 2.5 %collective-permute-start.2 = (bf16[256,1024]{1,0:T(8,128)(2,1)S(1)}, bf16[256,1024]{1,0:T(8,128)(2,1)S(1)}, u32[]{:S(2)}, u32[]{:S(2)}) collective-permute-start(bf16[256,1024]{1,0:T(8,128)(2,1)S(1)} %get-tuple-element.22.late_rows.frames), channel_id=1, source_target_pairs={{0,16},{16,0},{1,17},{17,1},{2,18},{18,2},{3,19},{19,3},{4,20},{20... | collective-permute-start | bytes 1572872 | tf_op jit(solution)/shard_map/ppermute | solution.py:389
  4.5 0.0 collective-permute-done.near.mate
  4.6 3.6 %collective-permute-start.1 = (bf16[256,1024]{1,0:T(8,128)(2,1)S(1)}, bf16[256,1024]{1,0:T(8,128)(2,1)S(1)}, u32[]{:S(2)}, u32[]{:S(2)}) collective-permute-start(bf16[256,1024]{1,0:T(8,128)(2,1)S(1)} %mate.1), channel_id=1, source_target_pairs={{0,2},{2,4},{4,6},{6,8},{8,10},{10,12},{12,14},{3,1},{5,3},{7,5},{... | collective-permute-start | bytes 1572872 | tf_op jit(solution)/shard_map/ppermute | solution.py:414
  8.1 0.0 copy-done.7
  8.2 6.4 %near.1 = (bf16[256,512]{1,0:T(8,128)(2,1)S(1)}, bf16[640,1024]{1,0:T(8,128)(2,1)S(1)}, bf16[128,1024]{1,0:T(8,128)(2,1)S(1)}, bf16[128,512]{1,0:T(8,128)(2,1)S(...) custom-call(s32[2]{0:T(128)S(1)} %copy-done.7, f32[6,50,1024]{2,1,0:T(8,128)S(1)} %bitcast.1, ...), custom_call_target="tpu_custom_call" | custom-call | flops 2000000000 | bytes 6000000 | tf_op jit(solution)/shard_map/near/pallas_call | solution.py:395
  14.6 1.1 %collective-permute-start.3 = (bf16[128,1024]{1,0:T(8,128)(2,1)S(1)}, bf16[128,1024]{1,0:T(8,128)(2,1)S(1)}, u32[]{:S(2)}, u32[]{:S(2)}) collective-permute-start(bf16[128,1024]{1,0:T(8,128)(2,1)S(1)} %get-tuple-element.36.kv), channel_id=1, source_target_pairs={{0,16},{16,0},{1,17},{17,1},{2,18},{18,2},{3,19},{19,3},{4,20},{20... | collective-permute-start | bytes 786440 | tf_op jit(solution)/shard_map/ppermute | solution.py:389
  15.8 1.9 %part.1 = (f32[256,512]{1,0:T(8,128)S(1)}, f32[256,512]{1,0:T(8,128)S(1)}, f32[256,512]{1,0:T(8,128)S(1)}) custom-call(bf16[256,512]{1,0:T(8,128)(2,1)S(1)} %get-tuple-element.24.query.refs_4_, bf16[640,1024]{1,0:T(8,128)(2,1)S(1)} %get-tuple-element.25.kv), custom_call_target="tpu_custom_call" | custom-call | flops 300000000 | bytes 900000 | tf_op jit(solution)/shard_map/part/pallas_call | solution.py:395
  17.7 0.0 collective-permute-done.2.refs_8_.refs_6_.refs_7_
  17.7 2.7 %collective-permute-done.1.refs_1_ = bf16[256,1024]{1,0:T(8,128)(2,1)S(1)} collective-permute-done((bf16[256,1024]{1,0:T(8,128)(2,1)S(1)}, bf16[256,1024]{1,0:T(8,128)(2,1)S(1)}, u32[]{:S(2)}, u32[]{:S(2)}) %collective-permute-start.1) | collective-permute-done | bytes 524320 | tf_op jit(solution)/shard_map/ppermute | solution.py:414
  20.4 1.4 %far_inner.1 = (bf16[128,512]{1,0:T(8,128)(2,1)S(1)}, bf16[128,1024]{1,0:T(8,128)(2,1)S(1)}) custom-call(f32[2,8,1024]{2,1,0:T(8,128)S(1)} %get-tuple-element.23.refs_0_.held.refs_1_, bf16[256,1024]{1,0:T(8,128)(2,1)S(1)} %collective-permute-done.1.refs_1_, bf16[1024,1536]{1,0:T(8,128)(2,1)S(1)} %copy-done.2, f32[2,64]{1,0:T(2,128)S(1)} %copy-done.6, ...), custom_call_target="tpu_custom_call" | custom-call | flops 2000000000 | bytes 6000000 | tf_op jit(solution)/shard_map/far_inner/pallas_call | solution.py:395
  21.8 1.1 %collective-permute-start.4 = (bf16[128,512]{1,0:T(8,128)(2,1)S(1)}, bf16[128,512]{1,0:T(8,128)(2,1)S(1)}, u32[]{:S(2)}, u32[]{:S(2)}) collective-permute-start(bf16[128,512]{1,0:T(8,128)(2,1)S(1)} %get-tuple-element.29.inner), channel_id=1, source_target_pairs={{0,16},{16,0},{1,17},{17,1},{2,18},{18,2},{3,19},{19,3},{4,20},{20... | collective-permute-start | bytes 393224 | tf_op jit(solution)/shard_map/ppermute | solution.py:389
  22.9 1.3 %far_outer.1.outer = bf16[128,512]{1,0:T(8,128)(2,1)S(1)} custom-call(f32[2,8,1024]{2,1,0:T(8,128)S(1)} %get-tuple-element.23.refs_0_.held.refs_1_, bf16[256,1024]{1,0:T(8,128)(2,1)S(1)} %collective-permute-done.1.refs_1_, bf16[1024,1536]{1,0:T(8,128)(2,1)S(1)} %copy-done.2, f32[2,64]{1,0:T(2,128)S(1)} %copy-done.6, ...), custom_call_target="tpu_custom_call" | custom-call | flops 300000000 | bytes 900000 | tf_op jit(solution)/shard_map/far_outer/pallas_call | solution.py:395
  24.3 0.0 copy-start.3
  24.3 1.1 %collective-permute-start.5 = (bf16[128,512]{1,0:T(8,128)(2,1)S(1)}, bf16[128,512]{1,0:T(8,128)(2,1)S(1)}, u32[]{:S(2)}, u32[]{:S(2)}) collective-permute-start(bf16[128,512]{1,0:T(8,128)(2,1)S(1)} %far_outer.1.outer), channel_id=1, source_target_pairs={{0,16},{16,0},{1,17},{17,1},{2,18},{18,2},{3,19},{19,3},{4,20},{20... | collective-permute-start | bytes 393224 | tf_op jit(solution)/shard_map/ppermute | solution.py:389
  25.3 2.0 %own.1 = (bf16[256,1024]{1,0:T(8,128)(2,1)S(1)}, bf16[256,512]{1,0:T(8,128)(2,1)S(1)}, bf16[256,1024]{1,0:T(8,128)(2,1)S(1)}) custom-call(f32[2,8,1024]{2,1,0:T(8,128)S(1)} %get-tuple-element.23.refs_0_.held.refs_1_, bf16[256,1024]{1,0:T(8,128)(2,1)S(1)} %get-tuple-element.22.late_rows.frames, bf16[128,512]{1,0:T(8,128)(2,1)S(1)} %get-tuple-element.29.inner, ...), custom_call_target="tpu_custom_call" | custom-call | flops 300000000 | bytes 900000 | tf_op jit(solution)/shard_map/own/pallas_call | solution.py:395
  27.3 0.0 collective-permute-done.3.refs_0_
  27.3 0.6 %early.1.refs_0_.refs_4_ = bf16[128,1024]{1,0:T(8,128)(2,1)S(1)} custom-call(bf16[256,1024]{1,0:T(8,128)(2,1)S(1)} %get-tuple-element.31._.refs_2_.refs_1_, f32[2,8,1024]{2,1,0:T(8,128)S(1)} %get-tuple-element.23.refs_0_.held.refs_1_, bf16[128,1024]{1,0:T(8,128)(2,1)S(1)} %get-tuple-element.34.first, bf16[128,512]{1,0:T(8,128)(2,1)S(1)} %get-tuple-element.35.query, ...), custom_call_target="tpu_custom_call" | custom-call | flops 300000000 | bytes 900000 | tf_op jit(solution)/shard_map/early/pallas_call | solution.py:395
  28.0 0.0 collective-permute-done.4.refs_5_
  28.0 1.5 %inner.1.refs_5_ = bf16[128,1024]{1,0:T(8,128)(2,1)S(1)} custom-call(bf16[128,1024]{1,0:T(8,128)(2,1)S(1)} %early.1.refs_0_.refs_4_, f32[2,8,1024]{2,1,0:T(8,128)S(1)} %get-tuple-element.23.refs_0_.held.refs_1_, bf16[256,1024]{1,0:T(8,128)(2,1)S(1)} %get-tuple-element.31._.refs_2_.refs_1_, bf16[256,512]{1,0:T(8,128)(2,1)S(1)} %get-tuple-element.32.refs_3_.refs_2_, ...), custom_call_target="tpu_custom_call" | custom-call | flops 600000000 | bytes 1800000 | tf_op jit(solution)/shard_map/inner/pallas_call | solution.py:395
  29.5 0.0 collective-permute-done.5.refs_6_
  29.5 2.3 %outer.1 = bf16[1,384,1024]{2,1,0:T(8,128)(2,1)} custom-call(f32[2,8,1024]{2,1,0:T(8,128)S(1)} %get-tuple-element.23.refs_0_.held.refs_1_, bf16[256,1024]{1,0:T(8,128)(2,1)S(1)} %get-tuple-element.31._.refs_2_.refs_1_, bf16[256,512]{1,0:T(8,128)(2,1)S(1)} %get-tuple-element.32.refs_3_.refs_2_, bf16[256,1024]{1,0:T(8,128)(2,1)S(1)} %get-tuple-element.33.refs_4_.refs_3_, ...), custom_call_target="tpu_custom_call" | custom-call | flops 300000000 | bytes 900000 | tf_op jit(solution)/shard_map/outer/pallas_call | solution.py:395
  (16 shorter events, 0.1 us)
Async XLA Ops:
  0.0 8.1 %copy-start.7 = (s32[2]{0:T(128)S(1)}, s32[2]{0:T(128)}, u32[]{:S(2)}) copy-start(s32[2]{0:T(128)} %timestep.1) | copy-start | bytes 28
  0.0 8.1 %copy-start.4 = (f32[50,6,1024]{2,0,1:T(8,128)S(1)}, f32[50,6,1024]{2,0,1:T(8,128)}, u32[]{:S(2)}) copy-start(f32[50,6,1024]{2,0,1:T(8,128)} %param.11) | copy-start | bytes 3686404
  0.0 8.1 %copy-start.6 = (f32[2,64]{1,0:T(2,128)S(1)}, f32[2,64]{1,0:T(2,128)}, u32[]{:S(2)}) copy-start(f32[2,64]{1,0:T(2,128)} %refs_3_.3) | copy-start | bytes 1540
  0.0 8.2 %copy-start.1 = (bf16[512,1024]{1,0:T(8,128)(2,1)S(1)}, bf16[512,1024]{1,0:T(8,128)(2,1)}, u32[]{:S(2)}) copy-start(bf16[512,1024]{1,0:T(8,128)(2,1)} %refs_8_.3) | copy-start | bytes 3145732
  0.0 8.2 %copy-start.5 = (f32[2,64]{1,0:T(2,128)S(1)}, f32[2,64]{1,0:T(2,128)}, u32[]{:S(2)}) copy-start(f32[2,64]{1,0:T(2,128)} %refs_10_.3) | copy-start | bytes 1540
  0.0 4.5 %collective-permute-start = (bf16[1,384,1024]{2,1,0:T(8,128)(2,1)}, bf16[1,384,1024]{2,1,0:T(8,128)(2,1)S(1)}, u32[]{:S(2)}, u32[]{:S(2)}) collective-permute-start(bf16[1,384,1024]{2,1,0:T(8,128)(2,1)} %frames.1), channel_id=1, source_target_pairs={{0,1},{1,0},{2,3},{3,2},{4,5},{5,4},{6,7},{7,6},{8,9},{9,8},{10,11... | collective-permute-start | bytes 2359304 | tf_op jit(solution)/shard_map/ppermute | solution.py:412
  0.5 1.4 %copy-start.8 = (bf16[1,384,1024]{2,1,0:T(8,128)(2,1)S(1)}, bf16[1,384,1024]{2,1,0:T(8,128)(2,1)}, u32[]{:S(2)}) copy-start(bf16[1,384,1024]{2,1,0:T(8,128)(2,1)} %frames.1) | copy-start | bytes 2359300
  1.9 6.3 %copy-start = (bf16[1024,1536]{1,0:T(8,128)(2,1)S(1)}, bf16[1024,1536]{1,0:T(8,128)(2,1)}, u32[]{:S(2)}) copy-start(bf16[1024,1536]{1,0:T(8,128)(2,1)} %refs_9_.3) | copy-start | bytes 9437188
  1.9 6.3 %copy-start.2 = (bf16[1024,1536]{1,0:T(8,128)(2,1)S(1)}, bf16[1024,1536]{1,0:T(8,128)(2,1)}, u32[]{:S(2)}) copy-start(bf16[1024,1536]{1,0:T(8,128)(2,1)} %refs_2_.3) | copy-start | bytes 9437188
  2.0 15.7 %collective-permute-start.2 = (bf16[256,1024]{1,0:T(8,128)(2,1)S(1)}, bf16[256,1024]{1,0:T(8,128)(2,1)S(1)}, u32[]{:S(2)}, u32[]{:S(2)}) collective-permute-start(bf16[256,1024]{1,0:T(8,128)(2,1)S(1)} %get-tuple-element.22.late_rows.frames), channel_id=1, source_target_pairs={{0,16},{16,0},{1,17},{17,1},{2,18},{18,2},{3,19},{19,3},{4,20},{20... | collective-permute-start | bytes 1572872 | tf_op jit(solution)/shard_map/ppermute | solution.py:389
  4.6 15.8 %collective-permute-start.1 = (bf16[256,1024]{1,0:T(8,128)(2,1)S(1)}, bf16[256,1024]{1,0:T(8,128)(2,1)S(1)}, u32[]{:S(2)}, u32[]{:S(2)}) collective-permute-start(bf16[256,1024]{1,0:T(8,128)(2,1)S(1)} %mate.1), channel_id=1, source_target_pairs={{0,2},{2,4},{4,6},{6,8},{8,10},{10,12},{12,14},{3,1},{5,3},{7,5},{... | collective-permute-start | bytes 1572872 | tf_op jit(solution)/shard_map/ppermute | solution.py:414
  14.6 12.7 %collective-permute-start.3 = (bf16[128,1024]{1,0:T(8,128)(2,1)S(1)}, bf16[128,1024]{1,0:T(8,128)(2,1)S(1)}, u32[]{:S(2)}, u32[]{:S(2)}) collective-permute-start(bf16[128,1024]{1,0:T(8,128)(2,1)S(1)} %get-tuple-element.36.kv), channel_id=1, source_target_pairs={{0,16},{16,0},{1,17},{17,1},{2,18},{18,2},{3,19},{19,3},{4,20},{20... | collective-permute-start | bytes 786440 | tf_op jit(solution)/shard_map/ppermute | solution.py:389
  21.8 6.1 %collective-permute-start.4 = (bf16[128,512]{1,0:T(8,128)(2,1)S(1)}, bf16[128,512]{1,0:T(8,128)(2,1)S(1)}, u32[]{:S(2)}, u32[]{:S(2)}) collective-permute-start(bf16[128,512]{1,0:T(8,128)(2,1)S(1)} %get-tuple-element.29.inner), channel_id=1, source_target_pairs={{0,16},{16,0},{1,17},{17,1},{2,18},{18,2},{3,19},{19,3},{4,20},{20... | collective-permute-start | bytes 393224 | tf_op jit(solution)/shard_map/ppermute | solution.py:389
  24.3 3.1 %copy-start.3 = (bf16[512,1024]{1,0:T(8,128)(2,1)S(1)}, bf16[512,1024]{1,0:T(8,128)(2,1)}, u32[]{:S(2)}) copy-start(bf16[512,1024]{1,0:T(8,128)(2,1)} %refs_11_.1) | copy-start | bytes 3145732
  24.3 5.3 %collective-permute-start.5 = (bf16[128,512]{1,0:T(8,128)(2,1)S(1)}, bf16[128,512]{1,0:T(8,128)(2,1)S(1)}, u32[]{:S(2)}, u32[]{:S(2)}) collective-permute-start(bf16[128,512]{1,0:T(8,128)(2,1)S(1)} %far_outer.1.outer), channel_id=1, source_target_pairs={{0,16},{16,0},{1,17},{17,1},{2,18},{18,2},{3,19},{19,3},{4,20},{20... | collective-permute-start | bytes 393224 | tf_op jit(solution)/shard_map/ppermute | solution.py:389

commit v7 on v6

--- a/solution.py
+++ b/solution.py
@@ -383,6 +383,7 @@
     inside = [(i, i ^ 1) for i in range(count)]
     across = [(i, i + 2) for i in range(0, count - 2, 2)]
     across += [(i + 3, i + 1) for i in range(0, count - 2, 2)]
+    across += [(count - 2, count - 1), (1, 0)]
 
     def to_stems(array):
         return [

time: 32 us -> 30.6 us (0.956)
  starting transfers between devices: 9.9 us -> 7.95 us
  waiting for transfers between devices: 2.67 us -> 3.32 us
    ppermute x4, waiting for transfers between devices: 0.01 us -> 2.19 us  [to_stems(): lax.ppermute(array, 'stem', [(i, (i + k) % stems) for i in range(stems)])]
    ppermute x1, starting transfers between devices: 3.56 us -> 1.55 us  [on_device(): far = lax.ppermute(mate_rows, 'tm', across)]
    ppermute x1, waiting for transfers between devices: 2.66 us -> 1.13 us  [on_device(): far = lax.ppermute(mate_rows, 'tm', across)]
  transfers between devices with their start and end apart: 6 -> 6, of which waited for: 1 -> 4; matrix products, arithmetic and copies ran while one was open for 0% -> 0% of each run, Pallas kernels for 48% -> 51%
where the time goes in v7:
time: 30.6 us; the launch traced here: 30.5 us
  Pallas kernels  17.7 us (58%)
  starting transfers between devices  7.95 us (26%)
  waiting for transfers between devices  3.32 us (11%)
  local copies, waits for them, and re-layouts  1.39 us (5%)
    pallas_call x10, Pallas kernels, call(): pl.pallas_call(kernel, out_shape=outs, in_specs=in_specs or [VMEM] * len(...  17.7 us
    ppermute x4, starting transfers between devices, to_stems(): lax.ppermute(array, 'stem', [(i, (i + k) % stems) for i in range(stems)])  5.87 us
    ppermute x4, waiting for transfers between devices, to_stems(): lax.ppermute(array, 'stem', [(i, (i + k) % stems) for i in range(stems)])  2.19 us
    ppermute x1, starting transfers between devices, on_device(): far = lax.ppermute(mate_rows, 'tm', across)  1.55 us
    unnamed x18, local copies, waits for them, and re-layouts  1.39 us
    ppermute x1, waiting for transfers between devices, on_device(): far = lax.ppermute(mate_rows, 'tm', across)  1.13 us
  transfers between devices with their start and end apart: 6, of which 4 were waited for; matrix products, arithmetic and copies ran while one was open for 0% of the time, Pallas kernels for 51%

profile of v7, /device:TPU:0, one launch (start us, length us, event | category | flops | bytes accessed | tf_op | source)
XLA Modules:
  0.0 30.5 jit_solution(4618870656397066043)
XLA Ops:
  0.0 0.5 %collective-permute-start = (bf16[1,384,1024]{2,1,0:T(8,128)(2,1)}, bf16[1,384,1024]{2,1,0:T(8,128)(2,1)S(1)}, u32[]{:S(2)}, u32[]{:S(2)}) collective-permute-start(bf16[1,384,1024]{2,1,0:T(8,128)(2,1)} %frames.1), channel_id=1, source_target_pairs={{0,1},{1,0},{2,3},{3,2},{4,5},{5,4},{6,7},{7,6},{8,9},{9,8},{10,11... | collective-permute-start | bytes 2359304 | tf_op jit(solution)/shard_map/ppermute | solution.py:413
  0.6 1.4 %copy-done.8 = bf16[1,384,1024]{2,1,0:T(8,128)(2,1)S(1)} copy-done((bf16[1,384,1024]{2,1,0:T(8,128)(2,1)S(1)}, bf16[1,384,1024]{2,1,0:T(8,128)(2,1)}, u32[]{:S(2)}) %copy-start.8) | copy-done | bytes 786456
  1.9 0.1 split.1
  2.0 2.5 %collective-permute-start.2 = (bf16[256,1024]{1,0:T(8,128)(2,1)S(1)}, bf16[256,1024]{1,0:T(8,128)(2,1)S(1)}, u32[]{:S(2)}, u32[]{:S(2)}) collective-permute-start(bf16[256,1024]{1,0:T(8,128)(2,1)S(1)} %get-tuple-element.22.late_rows.frames), channel_id=1, source_target_pairs={{0,16},{16,0},{1,17},{17,1},{2,18},{18,2},{3,19},{19,3},{4,20},{20... | collective-permute-start | bytes 1572872 | tf_op jit(solution)/shard_map/ppermute | solution.py:390
  4.5 0.0 collective-permute-done.near.mate
  4.6 1.5 %collective-permute-start.1 = (bf16[256,1024]{1,0:T(8,128)(2,1)S(1)}, bf16[256,1024]{1,0:T(8,128)(2,1)S(1)}, u32[]{:S(2)}, u32[]{:S(2)}) collective-permute-start(bf16[256,1024]{1,0:T(8,128)(2,1)S(1)} %mate.1), channel_id=1, source_target_pairs={{0,2},{2,4},{4,6},{6,8},{8,10},{10,12},{12,14},{3,1},{5,3},{7,5},{... | collective-permute-start | bytes 1572872 | tf_op jit(solution)/shard_map/ppermute | solution.py:415
  6.1 0.0 copy-done.7
  6.2 6.5 %near.1 = (bf16[256,512]{1,0:T(8,128)(2,1)S(1)}, bf16[640,1024]{1,0:T(8,128)(2,1)S(1)}, bf16[128,1024]{1,0:T(8,128)(2,1)S(1)}, bf16[128,512]{1,0:T(8,128)(2,1)S(...) custom-call(s32[2]{0:T(128)S(1)} %copy-done.7, f32[6,50,1024]{2,1,0:T(8,128)S(1)} %bitcast.1, ...), custom_call_target="tpu_custom_call" | custom-call | flops 2000000000 | bytes 6000000 | tf_op jit(solution)/shard_map/near/pallas_call | solution.py:396
  12.6 1.2 %collective-permute-start.3 = (bf16[128,1024]{1,0:T(8,128)(2,1)S(1)}, bf16[128,1024]{1,0:T(8,128)(2,1)S(1)}, u32[]{:S(2)}, u32[]{:S(2)}) collective-permute-start(bf16[128,1024]{1,0:T(8,128)(2,1)S(1)} %get-tuple-element.36.kv), channel_id=1, source_target_pairs={{0,16},{16,0},{1,17},{17,1},{2,18},{18,2},{3,19},{19,3},{4,20},{20... | collective-permute-start | bytes 786440 | tf_op jit(solution)/shard_map/ppermute | solution.py:390
  13.8 1.9 %part.1 = (f32[256,512]{1,0:T(8,128)S(1)}, f32[256,512]{1,0:T(8,128)S(1)}, f32[256,512]{1,0:T(8,128)S(1)}) custom-call(bf16[256,512]{1,0:T(8,128)(2,1)S(1)} %get-tuple-element.24.query.refs_4_, bf16[640,1024]{1,0:T(8,128)(2,1)S(1)} %get-tuple-element.25.kv), custom_call_target="tpu_custom_call" | custom-call | flops 300000000 | bytes 900000 | tf_op jit(solution)/shard_map/part/pallas_call | solution.py:396
  15.8 1.5 %collective-permute-done.2.refs_8_.refs_6_.refs_7_ = bf16[256,1024]{1,0:T(8,128)(2,1)S(1)} collective-permute-done((bf16[256,1024]{1,0:T(8,128)(2,1)S(1)}, bf16[256,1024]{1,0:T(8,128)(2,1)S(1)}, u32[]{:S(2)}, u32[]{:S(2)}) %collective-permute-start.2) | collective-permute-done | bytes 524320 | tf_op jit(solution)/shard_map/ppermute | solution.py:390
  17.3 1.1 %collective-permute-done.1.refs_1_ = bf16[256,1024]{1,0:T(8,128)(2,1)S(1)} collective-permute-done((bf16[256,1024]{1,0:T(8,128)(2,1)S(1)}, bf16[256,1024]{1,0:T(8,128)(2,1)S(1)}, u32[]{:S(2)}, u32[]{:S(2)}) %collective-permute-start.1) | collective-permute-done | bytes 524320 | tf_op jit(solution)/shard_map/ppermute | solution.py:415
  18.4 1.4 %far_inner.1 = (bf16[128,512]{1,0:T(8,128)(2,1)S(1)}, bf16[128,1024]{1,0:T(8,128)(2,1)S(1)}) custom-call(f32[2,8,1024]{2,1,0:T(8,128)S(1)} %get-tuple-element.23.refs_0_.held.refs_1_, bf16[256,1024]{1,0:T(8,128)(2,1)S(1)} %collective-permute-done.1.refs_1_, bf16[1024,1536]{1,0:T(8,128)(2,1)S(1)} %copy-done.2, f32[2,64]{1,0:T(2,128)S(1)} %copy-done.6, ...), custom_call_target="tpu_custom_call" | custom-call | flops 2000000000 | bytes 6000000 | tf_op jit(solution)/shard_map/far_inner/pallas_call | solution.py:396
  19.9 1.1 %collective-permute-start.4 = (bf16[128,512]{1,0:T(8,128)(2,1)S(1)}, bf16[128,512]{1,0:T(8,128)(2,1)S(1)}, u32[]{:S(2)}, u32[]{:S(2)}) collective-permute-start(bf16[128,512]{1,0:T(8,128)(2,1)S(1)} %get-tuple-element.29.inner), channel_id=1, source_target_pairs={{0,16},{16,0},{1,17},{17,1},{2,18},{18,2},{3,19},{19,3},{4,20},{20... | collective-permute-start | bytes 393224 | tf_op jit(solution)/shard_map/ppermute | solution.py:390
  21.0 1.3 %far_outer.1.outer = bf16[128,512]{1,0:T(8,128)(2,1)S(1)} custom-call(f32[2,8,1024]{2,1,0:T(8,128)S(1)} %get-tuple-element.23.refs_0_.held.refs_1_, bf16[256,1024]{1,0:T(8,128)(2,1)S(1)} %collective-permute-done.1.refs_1_, bf16[1024,1536]{1,0:T(8,128)(2,1)S(1)} %copy-done.2, f32[2,64]{1,0:T(2,128)S(1)} %copy-done.6, ...), custom_call_target="tpu_custom_call" | custom-call | flops 300000000 | bytes 900000 | tf_op jit(solution)/shard_map/far_outer/pallas_call | solution.py:396
  22.3 0.0 copy-start.3
  22.3 1.1 %collective-permute-start.5 = (bf16[128,512]{1,0:T(8,128)(2,1)S(1)}, bf16[128,512]{1,0:T(8,128)(2,1)S(1)}, u32[]{:S(2)}, u32[]{:S(2)}) collective-permute-start(bf16[128,512]{1,0:T(8,128)(2,1)S(1)} %far_outer.1.outer), channel_id=1, source_target_pairs={{0,16},{16,0},{1,17},{17,1},{2,18},{18,2},{3,19},{19,3},{4,20},{20... | collective-permute-start | bytes 393224 | tf_op jit(solution)/shard_map/ppermute | solution.py:390
  23.4 2.0 %own.1 = (bf16[256,1024]{1,0:T(8,128)(2,1)S(1)}, bf16[256,512]{1,0:T(8,128)(2,1)S(1)}, bf16[256,1024]{1,0:T(8,128)(2,1)S(1)}) custom-call(f32[2,8,1024]{2,1,0:T(8,128)S(1)} %get-tuple-element.23.refs_0_.held.refs_1_, bf16[256,1024]{1,0:T(8,128)(2,1)S(1)} %get-tuple-element.22.late_rows.frames, bf16[128,512]{1,0:T(8,128)(2,1)S(1)} %get-tuple-element.29.inner, ...), custom_call_target="tpu_custom_call" | custom-call | flops 300000000 | bytes 900000 | tf_op jit(solution)/shard_map/own/pallas_call | solution.py:396
  25.4 0.0 collective-permute-done.3.refs_0_
  25.4 0.6 %early.1.refs_0_.refs_4_ = bf16[128,1024]{1,0:T(8,128)(2,1)S(1)} custom-call(bf16[256,1024]{1,0:T(8,128)(2,1)S(1)} %get-tuple-element.31._.refs_2_.refs_1_, f32[2,8,1024]{2,1,0:T(8,128)S(1)} %get-tuple-element.23.refs_0_.held.refs_1_, bf16[128,1024]{1,0:T(8,128)(2,1)S(1)} %get-tuple-element.34.first, bf16[128,512]{1,0:T(8,128)(2,1)S(1)} %get-tuple-element.35.query, ...), custom_call_target="tpu_custom_call" | custom-call | flops 300000000 | bytes 900000 | tf_op jit(solution)/shard_map/early/pallas_call | solution.py:396
  26.0 0.4 %collective-permute-done.4.refs_5_ = bf16[128,512]{1,0:T(8,128)(2,1)S(1)} collective-permute-done((bf16[128,512]{1,0:T(8,128)(2,1)S(1)}, bf16[128,512]{1,0:T(8,128)(2,1)S(1)}, u32[]{:S(2)}, u32[]{:S(2)}) %collective-permute-start.4) | collective-permute-done | bytes 131104 | tf_op jit(solution)/shard_map/ppermute | solution.py:390
  26.4 1.5 %inner.1.refs_5_ = bf16[128,1024]{1,0:T(8,128)(2,1)S(1)} custom-call(bf16[128,1024]{1,0:T(8,128)(2,1)S(1)} %early.1.refs_0_.refs_4_, f32[2,8,1024]{2,1,0:T(8,128)S(1)} %get-tuple-element.23.refs_0_.held.refs_1_, bf16[256,1024]{1,0:T(8,128)(2,1)S(1)} %get-tuple-element.31._.refs_2_.refs_1_, bf16[256,512]{1,0:T(8,128)(2,1)S(1)} %get-tuple-element.32.refs_3_.refs_2_, ...), custom_call_target="tpu_custom_call" | custom-call | flops 600000000 | bytes 1800000 | tf_op jit(solution)/shard_map/inner/pallas_call | solution.py:396
  27.9 0.3 collective-permute-done.5.refs_6_
  28.2 2.3 %outer.1 = bf16[1,384,1024]{2,1,0:T(8,128)(2,1)} custom-call(f32[2,8,1024]{2,1,0:T(8,128)S(1)} %get-tuple-element.23.refs_0_.held.refs_1_, bf16[256,1024]{1,0:T(8,128)(2,1)S(1)} %get-tuple-element.31._.refs_2_.refs_1_, bf16[256,512]{1,0:T(8,128)(2,1)S(1)} %get-tuple-element.32.refs_3_.refs_2_, bf16[256,1024]{1,0:T(8,128)(2,1)S(1)} %get-tuple-element.33.refs_4_.refs_3_, ...), custom_call_target="tpu_custom_call" | custom-call | flops 300000000 | bytes 900000 | tf_op jit(solution)/shard_map/outer/pallas_call | solution.py:396
  (16 shorter events, 0.1 us)
Async XLA Ops:
  0.0 6.1 %copy-start.7 = (s32[2]{0:T(128)S(1)}, s32[2]{0:T(128)}, u32[]{:S(2)}) copy-start(s32[2]{0:T(128)} %timestep.1) | copy-start | bytes 28
  0.0 6.1 %copy-start.4 = (f32[50,6,1024]{2,0,1:T(8,128)S(1)}, f32[50,6,1024]{2,0,1:T(8,128)}, u32[]{:S(2)}) copy-start(f32[50,6,1024]{2,0,1:T(8,128)} %param.11) | copy-start | bytes 3686404
  0.0 6.1 %copy-start.6 = (f32[2,64]{1,0:T(2,128)S(1)}, f32[2,64]{1,0:T(2,128)}, u32[]{:S(2)}) copy-start(f32[2,64]{1,0:T(2,128)} %refs_3_.3) | copy-start | bytes 1540
  0.0 6.1 %copy-start.1 = (bf16[512,1024]{1,0:T(8,128)(2,1)S(1)}, bf16[512,1024]{1,0:T(8,128)(2,1)}, u32[]{:S(2)}) copy-start(bf16[512,1024]{1,0:T(8,128)(2,1)} %refs_8_.3) | copy-start | bytes 3145732
  0.0 6.1 %copy-start.5 = (f32[2,64]{1,0:T(2,128)S(1)}, f32[2,64]{1,0:T(2,128)}, u32[]{:S(2)}) copy-start(f32[2,64]{1,0:T(2,128)} %refs_10_.3) | copy-start | bytes 1540
  0.0 4.5 %collective-permute-start = (bf16[1,384,1024]{2,1,0:T(8,128)(2,1)}, bf16[1,384,1024]{2,1,0:T(8,128)(2,1)S(1)}, u32[]{:S(2)}, u32[]{:S(2)}) collective-permute-start(bf16[1,384,1024]{2,1,0:T(8,128)(2,1)} %frames.1), channel_id=1, source_target_pairs={{0,1},{1,0},{2,3},{3,2},{4,5},{5,4},{6,7},{7,6},{8,9},{9,8},{10,11... | collective-permute-start | bytes 2359304 | tf_op jit(solution)/shard_map/ppermute | solution.py:413
  0.5 1.4 %copy-start.8 = (bf16[1,384,1024]{2,1,0:T(8,128)(2,1)S(1)}, bf16[1,384,1024]{2,1,0:T(8,128)(2,1)}, u32[]{:S(2)}) copy-start(bf16[1,384,1024]{2,1,0:T(8,128)(2,1)} %frames.1) | copy-start | bytes 2359300
  1.9 4.2 %copy-start = (bf16[1024,1536]{1,0:T(8,128)(2,1)S(1)}, bf16[1024,1536]{1,0:T(8,128)(2,1)}, u32[]{:S(2)}) copy-start(bf16[1024,1536]{1,0:T(8,128)(2,1)} %refs_9_.3) | copy-start | bytes 9437188
  1.9 4.2 %copy-start.2 = (bf16[1024,1536]{1,0:T(8,128)(2,1)S(1)}, bf16[1024,1536]{1,0:T(8,128)(2,1)}, u32[]{:S(2)}) copy-start(bf16[1024,1536]{1,0:T(8,128)(2,1)} %refs_2_.3) | copy-start | bytes 9437188
  2.0 15.3 %collective-permute-start.2 = (bf16[256,1024]{1,0:T(8,128)(2,1)S(1)}, bf16[256,1024]{1,0:T(8,128)(2,1)S(1)}, u32[]{:S(2)}, u32[]{:S(2)}) collective-permute-start(bf16[256,1024]{1,0:T(8,128)(2,1)S(1)} %get-tuple-element.22.late_rows.frames), channel_id=1, source_target_pairs={{0,16},{16,0},{1,17},{17,1},{2,18},{18,2},{3,19},{19,3},{4,20},{20... | collective-permute-start | bytes 1572872 | tf_op jit(solution)/shard_map/ppermute | solution.py:390
  4.6 13.9 %collective-permute-start.1 = (bf16[256,1024]{1,0:T(8,128)(2,1)S(1)}, bf16[256,1024]{1,0:T(8,128)(2,1)S(1)}, u32[]{:S(2)}, u32[]{:S(2)}) collective-permute-start(bf16[256,1024]{1,0:T(8,128)(2,1)S(1)} %mate.1), channel_id=1, source_target_pairs={{0,2},{2,4},{4,6},{6,8},{8,10},{10,12},{12,14},{3,1},{5,3},{7,5},{... | collective-permute-start | bytes 1572872 | tf_op jit(solution)/shard_map/ppermute | solution.py:415
  12.6 12.7 %collective-permute-start.3 = (bf16[128,1024]{1,0:T(8,128)(2,1)S(1)}, bf16[128,1024]{1,0:T(8,128)(2,1)S(1)}, u32[]{:S(2)}, u32[]{:S(2)}) collective-permute-start(bf16[128,1024]{1,0:T(8,128)(2,1)S(1)} %get-tuple-element.36.kv), channel_id=1, source_target_pairs={{0,16},{16,0},{1,17},{17,1},{2,18},{18,2},{3,19},{19,3},{4,20},{20... | collective-permute-start | bytes 786440 | tf_op jit(solution)/shard_map/ppermute | solution.py:390
  19.9 6.5 %collective-permute-start.4 = (bf16[128,512]{1,0:T(8,128)(2,1)S(1)}, bf16[128,512]{1,0:T(8,128)(2,1)S(1)}, u32[]{:S(2)}, u32[]{:S(2)}) collective-permute-start(bf16[128,512]{1,0:T(8,128)(2,1)S(1)} %get-tuple-element.29.inner), channel_id=1, source_target_pairs={{0,16},{16,0},{1,17},{17,1},{2,18},{18,2},{3,19},{19,3},{4,20},{20... | collective-permute-start | bytes 393224 | tf_op jit(solution)/shard_map/ppermute | solution.py:390
  22.3 3.1 %copy-start.3 = (bf16[512,1024]{1,0:T(8,128)(2,1)S(1)}, bf16[512,1024]{1,0:T(8,128)(2,1)}, u32[]{:S(2)}) copy-start(bf16[512,1024]{1,0:T(8,128)(2,1)} %refs_11_.1) | copy-start | bytes 3145732
  22.3 5.9 %collective-permute-start.5 = (bf16[128,512]{1,0:T(8,128)(2,1)S(1)}, bf16[128,512]{1,0:T(8,128)(2,1)S(1)}, u32[]{:S(2)}, u32[]{:S(2)}) collective-permute-start(bf16[128,512]{1,0:T(8,128)(2,1)S(1)} %far_outer.1.outer), channel_id=1, source_target_pairs={{0,16},{16,0},{1,17},{17,1},{2,18},{18,2},{3,19},{19,3},{4,20},{20... | collective-permute-start | bytes 393224 | tf_op jit(solution)/shard_map/ppermute | solution.py:390

commit v8 on v7

--- a/solution.py
+++ b/solution.py
@@ -152,10 +152,10 @@
         copy.wait()
 
 
-def mate_kernel(mate, rows):
+def mate_kernel(mate, outer_rows, inner_rows):
     _, _, inner, outer = places(mate.shape[1])
-    rows[:BLOCK] = mate[0, pl.ds(outer, BLOCK)]
-    rows[BLOCK:] = mate[0, inner : inner + BLOCK]
+    outer_rows[...] = mate[0, pl.ds(outer, BLOCK)]
+    inner_rows[...] = mate[0, inner : inner + BLOCK]
 
 
 def near_kernel(
@@ -264,15 +264,15 @@
 
 
 def far_inner_kernel(rows, held, far, qkv_self, gains, query, *refs):
-    parts, (attended, kv) = refs[:3], refs[-2:]
-    keys, values = far_keys(far[:BLOCK], held, qkv_self, gains)
+    *parts, attended, kv = refs
+    keys, values = far_keys(far[...], held, qkv_self, gains)
     far_attend(1, far_bias(rows, rows - HALF, False), query, keys, values, *parts, attended)
     kv[:, :HW], kv[:, HW:] = keys, values
 
 
 def far_outer_kernel(rows, held, far, qkv_self, gains, query, *refs):
     *parts, kv, attended = refs
-    keys, values = far_keys(far[BLOCK:], held, qkv_self, gains)
+    keys, values = far_keys(far[...], held, qkv_self, gains)
     keys = jnp.concatenate([kv[:, :HW], keys], axis=0)
     values = jnp.concatenate([kv[:, HW:], values], axis=0)
     start = lax.rem(lax.axis_index("tm"), 2) * HALF
@@ -406,53 +406,53 @@
 
     half = shape(BLOCK, D)
     late_rows, early_rows = call(
-        split_kernel, "split", 6, (shape(HALF, D), half), frames,
+        split_kernel, "split", 4, (shape(HALF, D), half), frames,
         scratch=[pltpu.SemaphoreType.DMA((3,))], in_specs=[ANY], out_specs=(ANY, ANY),
     )
     their_frames = to_stems(late_rows)
     near = lax.ppermute(frames, "tm", inside)
-    mate_rows = call(mate_kernel, "mate", 0.1, shape(HALF, D), near)
-    far = lax.ppermute(mate_rows, "tm", across)
+    mate_outer, mate_inner = call(mate_kernel, "mate", 0.1, (half, half), near)
+    far = lax.ppermute(mate_outer, "tm", across)
+    farther = lax.ppermute(mate_inner, "tm", across)
 
     late, block, part = shape(HALF, HW), shape(BLOCK, HW), shape(HALF, HW, dtype=F32)
     query, kv, first_early, q_early, kv_early, held = call(
-        near_kernel, "near", 2,
+        near_kernel, "near", 0.12,
         (late, shape(rows + HALF, 2 * HW), half, block, half, shape(stems, 8, D, dtype=F32)),
         timestep, modulation, early_rows, late_rows, near, qkv_self, qk_gain_self, out_self, qkv_cross, qk_gain_cross,
         in_specs=[SMEM] + [VMEM] * 9,
     )
     others_early = to_stems(kv_early)
-    parts = call(part_kernel, "part", 0.3, (part, part, part), query, kv)
+    parts = call(part_kernel, "part", 0.04, (part, part, part), query, kv)
 
     self_weights = (qkv_self, qk_gain_self)
     att_inner, far_kv = call(
-        lambda *refs: far_inner_kernel(rows, *refs), "far_inner", 2, (block, half),
-        held, far, *self_weights, query, *parts, *their_frames,
-        in_specs=[VMEM] * 8 + [ANY] * (stems - 1),
+        lambda *refs: far_inner_kernel(rows, *refs), "far_inner", 0.04, (block, half),
+        held, far, *self_weights, query, *parts,
     )
     others_inner = to_stems(att_inner)
     att_outer = call(
-        lambda *refs: far_outer_kernel(rows, *refs), "far_outer", 0.3, block,
-        held, far, *self_weights, query, *parts, far_kv,
+        lambda *refs: far_outer_kernel(rows, *refs), "far_outer", 0.006, block,
+        held, farther, *self_weights, query, *parts, far_kv,
     )
     others_outer = to_stems(att_outer)
 
     weights = (out_self, qkv_cross, qk_gain_cross)
     own = call(
-        own_kernel, "own", 0.3, (shape(HALF, D), late, shape(HALF, D)),
+        own_kernel, "own", 0.02, (shape(HALF, D), late, shape(HALF, D)),
         held, late_rows, att_inner, att_outer, *weights,
     )
     early_out = call(
-        early_kernel, "early", 0.3, half, own[0], held, first_early, q_early, kv_early, out_cross, *others_early,
+        early_kernel, "early", 0.012, half, own[0], held, first_early, q_early, kv_early, out_cross, *others_early,
         in_specs=[ANY] + [VMEM] * (4 + stems),
     )
     inner_out = call(
-        lambda *refs: inner_kernel(stems, *refs), "inner", 0.6, half,
+        lambda *refs: inner_kernel(stems, *refs), "inner", 0.04, half,
         early_out, held, *own, *others_inner, *their_frames, *weights, out_cross,
         in_specs=[ANY] + [VMEM] * (6 + 2 * stems),
     )
     return call(
-        lambda *refs: outer_kernel(stems, *refs), "outer", 0.3, shape(1, rows, D),
+        lambda *refs: outer_kernel(stems, *refs), "outer", 2, shape(1, rows, D),
         held, *own, early_out, inner_out, *others_outer, *their_frames, *weights, out_cross,
         scratch=[pltpu.VMEM((BLOCK, D), BF16), pltpu.SemaphoreType.DMA((3,))], out_specs=ANY,
     )

time: 30.6 us -> 31 us (1.013)
  starting transfers between devices: 7.95 us -> 9.35 us
  waiting for transfers between devices: 3.32 us -> 2.48 us
    ppermute x1 -> x2, starting transfers between devices: 1.55 us -> 3.1 us  [the longest x1 1.55 us: on_device(): far = lax.ppermute(mate_outer, 'tm', across)]
    ppermute x1 -> x2, waiting for transfers between devices: 1.13 us -> 0.01 us  [the longest x1 0.01 us: on_device(): far = lax.ppermute(mate_outer, 'tm', across)]
  transfers between devices with their start and end apart: 6 -> 7, of which waited for: 4 -> 2; matrix products, arithmetic and copies ran while one was open for 0% -> 0% of each run, Pallas kernels for 51% -> 49%
where the time goes in v8:
time: 31 us; the launch traced here: 30.8 us
  Pallas kernels  17.4 us (56%)
  starting transfers between devices  9.35 us (30%)
  waiting for transfers between devices  2.48 us (8%)
  local copies, waits for them, and re-layouts  1.45 us (5%)
    pallas_call x10, Pallas kernels, call(): pl.pallas_call(kernel, out_shape=outs, in_specs=in_specs or [VMEM] * len(...  17.4 us
    ppermute x4, starting transfers between devices, to_stems(): lax.ppermute(array, 'stem', [(i, (i + k) % stems) for i in range(stems)])  5.72 us
    ppermute x4, waiting for transfers between devices, to_stems(): lax.ppermute(array, 'stem', [(i, (i + k) % stems) for i in range(stems)])  2.47 us
    ppermute x1, starting transfers between devices, on_device(): far = lax.ppermute(mate_outer, 'tm', across)  1.55 us
    ppermute x1, starting transfers between devices, on_device(): farther = lax.ppermute(mate_inner, 'tm', across)  1.55 us
    unnamed x18, local copies, waits for them, and re-layouts  1.45 us
  transfers between devices with their start and end apart: 7, of which 2 were waited for; matrix products, arithmetic and copies ran while one was open for 0% of the time, Pallas kernels for 49%

profile of v8, /device:TPU:0, one launch (start us, length us, event | category | flops | bytes accessed | tf_op | source)
XLA Modules:
  0.0 30.8 jit_solution(13713975918688770115)
XLA Ops:
  0.0 0.5 %collective-permute-start = (bf16[1,384,1024]{2,1,0:T(8,128)(2,1)}, bf16[1,384,1024]{2,1,0:T(8,128)(2,1)S(1)}, u32[]{:S(2)}, u32[]{:S(2)}) collective-permute-start(bf16[1,384,1024]{2,1,0:T(8,128)(2,1)} %frames.1), channel_id=1, source_target_pairs={{0,1},{1,0},{2,3},{3,2},{4,5},{5,4},{6,7},{7,6},{8,9},{9,8},{10,11... | collective-permute-start | bytes 2359304 | tf_op jit(solution)/shard_map/ppermute | solution.py:413
  0.6 1.4 %copy-done.8 = bf16[1,384,1024]{2,1,0:T(8,128)(2,1)S(1)} copy-done((bf16[1,384,1024]{2,1,0:T(8,128)(2,1)S(1)}, bf16[1,384,1024]{2,1,0:T(8,128)(2,1)}, u32[]{:S(2)}) %copy-start.8) | copy-done | bytes 786456
  2.0 0.1 split.1
  2.1 2.5 %collective-permute-start.5 = (bf16[256,1024]{1,0:T(8,128)(2,1)S(1)}, bf16[256,1024]{1,0:T(8,128)(2,1)S(1)}, u32[]{:S(2)}, u32[]{:S(2)}) collective-permute-start(bf16[256,1024]{1,0:T(8,128)(2,1)S(1)} %get-tuple-element.24.late_rows.frames), channel_id=1, source_target_pairs={{0,16},{16,0},{1,17},{17,1},{2,18},{18,2},{3,19},{19,3},{4,20},{20... | collective-permute-start | bytes 1572872 | tf_op jit(solution)/shard_map/ppermute | solution.py:390
  4.5 0.0 collective-permute-done.near.mate
  4.6 1.5 %collective-permute-start.1 = (bf16[128,1024]{1,0:T(8,128)(2,1)S(1)}, bf16[128,1024]{1,0:T(8,128)(2,1)S(1)}, u32[]{:S(2)}, u32[]{:S(2)}) collective-permute-start(bf16[128,1024]{1,0:T(8,128)(2,1)S(1)} %get-tuple-element.26), channel_id=1, source_target_pairs={{0,2},{2,4},{4,6},{6,8},{8,10},{10,12},{12,14},{3,1},{5,3},{7,5},{... | collective-permute-start | bytes 786440 | tf_op jit(solution)/shard_map/ppermute | solution.py:415
  6.1 1.5 %collective-permute-start.2 = (bf16[128,1024]{1,0:T(8,128)(2,1)S(1)}, bf16[128,1024]{1,0:T(8,128)(2,1)S(1)}, u32[]{:S(2)}, u32[]{:S(2)}) collective-permute-start(bf16[128,1024]{1,0:T(8,128)(2,1)S(1)} %get-tuple-element.33), channel_id=1, source_target_pairs={{0,2},{2,4},{4,6},{6,8},{8,10},{10,12},{12,14},{3,1},{5,3},{7,5},{... | collective-permute-start | bytes 786440 | tf_op jit(solution)/shard_map/ppermute | solution.py:416
  7.7 6.2 %near.1 = (bf16[256,512]{1,0:T(8,128)(2,1)S(1)}, bf16[640,1024]{1,0:T(8,128)(2,1)S(1)}, bf16[128,1024]{1,0:T(8,128)(2,1)S(1)}, bf16[128,512]{1,0:T(8,128)(2,1)S(...) custom-call(s32[2]{0:T(128)S(1)} %copy-done.7, f32[6,50,1024]{2,1,0:T(8,128)S(1)} %bitcast.1, ...), custom_call_target="tpu_custom_call" | custom-call | flops 120000000 | bytes 360000 | tf_op jit(solution)/shard_map/near/pallas_call | solution.py:396
  13.9 1.1 %collective-permute-start.3 = (bf16[128,1024]{1,0:T(8,128)(2,1)S(1)}, bf16[128,1024]{1,0:T(8,128)(2,1)S(1)}, u32[]{:S(2)}, u32[]{:S(2)}) collective-permute-start(bf16[128,1024]{1,0:T(8,128)(2,1)S(1)} %get-tuple-element.40.kv), channel_id=1, source_target_pairs={{0,16},{16,0},{1,17},{17,1},{2,18},{18,2},{3,19},{19,3},{4,20},{20... | collective-permute-start | bytes 786440 | tf_op jit(solution)/shard_map/ppermute | solution.py:390
  15.0 1.9 %part.1 = (f32[256,512]{1,0:T(8,128)S(1)}, f32[256,512]{1,0:T(8,128)S(1)}, f32[256,512]{1,0:T(8,128)S(1)}) custom-call(bf16[256,512]{1,0:T(8,128)(2,1)S(1)} %get-tuple-element.27.query.refs_4_, bf16[640,1024]{1,0:T(8,128)(2,1)S(1)} %get-tuple-element.28.kv), custom_call_target="tpu_custom_call" | custom-call | flops 40000000 | bytes 120000 | tf_op jit(solution)/shard_map/part/pallas_call | solution.py:396
  17.0 0.0 collective-permute-done.1.refs_1_
  17.0 1.4 %far_inner.1 = (bf16[128,512]{1,0:T(8,128)(2,1)S(1)}, bf16[128,1024]{1,0:T(8,128)(2,1)S(1)}) custom-call(f32[2,8,1024]{2,1,0:T(8,128)S(1)} %get-tuple-element.25.refs_0_.held.refs_1_, bf16[128,1024]{1,0:T(8,128)(2,1)S(1)} %collective-permute-done.1.refs_1_, bf16[1024,1536]{1,0:T(8,128)(2,1)S(1)} %copy-done.1, f32[2,64]{1,0:T(2,128)S(1)} %copy-done.6, ...), custom_call_target="tpu_custom_call" | custom-call | flops 40000000 | bytes 120000 | tf_op jit(solution)/shard_map/far_inner/pallas_call | solution.py:396
  18.4 1.0 %collective-permute-start.4 = (bf16[128,512]{1,0:T(8,128)(2,1)S(1)}, bf16[128,512]{1,0:T(8,128)(2,1)S(1)}, u32[]{:S(2)}, u32[]{:S(2)}) collective-permute-start(bf16[128,512]{1,0:T(8,128)(2,1)S(1)} %get-tuple-element.32.inner), channel_id=1, source_target_pairs={{0,16},{16,0},{1,17},{17,1},{2,18},{18,2},{3,19},{19,3},{4,20},{20... | collective-permute-start | bytes 393224 | tf_op jit(solution)/shard_map/ppermute | solution.py:390
  19.4 1.3 %far_outer.1.outer = bf16[128,512]{1,0:T(8,128)(2,1)S(1)} custom-call(f32[2,8,1024]{2,1,0:T(8,128)S(1)} %get-tuple-element.25.refs_0_.held.refs_1_, bf16[128,1024]{1,0:T(8,128)(2,1)S(1)} %collective-permute-done.2.refs_1_, bf16[1024,1536]{1,0:T(8,128)(2,1)S(1)} %copy-done.1, f32[2,64]{1,0:T(2,128)S(1)} %copy-done.6, ...), custom_call_target="tpu_custom_call" | custom-call | flops 6000000 | bytes 18000 | tf_op jit(solution)/shard_map/far_outer/pallas_call | solution.py:396
  20.7 0.0 copy-start.3
  20.8 1.1 %collective-permute-start.6 = (bf16[128,512]{1,0:T(8,128)(2,1)S(1)}, bf16[128,512]{1,0:T(8,128)(2,1)S(1)}, u32[]{:S(2)}, u32[]{:S(2)}) collective-permute-start(bf16[128,512]{1,0:T(8,128)(2,1)S(1)} %far_outer.1.outer), channel_id=1, source_target_pairs={{0,16},{16,0},{1,17},{17,1},{2,18},{18,2},{3,19},{19,3},{4,20},{20... | collective-permute-start | bytes 393224 | tf_op jit(solution)/shard_map/ppermute | solution.py:390
  21.9 2.0 %own.1 = (bf16[256,1024]{1,0:T(8,128)(2,1)S(1)}, bf16[256,512]{1,0:T(8,128)(2,1)S(1)}, bf16[256,1024]{1,0:T(8,128)(2,1)S(1)}) custom-call(f32[2,8,1024]{2,1,0:T(8,128)S(1)} %get-tuple-element.25.refs_0_.held.refs_1_, bf16[256,1024]{1,0:T(8,128)(2,1)S(1)} %get-tuple-element.24.late_rows.frames, bf16[128,512]{1,0:T(8,128)(2,1)S(1)} %get-tuple-element.32.inner, ...), custom_call_target="tpu_custom_call" | custom-call | flops 20000000 | bytes 60000 | tf_op jit(solution)/shard_map/own/pallas_call | solution.py:396
  23.9 0.0 collective-permute-done.3.refs_0_
  23.9 0.6 %early.1.refs_0_.refs_4_ = bf16[128,1024]{1,0:T(8,128)(2,1)S(1)} custom-call(bf16[256,1024]{1,0:T(8,128)(2,1)S(1)} %get-tuple-element.35._.refs_2_.refs_1_, f32[2,8,1024]{2,1,0:T(8,128)S(1)} %get-tuple-element.25.refs_0_.held.refs_1_, bf16[128,1024]{1,0:T(8,128)(2,1)S(1)} %get-tuple-element.38.first, bf16[128,512]{1,0:T(8,128)(2,1)S(1)} %get-tuple-element.39.query, ...), custom_call_target="tpu_custom_call" | custom-call | flops 12000000 | bytes 36000 | tf_op jit(solution)/shard_map/early/pallas_call | solution.py:396
  24.5 0.0 collective-permute-done.5.refs_6_.refs_7_
  24.5 1.5 %collective-permute-done.4.refs_5_ = bf16[128,512]{1,0:T(8,128)(2,1)S(1)} collective-permute-done((bf16[128,512]{1,0:T(8,128)(2,1)S(1)}, bf16[128,512]{1,0:T(8,128)(2,1)S(1)}, u32[]{:S(2)}, u32[]{:S(2)}) %collective-permute-start.4) | collective-permute-done | bytes 131104 | tf_op jit(solution)/shard_map/ppermute | solution.py:390
  26.0 1.5 %inner.1.refs_5_ = bf16[128,1024]{1,0:T(8,128)(2,1)S(1)} custom-call(bf16[128,1024]{1,0:T(8,128)(2,1)S(1)} %early.1.refs_0_.refs_4_, f32[2,8,1024]{2,1,0:T(8,128)S(1)} %get-tuple-element.25.refs_0_.held.refs_1_, bf16[256,1024]{1,0:T(8,128)(2,1)S(1)} %get-tuple-element.35._.refs_2_.refs_1_, bf16[256,512]{1,0:T(8,128)(2,1)S(1)} %get-tuple-element.36.refs_3_.refs_2_, ...), custom_call_target="tpu_custom_call" | custom-call | flops 40000000 | bytes 120000 | tf_op jit(solution)/shard_map/inner/pallas_call | solution.py:396
  27.6 1.0 %collective-permute-done.6.refs_6_ = bf16[128,512]{1,0:T(8,128)(2,1)S(1)} collective-permute-done((bf16[128,512]{1,0:T(8,128)(2,1)S(1)}, bf16[128,512]{1,0:T(8,128)(2,1)S(1)}, u32[]{:S(2)}, u32[]{:S(2)}) %collective-permute-start.6) | collective-permute-done | bytes 131104 | tf_op jit(solution)/shard_map/ppermute | solution.py:390
  28.6 2.3 %outer.1 = bf16[1,384,1024]{2,1,0:T(8,128)(2,1)} custom-call(f32[2,8,1024]{2,1,0:T(8,128)S(1)} %get-tuple-element.25.refs_0_.held.refs_1_, bf16[256,1024]{1,0:T(8,128)(2,1)S(1)} %get-tuple-element.35._.refs_2_.refs_1_, bf16[256,512]{1,0:T(8,128)(2,1)S(1)} %get-tuple-element.36.refs_3_.refs_2_, bf16[256,1024]{1,0:T(8,128)(2,1)S(1)} %get-tuple-element.37.refs_4_.refs_3_, ...), custom_call_target="tpu_custom_call" | custom-call | flops 2000000000 | bytes 6000000 | tf_op jit(solution)/shard_map/outer/pallas_call | solution.py:396
  (18 shorter events, 0.1 us)
Async XLA Ops:
  0.0 7.7 %copy-start.7 = (s32[2]{0:T(128)S(1)}, s32[2]{0:T(128)}, u32[]{:S(2)}) copy-start(s32[2]{0:T(128)} %timestep.1) | copy-start | bytes 28
  0.0 7.7 %copy-start.4 = (f32[50,6,1024]{2,0,1:T(8,128)S(1)}, f32[50,6,1024]{2,0,1:T(8,128)}, u32[]{:S(2)}) copy-start(f32[50,6,1024]{2,0,1:T(8,128)} %param.11) | copy-start | bytes 3686404
  0.0 7.7 %copy-start.1 = (bf16[1024,1536]{1,0:T(8,128)(2,1)S(1)}, bf16[1024,1536]{1,0:T(8,128)(2,1)}, u32[]{:S(2)}) copy-start(bf16[1024,1536]{1,0:T(8,128)(2,1)} %refs_2_.3) | copy-start | bytes 9437188
  0.0 7.7 %copy-start.6 = (f32[2,64]{1,0:T(2,128)S(1)}, f32[2,64]{1,0:T(2,128)}, u32[]{:S(2)}) copy-start(f32[2,64]{1,0:T(2,128)} %refs_3_.3) | copy-start | bytes 1540
  0.0 7.7 %copy-start.2 = (bf16[512,1024]{1,0:T(8,128)(2,1)S(1)}, bf16[512,1024]{1,0:T(8,128)(2,1)}, u32[]{:S(2)}) copy-start(bf16[512,1024]{1,0:T(8,128)(2,1)} %refs_8_.3) | copy-start | bytes 3145732
  0.0 7.7 %copy-start = (bf16[1024,1536]{1,0:T(8,128)(2,1)S(1)}, bf16[1024,1536]{1,0:T(8,128)(2,1)}, u32[]{:S(2)}) copy-start(bf16[1024,1536]{1,0:T(8,128)(2,1)} %refs_9_.3) | copy-start | bytes 9437188
  0.0 7.7 %copy-start.5 = (f32[2,64]{1,0:T(2,128)S(1)}, f32[2,64]{1,0:T(2,128)}, u32[]{:S(2)}) copy-start(f32[2,64]{1,0:T(2,128)} %refs_10_.3) | copy-start | bytes 1540
  0.0 4.5 %collective-permute-start = (bf16[1,384,1024]{2,1,0:T(8,128)(2,1)}, bf16[1,384,1024]{2,1,0:T(8,128)(2,1)S(1)}, u32[]{:S(2)}, u32[]{:S(2)}) collective-permute-start(bf16[1,384,1024]{2,1,0:T(8,128)(2,1)} %frames.1), channel_id=1, source_target_pairs={{0,1},{1,0},{2,3},{3,2},{4,5},{5,4},{6,7},{7,6},{8,9},{9,8},{10,11... | collective-permute-start | bytes 2359304 | tf_op jit(solution)/shard_map/ppermute | solution.py:413
  0.6 1.4 %copy-start.8 = (bf16[1,384,1024]{2,1,0:T(8,128)(2,1)S(1)}, bf16[1,384,1024]{2,1,0:T(8,128)(2,1)}, u32[]{:S(2)}) copy-start(bf16[1,384,1024]{2,1,0:T(8,128)(2,1)} %frames.1) | copy-start | bytes 2359300
  2.1 22.4 %collective-permute-start.5 = (bf16[256,1024]{1,0:T(8,128)(2,1)S(1)}, bf16[256,1024]{1,0:T(8,128)(2,1)S(1)}, u32[]{:S(2)}, u32[]{:S(2)}) collective-permute-start(bf16[256,1024]{1,0:T(8,128)(2,1)S(1)} %get-tuple-element.24.late_rows.frames), channel_id=1, source_target_pairs={{0,16},{16,0},{1,17},{17,1},{2,18},{18,2},{3,19},{19,3},{4,20},{20... | collective-permute-start | bytes 1572872 | tf_op jit(solution)/shard_map/ppermute | solution.py:390
  4.6 12.4 %collective-permute-start.1 = (bf16[128,1024]{1,0:T(8,128)(2,1)S(1)}, bf16[128,1024]{1,0:T(8,128)(2,1)S(1)}, u32[]{:S(2)}, u32[]{:S(2)}) collective-permute-start(bf16[128,1024]{1,0:T(8,128)(2,1)S(1)} %get-tuple-element.26), channel_id=1, source_target_pairs={{0,2},{2,4},{4,6},{6,8},{8,10},{10,12},{12,14},{3,1},{5,3},{7,5},{... | collective-permute-start | bytes 786440 | tf_op jit(solution)/shard_map/ppermute | solution.py:415
  6.1 13.3 %collective-permute-start.2 = (bf16[128,1024]{1,0:T(8,128)(2,1)S(1)}, bf16[128,1024]{1,0:T(8,128)(2,1)S(1)}, u32[]{:S(2)}, u32[]{:S(2)}) collective-permute-start(bf16[128,1024]{1,0:T(8,128)(2,1)S(1)} %get-tuple-element.33), channel_id=1, source_target_pairs={{0,2},{2,4},{4,6},{6,8},{8,10},{10,12},{12,14},{3,1},{5,3},{7,5},{... | collective-permute-start | bytes 786440 | tf_op jit(solution)/shard_map/ppermute | solution.py:416
  13.9 10.0 %collective-permute-start.3 = (bf16[128,1024]{1,0:T(8,128)(2,1)S(1)}, bf16[128,1024]{1,0:T(8,128)(2,1)S(1)}, u32[]{:S(2)}, u32[]{:S(2)}) collective-permute-start(bf16[128,1024]{1,0:T(8,128)(2,1)S(1)} %get-tuple-element.40.kv), channel_id=1, source_target_pairs={{0,16},{16,0},{1,17},{17,1},{2,18},{18,2},{3,19},{19,3},{4,20},{20... | collective-permute-start | bytes 786440 | tf_op jit(solution)/shard_map/ppermute | solution.py:390
  18.4 7.6 %collective-permute-start.4 = (bf16[128,512]{1,0:T(8,128)(2,1)S(1)}, bf16[128,512]{1,0:T(8,128)(2,1)S(1)}, u32[]{:S(2)}, u32[]{:S(2)}) collective-permute-start(bf16[128,512]{1,0:T(8,128)(2,1)S(1)} %get-tuple-element.32.inner), channel_id=1, source_target_pairs={{0,16},{16,0},{1,17},{17,1},{2,18},{18,2},{3,19},{19,3},{4,20},{20... | collective-permute-start | bytes 393224 | tf_op jit(solution)/shard_map/ppermute | solution.py:390
  20.7 3.1 %copy-start.3 = (bf16[512,1024]{1,0:T(8,128)(2,1)S(1)}, bf16[512,1024]{1,0:T(8,128)(2,1)}, u32[]{:S(2)}) copy-start(bf16[512,1024]{1,0:T(8,128)(2,1)} %refs_11_.1) | copy-start | bytes 3145732
  20.8 7.8 %collective-permute-start.6 = (bf16[128,512]{1,0:T(8,128)(2,1)S(1)}, bf16[128,512]{1,0:T(8,128)(2,1)S(1)}, u32[]{:S(2)}, u32[]{:S(2)}) collective-permute-start(bf16[128,512]{1,0:T(8,128)(2,1)S(1)} %far_outer.1.outer), channel_id=1, source_target_pairs={{0,16},{16,0},{1,17},{17,1},{2,18},{18,2},{3,19},{19,3},{4,20},{20... | collective-permute-start | bytes 393224 | tf_op jit(solution)/shard_map/ppermute | solution.py:390

commit v9 on v8

--- a/solution.py
+++ b/solution.py
@@ -160,7 +160,7 @@
 
 def near_kernel(
     timestep, modulation, early_rows, late_rows, near, qkv_self, gains, out_self, qkv_cross, gains_cross,
-    query, kv, first, first_q, first_kv, held,
+    query, kv, first, first_q, first_k, first_v, held,
 ):
     rows = near.shape[1]
     for k in range(held.shape[0]):
@@ -209,7 +209,7 @@
 
     f = first_of(early_rows[...], attended, out_self, mods(2))
     first[...] = f
-    first_q[...], first_kv[:, :HW], first_kv[:, HW:] = projected_cross(
+    first_q[...], first_k[...], first_v[...] = projected_cross(
         f, mods, qkv_cross, gains_cross, ones, True
     )
 
@@ -270,8 +270,9 @@
     kv[:, :HW], kv[:, HW:] = keys, values
 
 
-def far_outer_kernel(rows, held, far, qkv_self, gains, query, *refs):
-    *parts, kv, attended = refs
+def far_outer_kernel(rows, early_values, held, far, qkv_self, gains, query, *refs):
+    *parts, kv, attended, passed = refs
+    passed[...] = early_values[...]
     keys, values = far_keys(far[...], held, qkv_self, gains)
     keys = jnp.concatenate([kv[:, :HW], keys], axis=0)
     values = jnp.concatenate([kv[:, HW:], values], axis=0)
@@ -298,7 +299,8 @@
     return (first.astype(F32) + gate * out.astype(F32)).astype(BF16)
 
 
-def own_kernel(held, frames, inner, outer, out_self, qkv_cross, gains, first, query, kv):
+def own_kernel(held, frames, inner, outer, out_self, qkv_cross, gains, *refs):
+    first, query, kv = refs[-3:]
     mods = mods_held(held, 0)
     ones = head_ones()
     parts = [slice(0, BLOCK), slice(BLOCK, HALF)]
@@ -318,14 +320,6 @@
         kv[part, HW:] = raw[0].astype(BF16)
         query[part] = head_norm(raw[1], gains[0], ones)
         kv[part, :HW] = head_norm(raw[2], gains[1], ones)
-
-
-def early_kernel(_, held, first, query, kv, out_cross, *refs):
-    others, out = refs[:-1], refs[-1]
-    keys = [each[:, :HW] for each in (kv, *others)]
-    values = [each[:, HW:] for each in (kv, *others)]
-    mixed = cross_attend(query[...], keys, values, head_ones())
-    out[...] = finished(first[...], mixed, out_cross, mods_held(held, 0)(5))
 
 
 def late_block(block, held, first, query, kv, others, their_frames, out_self, qkv_cross, gains, out_cross):
@@ -342,23 +336,26 @@
     return finished(first[part], mixed, out_cross, mods_held(held, 0)(5))
 
 
-def inner_kernel(count, _, held, first, query, kv, *refs):
+def late_kernel(block, count, held, first, query, kv, *refs):
     others, their_frames = refs[: count - 1], refs[count - 1 : 2 * count - 2]
     *weights, out = refs[2 * count - 2 :]
-    out[...] = late_block(1, held, first, query, kv, others, their_frames, *weights)
-
-
-def outer_kernel(count, held, first, query, kv, early_out, inner_out, *refs):
-    others, their_frames = refs[: count - 1], refs[count - 1 : 2 * count - 2]
-    *weights, out, outer_out, sems = refs[2 * count - 2 :]
+    out[...] = late_block(block, held, first, query, kv, others, their_frames, *weights)
+
+
+def early_kernel(count, held, inner_out, outer_out, out_cross, first, query, *refs):
+    keys, values = refs[:count], refs[count : 2 * count]
+    out, early_out, sems = refs[2 * count :]
     _, outer, inner, early = places(out.shape[1])
     copies = [
         pltpu.make_async_copy(source, out.at[0, pl.ds(at, BLOCK)], sems.at[n])
-        for n, (source, at) in enumerate(((early_out, early), (inner_out, inner), (outer_out, outer)))
+        for n, (source, at) in enumerate(((inner_out, inner), (outer_out, outer), (early_out, early)))
     ]
     copies[0].start()
     copies[1].start()
-    outer_out[...] = late_block(0, held, first, query, kv, others, their_frames, *weights)
+    mixed = cross_attend(
+        query[...], [k[...] for k in keys], [v[...] for v in values], head_ones()
+    )
+    early_out[...] = finished(first[...], mixed, out_cross, mods_held(held, 0)(5))
     copies[2].start()
     for copy in copies:
         copy.wait()
@@ -416,13 +413,13 @@
     farther = lax.ppermute(mate_inner, "tm", across)
 
     late, block, part = shape(HALF, HW), shape(BLOCK, HW), shape(HALF, HW, dtype=F32)
-    query, kv, first_early, q_early, kv_early, held = call(
+    query, kv, first_early, q_early, k_early, v_early, held = call(
         near_kernel, "near", 0.12,
-        (late, shape(rows + HALF, 2 * HW), half, block, half, shape(stems, 8, D, dtype=F32)),
+        (late, shape(rows + HALF, 2 * HW), half, block, block, block, shape(stems, 8, D, dtype=F32)),
         timestep, modulation, early_rows, late_rows, near, qkv_self, qk_gain_self, out_self, qkv_cross, qk_gain_cross,
         in_specs=[SMEM] + [VMEM] * 9,
     )
-    others_early = to_stems(kv_early)
+    their_keys = to_stems(k_early)
     parts = call(part_kernel, "part", 0.04, (part, part, part), query, kv)
 
     self_weights = (qkv_self, qk_gain_self)
@@ -431,29 +428,29 @@
         held, far, *self_weights, query, *parts,
     )
     others_inner = to_stems(att_inner)
-    att_outer = call(
-        lambda *refs: far_outer_kernel(rows, *refs), "far_outer", 0.006, block,
-        held, farther, *self_weights, query, *parts, far_kv,
+    att_outer, passed = call(
+        lambda *refs: far_outer_kernel(rows, *refs), "far_outer", 0.006, (block, block),
+        v_early, held, farther, *self_weights, query, *parts, far_kv,
     )
     others_outer = to_stems(att_outer)
+    their_values = to_stems(passed)
 
     weights = (out_self, qkv_cross, qk_gain_cross)
     own = call(
         own_kernel, "own", 0.02, (shape(HALF, D), late, shape(HALF, D)),
-        held, late_rows, att_inner, att_outer, *weights,
-    )
-    early_out = call(
-        early_kernel, "early", 0.012, half, own[0], held, first_early, q_early, kv_early, out_cross, *others_early,
-        in_specs=[ANY] + [VMEM] * (4 + stems),
-    )
-    inner_out = call(
-        lambda *refs: inner_kernel(stems, *refs), "inner", 0.04, half,
-        early_out, held, *own, *others_inner, *their_frames, *weights, out_cross,
-        in_specs=[ANY] + [VMEM] * (6 + 2 * stems),
+        held, late_rows, att_inner, att_outer, *weights, *their_keys,
+        in_specs=[VMEM] * 7 + [ANY] * (stems - 1),
+    )
+    inner_out, outer_out = (
+        call(
+            lambda *refs, n=n: late_kernel(n, stems, *refs), name, us, half,
+            held, *own, *others, *their_frames, *weights, out_cross,
+        )
+        for n, name, us, others in ((1, "inner", 0.04, others_inner), (0, "outer", 0.04, others_outer))
     )
     return call(
-        lambda *refs: outer_kernel(stems, *refs), "outer", 2, shape(1, rows, D),
-        held, *own, early_out, inner_out, *others_outer, *their_frames, *weights, out_cross,
+        lambda *refs: early_kernel(stems, *refs), "early", 2, shape(1, rows, D),
+        held, inner_out, outer_out, out_cross, first_early, q_early, k_early, *their_keys, v_early, *their_values,
         scratch=[pltpu.VMEM((BLOCK, D), BF16), pltpu.SemaphoreType.DMA((3,))], out_specs=ANY,
     )
 

time: 31 us -> 30.5 us (0.984)
  waiting for transfers between devices: 2.48 us -> 1.06 us
  starting transfers between devices: 9.35 us -> 10.3 us
    ppermute x4 -> x5, waiting for transfers between devices: 2.47 us -> 1.05 us  [to_stems(): lax.ppermute(array, 'stem', [(i, (i + k) % stems) for i in range(stems)])]
    ppermute x4 -> x5, starting transfers between devices: 5.72 us -> 6.7 us  [to_stems(): lax.ppermute(array, 'stem', [(i, (i + k) % stems) for i in range(stems)])]
  transfers between devices with their start and end apart: 7 -> 8, of which waited for: 2 -> 1; matrix products, arithmetic and copies ran while one was open for 0% -> 0% of each run, Pallas kernels for 49% -> 53%
where the time goes in v9:
time: 30.5 us; the launch traced here: 30.4 us
  Pallas kernels  17.4 us (57%)
  starting transfers between devices  10.3 us (34%)
  local copies, waits for them, and re-layouts  1.45 us (5%)
  waiting for transfers between devices  1.06 us (3%)
    pallas_call x10, Pallas kernels, call(): pl.pallas_call(kernel, out_shape=outs, in_specs=in_specs or [VMEM] * len(...  17.4 us
    ppermute x5, starting transfers between devices, to_stems(): lax.ppermute(array, 'stem', [(i, (i + k) % stems) for i in range(stems)])  6.7 us
    ppermute x1, starting transfers between devices, on_device(): far = lax.ppermute(mate_outer, 'tm', across)  1.55 us
    ppermute x1, starting transfers between devices, on_device(): farther = lax.ppermute(mate_inner, 'tm', across)  1.55 us
    unnamed x18, local copies, waits for them, and re-layouts  1.45 us
    ppermute x5, waiting for transfers between devices, to_stems(): lax.ppermute(array, 'stem', [(i, (i + k) % stems) for i in range(stems)])  1.05 us
  transfers between devices with their start and end apart: 8, of which 1 were waited for; matrix products, arithmetic and copies ran while one was open for 0% of the time, Pallas kernels for 53%

profile of v9, /device:TPU:0, one launch (start us, length us, event | category | flops | bytes accessed | tf_op | source)
XLA Modules:
  0.0 30.4 jit_solution(2048601294732489330)
XLA Ops:
  0.0 0.5 %collective-permute-start = (bf16[1,384,1024]{2,1,0:T(8,128)(2,1)}, bf16[1,384,1024]{2,1,0:T(8,128)(2,1)S(1)}, u32[]{:S(2)}, u32[]{:S(2)}) collective-permute-start(bf16[1,384,1024]{2,1,0:T(8,128)(2,1)} %frames.1), channel_id=1, source_target_pairs={{0,1},{1,0},{2,3},{3,2},{4,5},{5,4},{6,7},{7,6},{8,9},{9,8},{10,11... | collective-permute-start | bytes 2359304 | tf_op jit(solution)/shard_map/ppermute | solution.py:410
  0.6 1.4 %copy-done.8 = bf16[1,384,1024]{2,1,0:T(8,128)(2,1)S(1)} copy-done((bf16[1,384,1024]{2,1,0:T(8,128)(2,1)S(1)}, bf16[1,384,1024]{2,1,0:T(8,128)(2,1)}, u32[]{:S(2)}) %copy-start.8) | copy-done | bytes 786456
  2.0 0.1 split.1
  2.1 2.5 %collective-permute-start.5 = (bf16[256,1024]{1,0:T(8,128)(2,1)S(1)}, bf16[256,1024]{1,0:T(8,128)(2,1)S(1)}, u32[]{:S(2)}, u32[]{:S(2)}) collective-permute-start(bf16[256,1024]{1,0:T(8,128)(2,1)S(1)} %get-tuple-element.27.late_rows.frames), channel_id=1, source_target_pairs={{0,16},{16,0},{1,17},{17,1},{2,18},{18,2},{3,19},{19,3},{4,20},{20... | collective-permute-start | bytes 1572872 | tf_op jit(solution)/shard_map/ppermute | solution.py:387
  4.5 0.0 collective-permute-done.near.mate
  4.6 1.5 %collective-permute-start.1 = (bf16[128,1024]{1,0:T(8,128)(2,1)S(1)}, bf16[128,1024]{1,0:T(8,128)(2,1)S(1)}, u32[]{:S(2)}, u32[]{:S(2)}) collective-permute-start(bf16[128,1024]{1,0:T(8,128)(2,1)S(1)} %get-tuple-element.29), channel_id=1, source_target_pairs={{0,2},{2,4},{4,6},{6,8},{8,10},{10,12},{12,14},{3,1},{5,3},{7,5},{... | collective-permute-start | bytes 786440 | tf_op jit(solution)/shard_map/ppermute | solution.py:412
  6.1 1.5 %collective-permute-start.2 = (bf16[128,1024]{1,0:T(8,128)(2,1)S(1)}, bf16[128,1024]{1,0:T(8,128)(2,1)S(1)}, u32[]{:S(2)}, u32[]{:S(2)}) collective-permute-start(bf16[128,1024]{1,0:T(8,128)(2,1)S(1)} %get-tuple-element.37), channel_id=1, source_target_pairs={{0,2},{2,4},{4,6},{6,8},{8,10},{10,12},{12,14},{3,1},{5,3},{7,5},{... | collective-permute-start | bytes 786440 | tf_op jit(solution)/shard_map/ppermute | solution.py:413
  7.7 6.2 %near.1 = (bf16[256,512]{1,0:T(8,128)(2,1)S(1)}, bf16[640,1024]{1,0:T(8,128)(2,1)S(1)}, bf16[128,1024]{1,0:T(8,128)(2,1)S(1)}, bf16[128,512]{1,0:T(8,128)(2,1)S(...) custom-call(s32[2]{0:T(128)S(1)} %copy-done.7, ...), custom_call_target="tpu_custom_call" | custom-call | flops 120000000 | bytes 360000 | tf_op jit(solution)/shard_map/near/pallas_call | solution.py:393
  13.9 1.1 %collective-permute-start.3 = (bf16[128,512]{1,0:T(8,128)(2,1)S(1)}, bf16[128,512]{1,0:T(8,128)(2,1)S(1)}, u32[]{:S(2)}, u32[]{:S(2)}) collective-permute-start(bf16[128,512]{1,0:T(8,128)(2,1)S(1)} %get-tuple-element.40.refs_6_), channel_id=1, source_target_pairs={{0,16},{16,0},{1,17},{17,1},{2,18},{18,2},{3,19},{19,3},{4,20},{20... | collective-permute-start | bytes 393224 | tf_op jit(solution)/shard_map/ppermute | solution.py:387
  15.0 1.9 %part.1 = (f32[256,512]{1,0:T(8,128)S(1)}, f32[256,512]{1,0:T(8,128)S(1)}, f32[256,512]{1,0:T(8,128)S(1)}) custom-call(bf16[256,512]{1,0:T(8,128)(2,1)S(1)} %get-tuple-element.30.query.refs_4_.refs_5_, bf16[640,1024]{1,0:T(8,128)(2,1)S(1)} %get-tuple-element.31.kv), custom_call_target="tpu_custom_call" | custom-call | flops 40000000 | bytes 120000 | tf_op jit(solution)/shard_map/part/pallas_call | solution.py:393
  17.0 1.4 %far_inner.1 = (bf16[128,512]{1,0:T(8,128)(2,1)S(1)}, bf16[128,1024]{1,0:T(8,128)(2,1)S(1)}) custom-call(f32[2,8,1024]{2,1,0:T(8,128)S(1)} %get-tuple-element.28.refs_0_.refs_1_.held, bf16[128,1024]{1,0:T(8,128)(2,1)S(1)} %collective-permute-done.1.refs_1_, bf16[1024,1536]{1,0:T(8,128)(2,1)S(1)} %copy-done.1, f32[2,64]{1,0:T(2,128)S(1)} %copy-done.6, ...), custom_call_target="tpu_custom_call" | custom-call | flops 40000000 | bytes 120000 | tf_op jit(solution)/shard_map/far_inner/pallas_call | solution.py:393
  18.4 1.0 %collective-permute-start.4 = (bf16[128,512]{1,0:T(8,128)(2,1)S(1)}, bf16[128,512]{1,0:T(8,128)(2,1)S(1)}, u32[]{:S(2)}, u32[]{:S(2)}) collective-permute-start(bf16[128,512]{1,0:T(8,128)(2,1)S(1)} %get-tuple-element.35.inner), channel_id=1, source_target_pairs={{0,16},{16,0},{1,17},{17,1},{2,18},{18,2},{3,19},{19,3},{4,20},{20... | collective-permute-start | bytes 393224 | tf_op jit(solution)/shard_map/ppermute | solution.py:387
  19.4 0.0 collective-permute-done.2.refs_2_
  19.4 1.3 %far_outer.1 = (bf16[128,512]{1,0:T(8,128)(2,1)S(1)}, bf16[128,512]{1,0:T(8,128)(2,1)S(1)}) custom-call(bf16[128,512]{1,0:T(8,128)(2,1)S(1)} %get-tuple-element.36.refs_0_.refs_8_, f32[2,8,1024]{2,1,0:T(8,128)S(1)} %get-tuple-element.28.refs_0_.refs_1_.held, bf16[128,1024]{1,0:T(8,128)(2,1)S(1)} %collective-permute-done.2.refs_2_, ...), custom_call_target="tpu_custom_call" | custom-call | flops 6000000 | bytes 18000 | tf_op jit(solution)/shard_map/far_outer/pallas_call | solution.py:393
  20.7 0.0 copy-start.3
  20.8 1.1 %collective-permute-start.6 = (bf16[128,512]{1,0:T(8,128)(2,1)S(1)}, bf16[128,512]{1,0:T(8,128)(2,1)S(1)}, u32[]{:S(2)}, u32[]{:S(2)}) collective-permute-start(bf16[128,512]{1,0:T(8,128)(2,1)S(1)} %get-tuple-element.39.outer), channel_id=1, source_target_pairs={{0,16},{16,0},{1,17},{17,1},{2,18},{18,2},{3,19},{19,3},{4,20},{20... | collective-permute-start | bytes 393224 | tf_op jit(solution)/shard_map/ppermute | solution.py:387
  21.9 1.0 %collective-permute-start.7 = (bf16[128,512]{1,0:T(8,128)(2,1)S(1)}, bf16[128,512]{1,0:T(8,128)(2,1)S(1)}, u32[]{:S(2)}, u32[]{:S(2)}) collective-permute-start(bf16[128,512]{1,0:T(8,128)(2,1)S(1)} %get-tuple-element.46), channel_id=1, source_target_pairs={{0,16},{16,0},{1,17},{17,1},{2,18},{18,2},{3,19},{19,3},{4,20},{20... | collective-permute-start | bytes 393224 | tf_op jit(solution)/shard_map/ppermute | solution.py:387
  22.9 2.0 %own.1 = (bf16[256,1024]{1,0:T(8,128)(2,1)S(1)}, bf16[256,512]{1,0:T(8,128)(2,1)S(1)}, bf16[256,1024]{1,0:T(8,128)(2,1)S(1)}) custom-call(f32[2,8,1024]{2,1,0:T(8,128)S(1)} %get-tuple-element.28.refs_0_.refs_1_.held, bf16[256,1024]{1,0:T(8,128)(2,1)S(1)} %get-tuple-element.27.late_rows.frames, bf16[128,512]{1,0:T(8,128)(2,1)S(1)} %get-tuple-element.35.inner, ...), custom_call_target="tpu_custom_call" | custom-call | flops 20000000 | bytes 60000 | tf_op jit(solution)/shard_map/own/pallas_call | solution.py:393
  24.8 0.0 collective-permute-done.5.refs_5_
  24.9 1.5 %inner.1.refs_1_ = bf16[128,1024]{1,0:T(8,128)(2,1)S(1)} custom-call(f32[2,8,1024]{2,1,0:T(8,128)S(1)} %get-tuple-element.28.refs_0_.refs_1_.held, bf16[256,1024]{1,0:T(8,128)(2,1)S(1)} %get-tuple-element.41.refs_1_, bf16[256,512]{1,0:T(8,128)(2,1)S(1)} %get-tuple-element.42.refs_2_, bf16[256,1024]{1,0:T(8,128)(2,1)S(1)} %get-tuple-element.43.refs_3_, ...), custom_call_target="tpu_custom_call" | custom-call | flops 40000000 | bytes 120000 | tf_op jit(solution)/shard_map/inner/pallas_call | solution.py:393
  26.4 1.0 %collective-permute-done.6.refs_4_ = bf16[128,512]{1,0:T(8,128)(2,1)S(1)} collective-permute-done((bf16[128,512]{1,0:T(8,128)(2,1)S(1)}, bf16[128,512]{1,0:T(8,128)(2,1)S(1)}, u32[]{:S(2)}, u32[]{:S(2)}) %collective-permute-start.6) | collective-permute-done | bytes 131104 | tf_op jit(solution)/shard_map/ppermute | solution.py:387
  27.5 1.5 %outer.1.refs_2_ = bf16[128,1024]{1,0:T(8,128)(2,1)S(1)} custom-call(f32[2,8,1024]{2,1,0:T(8,128)S(1)} %get-tuple-element.28.refs_0_.refs_1_.held, bf16[256,1024]{1,0:T(8,128)(2,1)S(1)} %get-tuple-element.41.refs_1_, bf16[256,512]{1,0:T(8,128)(2,1)S(1)} %get-tuple-element.42.refs_2_, bf16[256,1024]{1,0:T(8,128)(2,1)S(1)} %get-tuple-element.43.refs_3_, ...), custom_call_target="tpu_custom_call" | custom-call | flops 40000000 | bytes 120000 | tf_op jit(solution)/shard_map/outer/pallas_call | solution.py:393
  29.0 0.0 collective-permute-done.7.refs_9_
  29.0 1.4 %early.1 = bf16[1,384,1024]{2,1,0:T(8,128)(2,1)} custom-call(f32[2,8,1024]{2,1,0:T(8,128)S(1)} %get-tuple-element.28.refs_0_.refs_1_.held, bf16[128,1024]{1,0:T(8,128)(2,1)S(1)} %inner.1.refs_1_, bf16[128,1024]{1,0:T(8,128)(2,1)S(1)} %outer.1.refs_2_, bf16[512,1024]{1,0:T(8,128)(2,1)S(1)} %copy-done.3, bf16[128,1024]{1,0:T(8,128)(2,1)S(1)} %get-tuple-element.44.refs_4_, ...), custom_call_target="tpu_custom_call" | custom-call | flops 2000000000 | bytes 6000000 | tf_op jit(solution)/shard_map/early/pallas_call | solution.py:393
  (20 shorter events, 0.1 us)
Async XLA Ops:
  0.0 7.7 %copy-start.7 = (s32[2]{0:T(128)S(1)}, s32[2]{0:T(128)}, u32[]{:S(2)}) copy-start(s32[2]{0:T(128)} %timestep.1) | copy-start | bytes 28
  0.0 7.7 %copy-start.4 = (f32[50,6,1024]{2,0,1:T(8,128)S(1)}, f32[50,6,1024]{2,0,1:T(8,128)}, u32[]{:S(2)}) copy-start(f32[50,6,1024]{2,0,1:T(8,128)} %param.11) | copy-start | bytes 3686404
  0.0 7.7 %copy-start.1 = (bf16[1024,1536]{1,0:T(8,128)(2,1)S(1)}, bf16[1024,1536]{1,0:T(8,128)(2,1)}, u32[]{:S(2)}) copy-start(bf16[1024,1536]{1,0:T(8,128)(2,1)} %refs_3_.4) | copy-start | bytes 9437188
  0.0 7.7 %copy-start.6 = (f32[2,64]{1,0:T(2,128)S(1)}, f32[2,64]{1,0:T(2,128)}, u32[]{:S(2)}) copy-start(f32[2,64]{1,0:T(2,128)} %refs_4_.1) | copy-start | bytes 1540
  0.0 7.7 %copy-start.2 = (bf16[512,1024]{1,0:T(8,128)(2,1)S(1)}, bf16[512,1024]{1,0:T(8,128)(2,1)}, u32[]{:S(2)}) copy-start(bf16[512,1024]{1,0:T(8,128)(2,1)} %refs_6_.3) | copy-start | bytes 3145732
  0.0 7.7 %copy-start = (bf16[1024,1536]{1,0:T(8,128)(2,1)S(1)}, bf16[1024,1536]{1,0:T(8,128)(2,1)}, u32[]{:S(2)}) copy-start(bf16[1024,1536]{1,0:T(8,128)(2,1)} %refs_7_.3) | copy-start | bytes 9437188
  0.0 7.7 %copy-start.5 = (f32[2,64]{1,0:T(2,128)S(1)}, f32[2,64]{1,0:T(2,128)}, u32[]{:S(2)}) copy-start(f32[2,64]{1,0:T(2,128)} %refs_8_.3) | copy-start | bytes 1540
  0.0 4.5 %collective-permute-start = (bf16[1,384,1024]{2,1,0:T(8,128)(2,1)}, bf16[1,384,1024]{2,1,0:T(8,128)(2,1)S(1)}, u32[]{:S(2)}, u32[]{:S(2)}) collective-permute-start(bf16[1,384,1024]{2,1,0:T(8,128)(2,1)} %frames.1), channel_id=1, source_target_pairs={{0,1},{1,0},{2,3},{3,2},{4,5},{5,4},{6,7},{7,6},{8,9},{9,8},{10,11... | collective-permute-start | bytes 2359304 | tf_op jit(solution)/shard_map/ppermute | solution.py:410
  0.6 1.4 %copy-start.8 = (bf16[1,384,1024]{2,1,0:T(8,128)(2,1)S(1)}, bf16[1,384,1024]{2,1,0:T(8,128)(2,1)}, u32[]{:S(2)}) copy-start(bf16[1,384,1024]{2,1,0:T(8,128)(2,1)} %frames.1) | copy-start | bytes 2359300
  2.1 22.8 %collective-permute-start.5 = (bf16[256,1024]{1,0:T(8,128)(2,1)S(1)}, bf16[256,1024]{1,0:T(8,128)(2,1)S(1)}, u32[]{:S(2)}, u32[]{:S(2)}) collective-permute-start(bf16[256,1024]{1,0:T(8,128)(2,1)S(1)} %get-tuple-element.27.late_rows.frames), channel_id=1, source_target_pairs={{0,16},{16,0},{1,17},{17,1},{2,18},{18,2},{3,19},{19,3},{4,20},{20... | collective-permute-start | bytes 1572872 | tf_op jit(solution)/shard_map/ppermute | solution.py:387
  4.6 12.4 %collective-permute-start.1 = (bf16[128,1024]{1,0:T(8,128)(2,1)S(1)}, bf16[128,1024]{1,0:T(8,128)(2,1)S(1)}, u32[]{:S(2)}, u32[]{:S(2)}) collective-permute-start(bf16[128,1024]{1,0:T(8,128)(2,1)S(1)} %get-tuple-element.29), channel_id=1, source_target_pairs={{0,2},{2,4},{4,6},{6,8},{8,10},{10,12},{12,14},{3,1},{5,3},{7,5},{... | collective-permute-start | bytes 786440 | tf_op jit(solution)/shard_map/ppermute | solution.py:412
  6.1 13.3 %collective-permute-start.2 = (bf16[128,1024]{1,0:T(8,128)(2,1)S(1)}, bf16[128,1024]{1,0:T(8,128)(2,1)S(1)}, u32[]{:S(2)}, u32[]{:S(2)}) collective-permute-start(bf16[128,1024]{1,0:T(8,128)(2,1)S(1)} %get-tuple-element.37), channel_id=1, source_target_pairs={{0,2},{2,4},{4,6},{6,8},{8,10},{10,12},{12,14},{3,1},{5,3},{7,5},{... | collective-permute-start | bytes 786440 | tf_op jit(solution)/shard_map/ppermute | solution.py:413
  13.9 8.9 %collective-permute-start.3 = (bf16[128,512]{1,0:T(8,128)(2,1)S(1)}, bf16[128,512]{1,0:T(8,128)(2,1)S(1)}, u32[]{:S(2)}, u32[]{:S(2)}) collective-permute-start(bf16[128,512]{1,0:T(8,128)(2,1)S(1)} %get-tuple-element.40.refs_6_), channel_id=1, source_target_pairs={{0,16},{16,0},{1,17},{17,1},{2,18},{18,2},{3,19},{19,3},{4,20},{20... | collective-permute-start | bytes 393224 | tf_op jit(solution)/shard_map/ppermute | solution.py:387
  18.4 6.5 %collective-permute-start.4 = (bf16[128,512]{1,0:T(8,128)(2,1)S(1)}, bf16[128,512]{1,0:T(8,128)(2,1)S(1)}, u32[]{:S(2)}, u32[]{:S(2)}) collective-permute-start(bf16[128,512]{1,0:T(8,128)(2,1)S(1)} %get-tuple-element.35.inner), channel_id=1, source_target_pairs={{0,16},{16,0},{1,17},{17,1},{2,18},{18,2},{3,19},{19,3},{4,20},{20... | collective-permute-start | bytes 393224 | tf_op jit(solution)/shard_map/ppermute | solution.py:387
  20.7 4.1 %copy-start.3 = (bf16[512,1024]{1,0:T(8,128)(2,1)S(1)}, bf16[512,1024]{1,0:T(8,128)(2,1)}, u32[]{:S(2)}) copy-start(bf16[512,1024]{1,0:T(8,128)(2,1)} %refs_3_.5) | copy-start | bytes 3145732
  20.8 6.7 %collective-permute-start.6 = (bf16[128,512]{1,0:T(8,128)(2,1)S(1)}, bf16[128,512]{1,0:T(8,128)(2,1)S(1)}, u32[]{:S(2)}, u32[]{:S(2)}) collective-permute-start(bf16[128,512]{1,0:T(8,128)(2,1)S(1)} %get-tuple-element.39.outer), channel_id=1, source_target_pairs={{0,16},{16,0},{1,17},{17,1},{2,18},{18,2},{3,19},{19,3},{4,20},{20... | collective-permute-start | bytes 393224 | tf_op jit(solution)/shard_map/ppermute | solution.py:387
  21.9 7.1 %collective-permute-start.7 = (bf16[128,512]{1,0:T(8,128)(2,1)S(1)}, bf16[128,512]{1,0:T(8,128)(2,1)S(1)}, u32[]{:S(2)}, u32[]{:S(2)}) collective-permute-start(bf16[128,512]{1,0:T(8,128)(2,1)S(1)} %get-tuple-element.46), channel_id=1, source_target_pairs={{0,16},{16,0},{1,17},{17,1},{2,18},{18,2},{3,19},{19,3},{4,20},{20... | collective-permute-start | bytes 393224 | tf_op jit(solution)/shard_map/ppermute | solution.py:387

commit v10 on v9

--- a/solution.py
+++ b/solution.py
@@ -17,7 +17,6 @@
 F32 = jnp.float32
 BF16 = jnp.bfloat16
 VMEM = pl.BlockSpec(memory_space=pltpu.VMEM)
-SMEM = pl.BlockSpec(memory_space=pltpu.SMEM)
 ANY = pl.BlockSpec(memory_space=pl.ANY)
 LIMIT = 16 * 1024 * 1024
 
@@ -88,18 +87,24 @@
     return jnp.where(left_half(), pair[:BLOCK], pair[BLOCK:])
 
 
-def raised_scores(query, keys, bias):
+def window_scores(query, keys, bias):
     half, zero = left_half(), jnp.zeros_like(query)
     pair = jnp.concatenate([jnp.where(half, query, zero), jnp.where(half, zero, query)], axis=0)
     scores = dot(pair, keys, ((1,), (1,)))
-    scores = jnp.concatenate([scores[:BLOCK] + bias, scores[BLOCK:] + bias], axis=0)
+    return jnp.concatenate([scores[:BLOCK] + bias, scores[BLOCK:] + bias], axis=0)
+
+
+def raised(scores):
     top = jnp.max(scores, axis=-1, keepdims=True)
     return jnp.exp(scores - top).astype(BF16), top
 
 
-def weighted(raised, values):
-    summed = dot(raised, jnp.concatenate([values, jnp.ones_like(values)], axis=1))
+def weighted(powers, values):
+    summed = dot(powers, jnp.concatenate([values, jnp.ones_like(values)], axis=1))
     return by_head(summed[:, :SLAB]), by_head(summed[:, SLAB:])
+
+
+SLABS = [slice(at, at + SLAB) for at in range(0, HW, SLAB)]
 
 
 def cross_attend(query, keys, values, ones):
@@ -111,21 +116,27 @@
     top = jnp.zeros_like(query)
     for s in scores:
         top = jnp.maximum(top, s)
-    raised = [jnp.exp(-top)] + [jnp.exp(s - top) for s in scores]
-    total = raised[0]
-    for r in raised[1:]:
-        total = total + r
+    powers = [jnp.exp(-top)] + [jnp.exp(s - top) for s in scores]
+    total = powers[0]
+    for p in powers[1:]:
+        total = total + p
     scale = 1.0 / total
     out = jnp.zeros_like(query)
-    for r, v in zip(raised, values):
-        out = out + (r * scale).astype(BF16).astype(F32) * v.astype(F32)
+    for p, v in zip(powers, values):
+        out = out + (p * scale).astype(BF16).astype(F32) * v.astype(F32)
     return out.astype(BF16)
 
 
 def mods_of(timestep, modulation, back):
     count = lax.axis_size("stem")
-    step = timestep[lax.rem(lax.axis_index("stem") + count - back, count)]
-    return lambda i: modulation[i, pl.ds(step, 1), :]
+    stem = lax.rem(lax.axis_index("stem") + count - back, count)
+    at = lax.broadcasted_iota(jnp.int32, (1, count), 1)
+    step = jnp.sum(jnp.where(at == stem, timestep[...], 0).astype(F32), axis=1, keepdims=True)
+    rows = lax.broadcasted_iota(jnp.int32, (modulation.shape[1], 1), 0).astype(F32)
+    picked = rows == step
+    return [
+        jnp.sum(jnp.where(picked, modulation[i], 0.0), axis=0, keepdims=True) for i in range(6)
+    ]
 
 
 def mods_held(held, back):
@@ -158,17 +169,36 @@
     inner_rows[...] = mate[0, inner : inner + BLOCK]
 
 
+def part_steps(block, query, kv, part_out, part_sum, part_top):
+    parity = lax.rem(lax.axis_index("tm"), 2)
+    width = (HALF, BLOCK)[block]
+    start = pl.multiple_of(parity * width, BLOCK)
+    count = kv.shape[0] - width
+    bias = window_bias(count, (1 - parity) * width)
+    to = slice(block * BLOCK, (block + 1) * BLOCK)
+    for cols in SLABS:
+        scores = window_scores(query[:, cols], kv[pl.ds(start, count), cols], bias)
+        yield
+        powers, top = raised(scores)
+        values = kv[pl.ds(start, count), HW + cols.start : HW + cols.stop]
+        part_out[to, cols], part_sum[to, cols] = weighted(powers, values)
+        part_top[to, cols] = by_head(jnp.broadcast_to(top, (2 * BLOCK, SLAB)))
+        yield
+
+
 def near_kernel(
     timestep, modulation, early_rows, late_rows, near, qkv_self, gains, out_self, qkv_cross, gains_cross,
-    query, kv, first, first_q, first_k, first_v, held,
+    query, part_out, part_sum, part_top, first, first_q, first_k, first_v, held, kv,
 ):
     rows = near.shape[1]
-    for k in range(held.shape[0]):
-        row = mods_of(timestep, modulation, k)
-        for i in range(6):
-            held[k, i : i + 1] = row(i)
+
+    def hold(k):
+        for i, row in enumerate(mods_of(timestep, modulation, k)):
+            held[k, i : i + 1] = row
+
+    hold(0)
     parity, outer, inner, early = places(rows)
-    mods = mods_of(timestep, modulation, 0)
+    mods = mods_held(held, 0)
     shift, scale = mods(0), mods(1)
     ones = head_ones()
     q_gain = wide_gain(gains[0:1]) * (HD ** -0.5)
@@ -177,59 +207,63 @@
     near_at = (1 - parity) * rows
     near_from = parity * (rows - HALF)
 
-    sources = [(early_rows[...], own_at + early)]
-    sources += [(late_rows[:BLOCK], own_at + outer), (late_rows[BLOCK:], own_at + inner)]
-    sources += [
-        (near[0, pl.ds(pl.multiple_of(near_from + at, BLOCK), BLOCK)], near_at + at)
-        for at in range(0, HALF, BLOCK)
+    sources = [
+        (early_rows, 0, own_at + early),
+        (late_rows, 0, own_at + outer),
+        (late_rows, BLOCK, own_at + inner),
     ]
+    for at in range(0, HALF, BLOCK):
+        sources.append((near.at[0], pl.multiple_of(near_from + at, BLOCK), near_at + at))
+
+    def normed(n):
+        source, at, _ = sources[n]
+        return modulated(source[pl.ds(at, BLOCK)], shift, scale)
+
     queries = []
-    for n, (source, to) in enumerate(sources):
-        normed = modulated(source, shift, scale)
+    rows_n = normed(0)
+    for n, (_, _, to) in enumerate(sources):
+        at = pl.ds(pl.multiple_of(to, BLOCK), BLOCK)
+        columns = (0, HW, 2 * HW) if n < 3 else (HW, 2 * HW)
+        raw = [dot(rows_n, qkv_self[:, c : c + HW]) for c in columns]
+        if n + 1 < len(sources):
+            rows_n = normed(n + 1)
         if n < 3:
-            projected = dot(normed, qkv_self[...])
-            queries.append(head_norm(projected[:, :HW], q_gain, ones))
-            projected = projected[:, HW:]
-        else:
-            projected = dot(normed, qkv_self[:, HW:])
-        to = pl.multiple_of(to, BLOCK)
-        kv[pl.ds(to, BLOCK), :HW] = head_norm(projected[:, :HW], k_gain, ones)
-        kv[pl.ds(to, BLOCK), HW:] = projected[:, HW:].astype(BF16)
+            queries.append(head_norm(raw[0], q_gain, ones))
+        kv[at, :HW] = head_norm(raw[-2], k_gain, ones)
+        kv[at, HW:] = raw[-1].astype(BF16)
     query[:BLOCK] = queries[1]
     query[BLOCK:] = queries[2]
-
-    window = rows + HALF
-    bias = window_bias(window, 0)
+    for k in range(1, held.shape[0]):
+        hold(k)
+
+    parts = [part_steps(n, queries[n + 1], kv, part_out, part_sum, part_top) for n in range(2)]
+
+    def meanwhile(steps):
+        while steps and parts:
+            if next(parts[0], parts) is parts:
+                parts.pop(0)
+            else:
+                steps -= 1
+
+    bias = window_bias(rows + HALF, 0)
     attended = []
-    for at in range(0, HW, SLAB):
-        raised, _ = raised_scores(queries[0][:, at : at + SLAB], kv[:, at : at + SLAB], bias)
-        out, total = weighted(raised, kv[:, HW + at : HW + at + SLAB])
+    for cols in SLABS:
+        scores = window_scores(queries[0][:, cols], kv[:, cols], bias)
+        meanwhile(2)
+        powers, _ = raised(scores)
+        out, total = weighted(powers, kv[:, HW + cols.start : HW + cols.stop])
         attended.append((out / total).astype(BF16))
-    attended = jnp.concatenate(attended, axis=1)
-
-    f = first_of(early_rows[...], attended, out_self, mods(2))
+    f = first_of(early_rows[...], jnp.concatenate(attended, axis=1), out_self, mods(2))
     first[...] = f
-    first_q[...], first_k[...], first_v[...] = projected_cross(
-        f, mods, qkv_cross, gains_cross, ones, True
-    )
-
-
-def part_kernel(query, kv, part_out, part_sum, part_top):
-    parity = lax.rem(lax.axis_index("tm"), 2)
-    for n, width in ((0, HALF), (1, BLOCK)):
-        start = pl.multiple_of(parity * width, BLOCK)
-        count = kv.shape[0] - width
-        bias = window_bias(count, (1 - parity) * width)
-        to = slice(n * BLOCK, (n + 1) * BLOCK)
-        for at in range(0, HW, SLAB):
-            cols = slice(at, at + SLAB)
-            raised, top = raised_scores(
-                query[to, cols], kv[pl.ds(start, count), cols], bias
-            )
-            out, total = weighted(raised, kv[pl.ds(start, count), HW + at : HW + at + SLAB])
-            part_out[to, cols] = out
-            part_sum[to, cols] = total
-            part_top[to, cols] = by_head(jnp.broadcast_to(top, (2 * BLOCK, SLAB)))
+    meanwhile(3)
+    normed_f = modulated(f, mods(3), mods(4))
+    meanwhile(3)
+    raw = [dot(normed_f, qkv_cross[:, at : at + HW]) for at in range(0, 3 * HW, HW)]
+    meanwhile(4)
+    first_q[...] = head_norm(raw[0], wide_gain(gains_cross[0:1]), ones)
+    first_k[...] = head_norm(raw[1], wide_gain(gains_cross[1:2]), ones)
+    first_v[...] = raw[2].astype(BF16)
+    meanwhile(4 * HW)
 
 
 def far_keys(rows, held, qkv_self, gains):
@@ -250,10 +284,10 @@
 
 def far_attend(block, bias, query, keys, values, part_out, part_sum, part_top, attended):
     to = slice(block * BLOCK, (block + 1) * BLOCK)
-    for at in range(0, HW, SLAB):
-        cols = slice(at, at + SLAB)
-        raised, top = raised_scores(query[to, cols], keys[:, cols], bias)
-        out, summed = weighted(raised, values[:, cols])
+    scores = [window_scores(query[to, cols], keys[:, cols], bias) for cols in SLABS]
+    powers = [raised(each) for each in scores]
+    sums = [weighted(each, values[:, cols]) for (each, _), cols in zip(powers, SLABS)]
+    for cols, (_, top), (out, summed) in zip(SLABS, powers, sums):
         top = by_head(jnp.broadcast_to(top, (2 * BLOCK, SLAB)))
         both = jnp.maximum(top, part_top[to, cols])
         here = jnp.exp(top - both)
@@ -413,14 +447,14 @@
     farther = lax.ppermute(mate_inner, "tm", across)
 
     late, block, part = shape(HALF, HW), shape(BLOCK, HW), shape(HALF, HW, dtype=F32)
-    query, kv, first_early, q_early, k_early, v_early, held = call(
+    query, part_out, part_sum, part_top, first_early, q_early, k_early, v_early, held = call(
         near_kernel, "near", 0.12,
-        (late, shape(rows + HALF, 2 * HW), half, block, block, block, shape(stems, 8, D, dtype=F32)),
-        timestep, modulation, early_rows, late_rows, near, qkv_self, qk_gain_self, out_self, qkv_cross, qk_gain_cross,
-        in_specs=[SMEM] + [VMEM] * 9,
+        (late, part, part, part, half, block, block, block, shape(stems, 8, D, dtype=F32)),
+        timestep.reshape(1, -1), modulation, early_rows, late_rows, near, qkv_self, qk_gain_self, out_self, qkv_cross, qk_gain_cross,
+        scratch=[pltpu.VMEM((rows + HALF, 2 * HW), BF16)],
     )
     their_keys = to_stems(k_early)
-    parts = call(part_kernel, "part", 0.04, (part, part, part), query, kv)
+    parts = (part_out, part_sum, part_top)
 
     self_weights = (qkv_self, qk_gain_self)
     att_inner, far_kv = call(
@@ -441,12 +475,14 @@
         held, late_rows, att_inner, att_outer, *weights, *their_keys,
         in_specs=[VMEM] * 7 + [ANY] * (stems - 1),
     )
-    inner_out, outer_out = (
-        call(
-            lambda *refs, n=n: late_kernel(n, stems, *refs), name, us, half,
-            held, *own, *others, *their_frames, *weights, out_cross,
-        )
-        for n, name, us, others in ((1, "inner", 0.04, others_inner), (0, "outer", 0.04, others_outer))
+    inner_out = call(
+        lambda *refs: late_kernel(1, stems, *refs), "inner", 0.04, half,
+        held, *own, *others_inner, *their_frames, *weights, out_cross,
+    )
+    outer_out = call(
+        lambda _, *refs: late_kernel(0, stems, *refs), "outer", 0.04, half,
+        inner_out, held, *own, *others_outer, *their_frames, *weights, out_cross,
+        in_specs=[ANY] + [VMEM] * (6 + 2 * stems),
     )
     return call(
         lambda *refs: early_kernel(stems, *refs), "early", 2, shape(1, rows, D),

time: 30.5 us -> 30.1 us (0.987)
  Pallas kernels: 17.4 us -> 16.2 us
  waiting for transfers between devices: 1.06 us -> 1.8 us
    pallas_call x10 -> x9, Pallas kernels: 17.4 us -> 16.2 us  [call(): pl.pallas_call(kernel, out_shape=outs, in_specs=in_specs or [VMEM] * len(...]
    ppermute x5, waiting for transfers between devices: 1.05 us -> 1.65 us  [to_stems(): lax.ppermute(array, 'stem', [(i, (i + k) % stems) for i in range(stems)])]
  transfers between devices with their start and end apart: 8 -> 8, of which waited for: 1 -> 3; matrix products, arithmetic and copies ran while one was open for 0% -> 0% of each run, Pallas kernels for 53% -> 50%
where the time goes in v10:
time: 30.1 us; the launch traced here: 29.9 us
  Pallas kernels  16.2 us (54%)
  starting transfers between devices  10.3 us (34%)
  waiting for transfers between devices  1.8 us (6%)
  local copies, waits for them, and re-layouts  1.45 us (5%)
    pallas_call x9, Pallas kernels, call(): pl.pallas_call(kernel, out_shape=outs, in_specs=in_specs or [VMEM] * len(...  16.2 us
    ppermute x5, starting transfers between devices, to_stems(): lax.ppermute(array, 'stem', [(i, (i + k) % stems) for i in range(stems)])  6.7 us
    ppermute x5, waiting for transfers between devices, to_stems(): lax.ppermute(array, 'stem', [(i, (i + k) % stems) for i in range(stems)])  1.65 us
    ppermute x1, starting transfers between devices, on_device(): far = lax.ppermute(mate_outer, 'tm', across)  1.55 us
    ppermute x1, starting transfers between devices, on_device(): farther = lax.ppermute(mate_inner, 'tm', across)  1.55 us
    unnamed x18, local copies, waits for them, and re-layouts  1.45 us
  transfers between devices with their start and end apart: 8, of which 3 were waited for; matrix products, arithmetic and copies ran while one was open for 0% of the time, Pallas kernels for 50%

profile of v10, /device:TPU:0, one launch (start us, length us, event | category | flops | bytes accessed | tf_op | source)
XLA Modules:
  0.0 29.9 jit_solution(11059756135288714697)
XLA Ops:
  0.0 0.5 %collective-permute-start = (bf16[1,384,1024]{2,1,0:T(8,128)(2,1)}, bf16[1,384,1024]{2,1,0:T(8,128)(2,1)S(1)}, u32[]{:S(2)}, u32[]{:S(2)}) collective-permute-start(bf16[1,384,1024]{2,1,0:T(8,128)(2,1)} %frames.1), channel_id=1, source_target_pairs={{0,1},{1,0},{2,3},{3,2},{4,5},{5,4},{6,7},{7,6},{8,9},{9,8},{10,11... | collective-permute-start | bytes 2359304 | tf_op jit(solution)/shard_map/ppermute | solution.py:444
  0.6 1.4 %copy-done.8 = bf16[1,384,1024]{2,1,0:T(8,128)(2,1)S(1)} copy-done((bf16[1,384,1024]{2,1,0:T(8,128)(2,1)S(1)}, bf16[1,384,1024]{2,1,0:T(8,128)(2,1)}, u32[]{:S(2)}) %copy-start.8) | copy-done | bytes 786456
  2.0 0.1 split.1
  2.1 2.5 %collective-permute-start.5 = (bf16[256,1024]{1,0:T(8,128)(2,1)S(1)}, bf16[256,1024]{1,0:T(8,128)(2,1)S(1)}, u32[]{:S(2)}, u32[]{:S(2)}) collective-permute-start(bf16[256,1024]{1,0:T(8,128)(2,1)S(1)} %get-tuple-element.26.late_rows.frames), channel_id=1, source_target_pairs={{0,16},{16,0},{1,17},{17,1},{2,18},{18,2},{3,19},{19,3},{4,20},{20... | collective-permute-start | bytes 1572872 | tf_op jit(solution)/shard_map/ppermute | solution.py:421
  4.6 1.5 %collective-permute-start.1 = (bf16[128,1024]{1,0:T(8,128)(2,1)S(1)}, bf16[128,1024]{1,0:T(8,128)(2,1)S(1)}, u32[]{:S(2)}, u32[]{:S(2)}) collective-permute-start(bf16[128,1024]{1,0:T(8,128)(2,1)S(1)} %get-tuple-element.28), channel_id=1, source_target_pairs={{0,2},{2,4},{4,6},{6,8},{8,10},{10,12},{12,14},{3,1},{5,3},{7,5},{... | collective-permute-start | bytes 786440 | tf_op jit(solution)/shard_map/ppermute | solution.py:446
  6.1 1.5 %collective-permute-start.2 = (bf16[128,1024]{1,0:T(8,128)(2,1)S(1)}, bf16[128,1024]{1,0:T(8,128)(2,1)S(1)}, u32[]{:S(2)}, u32[]{:S(2)}) collective-permute-start(bf16[128,1024]{1,0:T(8,128)(2,1)S(1)} %get-tuple-element.35), channel_id=1, source_target_pairs={{0,2},{2,4},{4,6},{6,8},{8,10},{10,12},{12,14},{3,1},{5,3},{7,5},{... | collective-permute-start | bytes 786440 | tf_op jit(solution)/shard_map/ppermute | solution.py:447
  7.7 7.2 %near.1 = (bf16[256,512]{1,0:T(8,128)(2,1)S(1)}, f32[256,512]{1,0:T(8,128)S(1)}, f32[256,512]{1,0:T(8,128)S(1)}, f32[256,512]{1,0:T(8,128)S(1)}, bf16[128,1024]{...) custom-call(s32[1,2]{1,0:T(1,128)S(1)} %bitcast.3, ...), custom_call_target="tpu_custom_call" | custom-call | flops 120000000 | bytes 360000 | tf_op jit(solution)/shard_map/near/pallas_call | solution.py:427
  14.9 1.1 %collective-permute-start.3 = (bf16[128,512]{1,0:T(8,128)(2,1)S(1)}, bf16[128,512]{1,0:T(8,128)(2,1)S(1)}, u32[]{:S(2)}, u32[]{:S(2)}) collective-permute-start(bf16[128,512]{1,0:T(8,128)(2,1)S(1)} %get-tuple-element.38.refs_6_), channel_id=1, source_target_pairs={{0,16},{16,0},{1,17},{17,1},{2,18},{18,2},{3,19},{19,3},{4,20},{20... | collective-permute-start | bytes 393224 | tf_op jit(solution)/shard_map/ppermute | solution.py:421
  16.0 0.0 collective-permute-done.1.refs_1_
  16.0 1.2 %far_inner.1 = (bf16[128,512]{1,0:T(8,128)(2,1)S(1)}, bf16[128,1024]{1,0:T(8,128)(2,1)S(1)}) custom-call(f32[2,8,1024]{2,1,0:T(8,128)S(1)} %get-tuple-element.27.refs_0_.refs_1_.held, bf16[128,1024]{1,0:T(8,128)(2,1)S(1)} %collective-permute-done.1.refs_1_, bf16[1024,1536]{1,0:T(8,128)(2,1)S(1)} %copy-done.1, f32[2,64]{1,0:T(2,128)S(1)} %copy-done.6, ...), custom_call_target="tpu_custom_call" | custom-call | flops 40000000 | bytes 120000 | tf_op jit(solution)/shard_map/far_inner/pallas_call | solution.py:427
  17.2 1.1 %collective-permute-start.4 = (bf16[128,512]{1,0:T(8,128)(2,1)S(1)}, bf16[128,512]{1,0:T(8,128)(2,1)S(1)}, u32[]{:S(2)}, u32[]{:S(2)}) collective-permute-start(bf16[128,512]{1,0:T(8,128)(2,1)S(1)} %get-tuple-element.33.inner), channel_id=1, source_target_pairs={{0,16},{16,0},{1,17},{17,1},{2,18},{18,2},{3,19},{19,3},{4,20},{20... | collective-permute-start | bytes 393224 | tf_op jit(solution)/shard_map/ppermute | solution.py:421
  18.3 0.1 collective-permute-done.2.refs_2_
  18.4 1.3 %far_outer.1 = (bf16[128,512]{1,0:T(8,128)(2,1)S(1)}, bf16[128,512]{1,0:T(8,128)(2,1)S(1)}) custom-call(bf16[128,512]{1,0:T(8,128)(2,1)S(1)} %get-tuple-element.34.refs_0_.refs_8_, f32[2,8,1024]{2,1,0:T(8,128)S(1)} %get-tuple-element.27.refs_0_.refs_1_.held, bf16[128,1024]{1,0:T(8,128)(2,1)S(1)} %collective-permute-done.2.refs_2_, ...), custom_call_target="tpu_custom_call" | custom-call | flops 6000000 | bytes 18000 | tf_op jit(solution)/shard_map/far_outer/pallas_call | solution.py:427
  19.7 0.0 copy-start.3
  19.7 1.1 %collective-permute-start.6 = (bf16[128,512]{1,0:T(8,128)(2,1)S(1)}, bf16[128,512]{1,0:T(8,128)(2,1)S(1)}, u32[]{:S(2)}, u32[]{:S(2)}) collective-permute-start(bf16[128,512]{1,0:T(8,128)(2,1)S(1)} %get-tuple-element.37.outer), channel_id=1, source_target_pairs={{0,16},{16,0},{1,17},{17,1},{2,18},{18,2},{3,19},{19,3},{4,20},{20... | collective-permute-start | bytes 393224 | tf_op jit(solution)/shard_map/ppermute | solution.py:421
  20.8 1.0 %collective-permute-start.7 = (bf16[128,512]{1,0:T(8,128)(2,1)S(1)}, bf16[128,512]{1,0:T(8,128)(2,1)S(1)}, u32[]{:S(2)}, u32[]{:S(2)}) collective-permute-start(bf16[128,512]{1,0:T(8,128)(2,1)S(1)} %get-tuple-element.44), channel_id=1, source_target_pairs={{0,16},{16,0},{1,17},{17,1},{2,18},{18,2},{3,19},{19,3},{4,20},{20... | collective-permute-start | bytes 393224 | tf_op jit(solution)/shard_map/ppermute | solution.py:421
  21.8 0.0 collective-permute-done.3.refs_0_.refs_7_
  21.8 2.0 %own.1 = (bf16[256,1024]{1,0:T(8,128)(2,1)S(1)}, bf16[256,512]{1,0:T(8,128)(2,1)S(1)}, bf16[256,1024]{1,0:T(8,128)(2,1)S(1)}) custom-call(f32[2,8,1024]{2,1,0:T(8,128)S(1)} %get-tuple-element.27.refs_0_.refs_1_.held, bf16[256,1024]{1,0:T(8,128)(2,1)S(1)} %get-tuple-element.26.late_rows.frames, bf16[128,512]{1,0:T(8,128)(2,1)S(1)} %get-tuple-element.33.inner, ...), custom_call_target="tpu_custom_call" | custom-call | flops 20000000 | bytes 60000 | tf_op jit(solution)/shard_map/own/pallas_call | solution.py:427
  23.8 0.4 %collective-permute-done.4.refs_4_ = bf16[128,512]{1,0:T(8,128)(2,1)S(1)} collective-permute-done((bf16[128,512]{1,0:T(8,128)(2,1)S(1)}, bf16[128,512]{1,0:T(8,128)(2,1)S(1)}, u32[]{:S(2)}, u32[]{:S(2)}) %collective-permute-start.4) | collective-permute-done | bytes 131104 | tf_op jit(solution)/shard_map/ppermute | solution.py:421
  24.2 1.5 %inner.1._.refs_1_ = bf16[128,1024]{1,0:T(8,128)(2,1)S(1)} custom-call(f32[2,8,1024]{2,1,0:T(8,128)S(1)} %get-tuple-element.27.refs_0_.refs_1_.held, bf16[256,1024]{1,0:T(8,128)(2,1)S(1)} %get-tuple-element.39.refs_1_, bf16[256,512]{1,0:T(8,128)(2,1)S(1)} %get-tuple-element.40.refs_2_, bf16[256,1024]{1,0:T(8,128)(2,1)S(1)} %get-tuple-element.41.refs_3_, ...), custom_call_target="tpu_custom_call" | custom-call | flops 40000000 | bytes 120000 | tf_op jit(solution)/shard_map/inner/pallas_call | solution.py:427
  25.8 1.3 %collective-permute-done.6.refs_4_ = bf16[128,512]{1,0:T(8,128)(2,1)S(1)} collective-permute-done((bf16[128,512]{1,0:T(8,128)(2,1)S(1)}, bf16[128,512]{1,0:T(8,128)(2,1)S(1)}, u32[]{:S(2)}, u32[]{:S(2)}) %collective-permute-start.6) | collective-permute-done | bytes 131104 | tf_op jit(solution)/shard_map/ppermute | solution.py:421
  27.0 1.5 %outer.1.refs_2_ = bf16[128,1024]{1,0:T(8,128)(2,1)S(1)} custom-call(bf16[128,1024]{1,0:T(8,128)(2,1)S(1)} %inner.1._.refs_1_, f32[2,8,1024]{2,1,0:T(8,128)S(1)} %get-tuple-element.27.refs_0_.refs_1_.held, bf16[256,1024]{1,0:T(8,128)(2,1)S(1)} %get-tuple-element.39.refs_1_, bf16[256,512]{1,0:T(8,128)(2,1)S(1)} %get-tuple-element.40.refs_2_, ...), custom_call_target="tpu_custom_call" | custom-call | flops 40000000 | bytes 120000 | tf_op jit(solution)/shard_map/outer/pallas_call | solution.py:427
  28.6 0.0 collective-permute-done.7.refs_9_
  28.6 1.4 %early.1 = bf16[1,384,1024]{2,1,0:T(8,128)(2,1)} custom-call(f32[2,8,1024]{2,1,0:T(8,128)S(1)} %get-tuple-element.27.refs_0_.refs_1_.held, bf16[128,1024]{1,0:T(8,128)(2,1)S(1)} %inner.1._.refs_1_, bf16[128,1024]{1,0:T(8,128)(2,1)S(1)} %outer.1.refs_2_, bf16[512,1024]{1,0:T(8,128)(2,1)S(1)} %copy-done.3, bf16[128,1024]{1,0:T(8,128)(2,1)S(1)} %get-tuple-element.42.refs_4_, ...), custom_call_target="tpu_custom_call" | custom-call | flops 2000000000 | bytes 6000000 | tf_op jit(solution)/shard_map/early/pallas_call | solution.py:427
  (19 shorter events, 0.1 us)
Async XLA Ops:
  0.0 7.7 %copy-start.7 = (s32[2]{0:T(128)S(1)}, s32[2]{0:T(128)}, u32[]{:S(2)}) copy-start(s32[2]{0:T(128)} %param.10) | copy-start | bytes 28
  0.0 7.7 %copy-start.4 = (f32[50,6,1024]{2,0,1:T(8,128)S(1)}, f32[50,6,1024]{2,0,1:T(8,128)}, u32[]{:S(2)}) copy-start(f32[50,6,1024]{2,0,1:T(8,128)} %param.11) | copy-start | bytes 3686404
  0.0 7.7 %copy-start.1 = (bf16[1024,1536]{1,0:T(8,128)(2,1)S(1)}, bf16[1024,1536]{1,0:T(8,128)(2,1)}, u32[]{:S(2)}) copy-start(bf16[1024,1536]{1,0:T(8,128)(2,1)} %refs_3_.4) | copy-start | bytes 9437188
  0.0 7.7 %copy-start.2 = (bf16[512,1024]{1,0:T(8,128)(2,1)S(1)}, bf16[512,1024]{1,0:T(8,128)(2,1)}, u32[]{:S(2)}) copy-start(bf16[512,1024]{1,0:T(8,128)(2,1)} %refs_6_.3) | copy-start | bytes 3145732
  0.0 7.7 %copy-start.6 = (f32[2,64]{1,0:T(2,128)S(1)}, f32[2,64]{1,0:T(2,128)}, u32[]{:S(2)}) copy-start(f32[2,64]{1,0:T(2,128)} %refs_4_.1) | copy-start | bytes 1540
  0.0 7.7 %copy-start = (bf16[1024,1536]{1,0:T(8,128)(2,1)S(1)}, bf16[1024,1536]{1,0:T(8,128)(2,1)}, u32[]{:S(2)}) copy-start(bf16[1024,1536]{1,0:T(8,128)(2,1)} %refs_7_.3) | copy-start | bytes 9437188
  0.0 7.7 %copy-start.5 = (f32[2,64]{1,0:T(2,128)S(1)}, f32[2,64]{1,0:T(2,128)}, u32[]{:S(2)}) copy-start(f32[2,64]{1,0:T(2,128)} %refs_8_.3) | copy-start | bytes 1540
  0.0 4.5 %collective-permute-start = (bf16[1,384,1024]{2,1,0:T(8,128)(2,1)}, bf16[1,384,1024]{2,1,0:T(8,128)(2,1)S(1)}, u32[]{:S(2)}, u32[]{:S(2)}) collective-permute-start(bf16[1,384,1024]{2,1,0:T(8,128)(2,1)} %frames.1), channel_id=1, source_target_pairs={{0,1},{1,0},{2,3},{3,2},{4,5},{5,4},{6,7},{7,6},{8,9},{9,8},{10,11... | collective-permute-start | bytes 2359304 | tf_op jit(solution)/shard_map/ppermute | solution.py:444
  0.6 1.4 %copy-start.8 = (bf16[1,384,1024]{2,1,0:T(8,128)(2,1)S(1)}, bf16[1,384,1024]{2,1,0:T(8,128)(2,1)}, u32[]{:S(2)}) copy-start(bf16[1,384,1024]{2,1,0:T(8,128)(2,1)} %frames.1) | copy-start | bytes 2359300
  2.1 21.7 %collective-permute-start.5 = (bf16[256,1024]{1,0:T(8,128)(2,1)S(1)}, bf16[256,1024]{1,0:T(8,128)(2,1)S(1)}, u32[]{:S(2)}, u32[]{:S(2)}) collective-permute-start(bf16[256,1024]{1,0:T(8,128)(2,1)S(1)} %get-tuple-element.26.late_rows.frames), channel_id=1, source_target_pairs={{0,16},{16,0},{1,17},{17,1},{2,18},{18,2},{3,19},{19,3},{4,20},{20... | collective-permute-start | bytes 1572872 | tf_op jit(solution)/shard_map/ppermute | solution.py:421
  4.6 11.4 %collective-permute-start.1 = (bf16[128,1024]{1,0:T(8,128)(2,1)S(1)}, bf16[128,1024]{1,0:T(8,128)(2,1)S(1)}, u32[]{:S(2)}, u32[]{:S(2)}) collective-permute-start(bf16[128,1024]{1,0:T(8,128)(2,1)S(1)} %get-tuple-element.28), channel_id=1, source_target_pairs={{0,2},{2,4},{4,6},{6,8},{8,10},{10,12},{12,14},{3,1},{5,3},{7,5},{... | collective-permute-start | bytes 786440 | tf_op jit(solution)/shard_map/ppermute | solution.py:446
  6.1 12.3 %collective-permute-start.2 = (bf16[128,1024]{1,0:T(8,128)(2,1)S(1)}, bf16[128,1024]{1,0:T(8,128)(2,1)S(1)}, u32[]{:S(2)}, u32[]{:S(2)}) collective-permute-start(bf16[128,1024]{1,0:T(8,128)(2,1)S(1)} %get-tuple-element.35), channel_id=1, source_target_pairs={{0,2},{2,4},{4,6},{6,8},{8,10},{10,12},{12,14},{3,1},{5,3},{7,5},{... | collective-permute-start | bytes 786440 | tf_op jit(solution)/shard_map/ppermute | solution.py:447
  14.9 6.9 %collective-permute-start.3 = (bf16[128,512]{1,0:T(8,128)(2,1)S(1)}, bf16[128,512]{1,0:T(8,128)(2,1)S(1)}, u32[]{:S(2)}, u32[]{:S(2)}) collective-permute-start(bf16[128,512]{1,0:T(8,128)(2,1)S(1)} %get-tuple-element.38.refs_6_), channel_id=1, source_target_pairs={{0,16},{16,0},{1,17},{17,1},{2,18},{18,2},{3,19},{19,3},{4,20},{20... | collective-permute-start | bytes 393224 | tf_op jit(solution)/shard_map/ppermute | solution.py:421
  17.2 7.0 %collective-permute-start.4 = (bf16[128,512]{1,0:T(8,128)(2,1)S(1)}, bf16[128,512]{1,0:T(8,128)(2,1)S(1)}, u32[]{:S(2)}, u32[]{:S(2)}) collective-permute-start(bf16[128,512]{1,0:T(8,128)(2,1)S(1)} %get-tuple-element.33.inner), channel_id=1, source_target_pairs={{0,16},{16,0},{1,17},{17,1},{2,18},{18,2},{3,19},{19,3},{4,20},{20... | collective-permute-start | bytes 393224 | tf_op jit(solution)/shard_map/ppermute | solution.py:421
  19.7 4.5 %copy-start.3 = (bf16[512,1024]{1,0:T(8,128)(2,1)S(1)}, bf16[512,1024]{1,0:T(8,128)(2,1)}, u32[]{:S(2)}) copy-start(bf16[512,1024]{1,0:T(8,128)(2,1)} %refs_3_.5) | copy-start | bytes 3145732
  19.7 7.3 %collective-permute-start.6 = (bf16[128,512]{1,0:T(8,128)(2,1)S(1)}, bf16[128,512]{1,0:T(8,128)(2,1)S(1)}, u32[]{:S(2)}, u32[]{:S(2)}) collective-permute-start(bf16[128,512]{1,0:T(8,128)(2,1)S(1)} %get-tuple-element.37.outer), channel_id=1, source_target_pairs={{0,16},{16,0},{1,17},{17,1},{2,18},{18,2},{3,19},{19,3},{4,20},{20... | collective-permute-start | bytes 393224 | tf_op jit(solution)/shard_map/ppermute | solution.py:421
  20.8 7.7 %collective-permute-start.7 = (bf16[128,512]{1,0:T(8,128)(2,1)S(1)}, bf16[128,512]{1,0:T(8,128)(2,1)S(1)}, u32[]{:S(2)}, u32[]{:S(2)}) collective-permute-start(bf16[128,512]{1,0:T(8,128)(2,1)S(1)} %get-tuple-element.44), channel_id=1, source_target_pairs={{0,16},{16,0},{1,17},{17,1},{2,18},{18,2},{3,19},{19,3},{4,20},{20... | collective-permute-start | bytes 393224 | tf_op jit(solution)/shard_map/ppermute | solution.py:421

commit v11 on v10

--- a/solution.py
+++ b/solution.py
@@ -107,7 +107,7 @@
 SLABS = [slice(at, at + SLAB) for at in range(0, HW, SLAB)]
 
 
-def cross_attend(query, keys, values, ones):
+def cross_weights(query, keys, ones):
     query = query.astype(F32)
     base = keys[0].astype(F32)
     scores = [
@@ -121,9 +121,13 @@
     for p in powers[1:]:
         total = total + p
     scale = 1.0 / total
-    out = jnp.zeros_like(query)
-    for p, v in zip(powers, values):
-        out = out + (p * scale).astype(BF16).astype(F32) * v.astype(F32)
+    return [(p * scale).astype(BF16) for p in powers]
+
+
+def cross_sum(weights, values):
+    out = jnp.zeros(values[0].shape, F32)
+    for w, v in zip(weights, values):
+        out = out + w.astype(F32) * v.astype(F32)
     return out.astype(BF16)
 
 
@@ -366,7 +370,7 @@
         _, k, v = projected_cross(g, mods, qkv_cross, gains, ones, False)
         keys.append(k)
         values.append(v)
-    mixed = cross_attend(query[part], keys, values, ones)
+    mixed = cross_sum(cross_weights(query[part], keys, ones), values)
     return finished(first[part], mixed, out_cross, mods_held(held, 0)(5))
 
 
@@ -376,9 +380,15 @@
     out[...] = late_block(block, held, first, query, kv, others, their_frames, *weights)
 
 
-def early_kernel(count, held, inner_out, outer_out, out_cross, first, query, *refs):
-    keys, values = refs[:count], refs[count : 2 * count]
-    out, early_out, sems = refs[2 * count :]
+def weights_kernel(_, query, *refs):
+    keys, out = refs[:-1], refs[-1]
+    for n, each in enumerate(cross_weights(query[...], [k[...] for k in keys], head_ones())):
+        out[n] = each
+
+
+def early_kernel(count, held, inner_out, outer_out, out_cross, first, weights, *refs):
+    values = refs[:count]
+    out, early_out, sems = refs[count:]
     _, outer, inner, early = places(out.shape[1])
     copies = [
         pltpu.make_async_copy(source, out.at[0, pl.ds(at, BLOCK)], sems.at[n])
@@ -386,9 +396,7 @@
     ]
     copies[0].start()
     copies[1].start()
-    mixed = cross_attend(
-        query[...], [k[...] for k in keys], [v[...] for v in values], head_ones()
-    )
+    mixed = cross_sum([weights[n] for n in range(count)], [v[...] for v in values])
     early_out[...] = finished(first[...], mixed, out_cross, mods_held(held, 0)(5))
     copies[2].start()
     for copy in copies:
@@ -479,14 +487,19 @@
         lambda *refs: late_kernel(1, stems, *refs), "inner", 0.04, half,
         held, *own, *others_inner, *their_frames, *weights, out_cross,
     )
+    early_weights = call(
+        weights_kernel, "weights", 0.02, shape(stems, BLOCK, HW),
+        inner_out, q_early, k_early, *their_keys,
+        in_specs=[ANY] + [VMEM] * (1 + stems),
+    )
     outer_out = call(
         lambda _, *refs: late_kernel(0, stems, *refs), "outer", 0.04, half,
-        inner_out, held, *own, *others_outer, *their_frames, *weights, out_cross,
+        early_weights, held, *own, *others_outer, *their_frames, *weights, out_cross,
         in_specs=[ANY] + [VMEM] * (6 + 2 * stems),
     )
     return call(
         lambda *refs: early_kernel(stems, *refs), "early", 2, shape(1, rows, D),
-        held, inner_out, outer_out, out_cross, first_early, q_early, k_early, *their_keys, v_early, *their_values,
+        held, inner_out, outer_out, out_cross, first_early, early_weights, v_early, *their_values,
         scratch=[pltpu.VMEM((BLOCK, D), BF16), pltpu.SemaphoreType.DMA((3,))], out_specs=ANY,
     )
 

time: 30.1 us -> 29.8 us (0.990)
  waiting for transfers between devices: 1.8 us -> 1.44 us
    ppermute x5, waiting for transfers between devices: 1.65 us -> 1.29 us  [to_stems(): lax.ppermute(array, 'stem', [(i, (i + k) % stems) for i in range(stems)])]
    pallas_call x9 -> x10, Pallas kernels: 16.2 us -> 16.3 us  [call(): pl.pallas_call(kernel, out_shape=outs, in_specs=in_specs or [VMEM] * len(...]
  transfers between devices with their start and end apart: 8 -> 8, of which waited for: 3 -> 3; matrix products, arithmetic and copies ran while one was open for 0% -> 0% of each run, Pallas kernels for 50% -> 51%
where the time goes in v11:
time: 29.8 us; the launch traced here: 29.7 us
  Pallas kernels  16.3 us (55%)
  starting transfers between devices  10.3 us (35%)
  local copies, waits for them, and re-layouts  1.45 us (5%)
  waiting for transfers between devices  1.44 us (5%)
    pallas_call x10, Pallas kernels, call(): pl.pallas_call(kernel, out_shape=outs, in_specs=in_specs or [VMEM] * len(...  16.3 us
    ppermute x5, starting transfers between devices, to_stems(): lax.ppermute(array, 'stem', [(i, (i + k) % stems) for i in range(stems)])  6.7 us
    ppermute x1, starting transfers between devices, on_device(): far = lax.ppermute(mate_outer, 'tm', across)  1.55 us
    ppermute x1, starting transfers between devices, on_device(): farther = lax.ppermute(mate_inner, 'tm', across)  1.55 us
    unnamed x18, local copies, waits for them, and re-layouts  1.45 us
    ppermute x5, waiting for transfers between devices, to_stems(): lax.ppermute(array, 'stem', [(i, (i + k) % stems) for i in range(stems)])  1.29 us
  transfers between devices with their start and end apart: 8, of which 3 were waited for; matrix products, arithmetic and copies ran while one was open for 0% of the time, Pallas kernels for 51%

profile of v11, /device:TPU:0, one launch (start us, length us, event | category | flops | bytes accessed | tf_op | source)
XLA Modules:
  0.0 29.7 jit_solution(3492434667528618454)
XLA Ops:
  0.0 0.5 %collective-permute-start = (bf16[1,384,1024]{2,1,0:T(8,128)(2,1)}, bf16[1,384,1024]{2,1,0:T(8,128)(2,1)S(1)}, u32[]{:S(2)}, u32[]{:S(2)}) collective-permute-start(bf16[1,384,1024]{2,1,0:T(8,128)(2,1)} %frames.1), channel_id=1, source_target_pairs={{0,1},{1,0},{2,3},{3,2},{4,5},{5,4},{6,7},{7,6},{8,9},{9,8},{10,11... | collective-permute-start | bytes 2359304 | tf_op jit(solution)/shard_map/ppermute | solution.py:452
  0.6 1.4 %copy-done.8 = bf16[1,384,1024]{2,1,0:T(8,128)(2,1)S(1)} copy-done((bf16[1,384,1024]{2,1,0:T(8,128)(2,1)S(1)}, bf16[1,384,1024]{2,1,0:T(8,128)(2,1)}, u32[]{:S(2)}) %copy-start.8) | copy-done | bytes 786456
  2.0 0.1 split.1
  2.1 2.5 %collective-permute-start.5 = (bf16[256,1024]{1,0:T(8,128)(2,1)S(1)}, bf16[256,1024]{1,0:T(8,128)(2,1)S(1)}, u32[]{:S(2)}, u32[]{:S(2)}) collective-permute-start(bf16[256,1024]{1,0:T(8,128)(2,1)S(1)} %get-tuple-element.26.late_rows.frames), channel_id=1, source_target_pairs={{0,16},{16,0},{1,17},{17,1},{2,18},{18,2},{3,19},{19,3},{4,20},{20... | collective-permute-start | bytes 1572872 | tf_op jit(solution)/shard_map/ppermute | solution.py:429
  4.5 0.0 collective-permute-done.near.mate
  4.6 1.5 %collective-permute-start.1 = (bf16[128,1024]{1,0:T(8,128)(2,1)S(1)}, bf16[128,1024]{1,0:T(8,128)(2,1)S(1)}, u32[]{:S(2)}, u32[]{:S(2)}) collective-permute-start(bf16[128,1024]{1,0:T(8,128)(2,1)S(1)} %get-tuple-element.28), channel_id=1, source_target_pairs={{0,2},{2,4},{4,6},{6,8},{8,10},{10,12},{12,14},{3,1},{5,3},{7,5},{... | collective-permute-start | bytes 786440 | tf_op jit(solution)/shard_map/ppermute | solution.py:454
  6.1 1.5 %collective-permute-start.2 = (bf16[128,1024]{1,0:T(8,128)(2,1)S(1)}, bf16[128,1024]{1,0:T(8,128)(2,1)S(1)}, u32[]{:S(2)}, u32[]{:S(2)}) collective-permute-start(bf16[128,1024]{1,0:T(8,128)(2,1)S(1)} %get-tuple-element.35), channel_id=1, source_target_pairs={{0,2},{2,4},{4,6},{6,8},{8,10},{10,12},{12,14},{3,1},{5,3},{7,5},{... | collective-permute-start | bytes 786440 | tf_op jit(solution)/shard_map/ppermute | solution.py:455
  7.7 7.2 %near.1 = (bf16[256,512]{1,0:T(8,128)(2,1)S(1)}, f32[256,512]{1,0:T(8,128)S(1)}, f32[256,512]{1,0:T(8,128)S(1)}, f32[256,512]{1,0:T(8,128)S(1)}, bf16[128,1024]{...) custom-call(s32[1,2]{1,0:T(1,128)S(1)} %bitcast.3, ...), custom_call_target="tpu_custom_call" | custom-call | flops 120000000 | bytes 360000 | tf_op jit(solution)/shard_map/near/pallas_call | solution.py:435
  14.9 1.1 %collective-permute-start.3 = (bf16[128,512]{1,0:T(8,128)(2,1)S(1)}, bf16[128,512]{1,0:T(8,128)(2,1)S(1)}, u32[]{:S(2)}, u32[]{:S(2)}) collective-permute-start(bf16[128,512]{1,0:T(8,128)(2,1)S(1)} %get-tuple-element.38.refs_0_), channel_id=1, source_target_pairs={{0,16},{16,0},{1,17},{17,1},{2,18},{18,2},{3,19},{19,3},{4,20},{20... | collective-permute-start | bytes 393224 | tf_op jit(solution)/shard_map/ppermute | solution.py:429
  16.0 0.0 collective-permute-done.1.refs_1_
  16.0 1.2 %far_inner.1 = (bf16[128,512]{1,0:T(8,128)(2,1)S(1)}, bf16[128,1024]{1,0:T(8,128)(2,1)S(1)}) custom-call(f32[2,8,1024]{2,1,0:T(8,128)S(1)} %get-tuple-element.27.refs_0_.refs_1_.held, bf16[128,1024]{1,0:T(8,128)(2,1)S(1)} %collective-permute-done.1.refs_1_, bf16[1024,1536]{1,0:T(8,128)(2,1)S(1)} %copy-done.1, f32[2,64]{1,0:T(2,128)S(1)} %copy-done.6, ...), custom_call_target="tpu_custom_call" | custom-call | flops 40000000 | bytes 120000 | tf_op jit(solution)/shard_map/far_inner/pallas_call | solution.py:435
  17.2 1.1 %collective-permute-start.4 = (bf16[128,512]{1,0:T(8,128)(2,1)S(1)}, bf16[128,512]{1,0:T(8,128)(2,1)S(1)}, u32[]{:S(2)}, u32[]{:S(2)}) collective-permute-start(bf16[128,512]{1,0:T(8,128)(2,1)S(1)} %get-tuple-element.33.inner), channel_id=1, source_target_pairs={{0,16},{16,0},{1,17},{17,1},{2,18},{18,2},{3,19},{19,3},{4,20},{20... | collective-permute-start | bytes 393224 | tf_op jit(solution)/shard_map/ppermute | solution.py:429
  18.3 0.1 collective-permute-done.2.refs_2_
  18.4 1.3 %far_outer.1 = (bf16[128,512]{1,0:T(8,128)(2,1)S(1)}, bf16[128,512]{1,0:T(8,128)(2,1)S(1)}) custom-call(bf16[128,512]{1,0:T(8,128)(2,1)S(1)} %get-tuple-element.34.refs_0_.refs_6_, f32[2,8,1024]{2,1,0:T(8,128)S(1)} %get-tuple-element.27.refs_0_.refs_1_.held, bf16[128,1024]{1,0:T(8,128)(2,1)S(1)} %collective-permute-done.2.refs_2_, ...), custom_call_target="tpu_custom_call" | custom-call | flops 6000000 | bytes 18000 | tf_op jit(solution)/shard_map/far_outer/pallas_call | solution.py:435
  19.7 0.0 copy-start.3
  19.7 1.1 %collective-permute-start.6 = (bf16[128,512]{1,0:T(8,128)(2,1)S(1)}, bf16[128,512]{1,0:T(8,128)(2,1)S(1)}, u32[]{:S(2)}, u32[]{:S(2)}) collective-permute-start(bf16[128,512]{1,0:T(8,128)(2,1)S(1)} %get-tuple-element.37.outer), channel_id=1, source_target_pairs={{0,16},{16,0},{1,17},{17,1},{2,18},{18,2},{3,19},{19,3},{4,20},{20... | collective-permute-start | bytes 393224 | tf_op jit(solution)/shard_map/ppermute | solution.py:429
  20.8 1.0 %collective-permute-start.7 = (bf16[128,512]{1,0:T(8,128)(2,1)S(1)}, bf16[128,512]{1,0:T(8,128)(2,1)S(1)}, u32[]{:S(2)}, u32[]{:S(2)}) collective-permute-start(bf16[128,512]{1,0:T(8,128)(2,1)S(1)} %get-tuple-element.44), channel_id=1, source_target_pairs={{0,16},{16,0},{1,17},{17,1},{2,18},{18,2},{3,19},{19,3},{4,20},{20... | collective-permute-start | bytes 393224 | tf_op jit(solution)/shard_map/ppermute | solution.py:429
  21.8 2.0 %own.1 = (bf16[256,1024]{1,0:T(8,128)(2,1)S(1)}, bf16[256,512]{1,0:T(8,128)(2,1)S(1)}, bf16[256,1024]{1,0:T(8,128)(2,1)S(1)}) custom-call(f32[2,8,1024]{2,1,0:T(8,128)S(1)} %get-tuple-element.27.refs_0_.refs_1_.held, bf16[256,1024]{1,0:T(8,128)(2,1)S(1)} %get-tuple-element.26.late_rows.frames, bf16[128,512]{1,0:T(8,128)(2,1)S(1)} %get-tuple-element.33.inner, ...), custom_call_target="tpu_custom_call" | custom-call | flops 20000000 | bytes 60000 | tf_op jit(solution)/shard_map/own/pallas_call | solution.py:435
  23.8 0.4 %collective-permute-done.4.refs_4_ = bf16[128,512]{1,0:T(8,128)(2,1)S(1)} collective-permute-done((bf16[128,512]{1,0:T(8,128)(2,1)S(1)}, bf16[128,512]{1,0:T(8,128)(2,1)S(1)}, u32[]{:S(2)}, u32[]{:S(2)}) %collective-permute-start.4) | collective-permute-done | bytes 131104 | tf_op jit(solution)/shard_map/ppermute | solution.py:429
  24.2 1.6 %inner.1._.refs_1_ = bf16[128,1024]{1,0:T(8,128)(2,1)S(1)} custom-call(f32[2,8,1024]{2,1,0:T(8,128)S(1)} %get-tuple-element.27.refs_0_.refs_1_.held, bf16[256,1024]{1,0:T(8,128)(2,1)S(1)} %get-tuple-element.39.refs_1_, bf16[256,512]{1,0:T(8,128)(2,1)S(1)} %get-tuple-element.40.refs_2_, bf16[256,1024]{1,0:T(8,128)(2,1)S(1)} %get-tuple-element.41.refs_3_, ...), custom_call_target="tpu_custom_call" | custom-call | flops 40000000 | bytes 120000 | tf_op jit(solution)/shard_map/inner/pallas_call | solution.py:435
  25.8 0.3 %weights.1._.refs_5_ = bf16[2,128,512]{2,1,0:T(8,128)(2,1)S(1)} custom-call(bf16[128,1024]{1,0:T(8,128)(2,1)S(1)} %inner.1._.refs_1_, bf16[128,512]{1,0:T(8,128)(2,1)S(1)} %get-tuple-element.42.query, bf16[128,512]{1,0:T(8,128)(2,1)S(1)} %get-tuple-element.38.refs_0_, bf16[128,512]{1,0:T(8,128)(2,1)S(1)} %collective-permute-done.3.refs_0_.refs_1_), custom_call_target="tpu_custom_call" | custom-call | flops 20000000 | bytes 60000 | tf_op jit(solution)/shard_map/weights/pallas_call | solution.py:435
  26.1 0.9 %collective-permute-done.6.refs_4_ = bf16[128,512]{1,0:T(8,128)(2,1)S(1)} collective-permute-done((bf16[128,512]{1,0:T(8,128)(2,1)S(1)}, bf16[128,512]{1,0:T(8,128)(2,1)S(1)}, u32[]{:S(2)}, u32[]{:S(2)}) %collective-permute-start.6) | collective-permute-done | bytes 131104 | tf_op jit(solution)/shard_map/ppermute | solution.py:429
  27.0 1.6 %outer.1.refs_2_ = bf16[128,1024]{1,0:T(8,128)(2,1)S(1)} custom-call(bf16[2,128,512]{2,1,0:T(8,128)(2,1)S(1)} %weights.1._.refs_5_, f32[2,8,1024]{2,1,0:T(8,128)S(1)} %get-tuple-element.27.refs_0_.refs_1_.held, bf16[256,1024]{1,0:T(8,128)(2,1)S(1)} %get-tuple-element.39.refs_1_, bf16[256,512]{1,0:T(8,128)(2,1)S(1)} %get-tuple-element.40.refs_2_, ...), custom_call_target="tpu_custom_call" | custom-call | flops 40000000 | bytes 120000 | tf_op jit(solution)/shard_map/outer/pallas_call | solution.py:435
  28.6 1.1 %early.1 = bf16[1,384,1024]{2,1,0:T(8,128)(2,1)} custom-call(f32[2,8,1024]{2,1,0:T(8,128)S(1)} %get-tuple-element.27.refs_0_.refs_1_.held, bf16[128,1024]{1,0:T(8,128)(2,1)S(1)} %inner.1._.refs_1_, bf16[128,1024]{1,0:T(8,128)(2,1)S(1)} %outer.1.refs_2_, bf16[512,1024]{1,0:T(8,128)(2,1)S(1)} %copy-done.3, bf16[128,1024]{1,0:T(8,128)(2,1)S(1)} %get-tuple-element.43.refs_4_, ...), custom_call_target="tpu_custom_call" | custom-call | flops 2000000000 | bytes 6000000 | tf_op jit(solution)/shard_map/early/pallas_call | solution.py:435
  (20 shorter events, 0.1 us)
Async XLA Ops:
  0.0 7.7 %copy-start.7 = (s32[2]{0:T(128)S(1)}, s32[2]{0:T(128)}, u32[]{:S(2)}) copy-start(s32[2]{0:T(128)} %param.10) | copy-start | bytes 28
  0.0 7.7 %copy-start.4 = (f32[50,6,1024]{2,0,1:T(8,128)S(1)}, f32[50,6,1024]{2,0,1:T(8,128)}, u32[]{:S(2)}) copy-start(f32[50,6,1024]{2,0,1:T(8,128)} %param.11) | copy-start | bytes 3686404
  0.0 7.7 %copy-start.1 = (bf16[1024,1536]{1,0:T(8,128)(2,1)S(1)}, bf16[1024,1536]{1,0:T(8,128)(2,1)}, u32[]{:S(2)}) copy-start(bf16[1024,1536]{1,0:T(8,128)(2,1)} %refs_3_.4) | copy-start | bytes 9437188
  0.0 7.7 %copy-start.2 = (bf16[512,1024]{1,0:T(8,128)(2,1)S(1)}, bf16[512,1024]{1,0:T(8,128)(2,1)}, u32[]{:S(2)}) copy-start(bf16[512,1024]{1,0:T(8,128)(2,1)} %refs_6_.3) | copy-start | bytes 3145732
  0.0 7.7 %copy-start.6 = (f32[2,64]{1,0:T(2,128)S(1)}, f32[2,64]{1,0:T(2,128)}, u32[]{:S(2)}) copy-start(f32[2,64]{1,0:T(2,128)} %refs_4_.1) | copy-start | bytes 1540
  0.0 7.7 %copy-start = (bf16[1024,1536]{1,0:T(8,128)(2,1)S(1)}, bf16[1024,1536]{1,0:T(8,128)(2,1)}, u32[]{:S(2)}) copy-start(bf16[1024,1536]{1,0:T(8,128)(2,1)} %refs_7_.3) | copy-start | bytes 9437188
  0.0 7.7 %copy-start.5 = (f32[2,64]{1,0:T(2,128)S(1)}, f32[2,64]{1,0:T(2,128)}, u32[]{:S(2)}) copy-start(f32[2,64]{1,0:T(2,128)} %refs_8_.3) | copy-start | bytes 1540
  0.0 4.5 %collective-permute-start = (bf16[1,384,1024]{2,1,0:T(8,128)(2,1)}, bf16[1,384,1024]{2,1,0:T(8,128)(2,1)S(1)}, u32[]{:S(2)}, u32[]{:S(2)}) collective-permute-start(bf16[1,384,1024]{2,1,0:T(8,128)(2,1)} %frames.1), channel_id=1, source_target_pairs={{0,1},{1,0},{2,3},{3,2},{4,5},{5,4},{6,7},{7,6},{8,9},{9,8},{10,11... | collective-permute-start | bytes 2359304 | tf_op jit(solution)/shard_map/ppermute | solution.py:452
  0.6 1.4 %copy-start.8 = (bf16[1,384,1024]{2,1,0:T(8,128)(2,1)S(1)}, bf16[1,384,1024]{2,1,0:T(8,128)(2,1)}, u32[]{:S(2)}) copy-start(bf16[1,384,1024]{2,1,0:T(8,128)(2,1)} %frames.1) | copy-start | bytes 2359300
  2.1 21.7 %collective-permute-start.5 = (bf16[256,1024]{1,0:T(8,128)(2,1)S(1)}, bf16[256,1024]{1,0:T(8,128)(2,1)S(1)}, u32[]{:S(2)}, u32[]{:S(2)}) collective-permute-start(bf16[256,1024]{1,0:T(8,128)(2,1)S(1)} %get-tuple-element.26.late_rows.frames), channel_id=1, source_target_pairs={{0,16},{16,0},{1,17},{17,1},{2,18},{18,2},{3,19},{19,3},{4,20},{20... | collective-permute-start | bytes 1572872 | tf_op jit(solution)/shard_map/ppermute | solution.py:429
  4.6 11.4 %collective-permute-start.1 = (bf16[128,1024]{1,0:T(8,128)(2,1)S(1)}, bf16[128,1024]{1,0:T(8,128)(2,1)S(1)}, u32[]{:S(2)}, u32[]{:S(2)}) collective-permute-start(bf16[128,1024]{1,0:T(8,128)(2,1)S(1)} %get-tuple-element.28), channel_id=1, source_target_pairs={{0,2},{2,4},{4,6},{6,8},{8,10},{10,12},{12,14},{3,1},{5,3},{7,5},{... | collective-permute-start | bytes 786440 | tf_op jit(solution)/shard_map/ppermute | solution.py:454
  6.1 12.3 %collective-permute-start.2 = (bf16[128,1024]{1,0:T(8,128)(2,1)S(1)}, bf16[128,1024]{1,0:T(8,128)(2,1)S(1)}, u32[]{:S(2)}, u32[]{:S(2)}) collective-permute-start(bf16[128,1024]{1,0:T(8,128)(2,1)S(1)} %get-tuple-element.35), channel_id=1, source_target_pairs={{0,2},{2,4},{4,6},{6,8},{8,10},{10,12},{12,14},{3,1},{5,3},{7,5},{... | collective-permute-start | bytes 786440 | tf_op jit(solution)/shard_map/ppermute | solution.py:455
  14.9 6.9 %collective-permute-start.3 = (bf16[128,512]{1,0:T(8,128)(2,1)S(1)}, bf16[128,512]{1,0:T(8,128)(2,1)S(1)}, u32[]{:S(2)}, u32[]{:S(2)}) collective-permute-start(bf16[128,512]{1,0:T(8,128)(2,1)S(1)} %get-tuple-element.38.refs_0_), channel_id=1, source_target_pairs={{0,16},{16,0},{1,17},{17,1},{2,18},{18,2},{3,19},{19,3},{4,20},{20... | collective-permute-start | bytes 393224 | tf_op jit(solution)/shard_map/ppermute | solution.py:429
  17.2 7.0 %collective-permute-start.4 = (bf16[128,512]{1,0:T(8,128)(2,1)S(1)}, bf16[128,512]{1,0:T(8,128)(2,1)S(1)}, u32[]{:S(2)}, u32[]{:S(2)}) collective-permute-start(bf16[128,512]{1,0:T(8,128)(2,1)S(1)} %get-tuple-element.33.inner), channel_id=1, source_target_pairs={{0,16},{16,0},{1,17},{17,1},{2,18},{18,2},{3,19},{19,3},{4,20},{20... | collective-permute-start | bytes 393224 | tf_op jit(solution)/shard_map/ppermute | solution.py:429
  19.7 4.5 %copy-start.3 = (bf16[512,1024]{1,0:T(8,128)(2,1)S(1)}, bf16[512,1024]{1,0:T(8,128)(2,1)}, u32[]{:S(2)}) copy-start(bf16[512,1024]{1,0:T(8,128)(2,1)} %refs_3_.5) | copy-start | bytes 3145732
  19.7 7.3 %collective-permute-start.6 = (bf16[128,512]{1,0:T(8,128)(2,1)S(1)}, bf16[128,512]{1,0:T(8,128)(2,1)S(1)}, u32[]{:S(2)}, u32[]{:S(2)}) collective-permute-start(bf16[128,512]{1,0:T(8,128)(2,1)S(1)} %get-tuple-element.37.outer), channel_id=1, source_target_pairs={{0,16},{16,0},{1,17},{17,1},{2,18},{18,2},{3,19},{19,3},{4,20},{20... | collective-permute-start | bytes 393224 | tf_op jit(solution)/shard_map/ppermute | solution.py:429
  20.8 7.8 %collective-permute-start.7 = (bf16[128,512]{1,0:T(8,128)(2,1)S(1)}, bf16[128,512]{1,0:T(8,128)(2,1)S(1)}, u32[]{:S(2)}, u32[]{:S(2)}) collective-permute-start(bf16[128,512]{1,0:T(8,128)(2,1)S(1)} %get-tuple-element.44), channel_id=1, source_target_pairs={{0,16},{16,0},{1,17},{17,1},{2,18},{18,2},{3,19},{19,3},{4,20},{20... | collective-permute-start | bytes 393224 | tf_op jit(solution)/shard_map/ppermute | solution.py:429

commit v12 on v11

--- a/solution.py
+++ b/solution.py
@@ -167,10 +167,8 @@
         copy.wait()
 
 
-def mate_kernel(mate, outer_rows, inner_rows):
-    _, _, inner, outer = places(mate.shape[1])
-    outer_rows[...] = mate[0, pl.ds(outer, BLOCK)]
-    inner_rows[...] = mate[0, inner : inner + BLOCK]
+def mate_kernel(mate, outer_rows):
+    outer_rows[...] = mate[0, pl.ds(places(mate.shape[1])[3], BLOCK)]
 
 
 def part_steps(block, query, kv, part_out, part_sum, part_top):
@@ -190,9 +188,8 @@
         yield
 
 
-def near_kernel(
-    timestep, modulation, early_rows, late_rows, near, qkv_self, gains, out_self, qkv_cross, gains_cross,
-    query, part_out, part_sum, part_top, first, first_q, first_k, first_v, held, kv,
+def qkv_kernel(
+    timestep, modulation, early_rows, late_rows, near, qkv_self, gains, query, kv, mate_kv, held
 ):
     rows = near.shape[1]
 
@@ -235,12 +232,20 @@
             queries.append(head_norm(raw[0], q_gain, ones))
         kv[at, :HW] = head_norm(raw[-2], k_gain, ones)
         kv[at, HW:] = raw[-1].astype(BF16)
-    query[:BLOCK] = queries[1]
-    query[BLOCK:] = queries[2]
+    for n, each in enumerate(queries):
+        query[n] = each
+    mate_kv[...] = kv[pl.ds(pl.multiple_of((1 - parity) * (rows + BLOCK), BLOCK), BLOCK)]
     for k in range(1, held.shape[0]):
         hold(k)
 
-    parts = [part_steps(n, queries[n + 1], kv, part_out, part_sum, part_top) for n in range(2)]
+
+def near_kernel(
+    _, held, early_rows, query, kv, out_self, qkv_cross, gains_cross,
+    part_out, part_sum, part_top, first, first_q, first_k, first_v,
+):
+    mods = mods_held(held, 0)
+    ones = head_ones()
+    parts = [part_steps(n, query.at[n + 1], kv, part_out, part_sum, part_top) for n in range(2)]
 
     def meanwhile(steps):
         while steps and parts:
@@ -249,10 +254,10 @@
             else:
                 steps -= 1
 
-    bias = window_bias(rows + HALF, 0)
+    bias = window_bias(kv.shape[0], 0)
     attended = []
     for cols in SLABS:
-        scores = window_scores(queries[0][:, cols], kv[:, cols], bias)
+        scores = window_scores(query[0, :, cols], kv[:, cols], bias)
         meanwhile(2)
         powers, _ = raised(scores)
         out, total = weighted(powers, kv[:, HW + cols.start : HW + cols.stop])
@@ -288,7 +293,7 @@
 
 def far_attend(block, bias, query, keys, values, part_out, part_sum, part_top, attended):
     to = slice(block * BLOCK, (block + 1) * BLOCK)
-    scores = [window_scores(query[to, cols], keys[:, cols], bias) for cols in SLABS]
+    scores = [window_scores(query[block + 1, :, cols], keys[:, cols], bias) for cols in SLABS]
     powers = [raised(each) for each in scores]
     sums = [weighted(each, values[:, cols]) for (each, _), cols in zip(powers, SLABS)]
     for cols, (_, top), (out, summed) in zip(SLABS, powers, sums):
@@ -308,12 +313,11 @@
     kv[:, :HW], kv[:, HW:] = keys, values
 
 
-def far_outer_kernel(rows, early_values, held, far, qkv_self, gains, query, *refs):
+def far_outer_kernel(rows, early_values, far_kv, query, *refs):
     *parts, kv, attended, passed = refs
     passed[...] = early_values[...]
-    keys, values = far_keys(far[...], held, qkv_self, gains)
-    keys = jnp.concatenate([kv[:, :HW], keys], axis=0)
-    values = jnp.concatenate([kv[:, HW:], values], axis=0)
+    keys = jnp.concatenate([kv[:, :HW], far_kv[:, :HW]], axis=0)
+    values = jnp.concatenate([kv[:, HW:], far_kv[:, HW:]], axis=0)
     start = lax.rem(lax.axis_index("tm"), 2) * HALF
     bias = [far_bias(rows, start, outermost) for outermost in (False, True)]
     far_attend(0, jnp.concatenate(bias, axis=1), query, keys, values, *parts, attended)
@@ -450,16 +454,20 @@
     )
     their_frames = to_stems(late_rows)
     near = lax.ppermute(frames, "tm", inside)
-    mate_outer, mate_inner = call(mate_kernel, "mate", 0.1, (half, half), near)
+    mate_outer = call(mate_kernel, "mate", 0.1, half, near)
     far = lax.ppermute(mate_outer, "tm", across)
-    farther = lax.ppermute(mate_inner, "tm", across)
 
     late, block, part = shape(HALF, HW), shape(BLOCK, HW), shape(HALF, HW, dtype=F32)
-    query, part_out, part_sum, part_top, first_early, q_early, k_early, v_early, held = call(
-        near_kernel, "near", 0.12,
-        (late, part, part, part, half, block, block, block, shape(stems, 8, D, dtype=F32)),
-        timestep.reshape(1, -1), modulation, early_rows, late_rows, near, qkv_self, qk_gain_self, out_self, qkv_cross, qk_gain_cross,
-        scratch=[pltpu.VMEM((rows + HALF, 2 * HW), BF16)],
+    query, kv, mate_kv, held = call(
+        qkv_kernel, "qkv", 0.06,
+        (shape(3, BLOCK, HW), shape(rows + HALF, 2 * HW), half, shape(stems, 8, D, dtype=F32)),
+        timestep.reshape(1, -1), modulation, early_rows, late_rows, near, qkv_self, qk_gain_self,
+    )
+    farther = lax.ppermute(mate_kv, "tm", across)
+    part_out, part_sum, part_top, first_early, q_early, k_early, v_early = call(
+        near_kernel, "near", 0.06, (part, part, part, half, block, block, block),
+        mate_kv, held, early_rows, query, kv, out_self, qkv_cross, qk_gain_cross,
+        in_specs=[ANY] + [VMEM] * 7,
     )
     their_keys = to_stems(k_early)
     parts = (part_out, part_sum, part_top)
@@ -472,7 +480,7 @@
     others_inner = to_stems(att_inner)
     att_outer, passed = call(
         lambda *refs: far_outer_kernel(rows, *refs), "far_outer", 0.006, (block, block),
-        v_early, held, farther, *self_weights, query, *parts, far_kv,
+        v_early, farther, query, *parts, far_kv,
     )
     others_outer = to_stems(att_outer)
     their_values = to_stems(passed)

time: 29.8 us -> 30.5 us (1.023)
  starting transfers between devices: 10.3 us -> 10.8 us
  waiting for transfers between devices: 1.44 us -> 1.91 us
    ppermute x5, waiting for transfers between devices: 1.29 us -> 1.9 us  [to_stems(): lax.ppermute(array, 'stem', [(i, (i + k) % stems) for i in range(stems)])]
    pallas_call x10 -> x11, Pallas kernels: 16.3 us -> 16.2 us  [call(): pl.pallas_call(kernel, out_shape=outs, in_specs=in_specs or [VMEM] * len(...]
  transfers between devices with their start and end apart: 8 -> 8, of which waited for: 3 -> 3; matrix products, arithmetic and copies ran while one was open for 0% -> 0% of each run, Pallas kernels for 51% -> 50%
where the time goes in v12:
time: 30.5 us; the launch traced here: 30.3 us
  Pallas kernels  16.2 us (53%)
  starting transfers between devices  10.8 us (35%)
  waiting for transfers between devices  1.91 us (6%)
  local copies, waits for them, and re-layouts  1.17 us (4%)
    pallas_call x11, Pallas kernels, call(): pl.pallas_call(kernel, out_shape=outs, in_specs=in_specs or [VMEM] * len(...  16.2 us
    ppermute x5, starting transfers between devices, to_stems(): lax.ppermute(array, 'stem', [(i, (i + k) % stems) for i in range(stems)])  6.93 us
    ppermute x5, waiting for transfers between devices, to_stems(): lax.ppermute(array, 'stem', [(i, (i + k) % stems) for i in range(stems)])  1.9 us
    ppermute x1, starting transfers between devices, on_device(): farther = lax.ppermute(mate_kv, 'tm', across)  1.78 us
    ppermute x1, starting transfers between devices, on_device(): far = lax.ppermute(mate_outer, 'tm', across)  1.55 us
    unnamed x18, local copies, waits for them, and re-layouts  1.17 us
  transfers between devices with their start and end apart: 8, of which 3 were waited for; matrix products, arithmetic and copies ran while one was open for 0% of the time, Pallas kernels for 50%

profile of v12, /device:TPU:0, one launch (start us, length us, event | category | flops | bytes accessed | tf_op | source)
XLA Modules:
  0.0 30.3 jit_solution(362374575586803109)
XLA Ops:
  0.0 0.5 %collective-permute-start = (bf16[1,384,1024]{2,1,0:T(8,128)(2,1)}, bf16[1,384,1024]{2,1,0:T(8,128)(2,1)S(1)}, u32[]{:S(2)}, u32[]{:S(2)}) collective-permute-start(bf16[1,384,1024]{2,1,0:T(8,128)(2,1)} %frames.1), channel_id=1, source_target_pairs={{0,1},{1,0},{2,3},{3,2},{4,5},{5,4},{6,7},{7,6},{8,9},{9,8},{10,11... | collective-permute-start | bytes 2359304 | tf_op jit(solution)/shard_map/ppermute | solution.py:456
  0.5 1.1 %copy-done.8 = bf16[1,384,1024]{2,1,0:T(8,128)(2,1)S(1)} copy-done((bf16[1,384,1024]{2,1,0:T(8,128)(2,1)S(1)}, bf16[1,384,1024]{2,1,0:T(8,128)(2,1)}, u32[]{:S(2)}) %copy-start.8) | copy-done | bytes 786456
  1.7 0.1 split.1
  1.8 2.7 %collective-permute-start.5 = (bf16[256,1024]{1,0:T(8,128)(2,1)S(1)}, bf16[256,1024]{1,0:T(8,128)(2,1)S(1)}, u32[]{:S(2)}, u32[]{:S(2)}) collective-permute-start(bf16[256,1024]{1,0:T(8,128)(2,1)S(1)} %get-tuple-element.26.late_rows.frames), channel_id=1, source_target_pairs={{0,16},{16,0},{1,17},{17,1},{2,18},{18,2},{3,19},{19,3},{4,20},{20... | collective-permute-start | bytes 1572872 | tf_op jit(solution)/shard_map/ppermute | solution.py:433
  4.5 0.0 copy-start.5
  4.5 1.5 %collective-permute-start.1 = (bf16[128,1024]{1,0:T(8,128)(2,1)S(1)}, bf16[128,1024]{1,0:T(8,128)(2,1)S(1)}, u32[]{:S(2)}, u32[]{:S(2)}) collective-permute-start(bf16[128,1024]{1,0:T(8,128)(2,1)S(1)} %mate.1), channel_id=1, source_target_pairs={{0,2},{2,4},{4,6},{6,8},{8,10},{10,12},{12,14},{3,1},{5,3},{7,5},{... | collective-permute-start | bytes 786440 | tf_op jit(solution)/shard_map/ppermute | solution.py:458
  6.1 3.5 %qkv.1 = (bf16[3,128,512]{2,1,0:T(8,128)(2,1)S(1)}, bf16[640,1024]{1,0:T(8,128)(2,1)S(1)}, bf16[128,1024]{1,0:T(8,128)(2,1)S(1)}, f32[2,8,1024]{2,1,0:T(8,128)S(1)}) custom-call(s32[1,2]{1,0:T(1,128)S(1)} %bitcast.3, f32[6,50,1024]{2,1,0:T(8,128)S(1)} %bitcast.2, bf16[128,1024]{1,0:T(8,128)(2,1)S(1)} %get-tuple-element.25.early_rows, ...), custom_call_target="tpu_custom_call" | custom-call | flops 60000000 | bytes 180000 | tf_op jit(solution)/shard_map/qkv/pallas_call | solution.py:439
  9.6 1.8 %collective-permute-start.2 = (bf16[128,1024]{1,0:T(8,128)(2,1)S(1)}, bf16[128,1024]{1,0:T(8,128)(2,1)S(1)}, u32[]{:S(2)}, u32[]{:S(2)}) collective-permute-start(bf16[128,1024]{1,0:T(8,128)(2,1)S(1)} %get-tuple-element.29._), channel_id=1, source_target_pairs={{0,2},{2,4},{4,6},{6,8},{8,10},{10,12},{12,14},{3,1},{5,3},{7,5},{... | collective-permute-start | bytes 786440 | tf_op jit(solution)/shard_map/ppermute | solution.py:466
  11.4 4.2 %near.1 = (f32[256,512]{1,0:T(8,128)S(1)}, f32[256,512]{1,0:T(8,128)S(1)}, f32[256,512]{1,0:T(8,128)S(1)}, bf16[128,1024]{1,0:T(8,128)(2,1)S(1)}, bf16[128,512]{...) custom-call(bf16[128,1024]{1,0:T(8,128)(2,1)S(1)} %get-tuple-element.29._, ...), custom_call_target="tpu_custom_call" | custom-call | flops 60000000 | bytes 180000 | tf_op jit(solution)/shard_map/near/pallas_call | solution.py:439
  15.6 1.2 %collective-permute-start.3 = (bf16[128,512]{1,0:T(8,128)(2,1)S(1)}, bf16[128,512]{1,0:T(8,128)(2,1)S(1)}, u32[]{:S(2)}, u32[]{:S(2)}) collective-permute-start(bf16[128,512]{1,0:T(8,128)(2,1)S(1)} %get-tuple-element.38.refs_0_), channel_id=1, source_target_pairs={{0,16},{16,0},{1,17},{17,1},{2,18},{18,2},{3,19},{19,3},{4,20},{20... | collective-permute-start | bytes 393224 | tf_op jit(solution)/shard_map/ppermute | solution.py:433
  16.7 1.2 %far_inner.1 = (bf16[128,512]{1,0:T(8,128)(2,1)S(1)}, bf16[128,1024]{1,0:T(8,128)(2,1)S(1)}) custom-call(f32[2,8,1024]{2,1,0:T(8,128)S(1)} %get-tuple-element.27.held.refs_0_, bf16[128,1024]{1,0:T(8,128)(2,1)S(1)} %collective-permute-done.1.refs_1_, bf16[1024,1536]{1,0:T(8,128)(2,1)S(1)} %copy-done.2, f32[2,64]{1,0:T(2,128)S(1)} %copy-done.6, ...), custom_call_target="tpu_custom_call" | custom-call | flops 40000000 | bytes 120000 | tf_op jit(solution)/shard_map/far_inner/pallas_call | solution.py:439
  18.0 1.0 %collective-permute-start.4 = (bf16[128,512]{1,0:T(8,128)(2,1)S(1)}, bf16[128,512]{1,0:T(8,128)(2,1)S(1)}, u32[]{:S(2)}, u32[]{:S(2)}) collective-permute-start(bf16[128,512]{1,0:T(8,128)(2,1)S(1)} %get-tuple-element.34.inner), channel_id=1, source_target_pairs={{0,16},{16,0},{1,17},{17,1},{2,18},{18,2},{3,19},{19,3},{4,20},{20... | collective-permute-start | bytes 393224 | tf_op jit(solution)/shard_map/ppermute | solution.py:433
  19.0 0.6 %far_outer.1 = (bf16[128,512]{1,0:T(8,128)(2,1)S(1)}, bf16[128,512]{1,0:T(8,128)(2,1)S(1)}) custom-call(bf16[128,512]{1,0:T(8,128)(2,1)S(1)} %get-tuple-element.35.refs_0_.refs_6_, bf16[128,1024]{1,0:T(8,128)(2,1)S(1)} %collective-permute-done.2.refs_1_, bf16[3,128,512]{2,1,0:T(8,128)(2,1)S(1)} %get-tuple-element.28.query.refs_4_.refs_2_, ...), custom_call_target="tpu_custom_call" | custom-call | flops 6000000 | bytes 18000 | tf_op jit(solution)/shard_map/far_outer/pallas_call | solution.py:439
  19.6 0.0 copy-start.3
  19.6 1.2 %collective-permute-start.6 = (bf16[128,512]{1,0:T(8,128)(2,1)S(1)}, bf16[128,512]{1,0:T(8,128)(2,1)S(1)}, u32[]{:S(2)}, u32[]{:S(2)}) collective-permute-start(bf16[128,512]{1,0:T(8,128)(2,1)S(1)} %get-tuple-element.37.outer), channel_id=1, source_target_pairs={{0,16},{16,0},{1,17},{17,1},{2,18},{18,2},{3,19},{19,3},{4,20},{20... | collective-permute-start | bytes 393224 | tf_op jit(solution)/shard_map/ppermute | solution.py:433
  20.8 0.9 %collective-permute-start.7 = (bf16[128,512]{1,0:T(8,128)(2,1)S(1)}, bf16[128,512]{1,0:T(8,128)(2,1)S(1)}, u32[]{:S(2)}, u32[]{:S(2)}) collective-permute-start(bf16[128,512]{1,0:T(8,128)(2,1)S(1)} %get-tuple-element.44), channel_id=1, source_target_pairs={{0,16},{16,0},{1,17},{17,1},{2,18},{18,2},{3,19},{19,3},{4,20},{20... | collective-permute-start | bytes 393224 | tf_op jit(solution)/shard_map/ppermute | solution.py:433
  21.7 0.2 collective-permute-done.3.refs_0_.refs_1_
  21.9 2.0 %own.1 = (bf16[256,1024]{1,0:T(8,128)(2,1)S(1)}, bf16[256,512]{1,0:T(8,128)(2,1)S(1)}, bf16[256,1024]{1,0:T(8,128)(2,1)S(1)}) custom-call(f32[2,8,1024]{2,1,0:T(8,128)S(1)} %get-tuple-element.27.held.refs_0_, bf16[256,1024]{1,0:T(8,128)(2,1)S(1)} %get-tuple-element.26.late_rows.frames, bf16[128,512]{1,0:T(8,128)(2,1)S(1)} %get-tuple-element.34.inner, ...), custom_call_target="tpu_custom_call" | custom-call | flops 20000000 | bytes 60000 | tf_op jit(solution)/shard_map/own/pallas_call | solution.py:439
  23.9 0.8 %collective-permute-done.4.refs_4_ = bf16[128,512]{1,0:T(8,128)(2,1)S(1)} collective-permute-done((bf16[128,512]{1,0:T(8,128)(2,1)S(1)}, bf16[128,512]{1,0:T(8,128)(2,1)S(1)}, u32[]{:S(2)}, u32[]{:S(2)}) %collective-permute-start.4) | collective-permute-done | bytes 131104 | tf_op jit(solution)/shard_map/ppermute | solution.py:433
  24.7 1.5 %inner.1._.refs_1_ = bf16[128,1024]{1,0:T(8,128)(2,1)S(1)} custom-call(f32[2,8,1024]{2,1,0:T(8,128)S(1)} %get-tuple-element.27.held.refs_0_, bf16[256,1024]{1,0:T(8,128)(2,1)S(1)} %get-tuple-element.39.refs_1_, bf16[256,512]{1,0:T(8,128)(2,1)S(1)} %get-tuple-element.40.refs_2_, bf16[256,1024]{1,0:T(8,128)(2,1)S(1)} %get-tuple-element.41.refs_3_, ...), custom_call_target="tpu_custom_call" | custom-call | flops 40000000 | bytes 120000 | tf_op jit(solution)/shard_map/inner/pallas_call | solution.py:439
  26.3 0.3 %weights.1._.refs_5_ = bf16[2,128,512]{2,1,0:T(8,128)(2,1)S(1)} custom-call(bf16[128,1024]{1,0:T(8,128)(2,1)S(1)} %inner.1._.refs_1_, bf16[128,512]{1,0:T(8,128)(2,1)S(1)} %get-tuple-element.42.query, bf16[128,512]{1,0:T(8,128)(2,1)S(1)} %get-tuple-element.38.refs_0_, bf16[128,512]{1,0:T(8,128)(2,1)S(1)} %collective-permute-done.3.refs_0_.refs_1_), custom_call_target="tpu_custom_call" | custom-call | flops 20000000 | bytes 60000 | tf_op jit(solution)/shard_map/weights/pallas_call | solution.py:439
  26.6 0.9 %collective-permute-done.6.refs_4_ = bf16[128,512]{1,0:T(8,128)(2,1)S(1)} collective-permute-done((bf16[128,512]{1,0:T(8,128)(2,1)S(1)}, bf16[128,512]{1,0:T(8,128)(2,1)S(1)}, u32[]{:S(2)}, u32[]{:S(2)}) %collective-permute-start.6) | collective-permute-done | bytes 131104 | tf_op jit(solution)/shard_map/ppermute | solution.py:433
  27.5 1.6 %outer.1.refs_2_ = bf16[128,1024]{1,0:T(8,128)(2,1)S(1)} custom-call(bf16[2,128,512]{2,1,0:T(8,128)(2,1)S(1)} %weights.1._.refs_5_, f32[2,8,1024]{2,1,0:T(8,128)S(1)} %get-tuple-element.27.held.refs_0_, bf16[256,1024]{1,0:T(8,128)(2,1)S(1)} %get-tuple-element.39.refs_1_, bf16[256,512]{1,0:T(8,128)(2,1)S(1)} %get-tuple-element.40.refs_2_, ...), custom_call_target="tpu_custom_call" | custom-call | flops 40000000 | bytes 120000 | tf_op jit(solution)/shard_map/outer/pallas_call | solution.py:439
  29.1 1.1 %early.1 = bf16[1,384,1024]{2,1,0:T(8,128)(2,1)} custom-call(f32[2,8,1024]{2,1,0:T(8,128)S(1)} %get-tuple-element.27.held.refs_0_, bf16[128,1024]{1,0:T(8,128)(2,1)S(1)} %inner.1._.refs_1_, bf16[128,1024]{1,0:T(8,128)(2,1)S(1)} %outer.1.refs_2_, bf16[512,1024]{1,0:T(8,128)(2,1)S(1)} %copy-done.3, bf16[128,1024]{1,0:T(8,128)(2,1)S(1)} %get-tuple-element.43.refs_4_, ...), custom_call_target="tpu_custom_call" | custom-call | flops 2000000000 | bytes 6000000 | tf_op jit(solution)/shard_map/early/pallas_call | solution.py:439
  (21 shorter events, 0.1 us)
Async XLA Ops:
  0.0 6.1 %copy-start.7 = (s32[2]{0:T(128)S(1)}, s32[2]{0:T(128)}, u32[]{:S(2)}) copy-start(s32[2]{0:T(128)} %param.10) | copy-start | bytes 28
  0.0 6.1 %copy-start.4 = (f32[50,6,1024]{2,0,1:T(8,128)S(1)}, f32[50,6,1024]{2,0,1:T(8,128)}, u32[]{:S(2)}) copy-start(f32[50,6,1024]{2,0,1:T(8,128)} %param.11) | copy-start | bytes 3686404
  0.0 6.1 %copy-start.6 = (f32[2,64]{1,0:T(2,128)S(1)}, f32[2,64]{1,0:T(2,128)}, u32[]{:S(2)}) copy-start(f32[2,64]{1,0:T(2,128)} %refs_3_.2) | copy-start | bytes 1540
  0.0 4.4 %collective-permute-start = (bf16[1,384,1024]{2,1,0:T(8,128)(2,1)}, bf16[1,384,1024]{2,1,0:T(8,128)(2,1)S(1)}, u32[]{:S(2)}, u32[]{:S(2)}) collective-permute-start(bf16[1,384,1024]{2,1,0:T(8,128)(2,1)} %frames.1), channel_id=1, source_target_pairs={{0,1},{1,0},{2,3},{3,2},{4,5},{5,4},{6,7},{7,6},{8,9},{9,8},{10,11... | collective-permute-start | bytes 2359304 | tf_op jit(solution)/shard_map/ppermute | solution.py:456
  0.5 1.1 %copy-start.8 = (bf16[1,384,1024]{2,1,0:T(8,128)(2,1)S(1)}, bf16[1,384,1024]{2,1,0:T(8,128)(2,1)}, u32[]{:S(2)}) copy-start(bf16[1,384,1024]{2,1,0:T(8,128)(2,1)} %frames.1) | copy-start | bytes 2359300
  1.7 4.4 %copy-start.2 = (bf16[1024,1536]{1,0:T(8,128)(2,1)S(1)}, bf16[1024,1536]{1,0:T(8,128)(2,1)}, u32[]{:S(2)}) copy-start(bf16[1024,1536]{1,0:T(8,128)(2,1)} %refs_2_.1) | copy-start | bytes 9437188
  1.8 22.1 %collective-permute-start.5 = (bf16[256,1024]{1,0:T(8,128)(2,1)S(1)}, bf16[256,1024]{1,0:T(8,128)(2,1)S(1)}, u32[]{:S(2)}, u32[]{:S(2)}) collective-permute-start(bf16[256,1024]{1,0:T(8,128)(2,1)S(1)} %get-tuple-element.26.late_rows.frames), channel_id=1, source_target_pairs={{0,16},{16,0},{1,17},{17,1},{2,18},{18,2},{3,19},{19,3},{4,20},{20... | collective-permute-start | bytes 1572872 | tf_op jit(solution)/shard_map/ppermute | solution.py:433
  4.5 6.9 %copy-start = (bf16[1024,1536]{1,0:T(8,128)(2,1)S(1)}, bf16[1024,1536]{1,0:T(8,128)(2,1)}, u32[]{:S(2)}) copy-start(bf16[1024,1536]{1,0:T(8,128)(2,1)} %refs_7_.3) | copy-start | bytes 9437188
  4.5 6.9 %copy-start.1 = (bf16[512,1024]{1,0:T(8,128)(2,1)S(1)}, bf16[512,1024]{1,0:T(8,128)(2,1)}, u32[]{:S(2)}) copy-start(bf16[512,1024]{1,0:T(8,128)(2,1)} %refs_6_.3) | copy-start | bytes 3145732
  4.5 6.9 %copy-start.5 = (f32[2,64]{1,0:T(2,128)S(1)}, f32[2,64]{1,0:T(2,128)}, u32[]{:S(2)}) copy-start(f32[2,64]{1,0:T(2,128)} %refs_8_.3) | copy-start | bytes 1540
  4.5 12.2 %collective-permute-start.1 = (bf16[128,1024]{1,0:T(8,128)(2,1)S(1)}, bf16[128,1024]{1,0:T(8,128)(2,1)S(1)}, u32[]{:S(2)}, u32[]{:S(2)}) collective-permute-start(bf16[128,1024]{1,0:T(8,128)(2,1)S(1)} %mate.1), channel_id=1, source_target_pairs={{0,2},{2,4},{4,6},{6,8},{8,10},{10,12},{12,14},{3,1},{5,3},{7,5},{... | collective-permute-start | bytes 786440 | tf_op jit(solution)/shard_map/ppermute | solution.py:458
  9.6 9.4 %collective-permute-start.2 = (bf16[128,1024]{1,0:T(8,128)(2,1)S(1)}, bf16[128,1024]{1,0:T(8,128)(2,1)S(1)}, u32[]{:S(2)}, u32[]{:S(2)}) collective-permute-start(bf16[128,1024]{1,0:T(8,128)(2,1)S(1)} %get-tuple-element.29._), channel_id=1, source_target_pairs={{0,2},{2,4},{4,6},{6,8},{8,10},{10,12},{12,14},{3,1},{5,3},{7,5},{... | collective-permute-start | bytes 786440 | tf_op jit(solution)/shard_map/ppermute | solution.py:466
  15.6 6.3 %collective-permute-start.3 = (bf16[128,512]{1,0:T(8,128)(2,1)S(1)}, bf16[128,512]{1,0:T(8,128)(2,1)S(1)}, u32[]{:S(2)}, u32[]{:S(2)}) collective-permute-start(bf16[128,512]{1,0:T(8,128)(2,1)S(1)} %get-tuple-element.38.refs_0_), channel_id=1, source_target_pairs={{0,16},{16,0},{1,17},{17,1},{2,18},{18,2},{3,19},{19,3},{4,20},{20... | collective-permute-start | bytes 393224 | tf_op jit(solution)/shard_map/ppermute | solution.py:433
  18.0 6.7 %collective-permute-start.4 = (bf16[128,512]{1,0:T(8,128)(2,1)S(1)}, bf16[128,512]{1,0:T(8,128)(2,1)S(1)}, u32[]{:S(2)}, u32[]{:S(2)}) collective-permute-start(bf16[128,512]{1,0:T(8,128)(2,1)S(1)} %get-tuple-element.34.inner), channel_id=1, source_target_pairs={{0,16},{16,0},{1,17},{17,1},{2,18},{18,2},{3,19},{19,3},{4,20},{20... | collective-permute-start | bytes 393224 | tf_op jit(solution)/shard_map/ppermute | solution.py:433
  19.6 5.1 %copy-start.3 = (bf16[512,1024]{1,0:T(8,128)(2,1)S(1)}, bf16[512,1024]{1,0:T(8,128)(2,1)}, u32[]{:S(2)}) copy-start(bf16[512,1024]{1,0:T(8,128)(2,1)} %refs_3_.3) | copy-start | bytes 3145732
  19.6 7.9 %collective-permute-start.6 = (bf16[128,512]{1,0:T(8,128)(2,1)S(1)}, bf16[128,512]{1,0:T(8,128)(2,1)S(1)}, u32[]{:S(2)}, u32[]{:S(2)}) collective-permute-start(bf16[128,512]{1,0:T(8,128)(2,1)S(1)} %get-tuple-element.37.outer), channel_id=1, source_target_pairs={{0,16},{16,0},{1,17},{17,1},{2,18},{18,2},{3,19},{19,3},{4,20},{20... | collective-permute-start | bytes 393224 | tf_op jit(solution)/shard_map/ppermute | solution.py:433
  20.8 8.3 %collective-permute-start.7 = (bf16[128,512]{1,0:T(8,128)(2,1)S(1)}, bf16[128,512]{1,0:T(8,128)(2,1)S(1)}, u32[]{:S(2)}, u32[]{:S(2)}) collective-permute-start(bf16[128,512]{1,0:T(8,128)(2,1)S(1)} %get-tuple-element.44), channel_id=1, source_target_pairs={{0,16},{16,0},{1,17},{17,1},{2,18},{18,2},{3,19},{19,3},{4,20},{20... | collective-permute-start | bytes 393224 | tf_op jit(solution)/shard_map/ppermute | solution.py:433

commit v13 on v12

--- a/solution.py
+++ b/solution.py
@@ -313,9 +313,8 @@
     kv[:, :HW], kv[:, HW:] = keys, values
 
 
-def far_outer_kernel(rows, early_values, far_kv, query, *refs):
-    *parts, kv, attended, passed = refs
-    passed[...] = early_values[...]
+def far_outer_kernel(rows, far_kv, query, *refs):
+    *parts, kv, attended = refs
     keys = jnp.concatenate([kv[:, :HW], far_kv[:, :HW]], axis=0)
     values = jnp.concatenate([kv[:, HW:], far_kv[:, HW:]], axis=0)
     start = lax.rem(lax.axis_index("tm"), 2) * HALF
@@ -341,8 +340,9 @@
     return (first.astype(F32) + gate * out.astype(F32)).astype(BF16)
 
 
-def own_kernel(held, frames, inner, outer, out_self, qkv_cross, gains, *refs):
-    first, query, kv = refs[-3:]
+def own_kernel(early_values, held, frames, inner, outer, out_self, qkv_cross, gains, *refs):
+    first, query, kv, passed = refs[-4:]
+    passed[...] = early_values[...]
     mods = mods_held(held, 0)
     ones = head_ones()
     parts = [slice(0, BLOCK), slice(BLOCK, HALF)]
@@ -478,19 +478,19 @@
         held, far, *self_weights, query, *parts,
     )
     others_inner = to_stems(att_inner)
-    att_outer, passed = call(
-        lambda *refs: far_outer_kernel(rows, *refs), "far_outer", 0.006, (block, block),
-        v_early, farther, query, *parts, far_kv,
+    att_outer = call(
+        lambda *refs: far_outer_kernel(rows, *refs), "far_outer", 0.006, block,
+        farther, query, *parts, far_kv,
     )
     others_outer = to_stems(att_outer)
+
+    weights = (out_self, qkv_cross, qk_gain_cross)
+    *own, passed = call(
+        own_kernel, "own", 0.02, (shape(HALF, D), late, shape(HALF, D), block),
+        v_early, held, late_rows, att_inner, att_outer, *weights, *their_keys,
+        in_specs=[VMEM] * 8 + [ANY] * (stems - 1),
+    )
     their_values = to_stems(passed)
-
-    weights = (out_self, qkv_cross, qk_gain_cross)
-    own = call(
-        own_kernel, "own", 0.02, (shape(HALF, D), late, shape(HALF, D)),
-        held, late_rows, att_inner, att_outer, *weights, *their_keys,
-        in_specs=[VMEM] * 7 + [ANY] * (stems - 1),
-    )
     inner_out = call(
         lambda *refs: late_kernel(1, stems, *refs), "inner", 0.04, half,
         held, *own, *others_inner, *their_frames, *weights, out_cross,

time: 30.5 us -> 30.4 us (level)
  waiting for transfers between devices: 1.91 us -> 1.51 us
  starting transfers between devices: 10.8 us -> 11.2 us
    ppermute x5, waiting for transfers between devices: 1.9 us -> 1.51 us  [to_stems(): lax.ppermute(array, 'stem', [(i, (i + k) % stems) for i in range(stems)])]
    ppermute x5, starting transfers between devices: 6.93 us -> 7.3 us  [to_stems(): lax.ppermute(array, 'stem', [(i, (i + k) % stems) for i in range(stems)])]
  transfers between devices with their start and end apart: 8 -> 8, of which waited for: 3 -> 2; matrix products, arithmetic and copies ran while one was open for 0% -> 0% of each run, Pallas kernels for 50% -> 50%
where the time goes in v13:
time: 30.4 us; the launch traced here: 30.3 us
  Pallas kernels  16.2 us (53%)
  starting transfers between devices  11.2 us (37%)
  waiting for transfers between devices  1.51 us (5%)
  local copies, waits for them, and re-layouts  1.17 us (4%)
    pallas_call x11, Pallas kernels, call(): pl.pallas_call(kernel, out_shape=outs, in_specs=in_specs or [VMEM] * len(...  16.2 us
    ppermute x5, starting transfers between devices, to_stems(): lax.ppermute(array, 'stem', [(i, (i + k) % stems) for i in range(stems)])  7.3 us
    ppermute x1, starting transfers between devices, on_device(): farther = lax.ppermute(mate_kv, 'tm', across)  1.78 us
    ppermute x1, starting transfers between devices, on_device(): far = lax.ppermute(mate_outer, 'tm', across)  1.55 us
    ppermute x5, waiting for transfers between devices, to_stems(): lax.ppermute(array, 'stem', [(i, (i + k) % stems) for i in range(stems)])  1.51 us
    unnamed x18, local copies, waits for them, and re-layouts  1.17 us
  transfers between devices with their start and end apart: 8, of which 2 were waited for; matrix products, arithmetic and copies ran while one was open for 0% of the time, Pallas kernels for 50%

profile of v13, /device:TPU:0, one launch (start us, length us, event | category | flops | bytes accessed | tf_op | source)
XLA Modules:
  0.0 30.3 jit_solution(15768074169320826268)
XLA Ops:
  0.0 0.5 %collective-permute-start = (bf16[1,384,1024]{2,1,0:T(8,128)(2,1)}, bf16[1,384,1024]{2,1,0:T(8,128)(2,1)S(1)}, u32[]{:S(2)}, u32[]{:S(2)}) collective-permute-start(bf16[1,384,1024]{2,1,0:T(8,128)(2,1)} %frames.1), channel_id=1, source_target_pairs={{0,1},{1,0},{2,3},{3,2},{4,5},{5,4},{6,7},{7,6},{8,9},{9,8},{10,11... | collective-permute-start | bytes 2359304 | tf_op jit(solution)/shard_map/ppermute | solution.py:456
  0.5 1.1 %copy-done.8 = bf16[1,384,1024]{2,1,0:T(8,128)(2,1)S(1)} copy-done((bf16[1,384,1024]{2,1,0:T(8,128)(2,1)S(1)}, bf16[1,384,1024]{2,1,0:T(8,128)(2,1)}, u32[]{:S(2)}) %copy-start.8) | copy-done | bytes 786456
  1.7 0.1 split.1
  1.8 2.7 %collective-permute-start.5 = (bf16[256,1024]{1,0:T(8,128)(2,1)S(1)}, bf16[256,1024]{1,0:T(8,128)(2,1)S(1)}, u32[]{:S(2)}, u32[]{:S(2)}) collective-permute-start(bf16[256,1024]{1,0:T(8,128)(2,1)S(1)} %get-tuple-element.25.late_rows.frames), channel_id=1, source_target_pairs={{0,16},{16,0},{1,17},{17,1},{2,18},{18,2},{3,19},{19,3},{4,20},{20... | collective-permute-start | bytes 1572872 | tf_op jit(solution)/shard_map/ppermute | solution.py:433
  4.5 0.0 copy-start
  4.5 0.0 copy-start.1
  4.5 0.0 copy-start.5
  4.5 1.5 %collective-permute-start.1 = (bf16[128,1024]{1,0:T(8,128)(2,1)S(1)}, bf16[128,1024]{1,0:T(8,128)(2,1)S(1)}, u32[]{:S(2)}, u32[]{:S(2)}) collective-permute-start(bf16[128,1024]{1,0:T(8,128)(2,1)S(1)} %mate.1), channel_id=1, source_target_pairs={{0,2},{2,4},{4,6},{6,8},{8,10},{10,12},{12,14},{3,1},{5,3},{7,5},{... | collective-permute-start | bytes 786440 | tf_op jit(solution)/shard_map/ppermute | solution.py:458
  6.1 3.5 %qkv.1 = (bf16[3,128,512]{2,1,0:T(8,128)(2,1)S(1)}, bf16[640,1024]{1,0:T(8,128)(2,1)S(1)}, bf16[128,1024]{1,0:T(8,128)(2,1)S(1)}, f32[2,8,1024]{2,1,0:T(8,128)S(1)}) custom-call(s32[1,2]{1,0:T(1,128)S(1)} %bitcast.3, f32[6,50,1024]{2,1,0:T(8,128)S(1)} %bitcast.2, bf16[128,1024]{1,0:T(8,128)(2,1)S(1)} %get-tuple-element.24.early_rows, ...), custom_call_target="tpu_custom_call" | custom-call | flops 60000000 | bytes 180000 | tf_op jit(solution)/shard_map/qkv/pallas_call | solution.py:439
  9.6 1.8 %collective-permute-start.2 = (bf16[128,1024]{1,0:T(8,128)(2,1)S(1)}, bf16[128,1024]{1,0:T(8,128)(2,1)S(1)}, u32[]{:S(2)}, u32[]{:S(2)}) collective-permute-start(bf16[128,1024]{1,0:T(8,128)(2,1)S(1)} %get-tuple-element.27._), channel_id=1, source_target_pairs={{0,2},{2,4},{4,6},{6,8},{8,10},{10,12},{12,14},{3,1},{5,3},{7,5},{... | collective-permute-start | bytes 786440 | tf_op jit(solution)/shard_map/ppermute | solution.py:466
  11.4 4.2 %near.1 = (f32[256,512]{1,0:T(8,128)S(1)}, f32[256,512]{1,0:T(8,128)S(1)}, f32[256,512]{1,0:T(8,128)S(1)}, bf16[128,1024]{1,0:T(8,128)(2,1)S(1)}, bf16[128,512]{...) custom-call(bf16[128,1024]{1,0:T(8,128)(2,1)S(1)} %get-tuple-element.27._, ...), custom_call_target="tpu_custom_call" | custom-call | flops 60000000 | bytes 180000 | tf_op jit(solution)/shard_map/near/pallas_call | solution.py:439
  15.5 1.2 %collective-permute-start.3 = (bf16[128,512]{1,0:T(8,128)(2,1)S(1)}, bf16[128,512]{1,0:T(8,128)(2,1)S(1)}, u32[]{:S(2)}, u32[]{:S(2)}) collective-permute-start(bf16[128,512]{1,0:T(8,128)(2,1)S(1)} %get-tuple-element.36.refs_0_), channel_id=1, source_target_pairs={{0,16},{16,0},{1,17},{17,1},{2,18},{18,2},{3,19},{19,3},{4,20},{20... | collective-permute-start | bytes 393224 | tf_op jit(solution)/shard_map/ppermute | solution.py:433
  16.7 1.2 %far_inner.1 = (bf16[128,512]{1,0:T(8,128)(2,1)S(1)}, bf16[128,1024]{1,0:T(8,128)(2,1)S(1)}) custom-call(f32[2,8,1024]{2,1,0:T(8,128)S(1)} %get-tuple-element.26.held.refs_0_, bf16[128,1024]{1,0:T(8,128)(2,1)S(1)} %collective-permute-done.1.refs_1_, bf16[1024,1536]{1,0:T(8,128)(2,1)S(1)} %copy-done.2, f32[2,64]{1,0:T(2,128)S(1)} %copy-done.6, ...), custom_call_target="tpu_custom_call" | custom-call | flops 40000000 | bytes 120000 | tf_op jit(solution)/shard_map/far_inner/pallas_call | solution.py:439
  18.0 1.0 %collective-permute-start.4 = (bf16[128,512]{1,0:T(8,128)(2,1)S(1)}, bf16[128,512]{1,0:T(8,128)(2,1)S(1)}, u32[]{:S(2)}, u32[]{:S(2)}) collective-permute-start(bf16[128,512]{1,0:T(8,128)(2,1)S(1)} %get-tuple-element.34.inner), channel_id=1, source_target_pairs={{0,16},{16,0},{1,17},{17,1},{2,18},{18,2},{3,19},{19,3},{4,20},{20... | collective-permute-start | bytes 393224 | tf_op jit(solution)/shard_map/ppermute | solution.py:433
  19.0 0.6 %far_outer.1.outer = bf16[128,512]{1,0:T(8,128)(2,1)S(1)} custom-call(bf16[128,1024]{1,0:T(8,128)(2,1)S(1)} %collective-permute-done.2.refs_0_, bf16[3,128,512]{2,1,0:T(8,128)(2,1)S(1)} %get-tuple-element.28.query.refs_4_.refs_1_, f32[256,512]{1,0:T(8,128)S(1)} %get-tuple-element.31.refs_5_.refs_2_, f32[256,512]{1,0:T(8,128)S(1)} %get-tuple-element.32.refs_6_.refs_3_, ...), custom_call_target="tpu_custom_call" | custom-call | flops 6000000 | bytes 18000 | tf_op jit(solution)/shard_map/far_outer/pallas_call | solution.py:439
  19.6 1.2 %collective-permute-start.6 = (bf16[128,512]{1,0:T(8,128)(2,1)S(1)}, bf16[128,512]{1,0:T(8,128)(2,1)S(1)}, u32[]{:S(2)}, u32[]{:S(2)}) collective-permute-start(bf16[128,512]{1,0:T(8,128)(2,1)S(1)} %far_outer.1.outer), channel_id=1, source_target_pairs={{0,16},{16,0},{1,17},{17,1},{2,18},{18,2},{3,19},{19,3},{4,20},{20... | collective-permute-start | bytes 393224 | tf_op jit(solution)/shard_map/ppermute | solution.py:433
  20.8 1.1 %collective-permute-done.3.refs_0_.refs_1_ = bf16[128,512]{1,0:T(8,128)(2,1)S(1)} collective-permute-done((bf16[128,512]{1,0:T(8,128)(2,1)S(1)}, bf16[128,512]{1,0:T(8,128)(2,1)S(1)}, u32[]{:S(2)}, u32[]{:S(2)}) %collective-permute-start.3) | collective-permute-done | bytes 131104 | tf_op jit(solution)/shard_map/ppermute | solution.py:433
  21.9 2.0 %own.1 = (bf16[256,1024]{1,0:T(8,128)(2,1)S(1)}, bf16[256,512]{1,0:T(8,128)(2,1)S(1)}, bf16[256,1024]{1,0:T(8,128)(2,1)S(1)}, bf16[128,512]{1,0:T(8,128)(2,1)S(1)}) custom-call(bf16[128,512]{1,0:T(8,128)(2,1)S(1)} %get-tuple-element.30.early_values.refs_6_, f32[2,8,1024]{2,1,0:T(8,128)S(1)} %get-tuple-element.26.held.refs_0_, ...), custom_call_target="tpu_custom_call" | custom-call | flops 20000000 | bytes 60000 | tf_op jit(solution)/shard_map/own/pallas_call | solution.py:439
  23.9 1.3 %collective-permute-start.7 = (bf16[128,512]{1,0:T(8,128)(2,1)S(1)}, bf16[128,512]{1,0:T(8,128)(2,1)S(1)}, u32[]{:S(2)}, u32[]{:S(2)}) collective-permute-start(bf16[128,512]{1,0:T(8,128)(2,1)S(1)} %get-tuple-element.42), channel_id=1, source_target_pairs={{0,16},{16,0},{1,17},{17,1},{2,18},{18,2},{3,19},{19,3},{4,20},{20... | collective-permute-start | bytes 393224 | tf_op jit(solution)/shard_map/ppermute | solution.py:433
  25.2 1.5 %inner.1._.refs_1_ = bf16[128,1024]{1,0:T(8,128)(2,1)S(1)} custom-call(f32[2,8,1024]{2,1,0:T(8,128)S(1)} %get-tuple-element.26.held.refs_0_, bf16[256,1024]{1,0:T(8,128)(2,1)S(1)} %get-tuple-element.37.refs_1_, bf16[256,512]{1,0:T(8,128)(2,1)S(1)} %get-tuple-element.38.refs_2_, bf16[256,1024]{1,0:T(8,128)(2,1)S(1)} %get-tuple-element.39.refs_3_, ...), custom_call_target="tpu_custom_call" | custom-call | flops 40000000 | bytes 120000 | tf_op jit(solution)/shard_map/inner/pallas_call | solution.py:439
  26.7 0.3 %weights.1._.refs_5_ = bf16[2,128,512]{2,1,0:T(8,128)(2,1)S(1)} custom-call(bf16[128,1024]{1,0:T(8,128)(2,1)S(1)} %inner.1._.refs_1_, bf16[128,512]{1,0:T(8,128)(2,1)S(1)} %get-tuple-element.40.query, bf16[128,512]{1,0:T(8,128)(2,1)S(1)} %get-tuple-element.36.refs_0_, bf16[128,512]{1,0:T(8,128)(2,1)S(1)} %collective-permute-done.3.refs_0_.refs_1_), custom_call_target="tpu_custom_call" | custom-call | flops 20000000 | bytes 60000 | tf_op jit(solution)/shard_map/weights/pallas_call | solution.py:439
  27.1 0.4 %collective-permute-done.6.refs_4_ = bf16[128,512]{1,0:T(8,128)(2,1)S(1)} collective-permute-done((bf16[128,512]{1,0:T(8,128)(2,1)S(1)}, bf16[128,512]{1,0:T(8,128)(2,1)S(1)}, u32[]{:S(2)}, u32[]{:S(2)}) %collective-permute-start.6) | collective-permute-done | bytes 131104 | tf_op jit(solution)/shard_map/ppermute | solution.py:433
  27.5 1.5 %outer.1.refs_2_ = bf16[128,1024]{1,0:T(8,128)(2,1)S(1)} custom-call(bf16[2,128,512]{2,1,0:T(8,128)(2,1)S(1)} %weights.1._.refs_5_, f32[2,8,1024]{2,1,0:T(8,128)S(1)} %get-tuple-element.26.held.refs_0_, bf16[256,1024]{1,0:T(8,128)(2,1)S(1)} %get-tuple-element.37.refs_1_, bf16[256,512]{1,0:T(8,128)(2,1)S(1)} %get-tuple-element.38.refs_2_, ...), custom_call_target="tpu_custom_call" | custom-call | flops 40000000 | bytes 120000 | tf_op jit(solution)/shard_map/outer/pallas_call | solution.py:439
  29.0 1.1 %early.1 = bf16[1,384,1024]{2,1,0:T(8,128)(2,1)} custom-call(f32[2,8,1024]{2,1,0:T(8,128)S(1)} %get-tuple-element.26.held.refs_0_, bf16[128,1024]{1,0:T(8,128)(2,1)S(1)} %inner.1._.refs_1_, bf16[128,1024]{1,0:T(8,128)(2,1)S(1)} %outer.1.refs_2_, bf16[512,1024]{1,0:T(8,128)(2,1)S(1)} %copy-done.3, bf16[128,1024]{1,0:T(8,128)(2,1)S(1)} %get-tuple-element.41.refs_4_, ...), custom_call_target="tpu_custom_call" | custom-call | flops 2000000000 | bytes 6000000 | tf_op jit(solution)/shard_map/early/pallas_call | solution.py:439
  (21 shorter events, 0.1 us)
Async XLA Ops:
  0.0 6.1 %copy-start.7 = (s32[2]{0:T(128)S(1)}, s32[2]{0:T(128)}, u32[]{:S(2)}) copy-start(s32[2]{0:T(128)} %param.10) | copy-start | bytes 28
  0.0 6.1 %copy-start.4 = (f32[50,6,1024]{2,0,1:T(8,128)S(1)}, f32[50,6,1024]{2,0,1:T(8,128)}, u32[]{:S(2)}) copy-start(f32[50,6,1024]{2,0,1:T(8,128)} %param.11) | copy-start | bytes 3686404
  0.0 6.1 %copy-start.6 = (f32[2,64]{1,0:T(2,128)S(1)}, f32[2,64]{1,0:T(2,128)}, u32[]{:S(2)}) copy-start(f32[2,64]{1,0:T(2,128)} %refs_3_.2) | copy-start | bytes 1540
  0.0 4.4 %collective-permute-start = (bf16[1,384,1024]{2,1,0:T(8,128)(2,1)}, bf16[1,384,1024]{2,1,0:T(8,128)(2,1)S(1)}, u32[]{:S(2)}, u32[]{:S(2)}) collective-permute-start(bf16[1,384,1024]{2,1,0:T(8,128)(2,1)} %frames.1), channel_id=1, source_target_pairs={{0,1},{1,0},{2,3},{3,2},{4,5},{5,4},{6,7},{7,6},{8,9},{9,8},{10,11... | collective-permute-start | bytes 2359304 | tf_op jit(solution)/shard_map/ppermute | solution.py:456
  0.5 1.1 %copy-start.8 = (bf16[1,384,1024]{2,1,0:T(8,128)(2,1)S(1)}, bf16[1,384,1024]{2,1,0:T(8,128)(2,1)}, u32[]{:S(2)}) copy-start(bf16[1,384,1024]{2,1,0:T(8,128)(2,1)} %frames.1) | copy-start | bytes 2359300
  1.7 4.4 %copy-start.2 = (bf16[1024,1536]{1,0:T(8,128)(2,1)S(1)}, bf16[1024,1536]{1,0:T(8,128)(2,1)}, u32[]{:S(2)}) copy-start(bf16[1024,1536]{1,0:T(8,128)(2,1)} %refs_2_.1) | copy-start | bytes 9437188
  1.8 23.4 %collective-permute-start.5 = (bf16[256,1024]{1,0:T(8,128)(2,1)S(1)}, bf16[256,1024]{1,0:T(8,128)(2,1)S(1)}, u32[]{:S(2)}, u32[]{:S(2)}) collective-permute-start(bf16[256,1024]{1,0:T(8,128)(2,1)S(1)} %get-tuple-element.25.late_rows.frames), channel_id=1, source_target_pairs={{0,16},{16,0},{1,17},{17,1},{2,18},{18,2},{3,19},{19,3},{4,20},{20... | collective-permute-start | bytes 1572872 | tf_op jit(solution)/shard_map/ppermute | solution.py:433
  4.5 6.9 %copy-start = (bf16[1024,1536]{1,0:T(8,128)(2,1)S(1)}, bf16[1024,1536]{1,0:T(8,128)(2,1)}, u32[]{:S(2)}) copy-start(bf16[1024,1536]{1,0:T(8,128)(2,1)} %refs_7_.3) | copy-start | bytes 9437188
  4.5 6.9 %copy-start.1 = (bf16[512,1024]{1,0:T(8,128)(2,1)S(1)}, bf16[512,1024]{1,0:T(8,128)(2,1)}, u32[]{:S(2)}) copy-start(bf16[512,1024]{1,0:T(8,128)(2,1)} %refs_6_.3) | copy-start | bytes 3145732
  4.5 6.9 %copy-start.5 = (f32[2,64]{1,0:T(2,128)S(1)}, f32[2,64]{1,0:T(2,128)}, u32[]{:S(2)}) copy-start(f32[2,64]{1,0:T(2,128)} %refs_8_.3) | copy-start | bytes 1540
  4.5 12.2 %collective-permute-start.1 = (bf16[128,1024]{1,0:T(8,128)(2,1)S(1)}, bf16[128,1024]{1,0:T(8,128)(2,1)S(1)}, u32[]{:S(2)}, u32[]{:S(2)}) collective-permute-start(bf16[128,1024]{1,0:T(8,128)(2,1)S(1)} %mate.1), channel_id=1, source_target_pairs={{0,2},{2,4},{4,6},{6,8},{8,10},{10,12},{12,14},{3,1},{5,3},{7,5},{... | collective-permute-start | bytes 786440 | tf_op jit(solution)/shard_map/ppermute | solution.py:458
  9.6 9.4 %collective-permute-start.2 = (bf16[128,1024]{1,0:T(8,128)(2,1)S(1)}, bf16[128,1024]{1,0:T(8,128)(2,1)S(1)}, u32[]{:S(2)}, u32[]{:S(2)}) collective-permute-start(bf16[128,1024]{1,0:T(8,128)(2,1)S(1)} %get-tuple-element.27._), channel_id=1, source_target_pairs={{0,2},{2,4},{4,6},{6,8},{8,10},{10,12},{12,14},{3,1},{5,3},{7,5},{... | collective-permute-start | bytes 786440 | tf_op jit(solution)/shard_map/ppermute | solution.py:466
  15.5 6.3 %collective-permute-start.3 = (bf16[128,512]{1,0:T(8,128)(2,1)S(1)}, bf16[128,512]{1,0:T(8,128)(2,1)S(1)}, u32[]{:S(2)}, u32[]{:S(2)}) collective-permute-start(bf16[128,512]{1,0:T(8,128)(2,1)S(1)} %get-tuple-element.36.refs_0_), channel_id=1, source_target_pairs={{0,16},{16,0},{1,17},{17,1},{2,18},{18,2},{3,19},{19,3},{4,20},{20... | collective-permute-start | bytes 393224 | tf_op jit(solution)/shard_map/ppermute | solution.py:433
  18.0 7.2 %collective-permute-start.4 = (bf16[128,512]{1,0:T(8,128)(2,1)S(1)}, bf16[128,512]{1,0:T(8,128)(2,1)S(1)}, u32[]{:S(2)}, u32[]{:S(2)}) collective-permute-start(bf16[128,512]{1,0:T(8,128)(2,1)S(1)} %get-tuple-element.34.inner), channel_id=1, source_target_pairs={{0,16},{16,0},{1,17},{17,1},{2,18},{18,2},{3,19},{19,3},{4,20},{20... | collective-permute-start | bytes 393224 | tf_op jit(solution)/shard_map/ppermute | solution.py:433
  19.6 5.6 %copy-start.3 = (bf16[512,1024]{1,0:T(8,128)(2,1)S(1)}, bf16[512,1024]{1,0:T(8,128)(2,1)}, u32[]{:S(2)}) copy-start(bf16[512,1024]{1,0:T(8,128)(2,1)} %refs_3_.3) | copy-start | bytes 3145732
  19.6 7.9 %collective-permute-start.6 = (bf16[128,512]{1,0:T(8,128)(2,1)S(1)}, bf16[128,512]{1,0:T(8,128)(2,1)S(1)}, u32[]{:S(2)}, u32[]{:S(2)}) collective-permute-start(bf16[128,512]{1,0:T(8,128)(2,1)S(1)} %far_outer.1.outer), channel_id=1, source_target_pairs={{0,16},{16,0},{1,17},{17,1},{2,18},{18,2},{3,19},{19,3},{4,20},{20... | collective-permute-start | bytes 393224 | tf_op jit(solution)/shard_map/ppermute | solution.py:433
  23.9 5.2 %collective-permute-start.7 = (bf16[128,512]{1,0:T(8,128)(2,1)S(1)}, bf16[128,512]{1,0:T(8,128)(2,1)S(1)}, u32[]{:S(2)}, u32[]{:S(2)}) collective-permute-start(bf16[128,512]{1,0:T(8,128)(2,1)S(1)} %get-tuple-element.42), channel_id=1, source_target_pairs={{0,16},{16,0},{1,17},{17,1},{2,18},{18,2},{3,19},{19,3},{4,20},{20... | collective-permute-start | bytes 393224 | tf_op jit(solution)/shard_map/ppermute | solution.py:433

commit v14 on v11

--- a/solution.py
+++ b/solution.py
@@ -392,13 +392,19 @@
     _, outer, inner, early = places(out.shape[1])
     copies = [
         pltpu.make_async_copy(source, out.at[0, pl.ds(at, BLOCK)], sems.at[n])
-        for n, (source, at) in enumerate(((inner_out, inner), (outer_out, outer), (early_out, early)))
+        for n, (source, at) in enumerate(((inner_out, inner), (outer_out, outer)))
     ]
+    for n in range(2):
+        to = out.at[0, pl.ds(early, BLOCK), pl.ds(n * HW, HW)]
+        copies.append(pltpu.make_async_copy(early_out.at[n], to, sems.at[2 + n]))
     copies[0].start()
     copies[1].start()
     mixed = cross_sum([weights[n] for n in range(count)], [v[...] for v in values])
-    early_out[...] = finished(first[...], mixed, out_cross, mods_held(held, 0)(5))
-    copies[2].start()
+    gate = mods_held(held, 0)(5)
+    for n in range(2):
+        cols = slice(n * HW, (n + 1) * HW)
+        early_out[n] = finished(first[:, cols], mixed, out_cross.at[:, cols], gate[:, cols])
+        copies[2 + n].start()
     for copy in copies:
         copy.wait()
 
@@ -500,7 +506,7 @@
     return call(
         lambda *refs: early_kernel(stems, *refs), "early", 2, shape(1, rows, D),
         held, inner_out, outer_out, out_cross, first_early, early_weights, v_early, *their_values,
-        scratch=[pltpu.VMEM((BLOCK, D), BF16), pltpu.SemaphoreType.DMA((3,))], out_specs=ANY,
+        scratch=[pltpu.VMEM((2, BLOCK, HW), BF16), pltpu.SemaphoreType.DMA((4,))], out_specs=ANY,
     )
 
 

time: 29.8 us -> 29.8 us (level)
  no operation moved by 1% of the time
where the time goes in v14:
time: 29.8 us; the launch traced here: 29.6 us
  Pallas kernels  16.3 us (55%)
  starting transfers between devices  10.3 us (35%)
  local copies, waits for them, and re-layouts  1.45 us (5%)
  waiting for transfers between devices  1.44 us (5%)
    pallas_call x10, Pallas kernels, call(): pl.pallas_call(kernel, out_shape=outs, in_specs=in_specs or [VMEM] * len(...  16.3 us
    ppermute x5, starting transfers between devices, to_stems(): lax.ppermute(array, 'stem', [(i, (i + k) % stems) for i in range(stems)])  6.7 us
    ppermute x1, starting transfers between devices, on_device(): far = lax.ppermute(mate_outer, 'tm', across)  1.55 us
    ppermute x1, starting transfers between devices, on_device(): farther = lax.ppermute(mate_inner, 'tm', across)  1.55 us
    unnamed x18, local copies, waits for them, and re-layouts  1.45 us
    ppermute x5, waiting for transfers between devices, to_stems(): lax.ppermute(array, 'stem', [(i, (i + k) % stems) for i in range(stems)])  1.29 us
  transfers between devices with their start and end apart: 8, of which 3 were waited for; matrix products, arithmetic and copies ran while one was open for 0% of the time, Pallas kernels for 51%

profile of v14, /device:TPU:0, one launch (start us, length us, event | category | flops | bytes accessed | tf_op | source)
XLA Modules:
  0.0 29.6 jit_solution(604079893295224185)
XLA Ops:
  0.0 0.5 %collective-permute-start = (bf16[1,384,1024]{2,1,0:T(8,128)(2,1)}, bf16[1,384,1024]{2,1,0:T(8,128)(2,1)S(1)}, u32[]{:S(2)}, u32[]{:S(2)}) collective-permute-start(bf16[1,384,1024]{2,1,0:T(8,128)(2,1)} %frames.1), channel_id=1, source_target_pairs={{0,1},{1,0},{2,3},{3,2},{4,5},{5,4},{6,7},{7,6},{8,9},{9,8},{10,11... | collective-permute-start | bytes 2359304 | tf_op jit(solution)/shard_map/ppermute | solution.py:458
  0.6 1.4 %copy-done.8 = bf16[1,384,1024]{2,1,0:T(8,128)(2,1)S(1)} copy-done((bf16[1,384,1024]{2,1,0:T(8,128)(2,1)S(1)}, bf16[1,384,1024]{2,1,0:T(8,128)(2,1)}, u32[]{:S(2)}) %copy-start.8) | copy-done | bytes 786456
  2.0 0.1 split.1
  2.1 2.5 %collective-permute-start.5 = (bf16[256,1024]{1,0:T(8,128)(2,1)S(1)}, bf16[256,1024]{1,0:T(8,128)(2,1)S(1)}, u32[]{:S(2)}, u32[]{:S(2)}) collective-permute-start(bf16[256,1024]{1,0:T(8,128)(2,1)S(1)} %get-tuple-element.26.late_rows.frames), channel_id=1, source_target_pairs={{0,16},{16,0},{1,17},{17,1},{2,18},{18,2},{3,19},{19,3},{4,20},{20... | collective-permute-start | bytes 1572872 | tf_op jit(solution)/shard_map/ppermute | solution.py:435
  4.5 0.0 collective-permute-done.near.mate
  4.6 1.5 %collective-permute-start.1 = (bf16[128,1024]{1,0:T(8,128)(2,1)S(1)}, bf16[128,1024]{1,0:T(8,128)(2,1)S(1)}, u32[]{:S(2)}, u32[]{:S(2)}) collective-permute-start(bf16[128,1024]{1,0:T(8,128)(2,1)S(1)} %get-tuple-element.28), channel_id=1, source_target_pairs={{0,2},{2,4},{4,6},{6,8},{8,10},{10,12},{12,14},{3,1},{5,3},{7,5},{... | collective-permute-start | bytes 786440 | tf_op jit(solution)/shard_map/ppermute | solution.py:460
  6.1 1.5 %collective-permute-start.2 = (bf16[128,1024]{1,0:T(8,128)(2,1)S(1)}, bf16[128,1024]{1,0:T(8,128)(2,1)S(1)}, u32[]{:S(2)}, u32[]{:S(2)}) collective-permute-start(bf16[128,1024]{1,0:T(8,128)(2,1)S(1)} %get-tuple-element.35), channel_id=1, source_target_pairs={{0,2},{2,4},{4,6},{6,8},{8,10},{10,12},{12,14},{3,1},{5,3},{7,5},{... | collective-permute-start | bytes 786440 | tf_op jit(solution)/shard_map/ppermute | solution.py:461
  7.7 7.2 %near.1 = (bf16[256,512]{1,0:T(8,128)(2,1)S(1)}, f32[256,512]{1,0:T(8,128)S(1)}, f32[256,512]{1,0:T(8,128)S(1)}, f32[256,512]{1,0:T(8,128)S(1)}, bf16[128,1024]{...) custom-call(s32[1,2]{1,0:T(1,128)S(1)} %bitcast.3, ...), custom_call_target="tpu_custom_call" | custom-call | flops 120000000 | bytes 360000 | tf_op jit(solution)/shard_map/near/pallas_call | solution.py:441
  14.9 1.1 %collective-permute-start.3 = (bf16[128,512]{1,0:T(8,128)(2,1)S(1)}, bf16[128,512]{1,0:T(8,128)(2,1)S(1)}, u32[]{:S(2)}, u32[]{:S(2)}) collective-permute-start(bf16[128,512]{1,0:T(8,128)(2,1)S(1)} %get-tuple-element.38.refs_0_), channel_id=1, source_target_pairs={{0,16},{16,0},{1,17},{17,1},{2,18},{18,2},{3,19},{19,3},{4,20},{20... | collective-permute-start | bytes 393224 | tf_op jit(solution)/shard_map/ppermute | solution.py:435
  16.0 0.0 collective-permute-done.1.refs_1_
  16.0 1.2 %far_inner.1 = (bf16[128,512]{1,0:T(8,128)(2,1)S(1)}, bf16[128,1024]{1,0:T(8,128)(2,1)S(1)}) custom-call(f32[2,8,1024]{2,1,0:T(8,128)S(1)} %get-tuple-element.27.refs_0_.refs_1_.held, bf16[128,1024]{1,0:T(8,128)(2,1)S(1)} %collective-permute-done.1.refs_1_, bf16[1024,1536]{1,0:T(8,128)(2,1)S(1)} %copy-done.1, f32[2,64]{1,0:T(2,128)S(1)} %copy-done.6, ...), custom_call_target="tpu_custom_call" | custom-call | flops 40000000 | bytes 120000 | tf_op jit(solution)/shard_map/far_inner/pallas_call | solution.py:441
  17.2 1.1 %collective-permute-start.4 = (bf16[128,512]{1,0:T(8,128)(2,1)S(1)}, bf16[128,512]{1,0:T(8,128)(2,1)S(1)}, u32[]{:S(2)}, u32[]{:S(2)}) collective-permute-start(bf16[128,512]{1,0:T(8,128)(2,1)S(1)} %get-tuple-element.33.inner), channel_id=1, source_target_pairs={{0,16},{16,0},{1,17},{17,1},{2,18},{18,2},{3,19},{19,3},{4,20},{20... | collective-permute-start | bytes 393224 | tf_op jit(solution)/shard_map/ppermute | solution.py:435
  18.3 0.1 collective-permute-done.2.refs_2_
  18.4 1.3 %far_outer.1 = (bf16[128,512]{1,0:T(8,128)(2,1)S(1)}, bf16[128,512]{1,0:T(8,128)(2,1)S(1)}) custom-call(bf16[128,512]{1,0:T(8,128)(2,1)S(1)} %get-tuple-element.34.refs_0_.refs_6_, f32[2,8,1024]{2,1,0:T(8,128)S(1)} %get-tuple-element.27.refs_0_.refs_1_.held, bf16[128,1024]{1,0:T(8,128)(2,1)S(1)} %collective-permute-done.2.refs_2_, ...), custom_call_target="tpu_custom_call" | custom-call | flops 6000000 | bytes 18000 | tf_op jit(solution)/shard_map/far_outer/pallas_call | solution.py:441
  19.7 0.0 copy-start.3
  19.7 1.1 %collective-permute-start.6 = (bf16[128,512]{1,0:T(8,128)(2,1)S(1)}, bf16[128,512]{1,0:T(8,128)(2,1)S(1)}, u32[]{:S(2)}, u32[]{:S(2)}) collective-permute-start(bf16[128,512]{1,0:T(8,128)(2,1)S(1)} %get-tuple-element.37.outer), channel_id=1, source_target_pairs={{0,16},{16,0},{1,17},{17,1},{2,18},{18,2},{3,19},{19,3},{4,20},{20... | collective-permute-start | bytes 393224 | tf_op jit(solution)/shard_map/ppermute | solution.py:435
  20.8 1.0 %collective-permute-start.7 = (bf16[128,512]{1,0:T(8,128)(2,1)S(1)}, bf16[128,512]{1,0:T(8,128)(2,1)S(1)}, u32[]{:S(2)}, u32[]{:S(2)}) collective-permute-start(bf16[128,512]{1,0:T(8,128)(2,1)S(1)} %get-tuple-element.44), channel_id=1, source_target_pairs={{0,16},{16,0},{1,17},{17,1},{2,18},{18,2},{3,19},{19,3},{4,20},{20... | collective-permute-start | bytes 393224 | tf_op jit(solution)/shard_map/ppermute | solution.py:435
  21.8 2.0 %own.1 = (bf16[256,1024]{1,0:T(8,128)(2,1)S(1)}, bf16[256,512]{1,0:T(8,128)(2,1)S(1)}, bf16[256,1024]{1,0:T(8,128)(2,1)S(1)}) custom-call(f32[2,8,1024]{2,1,0:T(8,128)S(1)} %get-tuple-element.27.refs_0_.refs_1_.held, bf16[256,1024]{1,0:T(8,128)(2,1)S(1)} %get-tuple-element.26.late_rows.frames, bf16[128,512]{1,0:T(8,128)(2,1)S(1)} %get-tuple-element.33.inner, ...), custom_call_target="tpu_custom_call" | custom-call | flops 20000000 | bytes 60000 | tf_op jit(solution)/shard_map/own/pallas_call | solution.py:441
  23.8 0.4 %collective-permute-done.4.refs_4_ = bf16[128,512]{1,0:T(8,128)(2,1)S(1)} collective-permute-done((bf16[128,512]{1,0:T(8,128)(2,1)S(1)}, bf16[128,512]{1,0:T(8,128)(2,1)S(1)}, u32[]{:S(2)}, u32[]{:S(2)}) %collective-permute-start.4) | collective-permute-done | bytes 131104 | tf_op jit(solution)/shard_map/ppermute | solution.py:435
  24.2 1.6 %inner.1._.refs_1_ = bf16[128,1024]{1,0:T(8,128)(2,1)S(1)} custom-call(f32[2,8,1024]{2,1,0:T(8,128)S(1)} %get-tuple-element.27.refs_0_.refs_1_.held, bf16[256,1024]{1,0:T(8,128)(2,1)S(1)} %get-tuple-element.39.refs_1_, bf16[256,512]{1,0:T(8,128)(2,1)S(1)} %get-tuple-element.40.refs_2_, bf16[256,1024]{1,0:T(8,128)(2,1)S(1)} %get-tuple-element.41.refs_3_, ...), custom_call_target="tpu_custom_call" | custom-call | flops 40000000 | bytes 120000 | tf_op jit(solution)/shard_map/inner/pallas_call | solution.py:441
  25.8 0.3 %weights.1._.refs_5_ = bf16[2,128,512]{2,1,0:T(8,128)(2,1)S(1)} custom-call(bf16[128,1024]{1,0:T(8,128)(2,1)S(1)} %inner.1._.refs_1_, bf16[128,512]{1,0:T(8,128)(2,1)S(1)} %get-tuple-element.42.query, bf16[128,512]{1,0:T(8,128)(2,1)S(1)} %get-tuple-element.38.refs_0_, bf16[128,512]{1,0:T(8,128)(2,1)S(1)} %collective-permute-done.3.refs_0_.refs_1_), custom_call_target="tpu_custom_call" | custom-call | flops 20000000 | bytes 60000 | tf_op jit(solution)/shard_map/weights/pallas_call | solution.py:441
  26.1 0.9 %collective-permute-done.6.refs_4_ = bf16[128,512]{1,0:T(8,128)(2,1)S(1)} collective-permute-done((bf16[128,512]{1,0:T(8,128)(2,1)S(1)}, bf16[128,512]{1,0:T(8,128)(2,1)S(1)}, u32[]{:S(2)}, u32[]{:S(2)}) %collective-permute-start.6) | collective-permute-done | bytes 131104 | tf_op jit(solution)/shard_map/ppermute | solution.py:435
  27.0 1.6 %outer.1.refs_2_ = bf16[128,1024]{1,0:T(8,128)(2,1)S(1)} custom-call(bf16[2,128,512]{2,1,0:T(8,128)(2,1)S(1)} %weights.1._.refs_5_, f32[2,8,1024]{2,1,0:T(8,128)S(1)} %get-tuple-element.27.refs_0_.refs_1_.held, bf16[256,1024]{1,0:T(8,128)(2,1)S(1)} %get-tuple-element.39.refs_1_, bf16[256,512]{1,0:T(8,128)(2,1)S(1)} %get-tuple-element.40.refs_2_, ...), custom_call_target="tpu_custom_call" | custom-call | flops 40000000 | bytes 120000 | tf_op jit(solution)/shard_map/outer/pallas_call | solution.py:441
  28.6 1.0 %early.1 = bf16[1,384,1024]{2,1,0:T(8,128)(2,1)} custom-call(f32[2,8,1024]{2,1,0:T(8,128)S(1)} %get-tuple-element.27.refs_0_.refs_1_.held, bf16[128,1024]{1,0:T(8,128)(2,1)S(1)} %inner.1._.refs_1_, bf16[128,1024]{1,0:T(8,128)(2,1)S(1)} %outer.1.refs_2_, bf16[512,1024]{1,0:T(8,128)(2,1)S(1)} %copy-done.3, bf16[128,1024]{1,0:T(8,128)(2,1)S(1)} %get-tuple-element.43.refs_4_, ...), custom_call_target="tpu_custom_call" | custom-call | flops 2000000000 | bytes 6000000 | tf_op jit(solution)/shard_map/early/pallas_call | solution.py:441
  (20 shorter events, 0.1 us)
Async XLA Ops:
  0.0 7.7 %copy-start.7 = (s32[2]{0:T(128)S(1)}, s32[2]{0:T(128)}, u32[]{:S(2)}) copy-start(s32[2]{0:T(128)} %param.10) | copy-start | bytes 28
  0.0 7.7 %copy-start.4 = (f32[50,6,1024]{2,0,1:T(8,128)S(1)}, f32[50,6,1024]{2,0,1:T(8,128)}, u32[]{:S(2)}) copy-start(f32[50,6,1024]{2,0,1:T(8,128)} %param.11) | copy-start | bytes 3686404
  0.0 7.7 %copy-start.1 = (bf16[1024,1536]{1,0:T(8,128)(2,1)S(1)}, bf16[1024,1536]{1,0:T(8,128)(2,1)}, u32[]{:S(2)}) copy-start(bf16[1024,1536]{1,0:T(8,128)(2,1)} %refs_3_.4) | copy-start | bytes 9437188
  0.0 7.7 %copy-start.2 = (bf16[512,1024]{1,0:T(8,128)(2,1)S(1)}, bf16[512,1024]{1,0:T(8,128)(2,1)}, u32[]{:S(2)}) copy-start(bf16[512,1024]{1,0:T(8,128)(2,1)} %refs_6_.3) | copy-start | bytes 3145732
  0.0 7.7 %copy-start.6 = (f32[2,64]{1,0:T(2,128)S(1)}, f32[2,64]{1,0:T(2,128)}, u32[]{:S(2)}) copy-start(f32[2,64]{1,0:T(2,128)} %refs_4_.1) | copy-start | bytes 1540
  0.0 7.7 %copy-start = (bf16[1024,1536]{1,0:T(8,128)(2,1)S(1)}, bf16[1024,1536]{1,0:T(8,128)(2,1)}, u32[]{:S(2)}) copy-start(bf16[1024,1536]{1,0:T(8,128)(2,1)} %refs_7_.3) | copy-start | bytes 9437188
  0.0 7.7 %copy-start.5 = (f32[2,64]{1,0:T(2,128)S(1)}, f32[2,64]{1,0:T(2,128)}, u32[]{:S(2)}) copy-start(f32[2,64]{1,0:T(2,128)} %refs_8_.3) | copy-start | bytes 1540
  0.0 4.5 %collective-permute-start = (bf16[1,384,1024]{2,1,0:T(8,128)(2,1)}, bf16[1,384,1024]{2,1,0:T(8,128)(2,1)S(1)}, u32[]{:S(2)}, u32[]{:S(2)}) collective-permute-start(bf16[1,384,1024]{2,1,0:T(8,128)(2,1)} %frames.1), channel_id=1, source_target_pairs={{0,1},{1,0},{2,3},{3,2},{4,5},{5,4},{6,7},{7,6},{8,9},{9,8},{10,11... | collective-permute-start | bytes 2359304 | tf_op jit(solution)/shard_map/ppermute | solution.py:458
  0.6 1.4 %copy-start.8 = (bf16[1,384,1024]{2,1,0:T(8,128)(2,1)S(1)}, bf16[1,384,1024]{2,1,0:T(8,128)(2,1)}, u32[]{:S(2)}) copy-start(bf16[1,384,1024]{2,1,0:T(8,128)(2,1)} %frames.1) | copy-start | bytes 2359300
  2.1 21.7 %collective-permute-start.5 = (bf16[256,1024]{1,0:T(8,128)(2,1)S(1)}, bf16[256,1024]{1,0:T(8,128)(2,1)S(1)}, u32[]{:S(2)}, u32[]{:S(2)}) collective-permute-start(bf16[256,1024]{1,0:T(8,128)(2,1)S(1)} %get-tuple-element.26.late_rows.frames), channel_id=1, source_target_pairs={{0,16},{16,0},{1,17},{17,1},{2,18},{18,2},{3,19},{19,3},{4,20},{20... | collective-permute-start | bytes 1572872 | tf_op jit(solution)/shard_map/ppermute | solution.py:435
  4.6 11.4 %collective-permute-start.1 = (bf16[128,1024]{1,0:T(8,128)(2,1)S(1)}, bf16[128,1024]{1,0:T(8,128)(2,1)S(1)}, u32[]{:S(2)}, u32[]{:S(2)}) collective-permute-start(bf16[128,1024]{1,0:T(8,128)(2,1)S(1)} %get-tuple-element.28), channel_id=1, source_target_pairs={{0,2},{2,4},{4,6},{6,8},{8,10},{10,12},{12,14},{3,1},{5,3},{7,5},{... | collective-permute-start | bytes 786440 | tf_op jit(solution)/shard_map/ppermute | solution.py:460
  6.1 12.3 %collective-permute-start.2 = (bf16[128,1024]{1,0:T(8,128)(2,1)S(1)}, bf16[128,1024]{1,0:T(8,128)(2,1)S(1)}, u32[]{:S(2)}, u32[]{:S(2)}) collective-permute-start(bf16[128,1024]{1,0:T(8,128)(2,1)S(1)} %get-tuple-element.35), channel_id=1, source_target_pairs={{0,2},{2,4},{4,6},{6,8},{8,10},{10,12},{12,14},{3,1},{5,3},{7,5},{... | collective-permute-start | bytes 786440 | tf_op jit(solution)/shard_map/ppermute | solution.py:461
  14.9 6.9 %collective-permute-start.3 = (bf16[128,512]{1,0:T(8,128)(2,1)S(1)}, bf16[128,512]{1,0:T(8,128)(2,1)S(1)}, u32[]{:S(2)}, u32[]{:S(2)}) collective-permute-start(bf16[128,512]{1,0:T(8,128)(2,1)S(1)} %get-tuple-element.38.refs_0_), channel_id=1, source_target_pairs={{0,16},{16,0},{1,17},{17,1},{2,18},{18,2},{3,19},{19,3},{4,20},{20... | collective-permute-start | bytes 393224 | tf_op jit(solution)/shard_map/ppermute | solution.py:435
  17.2 7.0 %collective-permute-start.4 = (bf16[128,512]{1,0:T(8,128)(2,1)S(1)}, bf16[128,512]{1,0:T(8,128)(2,1)S(1)}, u32[]{:S(2)}, u32[]{:S(2)}) collective-permute-start(bf16[128,512]{1,0:T(8,128)(2,1)S(1)} %get-tuple-element.33.inner), channel_id=1, source_target_pairs={{0,16},{16,0},{1,17},{17,1},{2,18},{18,2},{3,19},{19,3},{4,20},{20... | collective-permute-start | bytes 393224 | tf_op jit(solution)/shard_map/ppermute | solution.py:435
  19.7 4.5 %copy-start.3 = (bf16[512,1024]{1,0:T(8,128)(2,1)S(1)}, bf16[512,1024]{1,0:T(8,128)(2,1)}, u32[]{:S(2)}) copy-start(bf16[512,1024]{1,0:T(8,128)(2,1)} %refs_3_.5) | copy-start | bytes 3145732
  19.7 7.3 %collective-permute-start.6 = (bf16[128,512]{1,0:T(8,128)(2,1)S(1)}, bf16[128,512]{1,0:T(8,128)(2,1)S(1)}, u32[]{:S(2)}, u32[]{:S(2)}) collective-permute-start(bf16[128,512]{1,0:T(8,128)(2,1)S(1)} %get-tuple-element.37.outer), channel_id=1, source_target_pairs={{0,16},{16,0},{1,17},{17,1},{2,18},{18,2},{3,19},{19,3},{4,20},{20... | collective-permute-start | bytes 393224 | tf_op jit(solution)/shard_map/ppermute | solution.py:435
  20.8 7.8 %collective-permute-start.7 = (bf16[128,512]{1,0:T(8,128)(2,1)S(1)}, bf16[128,512]{1,0:T(8,128)(2,1)S(1)}, u32[]{:S(2)}, u32[]{:S(2)}) collective-permute-start(bf16[128,512]{1,0:T(8,128)(2,1)S(1)} %get-tuple-element.44), channel_id=1, source_target_pairs={{0,16},{16,0},{1,17},{17,1},{2,18},{18,2},{3,19},{19,3},{4,20},{20... | collective-permute-start | bytes 393224 | tf_op jit(solution)/shard_map/ppermute | solution.py:435

commit v15 on v14

--- a/solution.py
+++ b/solution.py
@@ -154,12 +154,13 @@
     return parity, outer, rows - HALF, early
 
 
-def split_kernel(frames, late_rows, early_rows, sems):
-    _, outer, inner, early = places(frames.shape[1])
-    targets = (late_rows.at[pl.ds(0, BLOCK)], late_rows.at[pl.ds(BLOCK, BLOCK)], early_rows)
+def split_kernel(frames, late_rows, sems):
+    _, outer, inner, _ = places(frames.shape[1])
     copies = [
-        pltpu.make_async_copy(frames.at[0, pl.ds(at, BLOCK)], to, sems.at[n])
-        for n, (at, to) in enumerate(zip((outer, inner, early), targets))
+        pltpu.make_async_copy(
+            frames.at[0, pl.ds(at, BLOCK)], late_rows.at[pl.ds(n * BLOCK, BLOCK)], sems.at[n]
+        )
+        for n, at in enumerate((outer, inner))
     ]
     for copy in copies:
         copy.start()
@@ -191,10 +192,12 @@
 
 
 def near_kernel(
-    timestep, modulation, early_rows, late_rows, near, qkv_self, gains, out_self, qkv_cross, gains_cross,
-    query, part_out, part_sum, part_top, first, first_q, first_k, first_v, held, kv,
+    timestep, modulation, frames, late_rows, near, qkv_self, gains, out_self, qkv_cross, gains_cross,
+    query, part_out, part_sum, part_top, first, first_q, first_k, first_v, held, kv, early_rows, sem,
 ):
     rows = near.shape[1]
+    copy = pltpu.make_async_copy(frames.at[0, pl.ds(places(rows)[3], BLOCK)], early_rows, sem)
+    copy.start()
 
     def hold(k):
         for i, row in enumerate(mods_of(timestep, modulation, k)):
@@ -212,15 +215,17 @@
     near_from = parity * (rows - HALF)
 
     sources = [
-        (early_rows, 0, own_at + early),
         (late_rows, 0, own_at + outer),
         (late_rows, BLOCK, own_at + inner),
+        (early_rows, 0, own_at + early),
     ]
     for at in range(0, HALF, BLOCK):
         sources.append((near.at[0], pl.multiple_of(near_from + at, BLOCK), near_at + at))
 
     def normed(n):
         source, at, _ = sources[n]
+        if source is early_rows:
+            copy.wait()
         return modulated(source[pl.ds(at, BLOCK)], shift, scale)
 
     queries = []
@@ -235,12 +240,12 @@
             queries.append(head_norm(raw[0], q_gain, ones))
         kv[at, :HW] = head_norm(raw[-2], k_gain, ones)
         kv[at, HW:] = raw[-1].astype(BF16)
-    query[:BLOCK] = queries[1]
-    query[BLOCK:] = queries[2]
+    query[:BLOCK] = queries[0]
+    query[BLOCK:] = queries[1]
     for k in range(1, held.shape[0]):
         hold(k)
 
-    parts = [part_steps(n, queries[n + 1], kv, part_out, part_sum, part_top) for n in range(2)]
+    parts = [part_steps(n, queries[n], kv, part_out, part_sum, part_top) for n in range(2)]
 
     def meanwhile(steps):
         while steps and parts:
@@ -252,7 +257,7 @@
     bias = window_bias(rows + HALF, 0)
     attended = []
     for cols in SLABS:
-        scores = window_scores(queries[0][:, cols], kv[:, cols], bias)
+        scores = window_scores(queries[2][:, cols], kv[:, cols], bias)
         meanwhile(2)
         powers, _ = raised(scores)
         out, total = weighted(powers, kv[:, HW + cols.start : HW + cols.stop])
@@ -450,9 +455,10 @@
         )(*args)
 
     half = shape(BLOCK, D)
-    late_rows, early_rows = call(
-        split_kernel, "split", 4, (shape(HALF, D), half), frames,
-        scratch=[pltpu.SemaphoreType.DMA((3,))], in_specs=[ANY], out_specs=(ANY, ANY),
+    own_rows = pltpu.with_memory_space_constraint(frames, pltpu.HBM)
+    late_rows = call(
+        split_kernel, "split", 4, shape(HALF, D), own_rows,
+        scratch=[pltpu.SemaphoreType.DMA((2,))], in_specs=[ANY], out_specs=ANY,
     )
     their_frames = to_stems(late_rows)
     near = lax.ppermute(frames, "tm", inside)
@@ -464,8 +470,9 @@
     query, part_out, part_sum, part_top, first_early, q_early, k_early, v_early, held = call(
         near_kernel, "near", 0.12,
         (late, part, part, part, half, block, block, block, shape(stems, 8, D, dtype=F32)),
-        timestep.reshape(1, -1), modulation, early_rows, late_rows, near, qkv_self, qk_gain_self, out_self, qkv_cross, qk_gain_cross,
-        scratch=[pltpu.VMEM((rows + HALF, 2 * HW), BF16)],
+        timestep.reshape(1, -1), modulation, own_rows, late_rows, near, qkv_self, qk_gain_self, out_self, qkv_cross, qk_gain_cross,
+        scratch=[pltpu.VMEM((rows + HALF, 2 * HW), BF16), pltpu.VMEM((BLOCK, D), BF16), pltpu.SemaphoreType.DMA],
+        in_specs=[VMEM] * 2 + [ANY] + [VMEM] * 7,
     )
     their_keys = to_stems(k_early)
     parts = (part_out, part_sum, part_top)

time: 29.8 us -> 29.6 us (level)
  local copies, waits for them, and re-layouts: 1.45 us -> 0.03 us
  Pallas kernels: 16.3 us -> 17.7 us
    pallas_call x10, Pallas kernels: 16.3 us -> 17.7 us  [call(): pl.pallas_call(kernel, out_shape=outs, in_specs=in_specs or [VMEM] * len(...]
    unnamed x18 -> x16, local copies, waits for them, and re-layouts: 1.45 us -> 0.03 us
  transfers between devices with their start and end apart: 8 -> 8, of which waited for: 3 -> 3; matrix products, arithmetic and copies ran while one was open for 0% -> 0% of each run, Pallas kernels for 51% -> 57%
where the time goes in v15:
time: 29.6 us; the launch traced here: 29.5 us
  Pallas kernels  17.7 us (60%)
  starting transfers between devices  10.3 us (35%)
  waiting for transfers between devices  1.22 us (4%)
    pallas_call x10, Pallas kernels, call(): pl.pallas_call(kernel, out_shape=outs, in_specs=in_specs or [VMEM] * len(...  17.7 us
    ppermute x5, starting transfers between devices, to_stems(): lax.ppermute(array, 'stem', [(i, (i + k) % stems) for i in range(stems)])  6.71 us
    ppermute x1, starting transfers between devices, on_device(): far = lax.ppermute(mate_outer, 'tm', across)  1.55 us
    ppermute x1, starting transfers between devices, on_device(): farther = lax.ppermute(mate_inner, 'tm', across)  1.55 us
    ppermute x5, waiting for transfers between devices, to_stems(): lax.ppermute(array, 'stem', [(i, (i + k) % stems) for i in range(stems)])  1.21 us
  transfers between devices with their start and end apart: 8, of which 3 were waited for; matrix products, arithmetic and copies ran while one was open for 0% of the time, Pallas kernels for 57%

profile of v15, /device:TPU:0, one launch (start us, length us, event | category | flops | bytes accessed | tf_op | source)
XLA Modules:
  0.0 29.5 jit_solution(9406539595385957062)
XLA Ops:
  0.0 0.5 %collective-permute-start = (bf16[1,384,1024]{2,1,0:T(8,128)(2,1)}, bf16[1,384,1024]{2,1,0:T(8,128)(2,1)S(1)}, u32[]{:S(2)}, u32[]{:S(2)}) collective-permute-start(bf16[1,384,1024]{2,1,0:T(8,128)(2,1)} %frames.3), channel_id=1, source_target_pairs={{0,1},{1,0},{2,3},{3,2},{4,5},{5,4},{6,7},{7,6},{8,9},{9,8},{10,11... | collective-permute-start | bytes 2359304 | tf_op jit(solution)/shard_map/ppermute | solution.py:464
  0.6 1.3 %split.1.late_rows.frames = bf16[256,1024]{1,0:T(8,128)(2,1)S(1)} custom-call(bf16[1,384,1024]{2,1,0:T(8,128)(2,1)} %frames.3), custom_call_target="tpu_custom_call" | custom-call | flops 4000000000 | bytes 12000000 | tf_op jit(solution)/shard_map/split/pallas_call | solution.py:446
  1.9 2.5 %collective-permute-start.5 = (bf16[256,1024]{1,0:T(8,128)(2,1)S(1)}, bf16[256,1024]{1,0:T(8,128)(2,1)S(1)}, u32[]{:S(2)}, u32[]{:S(2)}) collective-permute-start(bf16[256,1024]{1,0:T(8,128)(2,1)S(1)} %split.1.late_rows.frames), channel_id=1, source_target_pairs={{0,16},{16,0},{1,17},{17,1},{2,18},{18,2},{3,19},{19,3},{4,20},{20... | collective-permute-start | bytes 1572872 | tf_op jit(solution)/shard_map/ppermute | solution.py:440
  4.4 1.5 %collective-permute-start.1 = (bf16[128,1024]{1,0:T(8,128)(2,1)S(1)}, bf16[128,1024]{1,0:T(8,128)(2,1)S(1)}, u32[]{:S(2)}, u32[]{:S(2)}) collective-permute-start(bf16[128,1024]{1,0:T(8,128)(2,1)S(1)} %get-tuple-element.24), channel_id=1, source_target_pairs={{0,2},{2,4},{4,6},{6,8},{8,10},{10,12},{12,14},{3,1},{5,3},{7,5},{... | collective-permute-start | bytes 786440 | tf_op jit(solution)/shard_map/ppermute | solution.py:466
  6.0 1.5 %collective-permute-start.2 = (bf16[128,1024]{1,0:T(8,128)(2,1)S(1)}, bf16[128,1024]{1,0:T(8,128)(2,1)S(1)}, u32[]{:S(2)}, u32[]{:S(2)}) collective-permute-start(bf16[128,1024]{1,0:T(8,128)(2,1)S(1)} %get-tuple-element.31), channel_id=1, source_target_pairs={{0,2},{2,4},{4,6},{6,8},{8,10},{10,12},{12,14},{3,1},{5,3},{7,5},{... | collective-permute-start | bytes 786440 | tf_op jit(solution)/shard_map/ppermute | solution.py:467
  7.6 7.4 %near.1 = (bf16[256,512]{1,0:T(8,128)(2,1)S(1)}, f32[256,512]{1,0:T(8,128)S(1)}, f32[256,512]{1,0:T(8,128)S(1)}, f32[256,512]{1,0:T(8,128)S(1)}, bf16[128,1024]{...) custom-call(s32[1,2]{1,0:T(1,128)S(1)} %bitcast.3, ...), custom_call_target="tpu_custom_call" | custom-call | flops 120000000 | bytes 360000 | tf_op jit(solution)/shard_map/near/pallas_call | solution.py:446
  15.0 1.3 %collective-permute-start.3 = (bf16[128,512]{1,0:T(8,128)(2,1)S(1)}, bf16[128,512]{1,0:T(8,128)(2,1)S(1)}, u32[]{:S(2)}, u32[]{:S(2)}) collective-permute-start(bf16[128,512]{1,0:T(8,128)(2,1)S(1)} %get-tuple-element.34.refs_0_), channel_id=1, source_target_pairs={{0,16},{16,0},{1,17},{17,1},{2,18},{18,2},{3,19},{19,3},{4,20},{20... | collective-permute-start | bytes 393224 | tf_op jit(solution)/shard_map/ppermute | solution.py:440
  16.2 0.0 collective-permute-done.1.refs_1_
  16.2 1.2 %far_inner.1 = (bf16[128,512]{1,0:T(8,128)(2,1)S(1)}, bf16[128,1024]{1,0:T(8,128)(2,1)S(1)}) custom-call(f32[2,8,1024]{2,1,0:T(8,128)S(1)} %get-tuple-element.23.refs_0_.refs_1_.held, bf16[128,1024]{1,0:T(8,128)(2,1)S(1)} %collective-permute-done.1.refs_1_, bf16[1024,1536]{1,0:T(8,128)(2,1)S(1)} %copy-done.1, f32[2,64]{1,0:T(2,128)S(1)} %copy-done.6, ...), custom_call_target="tpu_custom_call" | custom-call | flops 40000000 | bytes 120000 | tf_op jit(solution)/shard_map/far_inner/pallas_call | solution.py:446
  17.5 0.9 %collective-permute-start.4 = (bf16[128,512]{1,0:T(8,128)(2,1)S(1)}, bf16[128,512]{1,0:T(8,128)(2,1)S(1)}, u32[]{:S(2)}, u32[]{:S(2)}) collective-permute-start(bf16[128,512]{1,0:T(8,128)(2,1)S(1)} %get-tuple-element.29.inner), channel_id=1, source_target_pairs={{0,16},{16,0},{1,17},{17,1},{2,18},{18,2},{3,19},{19,3},{4,20},{20... | collective-permute-start | bytes 393224 | tf_op jit(solution)/shard_map/ppermute | solution.py:440
  18.4 0.0 collective-permute-done.2.refs_2_
  18.4 1.3 %far_outer.1 = (bf16[128,512]{1,0:T(8,128)(2,1)S(1)}, bf16[128,512]{1,0:T(8,128)(2,1)S(1)}) custom-call(bf16[128,512]{1,0:T(8,128)(2,1)S(1)} %get-tuple-element.30.refs_0_.refs_6_, f32[2,8,1024]{2,1,0:T(8,128)S(1)} %get-tuple-element.23.refs_0_.refs_1_.held, bf16[128,1024]{1,0:T(8,128)(2,1)S(1)} %collective-permute-done.2.refs_2_, ...), custom_call_target="tpu_custom_call" | custom-call | flops 6000000 | bytes 18000 | tf_op jit(solution)/shard_map/far_outer/pallas_call | solution.py:446
  19.6 0.0 copy-start.3
  19.7 1.3 %collective-permute-start.6 = (bf16[128,512]{1,0:T(8,128)(2,1)S(1)}, bf16[128,512]{1,0:T(8,128)(2,1)S(1)}, u32[]{:S(2)}, u32[]{:S(2)}) collective-permute-start(bf16[128,512]{1,0:T(8,128)(2,1)S(1)} %get-tuple-element.33.outer), channel_id=1, source_target_pairs={{0,16},{16,0},{1,17},{17,1},{2,18},{18,2},{3,19},{19,3},{4,20},{20... | collective-permute-start | bytes 393224 | tf_op jit(solution)/shard_map/ppermute | solution.py:440
  20.9 0.8 %collective-permute-start.7 = (bf16[128,512]{1,0:T(8,128)(2,1)S(1)}, bf16[128,512]{1,0:T(8,128)(2,1)S(1)}, u32[]{:S(2)}, u32[]{:S(2)}) collective-permute-start(bf16[128,512]{1,0:T(8,128)(2,1)S(1)} %get-tuple-element.40), channel_id=1, source_target_pairs={{0,16},{16,0},{1,17},{17,1},{2,18},{18,2},{3,19},{19,3},{4,20},{20... | collective-permute-start | bytes 393224 | tf_op jit(solution)/shard_map/ppermute | solution.py:440
  21.7 0.0 collective-permute-done.3.refs_0_.refs_1_
  21.7 2.0 %own.1 = (bf16[256,1024]{1,0:T(8,128)(2,1)S(1)}, bf16[256,512]{1,0:T(8,128)(2,1)S(1)}, bf16[256,1024]{1,0:T(8,128)(2,1)S(1)}) custom-call(f32[2,8,1024]{2,1,0:T(8,128)S(1)} %get-tuple-element.23.refs_0_.refs_1_.held, bf16[256,1024]{1,0:T(8,128)(2,1)S(1)} %split.1.late_rows.frames, bf16[128,512]{1,0:T(8,128)(2,1)S(1)} %get-tuple-element.29.inner, ...), custom_call_target="tpu_custom_call" | custom-call | flops 20000000 | bytes 60000 | tf_op jit(solution)/shard_map/own/pallas_call | solution.py:446
  23.7 0.3 collective-permute-done.4.refs_4_
  24.0 1.6 %inner.1._.refs_1_ = bf16[128,1024]{1,0:T(8,128)(2,1)S(1)} custom-call(f32[2,8,1024]{2,1,0:T(8,128)S(1)} %get-tuple-element.23.refs_0_.refs_1_.held, bf16[256,1024]{1,0:T(8,128)(2,1)S(1)} %get-tuple-element.35.refs_1_, bf16[256,512]{1,0:T(8,128)(2,1)S(1)} %get-tuple-element.36.refs_2_, bf16[256,1024]{1,0:T(8,128)(2,1)S(1)} %get-tuple-element.37.refs_3_, ...), custom_call_target="tpu_custom_call" | custom-call | flops 40000000 | bytes 120000 | tf_op jit(solution)/shard_map/inner/pallas_call | solution.py:446
  25.6 0.3 %weights.1._.refs_5_ = bf16[2,128,512]{2,1,0:T(8,128)(2,1)S(1)} custom-call(bf16[128,1024]{1,0:T(8,128)(2,1)S(1)} %inner.1._.refs_1_, bf16[128,512]{1,0:T(8,128)(2,1)S(1)} %get-tuple-element.38.query, bf16[128,512]{1,0:T(8,128)(2,1)S(1)} %get-tuple-element.34.refs_0_, bf16[128,512]{1,0:T(8,128)(2,1)S(1)} %collective-permute-done.3.refs_0_.refs_1_), custom_call_target="tpu_custom_call" | custom-call | flops 20000000 | bytes 60000 | tf_op jit(solution)/shard_map/weights/pallas_call | solution.py:446
  25.9 0.9 %collective-permute-done.6.refs_4_ = bf16[128,512]{1,0:T(8,128)(2,1)S(1)} collective-permute-done((bf16[128,512]{1,0:T(8,128)(2,1)S(1)}, bf16[128,512]{1,0:T(8,128)(2,1)S(1)}, u32[]{:S(2)}, u32[]{:S(2)}) %collective-permute-start.6) | collective-permute-done | bytes 131104 | tf_op jit(solution)/shard_map/ppermute | solution.py:440
  26.8 1.6 %outer.1.refs_2_ = bf16[128,1024]{1,0:T(8,128)(2,1)S(1)} custom-call(bf16[2,128,512]{2,1,0:T(8,128)(2,1)S(1)} %weights.1._.refs_5_, f32[2,8,1024]{2,1,0:T(8,128)S(1)} %get-tuple-element.23.refs_0_.refs_1_.held, bf16[256,1024]{1,0:T(8,128)(2,1)S(1)} %get-tuple-element.35.refs_1_, bf16[256,512]{1,0:T(8,128)(2,1)S(1)} %get-tuple-element.36.refs_2_, ...), custom_call_target="tpu_custom_call" | custom-call | flops 40000000 | bytes 120000 | tf_op jit(solution)/shard_map/outer/pallas_call | solution.py:446
  28.4 0.1 collective-permute-done.7.refs_7_
  28.4 1.0 %early.1 = bf16[1,384,1024]{2,1,0:T(8,128)(2,1)} custom-call(f32[2,8,1024]{2,1,0:T(8,128)S(1)} %get-tuple-element.23.refs_0_.refs_1_.held, bf16[128,1024]{1,0:T(8,128)(2,1)S(1)} %inner.1._.refs_1_, bf16[128,1024]{1,0:T(8,128)(2,1)S(1)} %outer.1.refs_2_, bf16[512,1024]{1,0:T(8,128)(2,1)S(1)} %copy-done.3, bf16[128,1024]{1,0:T(8,128)(2,1)S(1)} %get-tuple-element.39.refs_4_, ...), custom_call_target="tpu_custom_call" | custom-call | flops 2000000000 | bytes 6000000 | tf_op jit(solution)/shard_map/early/pallas_call | solution.py:446
  (18 shorter events, 0.1 us)
Async XLA Ops:
  0.0 7.5 %copy-start.7 = (s32[2]{0:T(128)S(1)}, s32[2]{0:T(128)}, u32[]{:S(2)}) copy-start(s32[2]{0:T(128)} %param.10) | copy-start | bytes 28
  0.0 7.5 %copy-start.4 = (f32[50,6,1024]{2,0,1:T(8,128)S(1)}, f32[50,6,1024]{2,0,1:T(8,128)}, u32[]{:S(2)}) copy-start(f32[50,6,1024]{2,0,1:T(8,128)} %param.11) | copy-start | bytes 3686404
  0.0 7.5 %copy-start.1 = (bf16[1024,1536]{1,0:T(8,128)(2,1)S(1)}, bf16[1024,1536]{1,0:T(8,128)(2,1)}, u32[]{:S(2)}) copy-start(bf16[1024,1536]{1,0:T(8,128)(2,1)} %refs_3_.4) | copy-start | bytes 9437188
  0.0 7.5 %copy-start.2 = (bf16[512,1024]{1,0:T(8,128)(2,1)S(1)}, bf16[512,1024]{1,0:T(8,128)(2,1)}, u32[]{:S(2)}) copy-start(bf16[512,1024]{1,0:T(8,128)(2,1)} %refs_6_.3) | copy-start | bytes 3145732
  0.0 7.5 %copy-start.6 = (f32[2,64]{1,0:T(2,128)S(1)}, f32[2,64]{1,0:T(2,128)}, u32[]{:S(2)}) copy-start(f32[2,64]{1,0:T(2,128)} %refs_4_.1) | copy-start | bytes 1540
  0.0 7.5 %copy-start = (bf16[1024,1536]{1,0:T(8,128)(2,1)S(1)}, bf16[1024,1536]{1,0:T(8,128)(2,1)}, u32[]{:S(2)}) copy-start(bf16[1024,1536]{1,0:T(8,128)(2,1)} %refs_7_.3) | copy-start | bytes 9437188
  0.0 7.5 %copy-start.5 = (f32[2,64]{1,0:T(2,128)S(1)}, f32[2,64]{1,0:T(2,128)}, u32[]{:S(2)}) copy-start(f32[2,64]{1,0:T(2,128)} %refs_8_.3) | copy-start | bytes 1540
  0.0 4.3 %collective-permute-start = (bf16[1,384,1024]{2,1,0:T(8,128)(2,1)}, bf16[1,384,1024]{2,1,0:T(8,128)(2,1)S(1)}, u32[]{:S(2)}, u32[]{:S(2)}) collective-permute-start(bf16[1,384,1024]{2,1,0:T(8,128)(2,1)} %frames.3), channel_id=1, source_target_pairs={{0,1},{1,0},{2,3},{3,2},{4,5},{5,4},{6,7},{7,6},{8,9},{9,8},{10,11... | collective-permute-start | bytes 2359304 | tf_op jit(solution)/shard_map/ppermute | solution.py:464
  1.9 21.8 %collective-permute-start.5 = (bf16[256,1024]{1,0:T(8,128)(2,1)S(1)}, bf16[256,1024]{1,0:T(8,128)(2,1)S(1)}, u32[]{:S(2)}, u32[]{:S(2)}) collective-permute-start(bf16[256,1024]{1,0:T(8,128)(2,1)S(1)} %split.1.late_rows.frames), channel_id=1, source_target_pairs={{0,16},{16,0},{1,17},{17,1},{2,18},{18,2},{3,19},{19,3},{4,20},{20... | collective-permute-start | bytes 1572872 | tf_op jit(solution)/shard_map/ppermute | solution.py:440
  4.4 11.8 %collective-permute-start.1 = (bf16[128,1024]{1,0:T(8,128)(2,1)S(1)}, bf16[128,1024]{1,0:T(8,128)(2,1)S(1)}, u32[]{:S(2)}, u32[]{:S(2)}) collective-permute-start(bf16[128,1024]{1,0:T(8,128)(2,1)S(1)} %get-tuple-element.24), channel_id=1, source_target_pairs={{0,2},{2,4},{4,6},{6,8},{8,10},{10,12},{12,14},{3,1},{5,3},{7,5},{... | collective-permute-start | bytes 786440 | tf_op jit(solution)/shard_map/ppermute | solution.py:466
  6.0 12.4 %collective-permute-start.2 = (bf16[128,1024]{1,0:T(8,128)(2,1)S(1)}, bf16[128,1024]{1,0:T(8,128)(2,1)S(1)}, u32[]{:S(2)}, u32[]{:S(2)}) collective-permute-start(bf16[128,1024]{1,0:T(8,128)(2,1)S(1)} %get-tuple-element.31), channel_id=1, source_target_pairs={{0,2},{2,4},{4,6},{6,8},{8,10},{10,12},{12,14},{3,1},{5,3},{7,5},{... | collective-permute-start | bytes 786440 | tf_op jit(solution)/shard_map/ppermute | solution.py:467
  15.0 6.8 %collective-permute-start.3 = (bf16[128,512]{1,0:T(8,128)(2,1)S(1)}, bf16[128,512]{1,0:T(8,128)(2,1)S(1)}, u32[]{:S(2)}, u32[]{:S(2)}) collective-permute-start(bf16[128,512]{1,0:T(8,128)(2,1)S(1)} %get-tuple-element.34.refs_0_), channel_id=1, source_target_pairs={{0,16},{16,0},{1,17},{17,1},{2,18},{18,2},{3,19},{19,3},{4,20},{20... | collective-permute-start | bytes 393224 | tf_op jit(solution)/shard_map/ppermute | solution.py:440
  17.5 6.5 %collective-permute-start.4 = (bf16[128,512]{1,0:T(8,128)(2,1)S(1)}, bf16[128,512]{1,0:T(8,128)(2,1)S(1)}, u32[]{:S(2)}, u32[]{:S(2)}) collective-permute-start(bf16[128,512]{1,0:T(8,128)(2,1)S(1)} %get-tuple-element.29.inner), channel_id=1, source_target_pairs={{0,16},{16,0},{1,17},{17,1},{2,18},{18,2},{3,19},{19,3},{4,20},{20... | collective-permute-start | bytes 393224 | tf_op jit(solution)/shard_map/ppermute | solution.py:440
  19.6 4.4 %copy-start.3 = (bf16[512,1024]{1,0:T(8,128)(2,1)S(1)}, bf16[512,1024]{1,0:T(8,128)(2,1)}, u32[]{:S(2)}) copy-start(bf16[512,1024]{1,0:T(8,128)(2,1)} %refs_3_.5) | copy-start | bytes 3145732
  19.7 7.1 %collective-permute-start.6 = (bf16[128,512]{1,0:T(8,128)(2,1)S(1)}, bf16[128,512]{1,0:T(8,128)(2,1)S(1)}, u32[]{:S(2)}, u32[]{:S(2)}) collective-permute-start(bf16[128,512]{1,0:T(8,128)(2,1)S(1)} %get-tuple-element.33.outer), channel_id=1, source_target_pairs={{0,16},{16,0},{1,17},{17,1},{2,18},{18,2},{3,19},{19,3},{4,20},{20... | collective-permute-start | bytes 393224 | tf_op jit(solution)/shard_map/ppermute | solution.py:440
  20.9 7.5 %collective-permute-start.7 = (bf16[128,512]{1,0:T(8,128)(2,1)S(1)}, bf16[128,512]{1,0:T(8,128)(2,1)S(1)}, u32[]{:S(2)}, u32[]{:S(2)}) collective-permute-start(bf16[128,512]{1,0:T(8,128)(2,1)S(1)} %get-tuple-element.40), channel_id=1, source_target_pairs={{0,16},{16,0},{1,17},{17,1},{2,18},{18,2},{3,19},{19,3},{4,20},{20... | collective-permute-start | bytes 393224 | tf_op jit(solution)/shard_map/ppermute | solution.py:440
